TPU v7x, 32 devices: a whole 2x2x4 slice. The times are simulated.
32 devices in a mesh: groups: 2 (over y), fsdp: 4 (over z), tp: 4 (over x, core).
Axes of the slice: x: 2, y: 2, z: 4, core: 2. Of those that a mesh axis runs over, the one named last changes fastest.
Arguments:
- activations: bfloat16 [1024, 8192], P(('groups', 'fsdp'), 'tp'), parts along dimension 0, may hold values from -6 to 6
- key_value_weight: bfloat16 [2048, 8192], P('fsdp', 'tp'), may hold values from -0.0625 to 0.0625
- token_adapter_index: int32 [1024, 1], P(('groups', 'fsdp')), parts along dimension 0, may hold values from 0 to 3; in each aligned block of 128 rows (0 to 127, 128 to 255, ...) at most 64 rows name the same one
- adapter_down_weight: bfloat16 [4, 64, 8192], P('fsdp', None, 'tp'), may hold values from -0.0625 to 0.0625
- adapter_up_weight: bfloat16 [4, 64, 2048], P('fsdp', None, 'tp'), may hold values from -0.19921875 to 0.19921875
- cotangent: bfloat16 [1024, 2048], P(('groups', 'fsdp'), 'tp'), parts along dimension 0, may hold values from -6 to 6
Outputs:
- key_value_output: bfloat16 [1024, 2048], P(('groups', 'fsdp'), 'tp'), parts along dimension 0
- input_gradient: bfloat16 [1024, 8192], P(('groups', 'fsdp'), 'tp'), parts along dimension 0
- grad_down: float32 [8, 64, 8192], P(('groups', 'fsdp'), None, 'tp'), parts along dimension 0
- up_gradient: float32 [8, 64, 2048], P(('groups', 'fsdp'), None, 'tp'), parts along dimension 0
There are 2 independent parts, one for each index of `groups`. A program takes and returns all parts, laid end to end along the dimension named above; an argument that names none is the same for every part. Nothing has to cross between parts.
Inputs may be any that keep to these rules, and one draw needn't show every extreme that they name: `token_adapter_index`: among the 128 tokens of one index of fsdp no adapter appears more than 64 times.
All inputs are finite; a program needn't handle non-finite values.
Results may differ from a plain program's by a relative error of at most 0.013.
Values may be sent and summed in bfloat16 or wider, within the bound.
No kernel may reach another device: no remote copies, remote signals or barrier semaphores. Data moves between devices by JAX's collectives and lax.ppermute only.
A program may use at most 64 MiB of HBM per device.

v0:
```python
import jax
import jax.numpy as jnp
from jax import lax
from jax.sharding import PartitionSpec as P

adapter_scale = 2.0


def placement_matrix(token_adapter_index, adapter_holders, slot_capacity):
    owner_of = token_adapter_index[:, 0]
    shard_member = (
        owner_of[:, None] == jnp.arange(adapter_holders, dtype=jnp.int32)[None, :]
    ).astype(jnp.int32)
    earlier = jnp.cumsum(shard_member, axis=0) - shard_member
    within = jnp.sum(earlier * shard_member, axis=1)
    target = owner_of * slot_capacity + within
    return (
        jnp.arange(adapter_holders * slot_capacity, dtype=jnp.int32)[:, None] == target[None, :]
    ).astype(jnp.bfloat16)


def pack_rows(placing, values, adapter_holders):
    packed = jnp.dot(placing, values, preferred_element_type=jnp.float32).astype(jnp.bfloat16)
    return packed.reshape(adapter_holders, -1, values.shape[1])


def unpack_rows(placing, returned):
    flat = returned.reshape(-1, returned.shape[2])
    return jnp.einsum("st,sk->tk", placing, flat, preferred_element_type=jnp.float32)


def per_device(
    activations,
    key_value_weight,
    token_adapter_index,
    adapter_down_weight,
    adapter_up_weight,
    cotangent,
):
    adapter_holders = lax.axis_size("fsdp")
    tok_rows = activations.shape[0]
    slot_capacity = 2 * tok_rows // adapter_holders
    feature_width = activations.shape[1]
    output_width = cotangent.shape[1]
    placing = placement_matrix(token_adapter_index, adapter_holders, slot_capacity)
    down_resident = adapter_down_weight[0]
    up_resident = adapter_up_weight[0]
    whole_cot = lax.all_gather(cotangent, "tp", axis=1, tiled=True)
    partial_value = jnp.dot(
        activations,
        lax.all_gather(key_value_weight, "fsdp", axis=0, tiled=True).T,
        preferred_element_type=jnp.float32,
    )
    base_gradient = jnp.dot(
        whole_cot,
        lax.all_gather(key_value_weight, "fsdp", axis=0, tiled=True),
        preferred_element_type=jnp.float32,
    )
    base_output = lax.psum_scatter(
        partial_value.astype(jnp.bfloat16), "tp", scatter_dimension=1, tiled=True
    ).astype(jnp.float32)
    rows_send = pack_rows(placing, activations, adapter_holders)
    cot_send = pack_rows(placing, cotangent, adapter_holders)
    rows_recv = lax.all_to_all(rows_send, "fsdp", split_axis=0, concat_axis=0, tiled=True)
    rows_flat = rows_recv.reshape(-1, feature_width)
    low_part = jnp.dot(rows_flat, down_resident.T, preferred_element_type=jnp.float32)
    rank_activation = lax.psum(low_part.astype(jnp.bfloat16), "tp")
    adapter_output = (
        adapter_scale * jnp.dot(rank_activation, up_resident, preferred_element_type=jnp.float32)
    ).astype(jnp.bfloat16)
    out_back = lax.all_to_all(
        adapter_output.reshape(adapter_holders, slot_capacity, output_width),
        "fsdp",
        split_axis=0,
        concat_axis=0,
        tiled=True,
    )
    cot_recv = lax.all_to_all(cot_send, "fsdp", split_axis=0, concat_axis=0, tiled=True)
    flat_output_gradient = cot_recv.reshape(-1, output_width)
    backward_piece = adapter_scale * jnp.dot(
        flat_output_gradient, up_resident.T, preferred_element_type=jnp.float32
    )
    backward_result = lax.psum(backward_piece.astype(jnp.bfloat16), "tp")
    adapter_input = jnp.dot(
        backward_result, down_resident, preferred_element_type=jnp.float32
    ).astype(jnp.bfloat16)
    in_back = lax.all_to_all(
        adapter_input.reshape(adapter_holders, slot_capacity, feature_width),
        "fsdp",
        split_axis=0,
        concat_axis=0,
        tiled=True,
    )
    grad_down = jnp.einsum(
        "sr,sd->rd", backward_result, rows_flat, preferred_element_type=jnp.float32
    )
    up_gradient = adapter_scale * jnp.einsum(
        "sr,sk->rk", rank_activation, flat_output_gradient, preferred_element_type=jnp.float32
    )
    key_value_output = (base_output + unpack_rows(placing, out_back)).astype(jnp.bfloat16)
    input_gradient = (base_gradient + unpack_rows(placing, in_back)).astype(jnp.bfloat16)
    return (key_value_output, input_gradient, grad_down[None], up_gradient[None])


def solution(mesh):
    return jax.shard_map(
        per_device,
        mesh=mesh,
        in_specs=(
            P(("groups", "fsdp"), "tp"),
            P("fsdp", "tp"),
            P(("groups", "fsdp"), None),
            P("fsdp", None, "tp"),
            P("fsdp", None, "tp"),
            P(("groups", "fsdp"), "tp"),
        ),
        out_specs=(
            P(("groups", "fsdp"), "tp"),
            P(("groups", "fsdp"), "tp"),
            P(("groups", "fsdp"), None, "tp"),
            P(("groups", "fsdp"), None, "tp"),
        ),
        check_vma=False,
    )
```

profile of v0, /device:TPU:0, one launch (start us, length us, event | category | flops | bytes accessed | tf_op | source)
XLA Modules:
  0.0 266.8 jit_solution(4228696527592676704)
XLA Ops:
  8.0 0.0 copy-start
  8.0 0.0 copy-start.2
  8.0 0.0 copy-start.1
  8.0 0.8 fusion.13
  8.9 0.2 reduce_window_sum.11
  9.0 0.8 select_reduce_fusion
  9.9 0.7 multiply_add_fusion
  10.5 1.8 convolution_convert_fusion.3
  12.3 6.3 %all-to-all-start.2 = ((bf16[4,64,512]{2,1,0:T(8,128)(2,1)}), bf16[4,64,512]{2,1,0:T(8,128)(2,1)S(1)}, u32[]{:S(2)}, u32[]{:S(2)}) async-start(bf16[4,64,512]{2,1,0:T(8,128)(2,1)} %bitcast.7), calls=%async_computation.3 | async-start | bytes 524288 | tf_op jit(solution)/shard_map/all_to_all | solution.py:78
  18.7 0.0 copy-done
  18.7 1.4 convolution_convert_fusion
  20.1 7.5 %all-to-all-done.2 = bf16[4,64,512]{2,1,0:T(8,128)(2,1)S(1)} async-done(((bf16[4,64,512]{2,1,0:T(8,128)(2,1)}), bf16[4,64,512]{2,1,0:T(8,128)(2,1)S(1)}, u32[]{:S(2)}, u32[]{:S(2)}) %all-to-all-start.2) | async-done | bytes 262176 | tf_op jit(solution)/shard_map/all_to_all | solution.py:78
  27.6 3.5 %all-to-all-start = ((bf16[4,64,2048]{2,1,0:T(8,128)(2,1)}), bf16[4,64,2048]{2,1,0:T(8,128)(2,1)S(1)}, u32[]{:S(2)}, u32[]{:S(2)}) async-start(bf16[4,64,2048]{2,1,0:T(8,128)(2,1)} %bitcast.1), calls=%async_computation.1 | async-start | bytes 2097152 | tf_op jit(solution)/shard_map/all_to_all | solution.py:64
  31.1 0.0 all-reduce.3.cloned.1.call-start
  31.2 1.7 fusion.4
  32.8 22.6 %all-to-all-done = bf16[4,64,2048]{2,1,0:T(8,128)(2,1)S(1)} async-done(((bf16[4,64,2048]{2,1,0:T(8,128)(2,1)}), bf16[4,64,2048]{2,1,0:T(8,128)(2,1)S(1)}, u32[]{:S(2)}, u32[]{:S(2)}) %all-to-all-start) | async-done | bytes 1048608 | tf_op jit(solution)/shard_map/all_to_all | solution.py:64
  55.4 2.0 convolution_convert_fusion.4
  57.5 0.0 all-reduce.3.cloned.1.call-update
  57.5 0.0 all-gather.2.cloned.1.call-start
  57.5 0.5 all-gather.2.cloned.1.call-update
  58.1 29.9 %all-reduce.3.cloned.1.call-done = (bf16[256,64]{0,1:T(8,128)(2,1)}, bf16[256,64]{0,1:T(8,128)(2,1)}) async-done(((bf16[256,64]{0,1:T(8,128)(2,1)}, bf16[256,64]{0,1:T(8,128)(2,1)}), (bf16[256,64]{0,1:T(8,128)(2,1)}, bf16[256,64]{0,1:T(8,128)(2,1)})) %all-reduce.3.cloned.1.call-update) | async-done | bytes 65552 | tf_op jit(solution)/shard_map/psum | solution.py:67
  88.0 0.0 copy-done.1
  88.0 2.3 convolution_convert_fusion.1
  90.3 4.6 %all-to-all-start.3 = ((bf16[4,64,2048]{2,1,0:T(8,128)(2,1)}), bf16[4,64,2048]{2,1,0:T(8,128)(2,1)S(1)}, u32[]{:S(2)}, u32[]{:S(2)}) async-start(bf16[4,64,2048]{2,1,0:T(8,128)(2,1)} %bitcast.43), calls=%async_computation.4 | async-start | bytes 2097152 | tf_op jit(solution)/shard_map/all_to_all | solution.py:87
  94.8 0.0 reduce-scatter.2.cloned.1.call-start
  94.8 0.0 copy-done.2
  94.8 6.5 %all_gather.8 = bf16[128,2048]{1,0:T(8,128)(2,1)S(1)} all-gather(bf16[128,512]{1,0:T(8,128)(2,1)S(1)} %copy-done.2), channel_id=1, replica_groups=mesh['groups'=2,'fsdp'=4,'tp'=4] {'tp'}, dimensions={1}, use_global_device_ids=true | all-gather | bytes 655360 | tf_op jit(solution)/shard_map/all_gather | solution.py:48
  101.3 0.0 copy-start.3
  101.3 1.7 fusion.3
  103.0 1.9 convolution_bitcast_fusion
  104.8 125.7 %all-gather.2.cloned.1.call-done = bf16[2048,2048]{1,0:T(8,128)(2,1)} async-done(((bf16[512,2048]{1,0:T(8,128)(2,1)}), bf16[2048,2048]{1,0:T(8,128)(2,1)}) %all-gather.2.cloned.1.call-update) | async-done | bytes 8388624 | tf_op jit(solution)/shard_map/all_gather | solution.py:51
  230.6 7.1 %convolution_convert_fusion.2 = bf16[128,2048]{1,0:T(8,128)(2,1)} fusion(bf16[128,2048]{1,0:T(8,128)(2,1)S(1)} %copy-done, bf16[2048,2048]{1,0:T(8,128)(2,1)} %all-gather.2.cloned.1.call-done), kind=kOutput, calls=%fused_computation.3 | convolution fusion | flops 1074003968 | bytes 9437184 | tf_op jit(solution)/shard_map/dot_general | solution.py:49
  237.6 0.0 reduce-scatter.2.cloned.1.call-update
  237.6 0.0 copy-done.3
  237.7 1.8 fusion.1
  239.5 0.0 all-to-all-done.3
  239.5 3.4 %all-to-all-start.1 = ((bf16[4,64,512]{2,1,0:T(8,128)(2,1)}), bf16[4,64,512]{2,1,0:T(8,128)(2,1)S(1)}, u32[]{:S(2)}, u32[]{:S(2)}) async-start(bf16[4,64,512]{2,1,0:T(8,128)(2,1)} %bitcast.5), calls=%async_computation.2 | async-start | bytes 524288 | tf_op jit(solution)/shard_map/all_to_all | solution.py:71
  242.9 4.7 %fusion.14 = f32[128,2048]{1,0:T(8,128)S(1)} fusion(bf16[128,2048]{1,0:T(8,128)(2,1)S(1)} %all_gather.8, bf16[2048,2048]{1,0:T(8,128)(2,1)} %all-gather.2.cloned.1.call-done), kind=kOutput, calls=%fused_computation.29 | convolution fusion | flops 1073741824 | bytes 9961472 | tf_op jit(solution)/shard_map/dot_general | solution.py:54
  247.6 1.2 fusion
  248.8 3.5 %all-to-all-done.1 = bf16[4,64,512]{2,1,0:T(8,128)(2,1)S(1)} async-done(((bf16[4,64,512]{2,1,0:T(8,128)(2,1)}), bf16[4,64,512]{2,1,0:T(8,128)(2,1)S(1)}, u32[]{:S(2)}, u32[]{:S(2)}) %all-to-all-start.1) | async-done | bytes 262176 | tf_op jit(solution)/shard_map/all_to_all | solution.py:71
  252.2 5.4 %reduce-scatter.2.cloned.1.call-done = bf16[128,512]{1,0:T(8,128)(2,1)} async-done(((bf16[128,2048]{1,0:T(8,128)(2,1)}), bf16[128,512]{1,0:T(8,128)(2,1)}) %reduce-scatter.2.cloned.1.call-update) | async-done | bytes 131088 | tf_op jit(solution)/shard_map/reduce_scatter | solution.py:59
  257.6 1.8 fusion.2
Async XLA Ops:
  8.0 10.7 %copy-start = (bf16[128,2048]{1,0:T(8,128)(2,1)S(1)}, bf16[128,2048]{1,0:T(8,128)(2,1)}, u32[]{:S(2)}) copy-start(bf16[128,2048]{1,0:T(8,128)(2,1)} %param.6) | copy-start | bytes 1572868
  8.0 86.8 %copy-start.2 = (bf16[128,512]{1,0:T(8,128)(2,1)S(1)}, bf16[128,512]{1,0:T(8,128)(2,1)}, u32[]{:S(2)}) copy-start(bf16[128,512]{1,0:T(8,128)(2,1)} %param.11) | copy-start | bytes 393220
  8.0 80.0 %copy-start.1 = (bf16[1,64,2048]{2,1,0:T(8,128)(2,1)S(1)}, bf16[1,64,2048]{2,1,0:T(8,128)(2,1)}, u32[]{:S(2)}) copy-start(bf16[1,64,2048]{2,1,0:T(8,128)(2,1)} %param.9) | copy-start | bytes 786436
  12.3 15.2 %all-to-all-start.2 = ((bf16[4,64,512]{2,1,0:T(8,128)(2,1)}), bf16[4,64,512]{2,1,0:T(8,128)(2,1)S(1)}, u32[]{:S(2)}, u32[]{:S(2)}) async-start(bf16[4,64,512]{2,1,0:T(8,128)(2,1)} %bitcast.7), calls=%async_computation.3 | async-start | bytes 524288 | tf_op jit(solution)/shard_map/all_to_all | solution.py:78
  27.6 27.9 %all-to-all-start = ((bf16[4,64,2048]{2,1,0:T(8,128)(2,1)}), bf16[4,64,2048]{2,1,0:T(8,128)(2,1)S(1)}, u32[]{:S(2)}, u32[]{:S(2)}) async-start(bf16[4,64,2048]{2,1,0:T(8,128)(2,1)} %bitcast.1), calls=%async_computation.1 | async-start | bytes 2097152 | tf_op jit(solution)/shard_map/all_to_all | solution.py:64
  31.1 56.9 %all-reduce.3.cloned.1.call-start = ((), (), s32[]{:S(2)}) async-start(), calls=%async_computation.7 | async-start | bytes 131072 | tf_op jit(solution)/shard_map/psum | solution.py:67
  57.5 173.1 %all-gather.2.cloned.1.call-start = ((), (), s32[]{:S(2)}) async-start(), calls=%async_computation.5 | async-start | bytes 10485760 | tf_op jit(solution)/shard_map/all_gather | solution.py:51
  90.3 149.2 %all-to-all-start.3 = ((bf16[4,64,2048]{2,1,0:T(8,128)(2,1)}), bf16[4,64,2048]{2,1,0:T(8,128)(2,1)S(1)}, u32[]{:S(2)}, u32[]{:S(2)}) async-start(bf16[4,64,2048]{2,1,0:T(8,128)(2,1)} %bitcast.43), calls=%async_computation.4 | async-start | bytes 2097152 | tf_op jit(solution)/shard_map/all_to_all | solution.py:87
  94.8 162.8 %reduce-scatter.2.cloned.1.call-start = ((), (), s32[]{:S(2)}) async-start(), calls=%async_computation.6 | async-start | bytes 655360 | tf_op jit(solution)/shard_map/reduce_scatter | solution.py:59
  101.3 136.3 %copy-start.3 = (bf16[256,64]{0,1:T(8,128)(2,1)S(1)}, bf16[256,64]{0,1:T(8,128)(2,1)}, u32[]{:S(2)}) copy-start(bf16[256,64]{0,1:T(8,128)(2,1)} %get-tuple-element.4) | copy-start | bytes 98308
  239.5 12.8 %all-to-all-start.1 = ((bf16[4,64,512]{2,1,0:T(8,128)(2,1)}), bf16[4,64,512]{2,1,0:T(8,128)(2,1)S(1)}, u32[]{:S(2)}, u32[]{:S(2)}) async-start(bf16[4,64,512]{2,1,0:T(8,128)(2,1)} %bitcast.5), calls=%async_computation.2 | async-start | bytes 524288 | tf_op jit(solution)/shard_map/all_to_all | solution.py:71
Sparse Core Ops, SparseCore 0:
  57.6 30.3 all-reduce.2
  237.8 19.7 reduce-scatter.1
Sparse Core Ops, SparseCore 1:
  59.6 170.9 all-gather.1
where the time goes:
time: 268 us; the launch traced here: 267 us
  waiting for transfers between devices  195 us (73%)
  matrix products  29.2 us (11%)
  starting transfers between devices  17.9 us (7%)
  between operations  15.6 us (6%)
  blocking collectives  6.51 us (2%)
    all_gather x1, waiting for transfers between devices, per_device(): lax.all_gather(key_value_weight, 'fsdp', axis=0, tiled=True)  126 us
    psum x1, waiting for transfers between devices, per_device(): rank_activation = lax.psum(low_part.astype(jnp.bfloat16), 'tp')  29.9 us
    all_to_all x1, waiting for transfers between devices, per_device(): lax.all_to_all(rows_send, 'fsdp', split_axis=0, concat_axis=0, tiled=True)  22.6 us
    all_to_all x1, waiting for transfers between devices, per_device(): lax.all_to_all(cot_send, 'fsdp', split_axis=0, concat_axis=0, tiled=True)  7.52 us
    dot_general x1, matrix products, per_device(): jnp.dot(activations, lax.all_gather(key_value_weight, 'fsdp', axis=0, til...  7.07 us
    all_gather x1, blocking collectives, per_device(): whole_cot = lax.all_gather(cotangent, 'tp', axis=1, tiled=True)  6.51 us
    all_to_all x1, starting transfers between devices, per_device(): lax.all_to_all(cot_send, 'fsdp', split_axis=0, concat_axis=0, tiled=True)  6.32 us
    reduce_scatter x1, waiting for transfers between devices, per_device(): lax.psum_scatter(partial_value.astype(jnp.bfloat16), 'tp', scatter_dimens...  5.39 us
  transfers between devices with their start and end apart: 7, of which 6 were waited for; matrix products, arithmetic and copies ran while one was open for 9% of the time, Pallas kernels for 0%

commit v1 on v0

--- a/solution.py
+++ b/solution.py
@@ -4,6 +4,8 @@
 from jax.sharding import PartitionSpec as P
 
 adapter_scale = 2.0
+f32 = jnp.float32
+bf16 = jnp.bfloat16
 
 
 def placement_matrix(token_adapter_index, adapter_holders, slot_capacity):
@@ -29,7 +31,7 @@
     return jnp.einsum("st,sk->tk", placing, flat, preferred_element_type=jnp.float32)
 
 
-def per_device(
+def gathered_plan(
     activations,
     key_value_weight,
     token_adapter_index,
@@ -46,16 +48,9 @@
     down_resident = adapter_down_weight[0]
     up_resident = adapter_up_weight[0]
     whole_cot = lax.all_gather(cotangent, "tp", axis=1, tiled=True)
-    partial_value = jnp.dot(
-        activations,
-        lax.all_gather(key_value_weight, "fsdp", axis=0, tiled=True).T,
-        preferred_element_type=jnp.float32,
-    )
-    base_gradient = jnp.dot(
-        whole_cot,
-        lax.all_gather(key_value_weight, "fsdp", axis=0, tiled=True),
-        preferred_element_type=jnp.float32,
-    )
+    whole_weight = lax.all_gather(key_value_weight, "fsdp", axis=0, tiled=True)
+    partial_value = jnp.dot(activations, whole_weight.T, preferred_element_type=jnp.float32)
+    base_gradient = jnp.dot(whole_cot, whole_weight, preferred_element_type=jnp.float32)
     base_output = lax.psum_scatter(
         partial_value.astype(jnp.bfloat16), "tp", scatter_dimension=1, tiled=True
     ).astype(jnp.float32)
@@ -102,9 +97,171 @@
     return (key_value_output, input_gradient, grad_down[None], up_gradient[None])
 
 
+def nn(a, b):
+    return lax.dot_general(a, b, (((1,), (0,)), ((), ())), preferred_element_type=f32)
+
+
+def nt(a, b):
+    return lax.dot_general(a, b, (((1,), (1,)), ((), ())), preferred_element_type=f32)
+
+
+def tn(a, b):
+    return lax.dot_general(a, b, (((0,), (0,)), ((), ())), preferred_element_type=f32)
+
+
+def swap(x, axis, bit):
+    return lax.ppermute(x, axis, [(i, i ^ bit) for i in range(lax.axis_size(axis))])
+
+
+def both(x, pairs):
+    flat = [(4 * a[0] + 2 * a[1] + a[2], 4 * b[0] + 2 * b[1] + b[2]) for a, b in pairs]
+    return lax.ppermute(x, ("fsdp", "tp"), flat)
+
+
+def tp_sum(part):
+    rows = part.shape[0] // 2
+    wide = jnp.concatenate([part[:rows], part[rows:]], axis=1)
+    parts = lax.all_gather(wide, "tp", axis=0)
+    total = jnp.sum(parts.astype(f32), axis=0)
+    return jnp.concatenate([total[:, : part.shape[1]], total[:, part.shape[1] :]], axis=0)
+
+
+CHUNKS = 2
+
+
+def pair_plan(
+    activations,
+    key_value_weight,
+    token_adapter_index,
+    adapter_down_weight,
+    adapter_up_weight,
+    cotangent,
+):
+    z = lax.axis_index("fsdp")
+    y = lax.axis_index("groups")
+    t = lax.axis_index("tp")
+    x, c = t // 2, t % 2
+    pair = z // 2
+    in_pair = x == pair
+    on_own = c == z % 2
+    rows, width = key_value_weight.shape
+    toks = activations.shape[0]
+    half = rows // 2
+    down = adapter_down_weight[0]
+    up = adapter_up_weight[0]
+    rank = down.shape[0]
+    places = [(zz, xx, cc) for zz in range(4) for xx in range(2) for cc in range(2)]
+
+    cot2 = jnp.concatenate([cotangent, swap(cotangent, "fsdp", 2)], axis=0)
+    index2 = jnp.concatenate([token_adapter_index, swap(token_adapter_index, "fsdp", 2)], axis=0)
+    up_sib = swap(up, "fsdp", 1)
+
+    step = width // CHUNKS
+    w_mine = lax.dynamic_slice(key_value_weight, (y * half, 0), (half, width))
+    d_mine = lax.dynamic_slice(down, (y * (rank // 2), 0), (rank // 2, width))
+    near, far = [], []
+    for k in range(CHUNKS):
+        piece = w_mine[:, k * step : (k + 1) * step]
+        if k == 0:
+            piece = jnp.concatenate(
+                [d_mine[:, j * step : (j + 1) * step] for j in range(CHUNKS)] + [piece], axis=0
+            )
+        got = swap(piece, "fsdp", 1)
+        near.append(got)
+        far.append(swap(got, "groups", 1))
+        if k == 0:
+            act2 = jnp.concatenate([activations, swap(activations, "fsdp", 2)], axis=0)
+    cut = rank // 2 * CHUNKS
+
+    def down_of(piece):
+        return jnp.concatenate(
+            [piece[j * (rank // 2) : (j + 1) * (rank // 2)] for j in range(CHUNKS)], axis=1
+        )
+
+    d_near, d_far = down_of(near[0]), down_of(far[0])
+    near[0], far[0] = near[0][cut:], far[0][cut:]
+
+    own = index2 == z
+    sib = index2 == (z ^ 1)
+    back_part = adapter_scale * jnp.where(
+        own, nt(cot2, up), jnp.where(sib, nt(cot2, up_sib), 0.0)
+    )
+    back = tp_sum(back_part.astype(bf16)).astype(bf16)
+    back_own = jnp.where(own, back, 0).astype(bf16)
+    back_sib = jnp.where(sib, back, 0).astype(bf16)
+
+    sent = both(
+        cot2, [((a, b, d), (a, 1 - b, d)) for a, b, d in places if b == a // 2]
+    )
+    block = jnp.where(in_pair, cot2, sent)
+    other = swap(block, "tp", 1)
+    c_own = jnp.where(on_own, block, other)
+    c_sib = jnp.where(on_own, other, block)
+    c_near = lax.dynamic_slice(c_sib, (0, y * half), (2 * toks, half))
+    c_far = lax.dynamic_slice(c_sib, (0, (1 - y) * half), (2 * toks, half))
+    hr = rank // 2
+    b_near = lax.dynamic_slice(back_sib, (0, y * hr), (2 * toks, hr))
+    b_far = lax.dynamic_slice(back_sib, (0, (1 - y) * hr), (2 * toks, hr))
+
+    grads = []
+    for k in range(CHUNKS):
+        cols = slice(k * step, (k + 1) * step)
+        g = (
+            nn(c_own, key_value_weight[:, cols])
+            + nn(c_near, near[k])
+            + nn(c_far, far[k])
+            + nn(back_own, down[:, cols])
+            + nn(b_near, d_near[:, cols])
+            + nn(b_far, d_far[:, cols])
+        )
+        grads.append((g[:toks] + swap(g[toks:].astype(bf16), "fsdp", 2)).astype(bf16))
+    input_gradient = jnp.concatenate(grads, axis=1)
+
+    low_far, low_near = nt(act2, d_far), nt(act2, d_near)
+    first = y == 0
+    low_sib = jnp.concatenate(
+        [jnp.where(first, low_near, low_far), jnp.where(first, low_far, low_near)], axis=1
+    )
+    low_part = jnp.where(own, nt(act2, down), jnp.where(sib, low_sib, 0.0))
+    low = tp_sum(low_part.astype(bf16)).astype(bf16)
+    low_own = jnp.where(own, low, 0).astype(bf16)
+    low_other = jnp.where(sib, low, 0).astype(bf16)
+    lora = (adapter_scale * (nn(low_own, up) + nn(low_other, up_sib))).astype(bf16)
+    lora_got = swap(lora[toks:], "fsdp", 2)
+
+    gd_sib = tn(back_sib, act2).astype(bf16)
+    gu_sib = (adapter_scale * tn(low_other, cot2)).astype(bf16)
+    got = swap(jnp.concatenate([gd_sib, gu_sib], axis=1), "fsdp", 1)
+    grad_down = tn(back_own, act2) + got[:, :width]
+    up_gradient = adapter_scale * tn(low_own, cot2) + got[:, width:]
+
+    p_own = nt(act2, key_value_weight)
+    p_near = p_far = 0.0
+    for k in range(CHUNKS):
+        cols = slice(k * step, (k + 1) * step)
+        p_near = p_near + nt(act2[:, cols], near[k])
+        p_far = p_far + nt(act2[:, cols], far[k])
+    p_sib = jnp.concatenate(
+        [jnp.where(first, p_near, p_far), jnp.where(first, p_far, p_near)], axis=1
+    )
+    keep = jnp.where(on_own, p_own, p_sib)
+    give = jnp.where(on_own, p_sib, p_own).astype(bf16)
+    held = (keep + swap(give, "tp", 1)).astype(bf16)
+    here, there = held[:toks], held[toks:]
+    one = both(
+        jnp.where(in_pair, there, here),
+        [((a, b, d), (a ^ 2, b, d) if b == a // 2 else (a, 1 - b, d)) for a, b, d in places],
+    )
+    two = both(there, [((a, b, d), (a ^ 2, 1 - b, d)) for a, b, d in places if b != a // 2])
+    base = one.astype(f32) + jnp.where(in_pair, here, two).astype(f32)
+    key_value_output = (base + lora[:toks].astype(f32) + lora_got.astype(f32)).astype(bf16)
+    return (key_value_output, input_gradient, grad_down[None], up_gradient[None])
+
+
 def solution(mesh):
+    paired = mesh.shape["fsdp"] == 4 and mesh.shape["tp"] == 4 and mesh.shape["groups"] == 2
     return jax.shard_map(
-        per_device,
+        pair_plan if paired else gathered_plan,
         mesh=mesh,
         in_specs=(
             P(("groups", "fsdp"), "tp"),

time: 268 us -> 129 us (0.48)
  the two profiles are of different devices: /device:TPU:0 before, /device:TPU:6 now
where the time goes in v1:
time: 129 us; the launch traced here: 128 us
  waiting for transfers between devices  57.1 us (44%)
  starting transfers between devices  23.5 us (18%)
  matrix products  22.7 us (18%)
  blocking collectives  11.3 us (9%)
  local copies, waits for them, and re-layouts  8.48 us (7%)
  other arithmetic  3.82 us (3%)
    ppermute x14, waiting for transfers between devices, swap(): lax.ppermute(x, axis, [(i, i ^ bit) for i in range(lax.axis_size(axis))])  56.5 us
    ppermute x14, starting transfers between devices, swap(): lax.ppermute(x, axis, [(i, i ^ bit) for i in range(lax.axis_size(axis))])  19.7 us
    dot_general x14, matrix products, nn(): lax.dot_general(a, b, (((1,), (0,)), ((), ())), preferred_element_type=f32)  12.3 us
    all_gather x2, blocking collectives, tp_sum(): parts = lax.all_gather(wide, 'tp', axis=0)  11.3 us
    dot_general x10, matrix products, nt(): lax.dot_general(a, b, (((1,), (1,)), ((), ())), preferred_element_type=f32)  7.28 us
    ppermute x3, starting transfers between devices, both(): return lax.ppermute(x, ('fsdp', 'tp'), flat)  3.79 us
    dot_general x4, matrix products, tn(): lax.dot_general(a, b, (((0,), (0,)), ((), ())), preferred_element_type=f32)  3.08 us
  transfers between devices with their start and end apart: 17, of which 8 were waited for; matrix products, arithmetic and copies ran while one was open for 21% of the time, Pallas kernels for 0%

profile of v1, /device:TPU:6, one launch (start us, length us, event | category | flops | bytes accessed | tf_op | source)
XLA Modules:
  0.0 128.1 jit_solution(6571396812047395313)
XLA Ops:
  0.7 2.7 %collective-permute-start.8 = (s32[128,1]{0,1:T(1,128)}, s32[128,1]{0,1:T(1,128)S(1)}, u32[]{:S(2)}, u32[]{:S(2)}) collective-permute-start(s32[128,1]{0,1:T(1,128)} %param.8), channel_id=1, source_target_pairs={{0,8},{4,12},{8,0},{12,4},{1,9},{5,13},{9,1},{13,5},{2,10},{6,14},... | collective-permute-start | bytes 1544 | tf_op jit(solution)/shard_map/ppermute | solution.py:113
  3.3 0.3 collective-permute-start
  3.7 0.9 dynamic-slice_bitcast_fusion
  4.6 2.1 %fusion.79 = (bf16[256,1024]{1,0:T(8,128)(2,1)}, bf16[256,1024]{1,0:T(8,128)(2,1)S(1)}) fusion(bf16[512,2048]{1,0:T(8,128)(2,1)} %param.7, s32[]{:T(128)S(6)} %select_n.131, s32[]{:T(128)S(6)} %add.114), kind=kLoop, calls=%fused_computation.134 | loop fusion | bytes 2097160 | tf_op jit(solution)/shard_map/slice | solution.py:164
  6.7 1.6 %collective-permute-start.1 = (bf16[320,1024]{1,0:T(8,128)(2,1)S(1)}, bf16[320,1024]{1,0:T(8,128)(2,1)}, u32[]{:S(2)}, u32[]{:S(2)}) collective-permute-start(bf16[320,1024]{1,0:T(8,128)(2,1)S(1)} %pad_maximum_fusion), channel_id=1, source_target_pairs={{0,4},{4,0},{8,12},{12,8},{1,5},{5,1},{9,13},{13,9},{2,6},{6,2},{1... | collective-permute-start | bytes 1966088 | tf_op jit(solution)/shard_map/ppermute | solution.py:113
  8.4 0.4 collective-permute-start.9
  8.8 2.6 %collective-permute-start.11 = (bf16[128,512]{1,0:T(8,128)(2,1)S(1)}, bf16[128,512]{1,0:T(8,128)(2,1)S(1)}, u32[]{:S(2)}, u32[]{:S(2)}) collective-permute-start(bf16[128,512]{1,0:T(8,128)(2,1)S(1)} %copy-done.15), channel_id=1, source_target_pairs={{0,8},{4,12},{8,0},{12,4},{1,9},{5,13},{9,1},{13,5},{2,10},{6,14},... | collective-permute-start | bytes 393224 | tf_op jit(solution)/shard_map/ppermute | solution.py:113
  11.5 1.6 %collective-permute-start.2 = (bf16[256,1024]{1,0:T(8,128)(2,1)}, bf16[256,1024]{1,0:T(8,128)(2,1)}, u32[]{:S(2)}, u32[]{:S(2)}) collective-permute-start(bf16[256,1024]{1,0:T(8,128)(2,1)} %get-tuple-element.4), channel_id=1, source_target_pairs={{0,4},{4,0},{8,12},{12,8},{1,5},{5,1},{9,13},{13,9},{2,6},{6,2},{1... | collective-permute-start | bytes 1572872 | tf_op jit(solution)/shard_map/ppermute | solution.py:113
  13.2 21.3 %collective-permute-done.11 = bf16[128,512]{1,0:T(8,128)(2,1)S(1)} collective-permute-done((bf16[128,512]{1,0:T(8,128)(2,1)S(1)}, bf16[128,512]{1,0:T(8,128)(2,1)S(1)}, u32[]{:S(2)}, u32[]{:S(2)}) %collective-permute-start.11) | collective-permute-done | bytes 131104 | tf_op jit(solution)/shard_map/ppermute | solution.py:113
  34.5 1.3 %collective-permute-start.12 = (bf16[256,512]{1,0:T(8,128)(2,1)S(1)}, bf16[256,512]{1,0:T(8,128)(2,1)S(1)}, u32[]{:S(2)}, u32[]{:S(2)}) collective-permute-start(bf16[256,512]{1,0:T(8,128)(2,1)S(1)} %constant_dynamic-update-slice_fusion.2), channel_id=1, source_target_pairs={{0,2},{1,3},{4,6},{5,7},{10,8},{11,9},{14,12},{15,13},{16,18},{17,... | collective-permute-start | bytes 786440 | tf_op jit(solution)/shard_map/ppermute | solution.py:118
  35.8 2.9 %collective-permute-done.9 = bf16[64,512]{1,0:T(8,128)(2,1)S(1)} collective-permute-done((bf16[64,512]{1,0:T(8,128)(2,1)S(1)}, bf16[64,512]{1,0:T(8,128)(2,1)S(1)}, u32[]{:S(2)}, u32[]{:S(2)}) %collective-permute-start.9) | collective-permute-done | bytes 65568 | tf_op jit(solution)/shard_map/ppermute | solution.py:113
  39.0 0.2 fusion.10
  39.2 5.4 %all-gather.1 = bf16[512,128]{0,1:T(8,128)(2,1)S(1)} all-gather(bf16[128,128]{0,1:T(8,128)(2,1)S(1)} %pad_maximum_fusion.6), channel_id=3, replica_groups=mesh['groups'=2,'fsdp'=4,'tp'=4] {'tp'}, dimensions={0}, use_global_device_ids=true | all-gather | bytes 163840 | tf_op jit(solution)/shard_map/all_gather | solution.py:124
  44.9 0.3 fusion.26
  45.2 1.3 %fusion.28 = f32[256,1024]{1,0:T(8,128)} fusion(bf16[64,2048]{1,0:T(8,128)(2,1)S(1)} %bitcast.39, pred[256]{0:T(512)(128)(4,1)S(1)} %get-tuple-element.27, bf16[128,64]{0,1:T(8,128)(2,1)S(1)} %get-tuple-element.17, bf16[128,64]{0,1:T(8,128)(2,1)S(1)} %get-tuple-element.16), kind=kOutput, calls=%fused_computation.60 | convolution fusion | flops 33636352 | bytes 1212928 | tf_op jit(solution)/shard_map/dot_general | solution.py:101
  46.6 0.4 collective-permute-start.13
  47.0 1.4 %collective-permute-done.2 = bf16[256,1024]{1,0:T(8,128)(2,1)} collective-permute-done((bf16[256,1024]{1,0:T(8,128)(2,1)}, bf16[256,1024]{1,0:T(8,128)(2,1)}, u32[]{:S(2)}, u32[]{:S(2)}) %collective-permute-start.2) | collective-permute-done | bytes 524320 | tf_op jit(solution)/shard_map/ppermute | solution.py:113
  48.4 0.5 collective-permute-start.4
  48.9 1.1 constant_dynamic-update-slice_fusion
  50.0 1.4 %fusion.19 = f32[256,256]{1,0:T(8,128)S(1)} fusion(bf16[256,1024]{1,0:T(8,128)(2,1)} %collective-permute-done.2, bf16[256,2048]{1,0:T(8,128)(2,1)S(1)} %constant_dynamic-update-slice_fusion), kind=kOutput, calls=%fused_computation.46 | convolution fusion | flops 134217728 | bytes 1310720 | tf_op jit(solution)/shard_map/dot_general | solution.py:105
  51.4 1.0 convolution_convert_fusion
  52.4 1.5 %collective-permute-start.3 = (bf16[320,1024]{1,0:T(8,128)(2,1)}, bf16[320,1024]{1,0:T(8,128)(2,1)S(1)}, u32[]{:S(2)}, u32[]{:S(2)}) collective-permute-start(bf16[320,1024]{1,0:T(8,128)(2,1)} %collective-permute-done.1), channel_id=1, source_target_pairs={{0,16},{16,0},{1,17},{17,1},{2,18},{18,2},{3,19},{19,3},{4,20},{20... | collective-permute-start | bytes 1966088 | tf_op jit(solution)/shard_map/ppermute | solution.py:113
  53.9 1.5 %fusion.40 = f32[256,1024]{1,0:T(8,128)S(1)} fusion(bf16[256,1024]{1,0:T(8,128)(2,1)} %collective-permute-done.2, bf16[256,512]{1,0:T(8,128)(2,1)S(1)} %broadcast_select_fusion.1, s32[]{:T(128)S(6)} %select_n.131), kind=kOutput, calls=%fused_computation.76 | convolution fusion | flops 134217728 | bytes 1703940 | tf_op jit(solution)/shard_map/dot_general | solution.py:101
  55.5 1.4 %fusion.21 = f32[256,1024]{1,0:T(8,128)S(1)} fusion(bf16[320,1024]{1,0:T(8,128)(2,1)} %collective-permute-done.1, bf16[256,512]{1,0:T(8,128)(2,1)S(1)} %broadcast_select_fusion.1, s32[]{:T(128)S(6)} %select_n.131), kind=kOutput, calls=%fused_computation.48 | convolution fusion | flops 134217728 | bytes 1703940 | tf_op jit(solution)/shard_map/dot_general | solution.py:101
  56.8 2.1 %convolution_add_fusion.11 = f32[256,256]{1,0:T(8,128)} fusion(f32[256,256]{1,0:T(8,128)S(1)} %fusion.19, bf16[320,1024]{1,0:T(8,128)(2,1)} %collective-permute-done.1, bf16[256,2048]{1,0:T(8,128)(2,1)S(1)} %constant_dynamic-update-slice_fusion), kind=kOutput, calls=%fused_computation.17 | convolution fusion | flops 134283264 | bytes 1572864 | tf_op jit(solution)/shard_map/dot_general | solution.py:105
  58.9 0.4 convolution_add_fusion.7
  59.3 0.9 fusion.80
  60.2 1.4 %convolution_add_fusion.8 = f32[256,1024]{1,0:T(8,128)} fusion(f32[256,1024]{1,0:T(8,128)S(1)} %fusion.21, bf16[512,2048]{1,0:T(8,128)(2,1)S(1)} %copy-done, bf16[256,512]{1,0:T(8,128)(2,1)S(1)} %broadcast_select_fusion, bf16[256,512]{1,0:T(8,128)(2,1)S(1)} %collective-permute-done.13, pred[]{:T(512)S(6)} %eq.35), kind=kOutput, calls=%fused_computation.12 | convolution fusion | flops 268828672 | bytes 3670017 | tf_op jit(solution)/shard_map/dot_general | solution.py:101
  61.6 1.8 %collective-permute-done.4 = bf16[256,1024]{1,0:T(8,128)(2,1)S(1)} collective-permute-done((bf16[256,1024]{1,0:T(8,128)(2,1)}, bf16[256,1024]{1,0:T(8,128)(2,1)S(1)}, u32[]{:S(2)}, u32[]{:S(2)}) %collective-permute-start.4) | collective-permute-done | bytes 524320 | tf_op jit(solution)/shard_map/ppermute | solution.py:113
  63.5 1.0 fusion.17
  64.5 0.3 fusion.1
  64.8 2.2 %convolution_add_fusion.2 = f32[256,1024]{1,0:T(8,128)} fusion(f32[256,1024]{1,0:T(8,128)S(1)} %fusion.1, bf16[256,64]{0,1:T(8,128)(2,1)S(1)} %broadcast_select_fusion.8, s32[]{:T(128)S(6)} %select_n.130, bf16[320,1024]{1,0:T(8,128)(2,1)} %collective-permute-done.1), kind=kOutput, calls=%fused_computation.4 | convolution fusion | flops 17039360 | bytes 2179076 | tf_op jit(solution)/shard_map/dot_general | solution.py:101
  67.0 8.2 %collective-permute-done.3 = bf16[320,1024]{1,0:T(8,128)(2,1)S(1)} collective-permute-done((bf16[320,1024]{1,0:T(8,128)(2,1)}, bf16[320,1024]{1,0:T(8,128)(2,1)S(1)}, u32[]{:S(2)}, u32[]{:S(2)}) %collective-permute-start.3) | collective-permute-done | bytes 655392 | tf_op jit(solution)/shard_map/ppermute | solution.py:113
  75.3 0.4 fusion.34
  75.7 0.4 broadcast_select_fusion.20
  76.1 0.5 fusion.9
  76.6 5.9 %all-gather = bf16[512,128]{0,1:T(8,128)(2,1)} all-gather(bf16[128,128]{0,1:T(8,128)(2,1)S(1)} %pad_maximum_fusion.4), channel_id=2, replica_groups=mesh['groups'=2,'fsdp'=4,'tp'=4] {'tp'}, dimensions={0}, use_global_device_ids=true | all-gather | bytes 163840 | tf_op jit(solution)/shard_map/all_gather | solution.py:124
  82.5 1.6 %reshape.45 = bf16[4,128,128]{1,0,2:T(4,128)(2,1)} reshape(bf16[512,128]{0,1:T(8,128)(2,1)} %all-gather) | data formatting | bytes 262144 | tf_op jit(solution)/shard_map/all_gather | solution.py:124
  84.1 1.7 %reduce = bf16[128,128]{0,1:T(8,128)(2,1)} reduce(bf16[4,128,128]{1,0,2:T(4,128)(2,1)} %reshape.45, bf16[]{:T(256)} %constant.65.clone.1), dimensions={0}, to_apply=%region_0.1.clone | reduce | flops 49152 | bytes 163842 | tf_op jit(solution)/shard_map/reduce_sum | solution.py:125
  85.8 0.8 fusion.86
  86.6 1.1 fusion.43
  87.9 0.3 fusion.4
  88.2 2.8 %collective-permute-start.10 = (bf16[128,512]{1,0:T(8,128)(2,1)S(1)}, bf16[128,512]{1,0:T(8,128)(2,1)S(1)}, u32[]{:S(2)}, u32[]{:S(2)}) collective-permute-start(bf16[128,512]{1,0:T(8,128)(2,1)S(1)} %slice.161), channel_id=1, source_target_pairs={{0,8},{4,12},{8,0},{12,4},{1,9},{5,13},{9,1},{13,5},{2,10},{6,14},... | collective-permute-start | bytes 393224 | tf_op jit(solution)/shard_map/ppermute | solution.py:113
  91.0 0.3 broadcast_select_fusion.4
  91.3 0.7 select_convert_fusion
  92.2 0.3 copy-done.1
  92.5 0.3 convolution_add_fusion.1
  92.9 0.3 collective-permute-start.15
  93.2 0.2 copy-done.2
  93.4 0.3 copy-done.3
  93.7 0.3 fusion.2
  94.0 1.2 convolution_add_fusion.5
  95.3 0.3 convolution_add_fusion.4
  95.6 2.2 %collective-permute-start.14 = (bf16[128,1024]{1,0:T(8,128)(2,1)S(1)}, bf16[128,1024]{1,0:T(8,128)(2,1)S(1)}, u32[]{:S(2)}, u32[]{:S(2)}) collective-permute-start(bf16[128,1024]{1,0:T(8,128)(2,1)S(1)} %slice.221), channel_id=1, source_target_pairs={{0,8},{4,12},{8,0},{12,4},{1,9},{5,13},{9,1},{13,5},{2,10},{6,14},... | collective-permute-start | bytes 786440 | tf_op jit(solution)/shard_map/ppermute | solution.py:113
  97.9 2.5 %collective-permute-start.16 = (bf16[64,2560]{1,0:T(8,128)(2,1)S(1)}, bf16[64,2560]{1,0:T(8,128)(2,1)S(1)}, u32[]{:S(2)}, u32[]{:S(2)}) collective-permute-start(bf16[64,2560]{1,0:T(8,128)(2,1)S(1)} %pad_maximum_fusion.3), channel_id=1, source_target_pairs={{0,4},{4,0},{8,12},{12,8},{1,5},{5,1},{9,13},{13,9},{2,6},{6,2},{1... | collective-permute-start | bytes 983048 | tf_op jit(solution)/shard_map/ppermute | solution.py:113
  100.6 0.6 collective-permute-start.6
  101.2 14.3 %collective-permute-done.15 = bf16[128,1024]{1,0:T(8,128)(2,1)S(1)} collective-permute-done((bf16[128,1024]{1,0:T(8,128)(2,1)S(1)}, bf16[128,1024]{1,0:T(8,128)(2,1)S(1)}, u32[]{:S(2)}, u32[]{:S(2)}) %collective-permute-start.15) | collective-permute-done | bytes 262176 | tf_op jit(solution)/shard_map/ppermute | solution.py:113
  115.5 1.9 %collective-permute-start.7 = (bf16[128,512]{1,0:T(8,128)(2,1)S(1)}, bf16[128,512]{1,0:T(8,128)(2,1)S(1)}, u32[]{:S(2)}, u32[]{:S(2)}) collective-permute-start(bf16[128,512]{1,0:T(8,128)(2,1)S(1)} %get-tuple-element.12), channel_id=1, source_target_pairs={{2,8},{3,9},{6,12},{7,13},{8,2},{9,3},{12,6},{13,7},{18,24},{19,25... | collective-permute-start | bytes 393224 | tf_op jit(solution)/shard_map/ppermute | solution.py:118
  117.5 6.4 %collective-permute-done.14 = bf16[128,1024]{1,0:T(8,128)(2,1)S(1)} collective-permute-done((bf16[128,1024]{1,0:T(8,128)(2,1)S(1)}, bf16[128,1024]{1,0:T(8,128)(2,1)S(1)}, u32[]{:S(2)}, u32[]{:S(2)}) %collective-permute-start.14) | collective-permute-done | bytes 262176 | tf_op jit(solution)/shard_map/ppermute | solution.py:113
  124.0 0.8 pad_maximum_fusion.2
  124.8 1.1 fusion
  125.9 0.8 fusion.6
  126.7 0.6 collective-permute-done.7
  127.4 0.7 add_convert_fusion.1
  (68 shorter events, 1.4 us)
Async XLA Ops:
  0.6 10.8 %copy-start.12 = (bf16[128,2048]{1,0:T(8,128)(2,1)S(1)}, bf16[128,2048]{1,0:T(8,128)(2,1)}, u32[]{:S(2)}) copy-start(bf16[128,2048]{1,0:T(8,128)(2,1)} %param.6) | copy-start | bytes 1572868
  0.6 7.7 %copy-start.14 = (bf16[1,64,512]{2,1,0:T(8,128)(2,1)S(1)}, bf16[1,64,512]{2,1,0:T(8,128)(2,1)}, u32[]{:S(2)}) copy-start(bf16[1,64,512]{2,1,0:T(8,128)(2,1)} %param.10) | copy-start | bytes 196612
  0.7 8.2 %copy-start.15 = (bf16[128,512]{1,0:T(8,128)(2,1)S(1)}, bf16[128,512]{1,0:T(8,128)(2,1)}, u32[]{:S(2)}) copy-start(bf16[128,512]{1,0:T(8,128)(2,1)} %param.11) | copy-start | bytes 393220
  0.7 10.9 %collective-permute-start.8 = (s32[128,1]{0,1:T(1,128)}, s32[128,1]{0,1:T(1,128)S(1)}, u32[]{:S(2)}, u32[]{:S(2)}) collective-permute-start(s32[128,1]{0,1:T(1,128)} %param.8), channel_id=1, source_target_pairs={{0,8},{4,12},{8,0},{12,4},{1,9},{5,13},{9,1},{13,5},{2,10},{6,14},... | collective-permute-start | bytes 1544 | tf_op jit(solution)/shard_map/ppermute | solution.py:113
  3.3 45.6 %collective-permute-start = (bf16[128,2048]{1,0:T(8,128)(2,1)}, bf16[128,2048]{1,0:T(8,128)(2,1)}, u32[]{:S(2)}, u32[]{:S(2)}) collective-permute-start(bf16[128,2048]{1,0:T(8,128)(2,1)} %param.6), channel_id=1, source_target_pairs={{0,8},{4,12},{8,0},{12,4},{1,9},{5,13},{9,1},{13,5},{2,10},{6,14},... | collective-permute-start | bytes 1572872 | tf_op jit(solution)/shard_map/ppermute | solution.py:113
  4.6 8.6 %copy-start.16 = (s32[128,1]{0,1:T(1,128)S(1)}, s32[128,1]{0,1:T(1,128)}, u32[]{:S(2)}) copy-start(s32[128,1]{0,1:T(1,128)} %param.8) | copy-start | bytes 1540
  6.7 38.2 %copy-start.8 = (bf16[1,64,2048]{2,1,0:T(8,128)(2,1)S(1)}, bf16[1,64,2048]{2,1,0:T(8,128)(2,1)}, u32[]{:S(2)}) copy-start(bf16[1,64,2048]{2,1,0:T(8,128)(2,1)} %param.9) | copy-start | bytes 786436
  6.7 45.7 %collective-permute-start.1 = (bf16[320,1024]{1,0:T(8,128)(2,1)S(1)}, bf16[320,1024]{1,0:T(8,128)(2,1)}, u32[]{:S(2)}, u32[]{:S(2)}) collective-permute-start(bf16[320,1024]{1,0:T(8,128)(2,1)S(1)} %pad_maximum_fusion), channel_id=1, source_target_pairs={{0,4},{4,0},{8,12},{12,8},{1,5},{5,1},{9,13},{13,9},{2,6},{6,2},{1... | collective-permute-start | bytes 1966088 | tf_op jit(solution)/shard_map/ppermute | solution.py:113
  8.4 30.4 %collective-permute-start.9 = (bf16[64,512]{1,0:T(8,128)(2,1)S(1)}, bf16[64,512]{1,0:T(8,128)(2,1)S(1)}, u32[]{:S(2)}, u32[]{:S(2)}) collective-permute-start(bf16[64,512]{1,0:T(8,128)(2,1)S(1)} %bitcast.40), channel_id=1, source_target_pairs={{0,4},{4,0},{8,12},{12,8},{1,5},{5,1},{9,13},{13,9},{2,6},{6,2},{1... | collective-permute-start | bytes 196616 | tf_op jit(solution)/shard_map/ppermute | solution.py:113
  8.8 25.7 %collective-permute-start.11 = (bf16[128,512]{1,0:T(8,128)(2,1)S(1)}, bf16[128,512]{1,0:T(8,128)(2,1)S(1)}, u32[]{:S(2)}, u32[]{:S(2)}) collective-permute-start(bf16[128,512]{1,0:T(8,128)(2,1)S(1)} %copy-done.15), channel_id=1, source_target_pairs={{0,8},{4,12},{8,0},{12,4},{1,9},{5,13},{9,1},{13,5},{2,10},{6,14},... | collective-permute-start | bytes 393224 | tf_op jit(solution)/shard_map/ppermute | solution.py:113
  11.5 36.9 %collective-permute-start.2 = (bf16[256,1024]{1,0:T(8,128)(2,1)}, bf16[256,1024]{1,0:T(8,128)(2,1)}, u32[]{:S(2)}, u32[]{:S(2)}) collective-permute-start(bf16[256,1024]{1,0:T(8,128)(2,1)} %get-tuple-element.4), channel_id=1, source_target_pairs={{0,4},{4,0},{8,12},{12,8},{1,5},{5,1},{9,13},{13,9},{2,6},{6,2},{1... | collective-permute-start | bytes 1572872 | tf_op jit(solution)/shard_map/ppermute | solution.py:113
  34.5 12.0 %collective-permute-start.12 = (bf16[256,512]{1,0:T(8,128)(2,1)S(1)}, bf16[256,512]{1,0:T(8,128)(2,1)S(1)}, u32[]{:S(2)}, u32[]{:S(2)}) collective-permute-start(bf16[256,512]{1,0:T(8,128)(2,1)S(1)} %constant_dynamic-update-slice_fusion.2), channel_id=1, source_target_pairs={{0,2},{1,3},{4,6},{5,7},{10,8},{11,9},{14,12},{15,13},{16,18},{17,... | collective-permute-start | bytes 786440 | tf_op jit(solution)/shard_map/ppermute | solution.py:118
  46.6 7.3 %collective-permute-start.13 = (bf16[256,512]{1,0:T(8,128)(2,1)S(1)}, bf16[256,512]{1,0:T(8,128)(2,1)S(1)}, u32[]{:S(2)}, u32[]{:S(2)}) collective-permute-start(bf16[256,512]{1,0:T(8,128)(2,1)S(1)} %broadcast_select_fusion), channel_id=1, source_target_pairs={{0,1},{1,0},{2,3},{3,2},{4,5},{5,4},{6,7},{7,6},{8,9},{9,8},{10,11... | collective-permute-start | bytes 786440 | tf_op jit(solution)/shard_map/ppermute | solution.py:113
  48.4 15.1 %collective-permute-start.4 = (bf16[256,1024]{1,0:T(8,128)(2,1)}, bf16[256,1024]{1,0:T(8,128)(2,1)S(1)}, u32[]{:S(2)}, u32[]{:S(2)}) collective-permute-start(bf16[256,1024]{1,0:T(8,128)(2,1)} %collective-permute-done.2), channel_id=1, source_target_pairs={{0,16},{16,0},{1,17},{17,1},{2,18},{18,2},{3,19},{19,3},{4,20},{20... | collective-permute-start | bytes 1572872 | tf_op jit(solution)/shard_map/ppermute | solution.py:113
  52.4 22.9 %collective-permute-start.3 = (bf16[320,1024]{1,0:T(8,128)(2,1)}, bf16[320,1024]{1,0:T(8,128)(2,1)S(1)}, u32[]{:S(2)}, u32[]{:S(2)}) collective-permute-start(bf16[320,1024]{1,0:T(8,128)(2,1)} %collective-permute-done.1), channel_id=1, source_target_pairs={{0,16},{16,0},{1,17},{17,1},{2,18},{18,2},{3,19},{19,3},{4,20},{20... | collective-permute-start | bytes 1966088 | tf_op jit(solution)/shard_map/ppermute | solution.py:113
  53.9 10.6 %copy-start.6 = (bf16[256,512]{1,0:T(8,128)(2,1)}, bf16[256,512]{1,0:T(8,128)(2,1)S(1)}, u32[]{:S(2)}) copy-start(bf16[256,512]{1,0:T(8,128)(2,1)S(1)} %broadcast_select_fusion.1) | copy-start | bytes 786436
  53.9 5.0 %copy-start = (bf16[512,2048]{1,0:T(8,128)(2,1)S(1)}, bf16[512,2048]{1,0:T(8,128)(2,1)}, u32[]{:S(2)}) copy-start(bf16[512,2048]{1,0:T(8,128)(2,1)} %param.7) | copy-start | bytes 6291460
  64.8 11.3 %copy-start.9 = (bf16[1,64,2048]{2,1,0:T(8,128)(2,1)S(1)}, bf16[1,64,2048]{2,1,0:T(8,128)(2,1)}, u32[]{:S(2)}) copy-start(bf16[1,64,2048]{2,1,0:T(8,128)(2,1)} %param.9) | copy-start | bytes 786436
  75.2 1.4 %copy-start.4 = (bf16[320,1024]{1,0:T(8,128)(2,1)}, bf16[320,1024]{1,0:T(8,128)(2,1)S(1)}, u32[]{:S(2)}) copy-start(bf16[320,1024]{1,0:T(8,128)(2,1)S(1)} %collective-permute-done.3) | copy-start | bytes 1966084
  85.8 5.2 %copy-start.5 = (bf16[320,1024]{1,0:T(8,128)(2,1)S(1)}, bf16[320,1024]{1,0:T(8,128)(2,1)}, u32[]{:S(2)}) copy-start(bf16[320,1024]{1,0:T(8,128)(2,1)} %copy-done.4) | copy-start | bytes 1966084
  85.8 5.2 %copy-start.10 = (f32[256,256]{1,0:T(8,128)S(1)}, f32[256,256]{1,0:T(8,128)}, u32[]{:S(2)}) copy-start(f32[256,256]{1,0:T(8,128)} %fusion.17) | copy-start | bytes 786436
  85.8 5.2 %copy-start.13 = (f32[256,256]{1,0:T(8,128)S(1)}, f32[256,256]{1,0:T(8,128)}, u32[]{:S(2)}) copy-start(f32[256,256]{1,0:T(8,128)} %convolution_add_fusion.11) | copy-start | bytes 786436
  88.2 38.6 %collective-permute-start.10 = (bf16[128,512]{1,0:T(8,128)(2,1)S(1)}, bf16[128,512]{1,0:T(8,128)(2,1)S(1)}, u32[]{:S(2)}, u32[]{:S(2)}) collective-permute-start(bf16[128,512]{1,0:T(8,128)(2,1)S(1)} %slice.161), channel_id=1, source_target_pairs={{0,8},{4,12},{8,0},{12,4},{1,9},{5,13},{9,1},{13,5},{2,10},{6,14},... | collective-permute-start | bytes 393224 | tf_op jit(solution)/shard_map/ppermute | solution.py:113
  91.3 1.2 copy-start.1
  92.1 1.3 %copy-start.2 = (f32[256,1024]{1,0:T(8,128)S(1)}, f32[256,1024]{1,0:T(8,128)}, u32[]{:S(2)}) copy-start(f32[256,1024]{1,0:T(8,128)} %fusion.28) | copy-start | bytes 3145732
  92.1 1.6 %copy-start.3 = (f32[256,1024]{1,0:T(8,128)S(1)}, f32[256,1024]{1,0:T(8,128)}, u32[]{:S(2)}) copy-start(f32[256,1024]{1,0:T(8,128)} %convolution_add_fusion.8) | copy-start | bytes 3145732
  92.1 1.6 %copy-start.7 = (bf16[256,512]{1,0:T(8,128)(2,1)S(1)}, bf16[256,512]{1,0:T(8,128)(2,1)}, u32[]{:S(2)}) copy-start(bf16[256,512]{1,0:T(8,128)(2,1)} %copy-done.6) | copy-start | bytes 786436
  92.1 8.3 %collective-permute-start.5 = (bf16[256,512]{1,0:T(8,128)(2,1)S(1)}, bf16[256,512]{1,0:T(8,128)(2,1)S(1)}, u32[]{:S(2)}, u32[]{:S(2)}) collective-permute-start(bf16[256,512]{1,0:T(8,128)(2,1)S(1)} %get-tuple-element.28), channel_id=1, source_target_pairs={{0,1},{1,0},{2,3},{3,2},{4,5},{5,4},{6,7},{7,6},{8,9},{9,8},{10,11... | collective-permute-start | bytes 786440 | tf_op jit(solution)/shard_map/ppermute | solution.py:113
  92.9 22.6 %collective-permute-start.15 = (bf16[128,1024]{1,0:T(8,128)(2,1)S(1)}, bf16[128,1024]{1,0:T(8,128)(2,1)S(1)}, u32[]{:S(2)}, u32[]{:S(2)}) collective-permute-start(bf16[128,1024]{1,0:T(8,128)(2,1)S(1)} %slice.220), channel_id=1, source_target_pairs={{0,8},{4,12},{8,0},{12,4},{1,9},{5,13},{9,1},{13,5},{2,10},{6,14},... | collective-permute-start | bytes 786440 | tf_op jit(solution)/shard_map/ppermute | solution.py:113
  94.0 3.8 %copy-start.11 = (bf16[64,2048]{1,0:T(8,128)(2,1)S(1)}, bf16[64,2048]{1,0:T(8,128)(2,1)}, u32[]{:S(2)}) copy-start(bf16[64,2048]{1,0:T(8,128)(2,1)} %convolution_convert_fusion) | copy-start | bytes 786436
  95.6 28.3 %collective-permute-start.14 = (bf16[128,1024]{1,0:T(8,128)(2,1)S(1)}, bf16[128,1024]{1,0:T(8,128)(2,1)S(1)}, u32[]{:S(2)}, u32[]{:S(2)}) collective-permute-start(bf16[128,1024]{1,0:T(8,128)(2,1)S(1)} %slice.221), channel_id=1, source_target_pairs={{0,8},{4,12},{8,0},{12,4},{1,9},{5,13},{9,1},{13,5},{2,10},{6,14},... | collective-permute-start | bytes 786440 | tf_op jit(solution)/shard_map/ppermute | solution.py:113
  97.9 26.9 %collective-permute-start.16 = (bf16[64,2560]{1,0:T(8,128)(2,1)S(1)}, bf16[64,2560]{1,0:T(8,128)(2,1)S(1)}, u32[]{:S(2)}, u32[]{:S(2)}) collective-permute-start(bf16[64,2560]{1,0:T(8,128)(2,1)S(1)} %pad_maximum_fusion.3), channel_id=1, source_target_pairs={{0,4},{4,0},{8,12},{12,8},{1,5},{5,1},{9,13},{13,9},{2,6},{6,2},{1... | collective-permute-start | bytes 983048 | tf_op jit(solution)/shard_map/ppermute | solution.py:113
  100.6 26.2 %collective-permute-start.6 = (bf16[128,512]{1,0:T(8,128)(2,1)S(1)}, bf16[128,512]{1,0:T(8,128)(2,1)S(1)}, u32[]{:S(2)}, u32[]{:S(2)}) collective-permute-start(bf16[128,512]{1,0:T(8,128)(2,1)S(1)} %get-tuple-element.13), channel_id=1, source_target_pairs={{0,8},{1,9},{2,0},{3,1},{4,12},{5,13},{6,4},{7,5},{8,10},{9,11},{1... | collective-permute-start | bytes 393224 | tf_op jit(solution)/shard_map/ppermute | solution.py:118
  115.5 11.9 %collective-permute-start.7 = (bf16[128,512]{1,0:T(8,128)(2,1)S(1)}, bf16[128,512]{1,0:T(8,128)(2,1)S(1)}, u32[]{:S(2)}, u32[]{:S(2)}) collective-permute-start(bf16[128,512]{1,0:T(8,128)(2,1)S(1)} %get-tuple-element.12), channel_id=1, source_target_pairs={{2,8},{3,9},{6,12},{7,13},{8,2},{9,3},{12,6},{13,7},{18,24},{19,25... | collective-permute-start | bytes 393224 | tf_op jit(solution)/shard_map/ppermute | solution.py:118

commit v2 on v0

--- a/solution.py
+++ b/solution.py
@@ -1,9 +1,13 @@
 import jax
 import jax.numpy as jnp
 from jax import lax
+from jax.experimental import pallas as pl
+from jax.experimental.pallas import tpu as pltpu
 from jax.sharding import PartitionSpec as P
 
 adapter_scale = 2.0
+f32 = jnp.float32
+bf16 = jnp.bfloat16
 
 
 def placement_matrix(token_adapter_index, adapter_holders, slot_capacity):
@@ -29,7 +33,7 @@
     return jnp.einsum("st,sk->tk", placing, flat, preferred_element_type=jnp.float32)
 
 
-def per_device(
+def gathered_plan(
     activations,
     key_value_weight,
     token_adapter_index,
@@ -46,16 +50,9 @@
     down_resident = adapter_down_weight[0]
     up_resident = adapter_up_weight[0]
     whole_cot = lax.all_gather(cotangent, "tp", axis=1, tiled=True)
-    partial_value = jnp.dot(
-        activations,
-        lax.all_gather(key_value_weight, "fsdp", axis=0, tiled=True).T,
-        preferred_element_type=jnp.float32,
-    )
-    base_gradient = jnp.dot(
-        whole_cot,
-        lax.all_gather(key_value_weight, "fsdp", axis=0, tiled=True),
-        preferred_element_type=jnp.float32,
-    )
+    whole_weight = lax.all_gather(key_value_weight, "fsdp", axis=0, tiled=True)
+    partial_value = jnp.dot(activations, whole_weight.T, preferred_element_type=jnp.float32)
+    base_gradient = jnp.dot(whole_cot, whole_weight, preferred_element_type=jnp.float32)
     base_output = lax.psum_scatter(
         partial_value.astype(jnp.bfloat16), "tp", scatter_dimension=1, tiled=True
     ).astype(jnp.float32)
@@ -102,9 +99,316 @@
     return (key_value_output, input_gradient, grad_down[None], up_gradient[None])
 
 
+def nn(a, b):
+    return lax.dot_general(a, b, (((1,), (0,)), ((), ())), preferred_element_type=f32)
+
+
+def nt(a, b):
+    return lax.dot_general(a, b, (((1,), (1,)), ((), ())), preferred_element_type=f32)
+
+
+def tn(a, b):
+    return lax.dot_general(a, b, (((0,), (0,)), ((), ())), preferred_element_type=f32)
+
+
+def rows2(a, b):
+    return jnp.concatenate([a, b], axis=0)
+
+
+def swap(x, axis, bit):
+    return lax.ppermute(x, axis, [(i, i ^ bit) for i in range(lax.axis_size(axis))])
+
+
+def both(x, pairs):
+    flat = [(4 * a[0] + 2 * a[1] + a[2], 4 * b[0] + 2 * b[1] + b[2]) for a, b in pairs]
+    return lax.ppermute(x, ("fsdp", "tp"), flat)
+
+
+Y, Z, IN_PAIR, ON_OWN = range(4)
+
+
+def local_kernel(body, outs, where, *args):
+    single = not isinstance(outs, list)
+    shapes = [jax.ShapeDtypeStruct(s, d) for s, d in ([outs] if single else outs)]
+    got = pl.pallas_call(
+        body,
+        out_shape=shapes,
+        in_specs=[pl.BlockSpec(memory_space=pltpu.SMEM)]
+        + [pl.BlockSpec(memory_space=pltpu.VMEM)] * len(args),
+        out_specs=[pl.BlockSpec(memory_space=pltpu.VMEM)] * len(shapes),
+        compiler_params=pltpu.CompilerParams(vmem_limit_bytes=24 * 1024 * 1024),
+        cost_estimate=pl.CostEstimate(flops=1000, bytes_accessed=1000, transcendentals=0),
+    )(where, *args)
+    return got[0] if single else got
+
+
+def member(where, idx, rank):
+    lane = lax.broadcasted_iota(jnp.int32, (idx.shape[0], 2 * rank), 1)
+    z = where[Z]
+    return idx == jnp.where(lane < rank, z, z ^ 1)
+
+
+def back_kernel(where, cot, cot_got, idx, idx_got, up, up_sib, out):
+    width = cot.shape[1]
+    cot2 = rows2(cot[...], cot_got[...])
+    part = adapter_scale * nt(cot2, rows2(up[...], up_sib[...]))
+    mine = member(where, rows2(idx[...], idx_got[...]), up.shape[0])
+    out[:, :width] = cot2
+    out[:, width:] = jnp.where(mine, part, 0.0).astype(bf16)
+
+
+def block_kernel(where, mine, got, out):
+    width = out.shape[1] - 128
+    in_pair = jnp.full((1, 1), where[IN_PAIR], jnp.int32) == 1
+    out[:, :width] = jnp.where(in_pair, mine[:, :width], got[:, :width])
+    out[:, width:] = (mine[:, width:].astype(f32) + got[:, width:].astype(f32)).astype(bf16)
+
+
+def pair_blocks(where, mine, got):
+    width = mine.shape[1] - 128
+    on_own = jnp.full((1, 1), where[ON_OWN], jnp.int32) == 1
+    a, b = mine[:, :width], got[:, :width]
+    return jnp.where(on_own, a, b), jnp.where(on_own, b, a)
+
+
+def whole_back(mine, got):
+    width = mine.shape[1] - 128
+    return (mine[:, width:].astype(f32) + got[:, width:].astype(f32)).astype(bf16)
+
+
+def gradient_kernel(where, mine, got, weight, down, first, second, top, bottom):
+    rank = down.shape[0]
+    half = second.shape[0]
+    c_own, c_sib = pair_blocks(where, mine, got)
+    back = whole_back(mine, got)
+    g = nn(c_own, weight[...])
+    g += nn(c_sib[:, :half], first[rank:, :])
+    g += nn(c_sib[:, half:], second[...])
+    g += nn(back, rows2(down[...], first[:rank, :]))
+    toks = top.shape[0]
+    top[...] = g[:toks]
+    bottom[...] = g[toks:].astype(bf16)
+
+
+def gradient_half(where, side, mine, got, weight, down, first, second):
+    toks, tile = mine.shape[0] // 2, 512
+    steps = first.shape[1] // tile
+    whole = lambda a: pl.BlockSpec(a.shape, lambda j, s: (0, 0))
+    by_side = lambda a: pl.BlockSpec((a.shape[0], tile), lambda j, s: (0, s[4] * steps + j))
+    tiled = lambda n: pl.BlockSpec((n, tile), lambda j, s: (0, j))
+    return pl.pallas_call(
+        gradient_kernel,
+        grid_spec=pltpu.PrefetchScalarGridSpec(
+            num_scalar_prefetch=1,
+            grid=(steps,),
+            in_specs=[
+                whole(mine),
+                whole(got),
+                by_side(weight),
+                by_side(down),
+                tiled(first.shape[0]),
+                tiled(second.shape[0]),
+            ],
+            out_specs=[tiled(toks), tiled(toks)],
+        ),
+        out_shape=[
+            jax.ShapeDtypeStruct((toks, steps * tile), f32),
+            jax.ShapeDtypeStruct((toks, steps * tile), bf16),
+        ],
+        compiler_params=pltpu.CompilerParams(vmem_limit_bytes=24 * 1024 * 1024),
+        cost_estimate=pl.CostEstimate(flops=1000, bytes_accessed=1000, transcendentals=0),
+    )(jnp.concatenate([where, side[None]]), mine, got, weight, down, first, second)
+
+
+def gradient_end_kernel(where, near, near_got, far, far_got, out):
+    half = near.shape[1]
+    y = where[Y]
+    at = pl.ds(pl.multiple_of(y * half, half), half)
+    out[:, at] = (near[...] + near_got[...].astype(f32)).astype(bf16)
+    at = pl.ds(pl.multiple_of((1 - y) * half, half), half)
+    out[:, at] = (far[...] + far_got[...].astype(f32)).astype(bf16)
+
+
+def low_kernel(where, act, act_got, idx, idx_got, down, near, far, out):
+    rank, half = down.shape[0], near.shape[1]
+    y = where[Y]
+    at_near = pl.ds(pl.multiple_of(y * half, half), half)
+    at_far = pl.ds(pl.multiple_of((1 - y) * half, half), half)
+    part = nt(rows2(act[:, at_near], act_got[:, at_near]), rows2(down[:, at_near], near[:rank, :]))
+    part += nt(rows2(act[:, at_far], act_got[:, at_far]), rows2(down[:, at_far], far[:rank, :]))
+    mine = member(where, rows2(idx[...], idx_got[...]), rank)
+    out[...] = jnp.where(mine, part, 0.0).astype(bf16)
+
+
+def adapter_kernel(
+    where, low, low_got, mine, got, act, act_got, cot, cot_got, up, up_sib,
+    lora, lora_far, down_own, up_own, sib,
+):
+    rank, width, toks = up.shape[0], act.shape[1], act.shape[0]
+    whole_low = (low[...].astype(f32) + low_got[...].astype(f32)).astype(bf16)
+    out = (adapter_scale * nn(whole_low, rows2(up[...], up_sib[...]))).astype(bf16)
+    lora[...] = out[:toks]
+    lora_far[...] = out[toks:]
+    grad = tn(whole_back(mine, got), rows2(act[...], act_got[...]))
+    down_own[...] = grad[:rank]
+    sib[:, :width] = grad[rank:].astype(bf16)
+    grad = adapter_scale * tn(whole_low, rows2(cot[...], cot_got[...]))
+    up_own[...] = grad[:rank]
+    sib[:, width:] = grad[rank:].astype(bf16)
+
+
+def adapter_end_kernel(where, down_own, up_own, got, down_out, up_out):
+    width = down_own.shape[1]
+    down_out[0] = down_own[...] + got[:, :width].astype(f32)
+    up_out[0] = up_own[...] + got[:, width:].astype(f32)
+
+
+def base_near_kernel(where, act, act_got, weight, first, second, out):
+    rows, half = weight.shape[0], second.shape[0]
+    cut = first.shape[0] - half
+    wide = first.shape[1]
+    at = pl.ds(pl.multiple_of(where[Y] * wide, wide), wide)
+    near = rows2(act[:, at], act_got[:, at])
+    out[:, :rows] = nt(rows2(act[...], act_got[...]), weight[...])
+    out[:, rows : rows + half] = nt(near, first[cut:, :])
+    out[:, rows + half :] = nt(near, second[...])
+
+
+def base_far_kernel(where, part, act, act_got, first, second, keep, give):
+    half = second.shape[0]
+    rows = 2 * half
+    cut = first.shape[0] - half
+    wide = first.shape[1]
+    at = pl.ds(pl.multiple_of((1 - where[Y]) * wide, wide), wide)
+    far = rows2(act[:, at], act_got[:, at])
+    on_own = jnp.full((1, 1), where[ON_OWN], jnp.int32) == 1
+    for k, block in ((0, first[cut:, :]), (1, second[...])):
+        at = slice(k * half, (k + 1) * half)
+        mine = part[:, k * half : (k + 1) * half]
+        other = part[:, rows + k * half : rows + (k + 1) * half] + nt(far, block)
+        keep[:, at] = jnp.where(on_own, mine, other)
+        give[:, at] = jnp.where(on_own, other, mine).astype(bf16)
+
+
+def held_kernel(where, keep, got, here, there, turn):
+    toks = here.shape[0]
+    held = (keep[...] + got[...].astype(f32)).astype(bf16)
+    in_pair = jnp.full((1, 1), where[IN_PAIR], jnp.int32) == 1
+    here[...] = held[:toks]
+    there[...] = held[toks:]
+    turn[...] = jnp.where(in_pair, held[toks:], held[:toks])
+
+
+def output_kernel(where, one, two, here, lora, lora_got, out):
+    in_pair = jnp.full((1, 1), where[IN_PAIR], jnp.int32) == 1
+    base = one[...].astype(f32) + jnp.where(in_pair, here[...], two[...]).astype(f32)
+    out[...] = (base + lora[...].astype(f32) + lora_got[...].astype(f32)).astype(bf16)
+
+
+def pair_plan(
+    activations,
+    key_value_weight,
+    token_adapter_index,
+    adapter_down_weight,
+    adapter_up_weight,
+    cotangent,
+):
+    z = lax.axis_index("fsdp")
+    y = lax.axis_index("groups")
+    t = lax.axis_index("tp")
+    x, c = t // 2, t % 2
+    where = jnp.stack([y, z, x == z // 2, c == z % 2]).astype(jnp.int32)
+    rows, width = key_value_weight.shape
+    toks, out_width = cotangent.shape
+    half, wide = rows // 2, width // 2
+    down = adapter_down_weight[0]
+    up = adapter_up_weight[0]
+    rank = down.shape[0]
+    places = [(zz, xx, cc) for zz in range(4) for xx in range(2) for cc in range(2)]
+
+    cot_got = swap(cotangent, "fsdp", 2)
+    idx_got = swap(token_adapter_index, "fsdp", 2)
+    up_sib = swap(up, "fsdp", 1)
+    w_mine = lax.dynamic_slice(key_value_weight, (0, y * wide), (rows, wide))
+    d_mine = lax.dynamic_slice(down, (0, y * wide), (rank, wide))
+    piece = jnp.concatenate([d_mine, w_mine[:half]], axis=0)
+    near0 = swap(piece, "fsdp", 1)
+    act_sent, _ = lax.optimization_barrier((activations, piece))
+    act_got = swap(act_sent, "fsdp", 2)
+    near1 = swap(w_mine[half:], "fsdp", 1)
+
+    mine = local_kernel(
+        back_kernel, ((2 * toks, out_width + 2 * rank), bf16), where,
+        cotangent, cot_got, token_adapter_index, idx_got, up, up_sib,
+    )
+    mine = local_kernel(block_kernel, (mine.shape, bf16), where, mine, swap(mine, "tp", 2))
+    got = swap(mine, "tp", 1)
+
+    far0 = swap(near0, "groups", 1)
+    far1 = swap(near1, "groups", 1)
+
+    near, near_sent = gradient_half(where, y, mine, got, key_value_weight, down, near0, near1)
+    near_got = swap(near_sent, "fsdp", 2)
+
+    part = local_kernel(
+        base_near_kernel, ((2 * toks, 2 * rows), f32), where,
+        activations, act_got, key_value_weight, near0, near1,
+    )
+
+    low = local_kernel(
+        low_kernel, ((2 * toks, 2 * rank), bf16), where,
+        activations, act_got, token_adapter_index, idx_got, down, near0, far0,
+    )
+    low = (low.astype(f32) + swap(low, "tp", 2).astype(f32)).astype(bf16)
+    low_got = swap(low, "tp", 1)
+
+    far, far_sent = gradient_half(where, 1 - y, mine, got, key_value_weight, down, far0, far1)
+    far_got = swap(far_sent, "fsdp", 2)
+
+    keep, give = local_kernel(
+        base_far_kernel, [((2 * toks, rows), f32), ((2 * toks, rows), bf16)], where,
+        part, activations, act_got, far0, far1,
+    )
+    here, there, turn = local_kernel(
+        held_kernel, [((toks, rows), bf16)] * 3, where, keep, swap(give, "tp", 1)
+    )
+    one = both(
+        turn,
+        [((a, b, d), (a ^ 2, b, d) if b == a // 2 else (a, 1 - b, d)) for a, b, d in places],
+    )
+    two = both(there, [((a, b, d), (a ^ 2, 1 - b, d)) for a, b, d in places if b != a // 2])
+
+    lora, lora_far, down_own, up_own, sib = local_kernel(
+        adapter_kernel,
+        [
+            ((toks, out_width), bf16),
+            ((toks, out_width), bf16),
+            ((rank, width), f32),
+            ((rank, out_width), f32),
+            ((rank, width + out_width), bf16),
+        ],
+        where,
+        low, low_got, mine, got, activations, act_got, cotangent, cot_got, up, up_sib,
+    )
+    lora_got = swap(lora_far, "fsdp", 2)
+    grad_down, up_gradient = local_kernel(
+        adapter_end_kernel, [((1, rank, width), f32), ((1, rank, out_width), f32)], where,
+        down_own, up_own, swap(sib, "fsdp", 1),
+    )
+
+    input_gradient = local_kernel(
+        gradient_end_kernel, ((toks, width), bf16), where, near, near_got, far, far_got
+    )
+    key_value_output = local_kernel(
+        output_kernel, ((toks, out_width), bf16), where, one, two, here, lora, lora_got
+    )
+    return (key_value_output, input_gradient, grad_down, up_gradient)
+
+
 def solution(mesh):
+    paired = mesh.shape["fsdp"] == 4 and mesh.shape["tp"] == 4 and mesh.shape["groups"] == 2
     return jax.shard_map(
-        per_device,
+        pair_plan if paired else gathered_plan,
         mesh=mesh,
         in_specs=(
             P(("groups", "fsdp"), "tp"),

time: 268 us -> 125 us (0.47)
  waiting for transfers between devices: 195 us -> 61.8 us
  matrix products: 29.2 us -> 0 us
  Pallas kernels: 0 us -> 22 us
  between operations: 15.6 us -> 0.92 us
  local copies, waits for them, and re-layouts: 0.03 us -> 13 us
  starting transfers between devices: 17.9 us -> 24.8 us
  blocking collectives: 6.51 us -> 0 us
    all_gather x1 -> x0, waiting for transfers between devices: 126 us -> none  [per_device(): lax.all_gather(key_value_weight, 'fsdp', axis=0, tiled=True)]
    ppermute x0 -> x19, waiting for transfers between devices: none -> 61.8 us  [the longest x17 61.8 us: swap(): lax.ppermute(x, axis, [(i, i ^ bit) for i in range(lax.axis_size(axis))])]
    all_to_all x4 -> x0, waiting for transfers between devices: 33.6 us -> none  [the longest x1 22.6 us: per_device(): lax.all_to_all(rows_send, 'fsdp', split_axis=0, concat_axis=0, tiled=True)]
    psum x1 -> x0, waiting for transfers between devices: 29.9 us -> none  [per_device(): rank_activation = lax.psum(low_part.astype(jnp.bfloat16), 'tp')]
    dot_general x12 -> x0, matrix products: 29.2 us -> none  [the longest x1 7.07 us: per_device(): jnp.dot(activations, lax.all_gather(key_value_weight, 'fsdp', axis=0, til...]
    ppermute x0 -> x19, starting transfers between devices: none -> 24.8 us  [the longest x17 23.8 us: swap(): lax.ppermute(x, axis, [(i, i ^ bit) for i in range(lax.axis_size(axis))])]
    pallas_call x0 -> x12, Pallas kernels: none -> 22 us  [the longest x10 15.8 us: local_kernel(): pl.pallas_call(body, out_shape=shapes, in_specs=[pl.BlockSpec(memory_spac...]
    all_to_all x4 -> x0, starting transfers between devices: 17.8 us -> none  [the longest x1 6.32 us: per_device(): lax.all_to_all(cot_send, 'fsdp', split_axis=0, concat_axis=0, tiled=True)]
  transfers between devices with their start and end apart: 7 -> 19, of which waited for: 6 -> 8; matrix products, arithmetic and copies ran while one was open for 9% -> 1% of each run, Pallas kernels for 0% -> 16%
where the time goes in v2:
time: 125 us; the launch traced here: 124 us
  waiting for transfers between devices  61.8 us (49%)
  starting transfers between devices  24.8 us (20%)
  Pallas kernels  22 us (18%)
  local copies, waits for them, and re-layouts  13 us (10%)
    ppermute x17, waiting for transfers between devices, swap(): lax.ppermute(x, axis, [(i, i ^ bit) for i in range(lax.axis_size(axis))])  61.8 us
    ppermute x17, starting transfers between devices, swap(): lax.ppermute(x, axis, [(i, i ^ bit) for i in range(lax.axis_size(axis))])  23.8 us
    pallas_call x10, Pallas kernels, local_kernel(): pl.pallas_call(body, out_shape=shapes, in_specs=[pl.BlockSpec(memory_spac...  15.8 us
    unnamed x71, local copies, waits for them, and re-layouts  10.6 us
    pallas_call x2, Pallas kernels, gradient_half(): pl.pallas_call(gradient_kernel, grid_spec=pltpu.PrefetchScalarGridSpec(nu...  6.21 us
  transfers between devices with their start and end apart: 19, of which 8 were waited for; matrix products, arithmetic and copies ran while one was open for 1% of the time, Pallas kernels for 16%

profile of v2, /device:TPU:0, one launch (start us, length us, event | category | flops | bytes accessed | tf_op | source)
XLA Modules:
  0.0 123.6 jit_solution(6350805452199297328)
XLA Ops:
  0.6 0.9 dynamic-slice_bitcast_fusion
  1.6 0.0 copy-start.18
  1.6 0.0 copy-start.34
  1.6 0.0 copy-start.22
  1.6 1.3 %fusion = (bf16[256,1024]{1,0:T(8,128)(2,1)S(1)}, bf16[256,1024]{1,0:T(8,128)(2,1)S(1)}) fusion(bf16[512,2048]{1,0:T(8,128)(2,1)} %weight.5, s32[]{:T(128)S(6)} %add.23, s32[]{:T(128)S(6)} %select_n.26), kind=kLoop, calls=%fused_computation.5 | loop fusion | bytes 2097160 | tf_op jit(solution)/shard_map/slice | solution.py:338
  2.9 0.0 copy-start.1
  3.0 3.1 %collective-permute-start.1 = (bf16[320,1024]{1,0:T(8,128)(2,1)S(1)}, bf16[320,1024]{1,0:T(8,128)(2,1)S(1)}, u32[]{:S(2)}, u32[]{:S(2)}) collective-permute-start(bf16[320,1024]{1,0:T(8,128)(2,1)S(1)} %pad_maximum_fusion), channel_id=1, source_target_pairs={{0,4},{4,0},{8,12},{12,8},{1,5},{5,1},{9,13},{13,9},{2,6},{6,2},{1... | collective-permute-start | bytes 1966088 | tf_op jit(solution)/shard_map/ppermute | solution.py:119
  6.1 0.1 collective-permute-start.2
  6.2 3.0 %collective-permute-start.11 = (bf16[128,512]{1,0:T(8,128)(2,1)S(1)}, bf16[128,512]{1,0:T(8,128)(2,1)S(1)}, u32[]{:S(2)}, u32[]{:S(2)}) collective-permute-start(bf16[128,512]{1,0:T(8,128)(2,1)S(1)} %copy-done.18), channel_id=1, source_target_pairs={{0,8},{4,12},{8,0},{12,4},{1,9},{5,13},{9,1},{13,5},{2,10},{6,14},... | collective-permute-start | bytes 393224 | tf_op jit(solution)/shard_map/ppermute | solution.py:119
  9.1 0.1 copy.11.idx
  9.3 0.1 collective-permute-start.8
  9.3 1.9 %collective-permute-start.12 = (bf16[64,512]{1,0:T(8,128)(2,1)S(1)}, bf16[64,512]{1,0:T(8,128)(2,1)S(1)}, u32[]{:S(2)}, u32[]{:S(2)}) collective-permute-start(bf16[64,512]{1,0:T(8,128)(2,1)S(1)} %bitcast.12), channel_id=1, source_target_pairs={{0,4},{4,0},{8,12},{12,8},{1,5},{5,1},{9,13},{13,9},{2,6},{6,2},{1... | collective-permute-start | bytes 196616 | tf_op jit(solution)/shard_map/ppermute | solution.py:119
  11.2 14.6 %collective-permute-done.1.first.near = bf16[320,1024]{1,0:T(8,128)(2,1)S(1)} collective-permute-done((bf16[320,1024]{1,0:T(8,128)(2,1)S(1)}, bf16[320,1024]{1,0:T(8,128)(2,1)S(1)}, u32[]{:S(2)}, u32[]{:S(2)}) %collective-permute-start.1) | collective-permute-done | bytes 655392 | tf_op jit(solution)/shard_map/ppermute | solution.py:119
  25.9 2.0 %collective-permute-start.3 = (bf16[320,1024]{1,0:T(8,128)(2,1)S(1)}, bf16[320,1024]{1,0:T(8,128)(2,1)S(1)}, u32[]{:S(2)}, u32[]{:S(2)}) collective-permute-start(bf16[320,1024]{1,0:T(8,128)(2,1)S(1)} %collective-permute-done.1.first.near), channel_id=1, source_target_pairs={{0,16},{16,0},{1,17},{17,1},{2,18},{18,2},{3,19},{19,3},{4,20},{20... | collective-permute-start | bytes 1966088 | tf_op jit(solution)/shard_map/ppermute | solution.py:119
  27.9 0.1 pad_add_fusion.where
  27.9 8.3 %collective-permute-done.8.idx_got = s32[128,1]{1,0:T(8,128)S(1)} collective-permute-done((s32[128,1]{1,0:T(8,128)S(1)}, s32[128,1]{1,0:T(8,128)S(1)}, u32[]{:S(2)}, u32[]{:S(2)}) %collective-permute-start.8) | collective-permute-done | bytes 544 | tf_op jit(solution)/shard_map/ppermute | solution.py:119
  36.2 1.4 %collective-permute-done.12.up_sib = bf16[64,512]{1,0:T(8,128)(2,1)S(1)} collective-permute-done((bf16[64,512]{1,0:T(8,128)(2,1)S(1)}, bf16[64,512]{1,0:T(8,128)(2,1)S(1)}, u32[]{:S(2)}, u32[]{:S(2)}) %collective-permute-start.12) | collective-permute-done | bytes 65568 | tf_op jit(solution)/shard_map/ppermute | solution.py:119
  37.7 0.0 collective-permute-done.11.cot_got
  37.7 0.8 shard_map.97.mine
  38.5 0.0 copy-start.26
  38.5 0.6 copy-done.26
  39.1 1.7 %collective-permute-start.13 = (bf16[256,640]{1,0:T(8,128)(2,1)S(1)}, bf16[256,640]{1,0:T(8,128)(2,1)S(1)}, u32[]{:S(2)}, u32[]{:S(2)}) collective-permute-start(bf16[256,640]{1,0:T(8,128)(2,1)S(1)} %shard_map.97.mine), channel_id=1, source_target_pairs={{0,2},{1,3},{2,0},{3,1},{4,6},{5,7},{6,4},{7,5},{8,10},{9,11},{10,... | collective-permute-start | bytes 983048 | tf_op jit(solution)/shard_map/ppermute | solution.py:119
  40.8 2.6 %collective-permute-start = (bf16[128,2048]{1,0:T(8,128)(2,1)S(1)}, bf16[128,2048]{1,0:T(8,128)(2,1)S(1)}, u32[]{:S(2)}, u32[]{:S(2)}) collective-permute-start(bf16[128,2048]{1,0:T(8,128)(2,1)S(1)} %copy-done.1), channel_id=1, source_target_pairs={{0,8},{4,12},{8,0},{12,4},{1,9},{5,13},{9,1},{13,5},{2,10},{6,14},... | collective-permute-start | bytes 1572872 | tf_op jit(solution)/shard_map/ppermute | solution.py:119
  43.4 1.5 %collective-permute-start.4 = (bf16[256,1024]{1,0:T(8,128)(2,1)}, bf16[256,1024]{1,0:T(8,128)(2,1)}, u32[]{:S(2)}, u32[]{:S(2)}) collective-permute-start(bf16[256,1024]{1,0:T(8,128)(2,1)} %collective-permute-done.2.second), channel_id=1, source_target_pairs={{0,16},{16,0},{1,17},{17,1},{2,18},{18,2},{3,19},{19,3},{4,20},{20... | collective-permute-start | bytes 1572872 | tf_op jit(solution)/shard_map/ppermute | solution.py:119
  44.9 3.2 %collective-permute-done.13.got = bf16[256,640]{1,0:T(8,128)(2,1)S(1)} collective-permute-done((bf16[256,640]{1,0:T(8,128)(2,1)S(1)}, bf16[256,640]{1,0:T(8,128)(2,1)S(1)}, u32[]{:S(2)}, u32[]{:S(2)}) %collective-permute-start.13) | collective-permute-done | bytes 327712 | tf_op jit(solution)/shard_map/ppermute | solution.py:119
  48.1 0.6 shard_map.98.mine
  48.7 0.1 collective-permute-start.14
  48.8 16.7 %collective-permute-done.act_got = bf16[128,2048]{1,0:T(8,128)(2,1)S(1)} collective-permute-done((bf16[128,2048]{1,0:T(8,128)(2,1)S(1)}, bf16[128,2048]{1,0:T(8,128)(2,1)S(1)}, u32[]{:S(2)}, u32[]{:S(2)}) %collective-permute-start) | collective-permute-done | bytes 524320 | tf_op jit(solution)/shard_map/ppermute | solution.py:119
  65.5 1.3 %copy-done.6 = bf16[320,1024]{1,0:T(8,128)(2,1)S(1)} copy-done((bf16[320,1024]{1,0:T(8,128)(2,1)S(1)}, bf16[320,1024]{1,0:T(8,128)(2,1)}, u32[]{:S(2)}) %copy-start.6) | copy-done | bytes 655384
  66.9 0.9 copy-done.9
  67.8 0.8 copy-done.27
  68.7 1.6 %shard_map.96 = bf16[256,128]{1,0:T(8,128)(2,1)} custom-call(s32[4]{0:T(128)S(1)} %pad_add_fusion.where, bf16[128,2048]{1,0:T(8,128)(2,1)S(1)} %copy-done.1, bf16[128,2048]{1,0:T(8,128)(2,1)S(1)} %collective-permute-done.act_got, s32[128,1]{1,0:T(8,128)S(1)} %copy.11.idx, s32[128,1]{1,0:T(8,128)S(1)} %copy-done.27, bf16[64,2048]{1,0:T(8,128)(2,1)S(1)} %bitcast.9, ...), custom_call_target="tpu_custom_call" | custom-call | flops 1000 | bytes 1000 | tf_op jit(solution)/shard_map/pallas_call | solution.py:133
  70.3 0.7 collective-permute-start.9
  71.0 0.1 concatenate.12.where
  71.1 1.1 copy-done.7
  72.1 2.1 %shard_map.93.part = f32[256,1024]{1,0:T(8,128)S(1)} custom-call(s32[4]{0:T(128)S(1)} %pad_add_fusion.where, bf16[128,2048]{1,0:T(8,128)(2,1)S(1)} %copy-done.1, bf16[128,2048]{1,0:T(8,128)(2,1)S(1)} %collective-permute-done.act_got, bf16[512,2048]{1,0:T(8,128)(2,1)S(1)} %copy-done, bf16[320,1024]{1,0:T(8,128)(2,1)S(1)} %copy-done.7, ...), custom_call_target="tpu_custom_call" | custom-call | flops 1000 | bytes 1000 | tf_op jit(solution)/shard_map/pallas_call | solution.py:133
  74.3 3.4 %shard_map.101 = (f32[128,1024]{1,0:T(8,128)S(1)}, bf16[128,1024]{1,0:T(8,128)(2,1)}) custom-call(s32[5]{0:T(128)S(1)} %concatenate.12.where, bf16[256,640]{1,0:T(8,128)(2,1)S(1)} %shard_map.98.mine, bf16[256,640]{1,0:T(8,128)(2,1)} %collective-permute-done.14.got, bf16[512,2048]{1,0:T(8,128)(2,1)S(1)} %copy-done, bf16[64,2048]{1,0:T(8,128)(2,1)S(1)} %bitcast.10, ...), custom_call_target="tpu_custom_call" | custom-call | flops 1000 | bytes 1000 | tf_op jit(solution)/shard_map/pallas_call | solution.py:199
  77.8 0.0 copy-start.23
  77.8 0.1 collective-permute-start.16
  77.9 2.5 %shard_map.94 = (f32[256,512]{1,0:T(8,128)S(1)}, bf16[256,512]{1,0:T(8,128)(2,1)}) custom-call(s32[4]{0:T(128)S(1)} %pad_add_fusion.where, f32[256,1024]{1,0:T(8,128)S(1)} %shard_map.93.part, bf16[128,2048]{1,0:T(8,128)(2,1)S(1)} %copy-done.1, bf16[128,2048]{1,0:T(8,128)(2,1)S(1)} %collective-permute-done.act_got, bf16[320,1024]{1,0:T(8,128)(2,1)S(1)} %copy-done.3, ...), custom_call_target="tpu_custom_call" | custom-call | flops 1000 | bytes 1000 | tf_op jit(solution)/shard_map/pallas_call | solution.py:133
  80.4 0.8 copy-done.16
  81.2 0.9 add_convert_fusion.low
  82.0 0.6 collective-permute-start.10
  82.6 0.9 collective-permute-done.10.low_got
  83.5 2.1 %shard_map.99 = (bf16[128,512]{1,0:T(8,128)(2,1)S(1)}, bf16[128,512]{1,0:T(8,128)(2,1)S(1)}, f32[64,2048]{1,0:T(8,128)S(1)}, f32[64,512]{1,0:T(8,128)S(1)}, bf16[64,2560]{1,0:T(8,128)(2,1)}) custom-call(s32[4]{0:T(128)S(1)} %pad_add_fusion.where, bf16[256,128]{1,0:T(8,128)(2,1)S(1)} %add_convert_fusion.low, ...), custom_call_target="tpu_custom_call" | custom-call | flops 1000 | bytes 1000 | tf_op jit(solution)/shard_map/pallas_call | solution.py:133
  85.6 0.8 copy-done.14
  86.4 0.6 copy-done.28
  87.1 0.7 copy-done.30
  87.7 0.7 copy-done.32
  88.4 3.5 %collective-permute-start.18 = (bf16[64,2560]{1,0:T(8,128)(2,1)}, bf16[64,2560]{1,0:T(8,128)(2,1)}, u32[]{:S(2)}, u32[]{:S(2)}) collective-permute-start(bf16[64,2560]{1,0:T(8,128)(2,1)} %get-tuple-element.35), channel_id=1, source_target_pairs={{0,4},{4,0},{8,12},{12,8},{1,5},{5,1},{9,13},{13,9},{2,6},{6,2},{1... | collective-permute-start | bytes 983048 | tf_op jit(solution)/shard_map/ppermute | solution.py:119
  91.9 0.1 concatenate.13.where
  92.0 1.1 copy-done.4
  93.1 0.9 copy-done.11
  94.1 2.8 %shard_map.102 = (f32[128,1024]{1,0:T(8,128)S(1)}, bf16[128,1024]{1,0:T(8,128)(2,1)S(1)}) custom-call(s32[5]{0:T(128)S(1)} %concatenate.13.where, bf16[256,640]{1,0:T(8,128)(2,1)S(1)} %shard_map.98.mine, bf16[256,640]{1,0:T(8,128)(2,1)} %collective-permute-done.14.got, bf16[512,2048]{1,0:T(8,128)(2,1)S(1)} %copy-done, bf16[64,2048]{1,0:T(8,128)(2,1)S(1)} %bitcast.11, ...), custom_call_target="tpu_custom_call" | custom-call | flops 1000 | bytes 1000 | tf_op jit(solution)/shard_map/pallas_call | solution.py:199
  96.9 0.3 collective-permute-start.17
  97.2 2.6 %collective-permute-start.15 = (bf16[128,512]{1,0:T(8,128)(2,1)S(1)}, bf16[128,512]{1,0:T(8,128)(2,1)S(1)}, u32[]{:S(2)}, u32[]{:S(2)}) collective-permute-start(bf16[128,512]{1,0:T(8,128)(2,1)S(1)} %copy-done.33), channel_id=1, source_target_pairs={{0,8},{4,12},{8,0},{12,4},{1,9},{5,13},{9,1},{13,5},{2,10},{6,14},... | collective-permute-start | bytes 393224 | tf_op jit(solution)/shard_map/ppermute | solution.py:119
  99.9 1.1 shard_map.95
  100.9 0.3 collective-permute-start.6
  101.3 0.7 collective-permute-start.7
  101.9 15.7 %collective-permute-done.17.far_got = bf16[128,1024]{1,0:T(8,128)(2,1)S(1)} collective-permute-done((bf16[128,1024]{1,0:T(8,128)(2,1)S(1)}, bf16[128,1024]{1,0:T(8,128)(2,1)S(1)}, u32[]{:S(2)}, u32[]{:S(2)}) %collective-permute-start.17) | collective-permute-done | bytes 262176 | tf_op jit(solution)/shard_map/ppermute | solution.py:119
  117.6 1.9 %shard_map.103 = bf16[128,2048]{1,0:T(8,128)(2,1)} custom-call(s32[4]{0:T(128)S(1)} %pad_add_fusion.where, f32[128,1024]{1,0:T(8,128)S(1)} %copy-done.13, bf16[128,1024]{1,0:T(8,128)(2,1)} %collective-permute-done.16.near_got, f32[128,1024]{1,0:T(8,128)S(1)} %get-tuple-element.31.far, bf16[128,1024]{1,0:T(8,128)(2,1)S(1)} %collective-permute-done.17.far_got), custom_call_target="tpu_custom_call" | custom-call | flops 1000 | bytes 1000 | tf_op jit(solution)/shard_map/pallas_call | solution.py:133
  119.5 0.9 collective-permute-done.15.lora_got
  120.4 1.3 %shard_map.100 = bf16[128,512]{1,0:T(8,128)(2,1)} custom-call(s32[4]{0:T(128)S(1)} %pad_add_fusion.where, bf16[128,512]{1,0:T(8,128)(2,1)S(1)} %collective-permute-done.6.one, bf16[128,512]{1,0:T(8,128)(2,1)S(1)} %collective-permute-done.7.two, bf16[128,512]{1,0:T(8,128)(2,1)S(1)} %get-tuple-element.26.here, bf16[128,512]{1,0:T(8,128)(2,1)S(1)} %copy-done.31, ...), custom_call_target="tpu_custom_call" | custom-call | flops 1000 | bytes 1000 | tf_op jit(solution)/shard_map/pallas_call | solution.py:133
  121.7 1.9 %shard_map.104 = (f32[1,64,2048]{2,1,0:T(8,128)}, f32[1,64,512]{2,1,0:T(8,128)}) custom-call(s32[4]{0:T(128)S(1)} %pad_add_fusion.where, f32[64,2048]{1,0:T(8,128)S(1)} %copy-done.15, f32[64,512]{1,0:T(8,128)S(1)} %copy-done.29, bf16[64,2560]{1,0:T(8,128)(2,1)} %collective-permute-done.18.got), custom_call_target="tpu_custom_call" | custom-call | flops 1000 | bytes 1000 | tf_op jit(solution)/shard_map/pallas_call | solution.py:133
  (64 shorter events, 0.2 us)
Async XLA Ops:
  1.6 4.6 %copy-start.18 = (bf16[128,512]{1,0:T(8,128)(2,1)S(1)}, bf16[128,512]{1,0:T(8,128)(2,1)}, u32[]{:S(2)}) copy-start(bf16[128,512]{1,0:T(8,128)(2,1)} %cot.3) | copy-start | bytes 393220
  1.6 7.6 %copy-start.34 = (s32[128,1]{0,1:T(1,128)S(1)}, s32[128,1]{0,1:T(1,128)}, u32[]{:S(2)}) copy-start(s32[128,1]{0,1:T(1,128)} %param.8) | copy-start | bytes 1540
  1.6 7.7 %copy-start.22 = (bf16[1,64,512]{2,1,0:T(8,128)(2,1)S(1)}, bf16[1,64,512]{2,1,0:T(8,128)(2,1)}, u32[]{:S(2)}) copy-start(bf16[1,64,512]{2,1,0:T(8,128)(2,1)} %param.10) | copy-start | bytes 196612
  2.9 37.8 %copy-start.1 = (bf16[128,2048]{1,0:T(8,128)(2,1)S(1)}, bf16[128,2048]{1,0:T(8,128)(2,1)}, u32[]{:S(2)}) copy-start(bf16[128,2048]{1,0:T(8,128)(2,1)} %act.7) | copy-start | bytes 1572868
  3.0 22.9 %collective-permute-start.1 = (bf16[320,1024]{1,0:T(8,128)(2,1)S(1)}, bf16[320,1024]{1,0:T(8,128)(2,1)S(1)}, u32[]{:S(2)}, u32[]{:S(2)}) collective-permute-start(bf16[320,1024]{1,0:T(8,128)(2,1)S(1)} %pad_maximum_fusion), channel_id=1, source_target_pairs={{0,4},{4,0},{8,12},{12,8},{1,5},{5,1},{9,13},{13,9},{2,6},{6,2},{1... | collective-permute-start | bytes 1966088 | tf_op jit(solution)/shard_map/ppermute | solution.py:119
  6.1 37.3 %collective-permute-start.2 = (bf16[256,1024]{1,0:T(8,128)(2,1)S(1)}, bf16[256,1024]{1,0:T(8,128)(2,1)}, u32[]{:S(2)}, u32[]{:S(2)}) collective-permute-start(bf16[256,1024]{1,0:T(8,128)(2,1)S(1)} %get-tuple-element.38), channel_id=1, source_target_pairs={{0,4},{4,0},{8,12},{12,8},{1,5},{5,1},{9,13},{13,9},{2,6},{6,2},{1... | collective-permute-start | bytes 1572872 | tf_op jit(solution)/shard_map/ppermute | solution.py:119
  6.2 31.5 %collective-permute-start.11 = (bf16[128,512]{1,0:T(8,128)(2,1)S(1)}, bf16[128,512]{1,0:T(8,128)(2,1)S(1)}, u32[]{:S(2)}, u32[]{:S(2)}) collective-permute-start(bf16[128,512]{1,0:T(8,128)(2,1)S(1)} %copy-done.18), channel_id=1, source_target_pairs={{0,8},{4,12},{8,0},{12,4},{1,9},{5,13},{9,1},{13,5},{2,10},{6,14},... | collective-permute-start | bytes 393224 | tf_op jit(solution)/shard_map/ppermute | solution.py:119
  9.3 27.0 %collective-permute-start.8 = (s32[128,1]{1,0:T(8,128)S(1)}, s32[128,1]{1,0:T(8,128)S(1)}, u32[]{:S(2)}, u32[]{:S(2)}) collective-permute-start(s32[128,1]{1,0:T(8,128)S(1)} %copy.11.idx), channel_id=1, source_target_pairs={{0,8},{4,12},{8,0},{12,4},{1,9},{5,13},{9,1},{13,5},{2,10},{6,14},... | collective-permute-start | bytes 1544 | tf_op jit(solution)/shard_map/ppermute | solution.py:119
  9.3 28.3 %collective-permute-start.12 = (bf16[64,512]{1,0:T(8,128)(2,1)S(1)}, bf16[64,512]{1,0:T(8,128)(2,1)S(1)}, u32[]{:S(2)}, u32[]{:S(2)}) collective-permute-start(bf16[64,512]{1,0:T(8,128)(2,1)S(1)} %bitcast.12), channel_id=1, source_target_pairs={{0,4},{4,0},{8,12},{12,8},{1,5},{5,1},{9,13},{13,9},{2,6},{6,2},{1... | collective-permute-start | bytes 196616 | tf_op jit(solution)/shard_map/ppermute | solution.py:119
  25.9 39.7 %copy-start.5 = (bf16[320,1024]{1,0:T(8,128)(2,1)}, bf16[320,1024]{1,0:T(8,128)(2,1)S(1)}, u32[]{:S(2)}) copy-start(bf16[320,1024]{1,0:T(8,128)(2,1)S(1)} %collective-permute-done.1.first.near) | copy-start | bytes 1966084
  25.9 39.7 %collective-permute-start.3 = (bf16[320,1024]{1,0:T(8,128)(2,1)S(1)}, bf16[320,1024]{1,0:T(8,128)(2,1)S(1)}, u32[]{:S(2)}, u32[]{:S(2)}) collective-permute-start(bf16[320,1024]{1,0:T(8,128)(2,1)S(1)} %collective-permute-done.1.first.near), channel_id=1, source_target_pairs={{0,16},{16,0},{1,17},{17,1},{2,18},{18,2},{3,19},{19,3},{4,20},{20... | collective-permute-start | bytes 1966088 | tf_op jit(solution)/shard_map/ppermute | solution.py:119
  37.7 0.8 copy-start.24
  37.7 0.8 copy-start.20
  38.5 0.6 copy-start.26
  39.1 9.0 %collective-permute-start.13 = (bf16[256,640]{1,0:T(8,128)(2,1)S(1)}, bf16[256,640]{1,0:T(8,128)(2,1)S(1)}, u32[]{:S(2)}, u32[]{:S(2)}) collective-permute-start(bf16[256,640]{1,0:T(8,128)(2,1)S(1)} %shard_map.97.mine), channel_id=1, source_target_pairs={{0,2},{1,3},{2,0},{3,1},{4,6},{5,7},{6,4},{7,5},{8,10},{9,11},{10,... | collective-permute-start | bytes 983048 | tf_op jit(solution)/shard_map/ppermute | solution.py:119
  40.8 24.8 %collective-permute-start = (bf16[128,2048]{1,0:T(8,128)(2,1)S(1)}, bf16[128,2048]{1,0:T(8,128)(2,1)S(1)}, u32[]{:S(2)}, u32[]{:S(2)}) collective-permute-start(bf16[128,2048]{1,0:T(8,128)(2,1)S(1)} %copy-done.1), channel_id=1, source_target_pairs={{0,8},{4,12},{8,0},{12,4},{1,9},{5,13},{9,1},{13,5},{2,10},{6,14},... | collective-permute-start | bytes 1572872 | tf_op jit(solution)/shard_map/ppermute | solution.py:119
  43.4 34.5 %collective-permute-start.4 = (bf16[256,1024]{1,0:T(8,128)(2,1)}, bf16[256,1024]{1,0:T(8,128)(2,1)}, u32[]{:S(2)}, u32[]{:S(2)}) collective-permute-start(bf16[256,1024]{1,0:T(8,128)(2,1)} %collective-permute-done.2.second), channel_id=1, source_target_pairs={{0,16},{16,0},{1,17},{17,1},{2,18},{18,2},{3,19},{19,3},{4,20},{20... | collective-permute-start | bytes 1572872 | tf_op jit(solution)/shard_map/ppermute | solution.py:119
  48.7 25.6 %collective-permute-start.14 = (bf16[256,640]{1,0:T(8,128)(2,1)S(1)}, bf16[256,640]{1,0:T(8,128)(2,1)}, u32[]{:S(2)}, u32[]{:S(2)}) collective-permute-start(bf16[256,640]{1,0:T(8,128)(2,1)S(1)} %shard_map.98.mine), channel_id=1, source_target_pairs={{0,1},{1,0},{2,3},{3,2},{4,5},{5,4},{6,7},{7,6},{8,9},{9,8},{10,11... | collective-permute-start | bytes 983048 | tf_op jit(solution)/shard_map/ppermute | solution.py:119
  65.5 4.7 %copy-start.2 = (bf16[320,1024]{1,0:T(8,128)(2,1)}, bf16[320,1024]{1,0:T(8,128)(2,1)S(1)}, u32[]{:S(2)}) copy-start(bf16[320,1024]{1,0:T(8,128)(2,1)S(1)} %collective-permute-done.3.first.far) | copy-start | bytes 1966084
  65.5 1.3 %copy-start.6 = (bf16[320,1024]{1,0:T(8,128)(2,1)S(1)}, bf16[320,1024]{1,0:T(8,128)(2,1)}, u32[]{:S(2)}) copy-start(bf16[320,1024]{1,0:T(8,128)(2,1)} %copy-done.5) | copy-start | bytes 1966084
  66.9 0.9 copy-start.9
  67.8 0.8 copy-start.27
  68.7 2.4 %copy-start = (bf16[512,2048]{1,0:T(8,128)(2,1)S(1)}, bf16[512,2048]{1,0:T(8,128)(2,1)}, u32[]{:S(2)}) copy-start(bf16[512,2048]{1,0:T(8,128)(2,1)} %weight.5) | copy-start | bytes 6291460
  70.3 10.9 %collective-permute-start.9 = (bf16[256,128]{1,0:T(8,128)(2,1)}, bf16[256,128]{1,0:T(8,128)(2,1)}, u32[]{:S(2)}, u32[]{:S(2)}) collective-permute-start(bf16[256,128]{1,0:T(8,128)(2,1)} %shard_map.96), channel_id=1, source_target_pairs={{0,2},{1,3},{2,0},{3,1},{4,6},{5,7},{6,4},{7,5},{8,10},{9,11},{10,... | collective-permute-start | bytes 196616 | tf_op jit(solution)/shard_map/ppermute | solution.py:119
  71.1 1.1 copy-start.7
  72.1 2.2 %copy-start.8 = (bf16[320,1024]{1,0:T(8,128)(2,1)S(1)}, bf16[320,1024]{1,0:T(8,128)(2,1)}, u32[]{:S(2)}) copy-start(bf16[320,1024]{1,0:T(8,128)(2,1)} %copy-done.5) | copy-start | bytes 1966084
  72.1 2.2 %copy-start.10 = (bf16[1,64,2048]{2,1,0:T(8,128)(2,1)S(1)}, bf16[1,64,2048]{2,1,0:T(8,128)(2,1)}, u32[]{:S(2)}) copy-start(bf16[1,64,2048]{2,1,0:T(8,128)(2,1)} %param.9) | copy-start | bytes 786436
  74.3 3.6 %copy-start.3 = (bf16[320,1024]{1,0:T(8,128)(2,1)S(1)}, bf16[320,1024]{1,0:T(8,128)(2,1)}, u32[]{:S(2)}) copy-start(bf16[320,1024]{1,0:T(8,128)(2,1)} %copy-done.2) | copy-start | bytes 1966084
  77.7 2.6 %copy-start.12 = (f32[128,1024]{1,0:T(8,128)}, f32[128,1024]{1,0:T(8,128)S(1)}, u32[]{:S(2)}) copy-start(f32[128,1024]{1,0:T(8,128)S(1)} %get-tuple-element.29.near) | copy-start | bytes 1572868
  77.8 5.8 %copy-start.19 = (bf16[128,512]{1,0:T(8,128)(2,1)S(1)}, bf16[128,512]{1,0:T(8,128)(2,1)}, u32[]{:S(2)}) copy-start(bf16[128,512]{1,0:T(8,128)(2,1)} %cot.3) | copy-start | bytes 393220
  77.8 5.8 %copy-start.21 = (bf16[128,512]{1,0:T(8,128)(2,1)S(1)}, bf16[128,512]{1,0:T(8,128)(2,1)}, u32[]{:S(2)}) copy-start(bf16[128,512]{1,0:T(8,128)(2,1)} %copy-done.20) | copy-start | bytes 393220
  77.8 5.8 %copy-start.23 = (bf16[1,64,512]{2,1,0:T(8,128)(2,1)S(1)}, bf16[1,64,512]{2,1,0:T(8,128)(2,1)}, u32[]{:S(2)}) copy-start(bf16[1,64,512]{2,1,0:T(8,128)(2,1)} %param.10) | copy-start | bytes 196612
  77.8 5.8 %copy-start.25 = (bf16[64,512]{1,0:T(8,128)(2,1)S(1)}, bf16[64,512]{1,0:T(8,128)(2,1)}, u32[]{:S(2)}) copy-start(bf16[64,512]{1,0:T(8,128)(2,1)} %copy-done.24) | copy-start | bytes 196612
  77.8 23.5 %collective-permute-start.16 = (bf16[128,1024]{1,0:T(8,128)(2,1)}, bf16[128,1024]{1,0:T(8,128)(2,1)}, u32[]{:S(2)}, u32[]{:S(2)}) collective-permute-start(bf16[128,1024]{1,0:T(8,128)(2,1)} %get-tuple-element.30), channel_id=1, source_target_pairs={{0,8},{4,12},{8,0},{12,4},{1,9},{5,13},{9,1},{13,5},{2,10},{6,14},... | collective-permute-start | bytes 786440 | tf_op jit(solution)/shard_map/ppermute | solution.py:119
  80.4 0.8 copy-start.16
  81.1 18.7 %collective-permute-start.5 = (bf16[256,512]{1,0:T(8,128)(2,1)}, bf16[256,512]{1,0:T(8,128)(2,1)}, u32[]{:S(2)}, u32[]{:S(2)}) collective-permute-start(bf16[256,512]{1,0:T(8,128)(2,1)} %get-tuple-element.23), channel_id=1, source_target_pairs={{0,1},{1,0},{2,3},{3,2},{4,5},{5,4},{6,7},{7,6},{8,9},{9,8},{10,11... | collective-permute-start | bytes 786440 | tf_op jit(solution)/shard_map/ppermute | solution.py:119
  82.0 1.5 %collective-permute-start.10 = (bf16[256,128]{1,0:T(8,128)(2,1)S(1)}, bf16[256,128]{1,0:T(8,128)(2,1)S(1)}, u32[]{:S(2)}, u32[]{:S(2)}) collective-permute-start(bf16[256,128]{1,0:T(8,128)(2,1)S(1)} %add_convert_fusion.low), channel_id=1, source_target_pairs={{0,1},{1,0},{2,3},{3,2},{4,5},{5,4},{6,7},{7,6},{8,9},{9,8},{10,11... | collective-permute-start | bytes 196616 | tf_op jit(solution)/shard_map/ppermute | solution.py:119
  85.6 0.8 copy-start.14
  86.4 0.6 copy-start.28
  87.1 0.7 copy-start.30
  87.7 0.7 copy-start.32
  88.4 33.3 %collective-permute-start.18 = (bf16[64,2560]{1,0:T(8,128)(2,1)}, bf16[64,2560]{1,0:T(8,128)(2,1)}, u32[]{:S(2)}, u32[]{:S(2)}) collective-permute-start(bf16[64,2560]{1,0:T(8,128)(2,1)} %get-tuple-element.35), channel_id=1, source_target_pairs={{0,4},{4,0},{8,12},{12,8},{1,5},{5,1},{9,13},{13,9},{2,6},{6,2},{1... | collective-permute-start | bytes 983048 | tf_op jit(solution)/shard_map/ppermute | solution.py:119
  92.0 1.1 copy-start.4
  93.1 0.9 copy-start.11
  94.1 3.1 %copy-start.33 = (bf16[128,512]{1,0:T(8,128)(2,1)S(1)}, bf16[128,512]{1,0:T(8,128)(2,1)}, u32[]{:S(2)}) copy-start(bf16[128,512]{1,0:T(8,128)(2,1)} %copy-done.32) | copy-start | bytes 393220
  94.1 5.8 %copy-start.17 = (f32[256,512]{1,0:T(8,128)S(1)}, f32[256,512]{1,0:T(8,128)}, u32[]{:S(2)}) copy-start(f32[256,512]{1,0:T(8,128)} %copy-done.16) | copy-start | bytes 1572868
  94.1 23.5 %copy-start.13 = (f32[128,1024]{1,0:T(8,128)S(1)}, f32[128,1024]{1,0:T(8,128)}, u32[]{:S(2)}) copy-start(f32[128,1024]{1,0:T(8,128)} %copy-done.12) | copy-start | bytes 1572868
  96.9 20.8 %collective-permute-start.17 = (bf16[128,1024]{1,0:T(8,128)(2,1)S(1)}, bf16[128,1024]{1,0:T(8,128)(2,1)S(1)}, u32[]{:S(2)}, u32[]{:S(2)}) collective-permute-start(bf16[128,1024]{1,0:T(8,128)(2,1)S(1)} %get-tuple-element.32), channel_id=1, source_target_pairs={{0,8},{4,12},{8,0},{12,4},{1,9},{5,13},{9,1},{13,5},{2,10},{6,14},... | collective-permute-start | bytes 786440 | tf_op jit(solution)/shard_map/ppermute | solution.py:119
  97.2 23.2 %collective-permute-start.15 = (bf16[128,512]{1,0:T(8,128)(2,1)S(1)}, bf16[128,512]{1,0:T(8,128)(2,1)S(1)}, u32[]{:S(2)}, u32[]{:S(2)}) collective-permute-start(bf16[128,512]{1,0:T(8,128)(2,1)S(1)} %copy-done.33), channel_id=1, source_target_pairs={{0,8},{4,12},{8,0},{12,4},{1,9},{5,13},{9,1},{13,5},{2,10},{6,14},... | collective-permute-start | bytes 393224 | tf_op jit(solution)/shard_map/ppermute | solution.py:119
  99.9 20.6 %copy-start.31 = (bf16[128,512]{1,0:T(8,128)(2,1)S(1)}, bf16[128,512]{1,0:T(8,128)(2,1)}, u32[]{:S(2)}) copy-start(bf16[128,512]{1,0:T(8,128)(2,1)} %copy-done.30) | copy-start | bytes 393220
  100.9 19.5 %collective-permute-start.6 = (bf16[128,512]{1,0:T(8,128)(2,1)S(1)}, bf16[128,512]{1,0:T(8,128)(2,1)S(1)}, u32[]{:S(2)}, u32[]{:S(2)}) collective-permute-start(bf16[128,512]{1,0:T(8,128)(2,1)S(1)} %get-tuple-element.24), channel_id=1, source_target_pairs={{0,8},{1,9},{2,0},{3,1},{4,12},{5,13},{6,4},{7,5},{8,10},{9,11},{1... | collective-permute-start | bytes 393224 | tf_op jit(solution)/shard_map/ppermute | solution.py:124
  101.3 19.2 %collective-permute-start.7 = (bf16[128,512]{1,0:T(8,128)(2,1)S(1)}, bf16[128,512]{1,0:T(8,128)(2,1)S(1)}, u32[]{:S(2)}, u32[]{:S(2)}) collective-permute-start(bf16[128,512]{1,0:T(8,128)(2,1)S(1)} %get-tuple-element.25), channel_id=1, source_target_pairs={{2,8},{3,9},{6,12},{7,13},{8,2},{9,3},{12,6},{13,7},{18,24},{19,25... | collective-permute-start | bytes 393224 | tf_op jit(solution)/shard_map/ppermute | solution.py:124
  117.6 4.1 %copy-start.15 = (f32[64,2048]{1,0:T(8,128)S(1)}, f32[64,2048]{1,0:T(8,128)}, u32[]{:S(2)}) copy-start(f32[64,2048]{1,0:T(8,128)} %copy-done.14) | copy-start | bytes 1572868
  117.6 4.1 %copy-start.29 = (f32[64,512]{1,0:T(8,128)S(1)}, f32[64,512]{1,0:T(8,128)}, u32[]{:S(2)}) copy-start(f32[64,512]{1,0:T(8,128)} %copy-done.28) | copy-start | bytes 393220

commit v3 on v2

--- a/solution.py
+++ b/solution.py
@@ -124,10 +124,18 @@
     return lax.ppermute(x, ("fsdp", "tp"), flat)
 
 
+def after(values, *earlier):
+    return lax.optimization_barrier((values, earlier))[0]
+
+
 Y, Z, IN_PAIR, ON_OWN = range(4)
 
 
-def local_kernel(body, outs, where, *args):
+def cost(us):
+    return pl.CostEstimate(flops=0, bytes_accessed=1000 + us * 3_000_000, transcendentals=0)
+
+
+def local_kernel(body, outs, where, *args, us=0):
     single = not isinstance(outs, list)
     shapes = [jax.ShapeDtypeStruct(s, d) for s, d in ([outs] if single else outs)]
     got = pl.pallas_call(
@@ -136,8 +144,8 @@
         in_specs=[pl.BlockSpec(memory_space=pltpu.SMEM)]
         + [pl.BlockSpec(memory_space=pltpu.VMEM)] * len(args),
         out_specs=[pl.BlockSpec(memory_space=pltpu.VMEM)] * len(shapes),
-        compiler_params=pltpu.CompilerParams(vmem_limit_bytes=24 * 1024 * 1024),
-        cost_estimate=pl.CostEstimate(flops=1000, bytes_accessed=1000, transcendentals=0),
+        compiler_params=pltpu.CompilerParams(vmem_limit_bytes=12 * 1024 * 1024),
+        cost_estimate=cost(us),
     )(where, *args)
     return got[0] if single else got
 
@@ -148,11 +156,21 @@
     return idx == jnp.where(lane < rank, z, z ^ 1)
 
 
-def back_kernel(where, cot, cot_got, idx, idx_got, up, up_sib, out):
+def column(row):
+    n = row.shape[1]
+    same = lax.broadcasted_iota(jnp.int32, (n, n), 0) == lax.broadcasted_iota(jnp.int32, (n, n), 1)
+    picked = jnp.where(same, jnp.broadcast_to(row, (n, n)).astype(f32), 0.0)
+    return jnp.sum(picked, axis=1, keepdims=True).astype(jnp.int32)
+
+
+def back_kernel(where, cot, cot_got, idx, up, up_sib, out, members):
     width = cot.shape[1]
-    cot2 = rows2(cot[...], cot_got[...])
+    toks = cot.shape[0]
+    cot2 = rows2(cot[...], cot_got[:toks, :])
     part = adapter_scale * nt(cot2, rows2(up[...], up_sib[...]))
-    mine = member(where, rows2(idx[...], idx_got[...]), up.shape[0])
+    idx_got = cot_got[toks:, :toks].astype(f32)[:1].astype(jnp.int32)
+    mine = member(where, rows2(column(idx[...]), column(idx_got)), up.shape[0])
+    members[...] = mine.astype(bf16)
     out[:, :width] = cot2
     out[:, width:] = jnp.where(mine, part, 0.0).astype(bf16)
 
@@ -178,12 +196,12 @@
 
 def gradient_kernel(where, mine, got, weight, down, first, second, top, bottom):
     rank = down.shape[0]
-    half = second.shape[0]
+    head = first.shape[0] - rank
     c_own, c_sib = pair_blocks(where, mine, got)
     back = whole_back(mine, got)
     g = nn(c_own, weight[...])
-    g += nn(c_sib[:, :half], first[rank:, :])
-    g += nn(c_sib[:, half:], second[...])
+    g += nn(c_sib[:, :head], first[rank:, :])
+    g += nn(c_sib[:, head:], second[...])
     g += nn(back, rows2(down[...], first[:rank, :]))
     toks = top.shape[0]
     top[...] = g[:toks]
@@ -215,8 +233,8 @@
             jax.ShapeDtypeStruct((toks, steps * tile), f32),
             jax.ShapeDtypeStruct((toks, steps * tile), bf16),
         ],
-        compiler_params=pltpu.CompilerParams(vmem_limit_bytes=24 * 1024 * 1024),
-        cost_estimate=pl.CostEstimate(flops=1000, bytes_accessed=1000, transcendentals=0),
+        compiler_params=pltpu.CompilerParams(vmem_limit_bytes=12 * 1024 * 1024),
+        cost_estimate=cost(0),
     )(jnp.concatenate([where, side[None]]), mine, got, weight, down, first, second)
 
 
@@ -229,30 +247,29 @@
     out[:, at] = (far[...] + far_got[...].astype(f32)).astype(bf16)
 
 
-def low_kernel(where, act, act_got, idx, idx_got, down, near, far, out):
+def low_kernel(where, act, act_got, members, down, near, far, out):
     rank, half = down.shape[0], near.shape[1]
     y = where[Y]
     at_near = pl.ds(pl.multiple_of(y * half, half), half)
     at_far = pl.ds(pl.multiple_of((1 - y) * half, half), half)
     part = nt(rows2(act[:, at_near], act_got[:, at_near]), rows2(down[:, at_near], near[:rank, :]))
     part += nt(rows2(act[:, at_far], act_got[:, at_far]), rows2(down[:, at_far], far[:rank, :]))
-    mine = member(where, rows2(idx[...], idx_got[...]), rank)
-    out[...] = jnp.where(mine, part, 0.0).astype(bf16)
+    out[...] = jnp.where(members[...] != 0, part, 0.0).astype(bf16)
 
 
 def adapter_kernel(
-    where, low, low_got, mine, got, act, act_got, cot, cot_got, up, up_sib,
+    where, give, give_got, mine, got, act, act_got, cot, cot_got, up, up_sib,
     lora, lora_far, down_own, up_own, sib,
 ):
     rank, width, toks = up.shape[0], act.shape[1], act.shape[0]
-    whole_low = (low[...].astype(f32) + low_got[...].astype(f32)).astype(bf16)
+    whole_low = whole_back(give, give_got)
     out = (adapter_scale * nn(whole_low, rows2(up[...], up_sib[...]))).astype(bf16)
     lora[...] = out[:toks]
     lora_far[...] = out[toks:]
     grad = tn(whole_back(mine, got), rows2(act[...], act_got[...]))
     down_own[...] = grad[:rank]
     sib[:, :width] = grad[rank:].astype(bf16)
-    grad = adapter_scale * tn(whole_low, rows2(cot[...], cot_got[...]))
+    grad = adapter_scale * tn(whole_low, rows2(cot[...], cot_got[: cot.shape[0], :]))
     up_own[...] = grad[:rank]
     sib[:, width:] = grad[rank:].astype(bf16)
 
@@ -264,35 +281,36 @@
 
 
 def base_near_kernel(where, act, act_got, weight, first, second, out):
-    rows, half = weight.shape[0], second.shape[0]
-    cut = first.shape[0] - half
+    rows = weight.shape[0]
+    head = rows - second.shape[0]
+    cut = first.shape[0] - head
     wide = first.shape[1]
     at = pl.ds(pl.multiple_of(where[Y] * wide, wide), wide)
     near = rows2(act[:, at], act_got[:, at])
     out[:, :rows] = nt(rows2(act[...], act_got[...]), weight[...])
-    out[:, rows : rows + half] = nt(near, first[cut:, :])
-    out[:, rows + half :] = nt(near, second[...])
-
-
-def base_far_kernel(where, part, act, act_got, first, second, keep, give):
-    half = second.shape[0]
-    rows = 2 * half
-    cut = first.shape[0] - half
+    out[:, rows : rows + head] = nt(near, first[cut:, :])
+    out[:, rows + head :] = nt(near, second[...])
+
+
+def base_far_kernel(where, part, act, act_got, first, second, low, low_got, keep, give):
+    rows = keep.shape[1]
+    head = rows - second.shape[0]
+    cut = first.shape[0] - head
     wide = first.shape[1]
     at = pl.ds(pl.multiple_of((1 - where[Y]) * wide, wide), wide)
     far = rows2(act[:, at], act_got[:, at])
     on_own = jnp.full((1, 1), where[ON_OWN], jnp.int32) == 1
-    for k, block in ((0, first[cut:, :]), (1, second[...])):
-        at = slice(k * half, (k + 1) * half)
-        mine = part[:, k * half : (k + 1) * half]
-        other = part[:, rows + k * half : rows + (k + 1) * half] + nt(far, block)
-        keep[:, at] = jnp.where(on_own, mine, other)
-        give[:, at] = jnp.where(on_own, other, mine).astype(bf16)
+    for lo, hi, block in ((0, head, first[cut:, :]), (head, rows, second[...])):
+        mine = part[:, lo:hi]
+        other = part[:, rows + lo : rows + hi] + nt(far, block)
+        keep[:, lo:hi] = jnp.where(on_own, mine, other)
+        give[:, lo:hi] = jnp.where(on_own, other, mine).astype(bf16)
+    give[:, rows:] = (low[...].astype(f32) + low_got[...].astype(f32)).astype(bf16)
 
 
 def held_kernel(where, keep, got, here, there, turn):
-    toks = here.shape[0]
-    held = (keep[...] + got[...].astype(f32)).astype(bf16)
+    toks, rows = here.shape
+    held = (keep[...] + got[:, :rows].astype(f32)).astype(bf16)
     in_pair = jnp.full((1, 1), where[IN_PAIR], jnp.int32) == 1
     here[...] = held[:toks]
     there[...] = held[toks:]
@@ -326,51 +344,64 @@
     rank = down.shape[0]
     places = [(zz, xx, cc) for zz in range(4) for xx in range(2) for cc in range(2)]
 
-    cot_got = swap(cotangent, "fsdp", 2)
-    idx_got = swap(token_adapter_index, "fsdp", 2)
+    idx = token_adapter_index.reshape(1, toks)
+    idx_row = jnp.pad(idx.astype(bf16), ((0, 15), (0, out_width - toks)))
+    cot_got = swap(jnp.concatenate([cotangent, idx_row], axis=0), "fsdp", 2)
     up_sib = swap(up, "fsdp", 1)
     w_mine = lax.dynamic_slice(key_value_weight, (0, y * wide), (rows, wide))
     d_mine = lax.dynamic_slice(down, (0, y * wide), (rank, wide))
-    piece = jnp.concatenate([d_mine, w_mine[:half]], axis=0)
-    near0 = swap(piece, "fsdp", 1)
-    act_sent, _ = lax.optimization_barrier((activations, piece))
-    act_got = swap(act_sent, "fsdp", 2)
-    near1 = swap(w_mine[half:], "fsdp", 1)
-
-    mine = local_kernel(
-        back_kernel, ((2 * toks, out_width + 2 * rank), bf16), where,
-        cotangent, cot_got, token_adapter_index, idx_got, up, up_sib,
-    )
-    mine = local_kernel(block_kernel, (mine.shape, bf16), where, mine, swap(mine, "tp", 2))
-    got = swap(mine, "tp", 1)
-
+    head = rows * 2 // 4
+    piece0 = jnp.concatenate([d_mine, w_mine[:head]], axis=0)
+    piece1 = w_mine[head:]
+    piece0, piece1 = after((piece0, piece1), cot_got, up_sib)
+    near0 = swap(piece0, "fsdp", 1)
+    near1 = swap(piece1, "fsdp", 1)
+
+    mine, members = local_kernel(
+        back_kernel,
+        [((2 * toks, out_width + 2 * rank), bf16), ((2 * toks, 2 * rank), bf16)],
+        where,
+        cotangent, cot_got, idx, up, up_sib, us=20,
+    )
+    mine_x = swap(mine, "tp", 2)
+    act_got = swap(after(activations, mine), "fsdp", 2)
+    near0 = after(near0, mine)
     far0 = swap(near0, "groups", 1)
     far1 = swap(near1, "groups", 1)
+    mine_x = after(mine_x, near1)
+    mine = local_kernel(block_kernel, (mine.shape, bf16), where, mine, mine_x)
+    got = swap(mine, "tp", 1)
 
     near, near_sent = gradient_half(where, y, mine, got, key_value_weight, down, near0, near1)
     near_got = swap(near_sent, "fsdp", 2)
 
+    act_got = after(act_got, near_sent)
     part = local_kernel(
         base_near_kernel, ((2 * toks, 2 * rows), f32), where,
-        activations, act_got, key_value_weight, near0, near1,
-    )
-
+        activations, act_got, key_value_weight, near0, near1, us=15,
+    )
+
+    far0 = after(far0, part)
     low = local_kernel(
         low_kernel, ((2 * toks, 2 * rank), bf16), where,
-        activations, act_got, token_adapter_index, idx_got, down, near0, far0,
-    )
-    low = (low.astype(f32) + swap(low, "tp", 2).astype(f32)).astype(bf16)
-    low_got = swap(low, "tp", 1)
-
+        activations, act_got, members, down, near0, far0,
+    )
+    low_x = swap(low, "tp", 2)
+
+    far1 = after(far1, low)
     far, far_sent = gradient_half(where, 1 - y, mine, got, key_value_weight, down, far0, far1)
     far_got = swap(far_sent, "fsdp", 2)
 
+    part, near_got = after((part, near_got), far_sent)
     keep, give = local_kernel(
-        base_far_kernel, [((2 * toks, rows), f32), ((2 * toks, rows), bf16)], where,
-        part, activations, act_got, far0, far1,
-    )
+        base_far_kernel,
+        [((2 * toks, rows), f32), ((2 * toks, rows + 2 * rank), bf16)],
+        where,
+        part, activations, act_got, far0, far1, low, low_x, us=10,
+    )
+    give_got = swap(give, "tp", 1)
     here, there, turn = local_kernel(
-        held_kernel, [((toks, rows), bf16)] * 3, where, keep, swap(give, "tp", 1)
+        held_kernel, [((toks, rows), bf16)] * 3, where, keep, give_got
     )
     one = both(
         turn,
@@ -378,6 +409,7 @@
     )
     two = both(there, [((a, b, d), (a ^ 2, 1 - b, d)) for a, b, d in places if b != a // 2])
 
+    give_got = after(give_got, here)
     lora, lora_far, down_own, up_own, sib = local_kernel(
         adapter_kernel,
         [
@@ -388,7 +420,7 @@
             ((rank, width + out_width), bf16),
         ],
         where,
-        low, low_got, mine, got, activations, act_got, cotangent, cot_got, up, up_sib,
+        give, give_got, mine, got, activations, act_got, cotangent, cot_got, up, up_sib, us=5,
     )
     lora_got = swap(lora_far, "fsdp", 2)
     grad_down, up_gradient = local_kernel(

time: 125 us -> 107 us (0.86)
  local copies, waits for them, and re-layouts: 13 us -> 5.63 us
  waiting for transfers between devices: 61.8 us -> 54.9 us
  starting transfers between devices: 24.8 us -> 20.6 us
  other arithmetic: 1.01 us -> 2.53 us
    unnamed x71 -> x40, local copies, waits for them, and re-layouts: 10.6 us -> 3.38 us
    ppermute x17 -> x15, waiting for transfers between devices: 61.8 us -> 54.9 us  [swap(): lax.ppermute(x, axis, [(i, i ^ bit) for i in range(lax.axis_size(axis))])]
    ppermute x17 -> x15, starting transfers between devices: 23.8 us -> 19.2 us  [swap(): lax.ppermute(x, axis, [(i, i ^ bit) for i in range(lax.axis_size(axis))])]
    concatenate x1 -> x2, other arithmetic: 0.04 us -> 1.79 us  [the longest x1 0.91 us: pair_plan(): cot_got = swap(jnp.concatenate([cotangent, idx_row], axis=0), 'fsdp', 2)]
  transfers between devices with their start and end apart: 19 -> 17, of which waited for: 8 -> 8; matrix products, arithmetic and copies ran while one was open for 1% -> 5% of each run, Pallas kernels for 16% -> 15%
where the time goes in v3:
time: 107 us; the launch traced here: 106 us
  waiting for transfers between devices  54.9 us (51%)
  Pallas kernels  21.2 us (20%)
  starting transfers between devices  20.6 us (19%)
  local copies, waits for them, and re-layouts  5.63 us (5%)
  other arithmetic  2.53 us (2%)
    ppermute x15, waiting for transfers between devices, swap(): lax.ppermute(x, axis, [(i, i ^ bit) for i in range(lax.axis_size(axis))])  54.9 us
    ppermute x15, starting transfers between devices, swap(): lax.ppermute(x, axis, [(i, i ^ bit) for i in range(lax.axis_size(axis))])  19.2 us
    pallas_call x10, Pallas kernels, local_kernel(): pl.pallas_call(body, out_shape=shapes, in_specs=[pl.BlockSpec(memory_spac...  14.8 us
    pallas_call x2, Pallas kernels, gradient_half(): pl.pallas_call(gradient_kernel, grid_spec=pltpu.PrefetchScalarGridSpec(nu...  6.35 us
    unnamed x40, local copies, waits for them, and re-layouts  3.38 us
  transfers between devices with their start and end apart: 17, of which 8 were waited for; matrix products, arithmetic and copies ran while one was open for 5% of the time, Pallas kernels for 15%

profile of v3, /device:TPU:0, one launch (start us, length us, event | category | flops | bytes accessed | tf_op | source)
XLA Modules:
  0.0 105.7 jit_solution(7767894974573944626)
XLA Ops:
  0.6 0.0 copy-start.4
  0.6 3.1 %collective-permute-start.1 = (bf16[64,512]{1,0:T(8,128)(2,1)}, bf16[64,512]{1,0:T(8,128)(2,1)S(1)}, u32[]{:S(2)}, u32[]{:S(2)}) collective-permute-start(bf16[64,512]{1,0:T(8,128)(2,1)} %bitcast.14), channel_id=1, source_target_pairs={{0,4},{4,0},{8,12},{12,8},{1,5},{5,1},{9,13},{13,9},{2,6},{6,2},{1... | collective-permute-start | bytes 196616 | tf_op jit(solution)/shard_map/ppermute | solution.py:119
  3.7 0.7 bitcast_convert_fusion
  4.4 0.9 fusion.1
  5.3 2.7 %collective-permute-start = (bf16[144,512]{1,0:T(8,128)(2,1)S(1)}, bf16[144,512]{1,0:T(8,128)(2,1)S(1)}, u32[]{:S(2)}, u32[]{:S(2)}) collective-permute-start(bf16[144,512]{1,0:T(8,128)(2,1)S(1)} %fusion.1), channel_id=1, source_target_pairs={{0,8},{4,12},{8,0},{12,4},{1,9},{5,13},{9,1},{13,5},{2,10},{6,14},... | collective-permute-start | bytes 442376 | tf_op jit(solution)/shard_map/ppermute | solution.py:119
  8.0 2.1 %fusion.2 = (bf16[256,1024]{1,0:T(8,128)(2,1)}, bf16[256,1024]{1,0:T(8,128)(2,1)S(1)}) fusion(bf16[512,2048]{1,0:T(8,128)(2,1)} %weight.5, s32[]{:T(128)S(6)} %add.21, s32[]{:T(128)S(6)} %select_n.26), kind=kLoop, calls=%fused_computation.8 | loop fusion | bytes 2097160 | tf_op jit(solution)/shard_map/slice | solution.py:355
  10.0 0.0 copy-start.1
  10.1 0.0 copy-start
  10.1 0.9 pad_maximum_fusion
  11.0 0.0 collective-permute-done.1.up_sib
  11.0 3.7 %collective-permute-done.cot_got = bf16[144,512]{1,0:T(8,128)(2,1)S(1)} collective-permute-done((bf16[144,512]{1,0:T(8,128)(2,1)S(1)}, bf16[144,512]{1,0:T(8,128)(2,1)S(1)}, u32[]{:S(2)}, u32[]{:S(2)}) %collective-permute-start) | collective-permute-done | bytes 147488 | tf_op jit(solution)/shard_map/ppermute | solution.py:119
  14.7 0.0 collective-permute-start.6
  14.7 2.0 %collective-permute-start.4 = (bf16[256,1024]{1,0:T(8,128)(2,1)}, bf16[256,1024]{1,0:T(8,128)(2,1)}, u32[]{:S(2)}, u32[]{:S(2)}) collective-permute-start(bf16[256,1024]{1,0:T(8,128)(2,1)} %get-tuple-element.35), channel_id=1, source_target_pairs={{0,4},{4,0},{8,12},{12,8},{1,5},{5,1},{9,13},{13,9},{2,6},{6,2},{1... | collective-permute-start | bytes 1572872 | tf_op jit(solution)/shard_map/ppermute | solution.py:119
  16.7 0.1 pad_add_fusion.where
  16.8 0.0 copy-done.8
  16.8 0.0 copy-done.19
  16.8 0.8 shard_map.93
  17.6 0.0 copy-start.17
  17.6 0.6 copy-done.17
  18.2 1.5 %collective-permute-start.3 = (bf16[256,640]{1,0:T(8,128)(2,1)S(1)}, bf16[256,640]{1,0:T(8,128)(2,1)S(1)}, u32[]{:S(2)}, u32[]{:S(2)}) collective-permute-start(bf16[256,640]{1,0:T(8,128)(2,1)S(1)} %get-tuple-element.33.mine), channel_id=1, source_target_pairs={{0,2},{1,3},{2,0},{3,1},{4,6},{5,7},{6,4},{7,5},{8,10},{9,11},{10,... | collective-permute-start | bytes 983048 | tf_op jit(solution)/shard_map/ppermute | solution.py:119
  19.7 12.9 %collective-permute-done.6.first.near = bf16[320,1024]{1,0:T(8,128)(2,1)} collective-permute-done((bf16[320,1024]{1,0:T(8,128)(2,1)}, bf16[320,1024]{1,0:T(8,128)(2,1)}, u32[]{:S(2)}, u32[]{:S(2)}) %collective-permute-start.6) | collective-permute-done | bytes 655392 | tf_op jit(solution)/shard_map/ppermute | solution.py:119
  32.6 1.5 %collective-permute-start.8 = (bf16[320,1024]{1,0:T(8,128)(2,1)}, bf16[320,1024]{1,0:T(8,128)(2,1)}, u32[]{:S(2)}, u32[]{:S(2)}) collective-permute-start(bf16[320,1024]{1,0:T(8,128)(2,1)} %collective-permute-done.6.first.near), channel_id=1, source_target_pairs={{0,16},{16,0},{1,17},{17,1},{2,18},{18,2},{3,19},{19,3},{4,20},{20... | collective-permute-start | bytes 1966088 | tf_op jit(solution)/shard_map/ppermute | solution.py:119
  34.1 1.1 %collective-permute-start.2 = (bf16[128,2048]{1,0:T(8,128)(2,1)S(1)}, bf16[128,2048]{1,0:T(8,128)(2,1)S(1)}, u32[]{:S(2)}, u32[]{:S(2)}) collective-permute-start(bf16[128,2048]{1,0:T(8,128)(2,1)S(1)} %copy-done.1), channel_id=1, source_target_pairs={{0,8},{4,12},{8,0},{12,4},{1,9},{5,13},{9,1},{13,5},{2,10},{6,14},... | collective-permute-start | bytes 1572872 | tf_op jit(solution)/shard_map/ppermute | solution.py:119
  35.3 0.0 collective-permute-done.3.got
  35.3 15.1 %collective-permute-done.4.second = bf16[256,1024]{1,0:T(8,128)(2,1)} collective-permute-done((bf16[256,1024]{1,0:T(8,128)(2,1)}, bf16[256,1024]{1,0:T(8,128)(2,1)}, u32[]{:S(2)}, u32[]{:S(2)}) %collective-permute-start.4) | collective-permute-done | bytes 524320 | tf_op jit(solution)/shard_map/ppermute | solution.py:119
  50.4 0.6 shard_map.94.mine
  51.0 0.1 collective-permute-start.5
  51.1 2.5 %collective-permute-start.9 = (bf16[256,1024]{1,0:T(8,128)(2,1)}, bf16[256,1024]{1,0:T(8,128)(2,1)}, u32[]{:S(2)}, u32[]{:S(2)}) collective-permute-start(bf16[256,1024]{1,0:T(8,128)(2,1)} %collective-permute-done.4.second), channel_id=1, source_target_pairs={{0,16},{16,0},{1,17},{17,1},{2,18},{18,2},{3,19},{19,3},{4,20},{20... | collective-permute-start | bytes 1572872 | tf_op jit(solution)/shard_map/ppermute | solution.py:119
  53.5 0.1 concatenate.15.where
  53.6 0.0 collective-permute-done.5.got
  53.6 0.9 copy-done.5
  54.6 3.5 %shard_map.95 = (f32[128,1024]{1,0:T(8,128)S(1)}, bf16[128,1024]{1,0:T(8,128)(2,1)}) custom-call(s32[5]{0:T(128)S(1)} %concatenate.15.where, bf16[256,640]{1,0:T(8,128)(2,1)S(1)} %shard_map.94.mine, bf16[256,640]{1,0:T(8,128)(2,1)} %collective-permute-done.5.got, bf16[512,2048]{1,0:T(8,128)(2,1)S(1)} %copy-done, bf16[64,2048]{1,0:T(8,128)(2,1)S(1)} %bitcast.11, ...), custom_call_target="tpu_custom_call" | custom-call | bytes 1000 | tf_op jit(solution)/shard_map/pallas_call | solution.py:217
  58.1 0.8 copy-done.12
  58.9 0.0 collective-permute-start.7
  58.9 0.0 collective-permute-done.2.act_got
  58.9 2.3 %shard_map.96.part = f32[256,1024]{1,0:T(8,128)S(1)} custom-call(s32[4]{0:T(128)S(1)} %pad_add_fusion.where, bf16[128,2048]{1,0:T(8,128)(2,1)S(1)} %copy-done.1, bf16[128,2048]{1,0:T(8,128)(2,1)S(1)} %collective-permute-done.2.act_got, bf16[512,2048]{1,0:T(8,128)(2,1)S(1)} %copy-done, bf16[320,1024]{1,0:T(8,128)(2,1)} %collective-permute-done.6.first.near, ...), custom_call_target="tpu_custom_call" | custom-call | bytes 45001000 | tf_op jit(solution)/shard_map/pallas_call | solution.py:141
  61.2 0.0 collective-permute-done.8.far.first
  61.2 2.7 %shard_map.97.low = bf16[256,128]{1,0:T(8,128)(2,1)} custom-call(s32[4]{0:T(128)S(1)} %pad_add_fusion.where, bf16[128,2048]{1,0:T(8,128)(2,1)S(1)} %copy-done.1, bf16[128,2048]{1,0:T(8,128)(2,1)S(1)} %collective-permute-done.2.act_got, bf16[256,128]{1,0:T(8,128)(2,1)S(1)} %copy-done.18, bf16[64,2048]{1,0:T(8,128)(2,1)S(1)} %bitcast.12, ...), custom_call_target="tpu_custom_call" | custom-call | bytes 1000 | tf_op jit(solution)/shard_map/pallas_call | solution.py:141
  64.0 1.6 %collective-permute-start.10 = (bf16[256,128]{1,0:T(8,128)(2,1)}, bf16[256,128]{1,0:T(8,128)(2,1)}, u32[]{:S(2)}, u32[]{:S(2)}) collective-permute-start(bf16[256,128]{1,0:T(8,128)(2,1)} %shard_map.97.low), channel_id=1, source_target_pairs={{0,2},{1,3},{2,0},{3,1},{4,6},{5,7},{6,4},{7,5},{8,10},{9,11},{10,... | collective-permute-start | bytes 196616 | tf_op jit(solution)/shard_map/ppermute | solution.py:119
  65.5 0.1 concatenate.17.where
  65.6 0.8 collective-permute-done.9.second
  66.4 0.9 copy-done.7
  67.3 2.9 %shard_map.98 = (f32[128,1024]{1,0:T(8,128)S(1)}, bf16[128,1024]{1,0:T(8,128)(2,1)S(1)}) custom-call(s32[5]{0:T(128)S(1)} %concatenate.17.where, bf16[256,640]{1,0:T(8,128)(2,1)S(1)} %shard_map.94.mine, bf16[256,640]{1,0:T(8,128)(2,1)} %collective-permute-done.5.got, bf16[512,2048]{1,0:T(8,128)(2,1)S(1)} %copy-done, bf16[64,2048]{1,0:T(8,128)(2,1)S(1)} %bitcast.13, ...), custom_call_target="tpu_custom_call" | custom-call | bytes 1000 | tf_op jit(solution)/shard_map/pallas_call | solution.py:217
  70.2 2.9 %collective-permute-done.7.near_got = bf16[128,1024]{1,0:T(8,128)(2,1)} collective-permute-done((bf16[128,1024]{1,0:T(8,128)(2,1)}, bf16[128,1024]{1,0:T(8,128)(2,1)}, u32[]{:S(2)}, u32[]{:S(2)}) %collective-permute-start.7) | collective-permute-done | bytes 262176 | tf_op jit(solution)/shard_map/ppermute | solution.py:119
  73.1 0.0 collective-permute-done.10.low_got
  73.1 1.8 %shard_map.99 = (f32[256,512]{1,0:T(8,128)S(1)}, bf16[256,640]{1,0:T(8,128)(2,1)S(1)}) custom-call(s32[4]{0:T(128)S(1)} %pad_add_fusion.where, f32[256,1024]{1,0:T(8,128)S(1)} %copy-done.3, bf16[128,2048]{1,0:T(8,128)(2,1)S(1)} %copy-done.1, bf16[128,2048]{1,0:T(8,128)(2,1)S(1)} %collective-permute-done.2.act_got, ...), custom_call_target="tpu_custom_call" | custom-call | bytes 30001000 | tf_op jit(solution)/shard_map/pallas_call | solution.py:141
  74.9 0.1 collective-permute-start.11
  75.0 1.6 %collective-permute-done.11.got.give_got = bf16[256,640]{1,0:T(8,128)(2,1)S(1)} collective-permute-done((bf16[256,640]{1,0:T(8,128)(2,1)S(1)}, bf16[256,640]{1,0:T(8,128)(2,1)S(1)}, u32[]{:S(2)}, u32[]{:S(2)}) %collective-permute-start.11) | collective-permute-done | bytes 327712 | tf_op jit(solution)/shard_map/ppermute | solution.py:119
  76.6 0.6 shard_map.100
  77.2 0.0 copy-start.13
  77.2 1.4 %shard_map.101 = (bf16[128,512]{1,0:T(8,128)(2,1)S(1)}, bf16[128,512]{1,0:T(8,128)(2,1)S(1)}, f32[64,2048]{1,0:T(8,128)S(1)}, f32[64,512]{1,0:T(8,128)S(1)}, bf16[64,2560]{1,0:T(8,128)(2,1)S(1)}) custom-call(s32[4]{0:T(128)S(1)} %pad_add_fusion.where, bf16[256,640]{1,0:T(8,128)(2,1)S(1)} %get-tuple-element.47.give, ...), custom_call_target="tpu_custom_call" | custom-call | bytes 15001000 | tf_op jit(solution)/shard_map/pallas_call | solution.py:141
  78.7 0.1 collective-permute-start.16
  78.8 0.8 collective-permute-start.15
  79.6 2.2 %collective-permute-start.14 = (bf16[128,512]{1,0:T(8,128)(2,1)S(1)}, bf16[128,512]{1,0:T(8,128)(2,1)S(1)}, u32[]{:S(2)}, u32[]{:S(2)}) collective-permute-start(bf16[128,512]{1,0:T(8,128)(2,1)S(1)} %get-tuple-element.53), channel_id=1, source_target_pairs={{0,8},{4,12},{8,0},{12,4},{1,9},{5,13},{9,1},{13,5},{2,10},{6,14},... | collective-permute-start | bytes 393224 | tf_op jit(solution)/shard_map/ppermute | solution.py:119
  81.8 0.8 collective-permute-start.12
  82.5 0.7 collective-permute-start.13
  83.2 17.0 %collective-permute-done.15.far_got = bf16[128,1024]{1,0:T(8,128)(2,1)S(1)} collective-permute-done((bf16[128,1024]{1,0:T(8,128)(2,1)S(1)}, bf16[128,1024]{1,0:T(8,128)(2,1)S(1)}, u32[]{:S(2)}, u32[]{:S(2)}) %collective-permute-start.15) | collective-permute-done | bytes 262176 | tf_op jit(solution)/shard_map/ppermute | solution.py:119
  100.2 1.9 %shard_map.103 = bf16[128,2048]{1,0:T(8,128)(2,1)} custom-call(s32[4]{0:T(128)S(1)} %pad_add_fusion.where, f32[128,1024]{1,0:T(8,128)S(1)} %copy-done.13, bf16[128,1024]{1,0:T(8,128)(2,1)} %collective-permute-done.7.near_got, f32[128,1024]{1,0:T(8,128)S(1)} %get-tuple-element.56.far, bf16[128,1024]{1,0:T(8,128)(2,1)S(1)} %collective-permute-done.15.far_got), custom_call_target="tpu_custom_call" | custom-call | bytes 1000 | tf_op jit(solution)/shard_map/pallas_call | solution.py:141
  102.0 1.0 collective-permute-done.14.lora_got
  103.0 0.0 collective-permute-done.12.one
  103.0 0.0 collective-permute-done.13.two
  103.0 1.3 %shard_map.102 = bf16[128,512]{1,0:T(8,128)(2,1)} custom-call(s32[4]{0:T(128)S(1)} %pad_add_fusion.where, bf16[128,512]{1,0:T(8,128)(2,1)S(1)} %collective-permute-done.12.one, bf16[128,512]{1,0:T(8,128)(2,1)S(1)} %collective-permute-done.13.two, bf16[128,512]{1,0:T(8,128)(2,1)S(1)} %get-tuple-element.50.here, bf16[128,512]{1,0:T(8,128)(2,1)S(1)} %get-tuple-element.52.lora, ...), custom_call_target="tpu_custom_call" | custom-call | bytes 1000 | tf_op jit(solution)/shard_map/pallas_call | solution.py:141
  104.3 0.0 collective-permute-done.16.got
  104.3 1.4 %shard_map.104 = (f32[1,64,2048]{2,1,0:T(8,128)}, f32[1,64,512]{2,1,0:T(8,128)}) custom-call(s32[4]{0:T(128)S(1)} %pad_add_fusion.where, f32[64,2048]{1,0:T(8,128)S(1)} %get-tuple-element.57.down_own, f32[64,512]{1,0:T(8,128)S(1)} %get-tuple-element.58.up_own, bf16[64,2560]{1,0:T(8,128)(2,1)S(1)} %collective-permute-done.16.got), custom_call_target="tpu_custom_call" | custom-call | bytes 1000 | tf_op jit(solution)/shard_map/pallas_call | solution.py:141
  (30 shorter events, 0.1 us)
Async XLA Ops:
  0.6 9.4 %copy-start.4 = (bf16[1,64,2048]{2,1,0:T(8,128)(2,1)S(1)}, bf16[1,64,2048]{2,1,0:T(8,128)(2,1)}, u32[]{:S(2)}) copy-start(bf16[1,64,2048]{2,1,0:T(8,128)(2,1)} %param.9) | copy-start | bytes 786436
  0.6 10.3 %collective-permute-start.1 = (bf16[64,512]{1,0:T(8,128)(2,1)}, bf16[64,512]{1,0:T(8,128)(2,1)S(1)}, u32[]{:S(2)}, u32[]{:S(2)}) collective-permute-start(bf16[64,512]{1,0:T(8,128)(2,1)} %bitcast.14), channel_id=1, source_target_pairs={{0,4},{4,0},{8,12},{12,8},{1,5},{5,1},{9,13},{13,9},{2,6},{6,2},{1... | collective-permute-start | bytes 196616 | tf_op jit(solution)/shard_map/ppermute | solution.py:119
  5.3 9.3 %collective-permute-start = (bf16[144,512]{1,0:T(8,128)(2,1)S(1)}, bf16[144,512]{1,0:T(8,128)(2,1)S(1)}, u32[]{:S(2)}, u32[]{:S(2)}) collective-permute-start(bf16[144,512]{1,0:T(8,128)(2,1)S(1)} %fusion.1), channel_id=1, source_target_pairs={{0,8},{4,12},{8,0},{12,4},{1,9},{5,13},{9,1},{13,5},{2,10},{6,14},... | collective-permute-start | bytes 442376 | tf_op jit(solution)/shard_map/ppermute | solution.py:119
  10.0 6.7 %copy-start.8 = (bf16[128,512]{1,0:T(8,128)(2,1)S(1)}, bf16[128,512]{1,0:T(8,128)(2,1)}, u32[]{:S(2)}) copy-start(bf16[128,512]{1,0:T(8,128)(2,1)} %cot.3) | copy-start | bytes 393220
  10.0 6.7 %copy-start.14 = (bf16[1,64,512]{2,1,0:T(8,128)(2,1)S(1)}, bf16[1,64,512]{2,1,0:T(8,128)(2,1)}, u32[]{:S(2)}) copy-start(bf16[1,64,512]{2,1,0:T(8,128)(2,1)} %param.10) | copy-start | bytes 196612
  10.0 6.7 %copy-start.19 = (s32[128,1]{0,1:T(1,128)S(1)}, s32[128,1]{0,1:T(1,128)}, u32[]{:S(2)}) copy-start(s32[128,1]{0,1:T(1,128)} %param.8) | copy-start | bytes 1540
  10.0 24.1 %copy-start.1 = (bf16[128,2048]{1,0:T(8,128)(2,1)S(1)}, bf16[128,2048]{1,0:T(8,128)(2,1)}, u32[]{:S(2)}) copy-start(bf16[128,2048]{1,0:T(8,128)(2,1)} %act.7) | copy-start | bytes 1572868
  10.1 43.6 %copy-start = (bf16[512,2048]{1,0:T(8,128)(2,1)S(1)}, bf16[512,2048]{1,0:T(8,128)(2,1)}, u32[]{:S(2)}) copy-start(bf16[512,2048]{1,0:T(8,128)(2,1)} %weight.5) | copy-start | bytes 6291460
  11.0 21.7 %copy-start.15 = (bf16[64,512]{1,0:T(8,128)(2,1)}, bf16[64,512]{1,0:T(8,128)(2,1)S(1)}, u32[]{:S(2)}) copy-start(bf16[64,512]{1,0:T(8,128)(2,1)S(1)} %collective-permute-done.1.up_sib) | copy-start | bytes 196612
  14.7 18.0 %copy-start.10 = (bf16[144,512]{1,0:T(8,128)(2,1)}, bf16[144,512]{1,0:T(8,128)(2,1)S(1)}, u32[]{:S(2)}) copy-start(bf16[144,512]{1,0:T(8,128)(2,1)S(1)} %collective-permute-done.cot_got) | copy-start | bytes 442372
  14.7 18.0 %collective-permute-start.6 = (bf16[320,1024]{1,0:T(8,128)(2,1)}, bf16[320,1024]{1,0:T(8,128)(2,1)}, u32[]{:S(2)}, u32[]{:S(2)}) collective-permute-start(bf16[320,1024]{1,0:T(8,128)(2,1)} %pad_maximum_fusion), channel_id=1, source_target_pairs={{0,4},{4,0},{8,12},{12,8},{1,5},{5,1},{9,13},{13,9},{2,6},{6,2},{1... | collective-permute-start | bytes 1966088 | tf_op jit(solution)/shard_map/ppermute | solution.py:119
  14.7 35.7 %collective-permute-start.4 = (bf16[256,1024]{1,0:T(8,128)(2,1)}, bf16[256,1024]{1,0:T(8,128)(2,1)}, u32[]{:S(2)}, u32[]{:S(2)}) collective-permute-start(bf16[256,1024]{1,0:T(8,128)(2,1)} %get-tuple-element.35), channel_id=1, source_target_pairs={{0,4},{4,0},{8,12},{12,8},{1,5},{5,1},{9,13},{13,9},{2,6},{6,2},{1... | collective-permute-start | bytes 1572872 | tf_op jit(solution)/shard_map/ppermute | solution.py:119
  17.6 0.6 copy-start.17
  18.2 17.1 %collective-permute-start.3 = (bf16[256,640]{1,0:T(8,128)(2,1)S(1)}, bf16[256,640]{1,0:T(8,128)(2,1)S(1)}, u32[]{:S(2)}, u32[]{:S(2)}) collective-permute-start(bf16[256,640]{1,0:T(8,128)(2,1)S(1)} %get-tuple-element.33.mine), channel_id=1, source_target_pairs={{0,2},{1,3},{2,0},{3,1},{4,6},{5,7},{6,4},{7,5},{8,10},{9,11},{10,... | collective-permute-start | bytes 983048 | tf_op jit(solution)/shard_map/ppermute | solution.py:119
  32.6 28.6 %collective-permute-start.8 = (bf16[320,1024]{1,0:T(8,128)(2,1)}, bf16[320,1024]{1,0:T(8,128)(2,1)}, u32[]{:S(2)}, u32[]{:S(2)}) collective-permute-start(bf16[320,1024]{1,0:T(8,128)(2,1)} %collective-permute-done.6.first.near), channel_id=1, source_target_pairs={{0,16},{16,0},{1,17},{17,1},{2,18},{18,2},{3,19},{19,3},{4,20},{20... | collective-permute-start | bytes 1966088 | tf_op jit(solution)/shard_map/ppermute | solution.py:119
  34.1 24.7 %collective-permute-start.2 = (bf16[128,2048]{1,0:T(8,128)(2,1)S(1)}, bf16[128,2048]{1,0:T(8,128)(2,1)S(1)}, u32[]{:S(2)}, u32[]{:S(2)}) collective-permute-start(bf16[128,2048]{1,0:T(8,128)(2,1)S(1)} %copy-done.1), channel_id=1, source_target_pairs={{0,8},{4,12},{8,0},{12,4},{1,9},{5,13},{9,1},{13,5},{2,10},{6,14},... | collective-permute-start | bytes 1572872 | tf_op jit(solution)/shard_map/ppermute | solution.py:119
  51.0 2.7 %collective-permute-start.5 = (bf16[256,640]{1,0:T(8,128)(2,1)S(1)}, bf16[256,640]{1,0:T(8,128)(2,1)}, u32[]{:S(2)}, u32[]{:S(2)}) collective-permute-start(bf16[256,640]{1,0:T(8,128)(2,1)S(1)} %shard_map.94.mine), channel_id=1, source_target_pairs={{0,1},{1,0},{2,3},{3,2},{4,5},{5,4},{6,7},{7,6},{8,9},{9,8},{10,11... | collective-permute-start | bytes 983048 | tf_op jit(solution)/shard_map/ppermute | solution.py:119
  51.1 15.3 %collective-permute-start.9 = (bf16[256,1024]{1,0:T(8,128)(2,1)}, bf16[256,1024]{1,0:T(8,128)(2,1)}, u32[]{:S(2)}, u32[]{:S(2)}) collective-permute-start(bf16[256,1024]{1,0:T(8,128)(2,1)} %collective-permute-done.4.second), channel_id=1, source_target_pairs={{0,16},{16,0},{1,17},{17,1},{2,18},{18,2},{3,19},{19,3},{4,20},{20... | collective-permute-start | bytes 1572872 | tf_op jit(solution)/shard_map/ppermute | solution.py:119
  53.6 1.0 copy-start.5
  58.1 0.8 copy-start.12
  58.9 2.3 %copy-start.6 = (bf16[1,64,2048]{2,1,0:T(8,128)(2,1)S(1)}, bf16[1,64,2048]{2,1,0:T(8,128)(2,1)}, u32[]{:S(2)}) copy-start(bf16[1,64,2048]{2,1,0:T(8,128)(2,1)} %param.9) | copy-start | bytes 786436
  58.9 2.4 %copy-start.18 = (bf16[256,128]{1,0:T(8,128)(2,1)S(1)}, bf16[256,128]{1,0:T(8,128)(2,1)}, u32[]{:S(2)}) copy-start(bf16[256,128]{1,0:T(8,128)(2,1)} %copy-done.17) | copy-start | bytes 196612
  58.9 14.2 %collective-permute-start.7 = (bf16[128,1024]{1,0:T(8,128)(2,1)}, bf16[128,1024]{1,0:T(8,128)(2,1)}, u32[]{:S(2)}, u32[]{:S(2)}) collective-permute-start(bf16[128,1024]{1,0:T(8,128)(2,1)} %get-tuple-element.39), channel_id=1, source_target_pairs={{0,8},{4,12},{8,0},{12,4},{1,9},{5,13},{9,1},{13,5},{2,10},{6,14},... | collective-permute-start | bytes 786440 | tf_op jit(solution)/shard_map/ppermute | solution.py:119
  61.2 2.8 %copy-start.2 = (f32[256,1024]{1,0:T(8,128)}, f32[256,1024]{1,0:T(8,128)S(1)}, u32[]{:S(2)}) copy-start(f32[256,1024]{1,0:T(8,128)S(1)} %shard_map.96.part) | copy-start | bytes 3145732
  64.0 9.1 %collective-permute-start.10 = (bf16[256,128]{1,0:T(8,128)(2,1)}, bf16[256,128]{1,0:T(8,128)(2,1)}, u32[]{:S(2)}, u32[]{:S(2)}) collective-permute-start(bf16[256,128]{1,0:T(8,128)(2,1)} %shard_map.97.low), channel_id=1, source_target_pairs={{0,2},{1,3},{2,0},{3,1},{4,6},{5,7},{6,4},{7,5},{8,10},{9,11},{10,... | collective-permute-start | bytes 196616 | tf_op jit(solution)/shard_map/ppermute | solution.py:119
  65.6 7.5 %copy-start.3 = (f32[256,1024]{1,0:T(8,128)S(1)}, f32[256,1024]{1,0:T(8,128)}, u32[]{:S(2)}) copy-start(f32[256,1024]{1,0:T(8,128)} %copy-done.2) | copy-start | bytes 3145732
  66.4 1.0 copy-start.7
  73.1 4.1 %copy-start.9 = (bf16[128,512]{1,0:T(8,128)(2,1)S(1)}, bf16[128,512]{1,0:T(8,128)(2,1)}, u32[]{:S(2)}) copy-start(bf16[128,512]{1,0:T(8,128)(2,1)} %cot.3) | copy-start | bytes 393220
  73.1 4.2 %copy-start.11 = (bf16[144,512]{1,0:T(8,128)(2,1)S(1)}, bf16[144,512]{1,0:T(8,128)(2,1)}, u32[]{:S(2)}) copy-start(bf16[144,512]{1,0:T(8,128)(2,1)} %copy-done.10) | copy-start | bytes 442372
  73.1 4.2 %copy-start.16 = (bf16[64,512]{1,0:T(8,128)(2,1)S(1)}, bf16[64,512]{1,0:T(8,128)(2,1)}, u32[]{:S(2)}) copy-start(bf16[64,512]{1,0:T(8,128)(2,1)} %copy-done.15) | copy-start | bytes 196612
  74.9 1.7 %collective-permute-start.11 = (bf16[256,640]{1,0:T(8,128)(2,1)S(1)}, bf16[256,640]{1,0:T(8,128)(2,1)S(1)}, u32[]{:S(2)}, u32[]{:S(2)}) collective-permute-start(bf16[256,640]{1,0:T(8,128)(2,1)S(1)} %get-tuple-element.47.give), channel_id=1, source_target_pairs={{0,1},{1,0},{2,3},{3,2},{4,5},{5,4},{6,7},{7,6},{8,9},{9,8},{10,11... | collective-permute-start | bytes 983048 | tf_op jit(solution)/shard_map/ppermute | solution.py:119
  77.2 23.0 %copy-start.13 = (f32[128,1024]{1,0:T(8,128)S(1)}, f32[128,1024]{1,0:T(8,128)}, u32[]{:S(2)}) copy-start(f32[128,1024]{1,0:T(8,128)} %copy-done.12) | copy-start | bytes 1572868
  78.7 25.6 %collective-permute-start.16 = (bf16[64,2560]{1,0:T(8,128)(2,1)S(1)}, bf16[64,2560]{1,0:T(8,128)(2,1)S(1)}, u32[]{:S(2)}, u32[]{:S(2)}) collective-permute-start(bf16[64,2560]{1,0:T(8,128)(2,1)S(1)} %get-tuple-element.59), channel_id=1, source_target_pairs={{0,4},{4,0},{8,12},{12,8},{1,5},{5,1},{9,13},{13,9},{2,6},{6,2},{1... | collective-permute-start | bytes 983048 | tf_op jit(solution)/shard_map/ppermute | solution.py:119
  78.8 21.4 %collective-permute-start.15 = (bf16[128,1024]{1,0:T(8,128)(2,1)S(1)}, bf16[128,1024]{1,0:T(8,128)(2,1)S(1)}, u32[]{:S(2)}, u32[]{:S(2)}) collective-permute-start(bf16[128,1024]{1,0:T(8,128)(2,1)S(1)} %get-tuple-element.44), channel_id=1, source_target_pairs={{0,8},{4,12},{8,0},{12,4},{1,9},{5,13},{9,1},{13,5},{2,10},{6,14},... | collective-permute-start | bytes 786440 | tf_op jit(solution)/shard_map/ppermute | solution.py:119
  79.6 23.4 %collective-permute-start.14 = (bf16[128,512]{1,0:T(8,128)(2,1)S(1)}, bf16[128,512]{1,0:T(8,128)(2,1)S(1)}, u32[]{:S(2)}, u32[]{:S(2)}) collective-permute-start(bf16[128,512]{1,0:T(8,128)(2,1)S(1)} %get-tuple-element.53), channel_id=1, source_target_pairs={{0,8},{4,12},{8,0},{12,4},{1,9},{5,13},{9,1},{13,5},{2,10},{6,14},... | collective-permute-start | bytes 393224 | tf_op jit(solution)/shard_map/ppermute | solution.py:119
  81.8 21.2 %collective-permute-start.12 = (bf16[128,512]{1,0:T(8,128)(2,1)S(1)}, bf16[128,512]{1,0:T(8,128)(2,1)S(1)}, u32[]{:S(2)}, u32[]{:S(2)}) collective-permute-start(bf16[128,512]{1,0:T(8,128)(2,1)S(1)} %get-tuple-element.48), channel_id=1, source_target_pairs={{0,8},{1,9},{2,0},{3,1},{4,12},{5,13},{6,4},{7,5},{8,10},{9,11},{1... | collective-permute-start | bytes 393224 | tf_op jit(solution)/shard_map/ppermute | solution.py:124
  82.5 20.5 %collective-permute-start.13 = (bf16[128,512]{1,0:T(8,128)(2,1)S(1)}, bf16[128,512]{1,0:T(8,128)(2,1)S(1)}, u32[]{:S(2)}, u32[]{:S(2)}) collective-permute-start(bf16[128,512]{1,0:T(8,128)(2,1)S(1)} %get-tuple-element.49), channel_id=1, source_target_pairs={{2,8},{3,9},{6,12},{7,13},{8,2},{9,3},{12,6},{13,7},{18,24},{19,25... | collective-permute-start | bytes 393224 | tf_op jit(solution)/shard_map/ppermute | solution.py:124

commit v4 on v3

--- a/solution.py
+++ b/solution.py
@@ -132,7 +132,7 @@
 
 
 def cost(us):
-    return pl.CostEstimate(flops=0, bytes_accessed=1000 + us * 3_000_000, transcendentals=0)
+    return pl.CostEstimate(flops=us * 1_000_000_000, bytes_accessed=1000 + us * 3_000_000, transcendentals=0)
 
 
 def local_kernel(body, outs, where, *args, us=0):
@@ -204,7 +204,7 @@
     g += nn(c_sib[:, head:], second[...])
     g += nn(back, rows2(down[...], first[:rank, :]))
     toks = top.shape[0]
-    top[...] = g[:toks]
+    top[...] = g[:toks].astype(bf16)
     bottom[...] = g[toks:].astype(bf16)
 
 
@@ -230,7 +230,7 @@
             out_specs=[tiled(toks), tiled(toks)],
         ),
         out_shape=[
-            jax.ShapeDtypeStruct((toks, steps * tile), f32),
+            jax.ShapeDtypeStruct((toks, steps * tile), bf16),
             jax.ShapeDtypeStruct((toks, steps * tile), bf16),
         ],
         compiler_params=pltpu.CompilerParams(vmem_limit_bytes=12 * 1024 * 1024),
@@ -242,9 +242,9 @@
     half = near.shape[1]
     y = where[Y]
     at = pl.ds(pl.multiple_of(y * half, half), half)
-    out[:, at] = (near[...] + near_got[...].astype(f32)).astype(bf16)
+    out[:, at] = (near[...].astype(f32) + near_got[...].astype(f32)).astype(bf16)
     at = pl.ds(pl.multiple_of((1 - y) * half, half), half)
-    out[:, at] = (far[...] + far_got[...].astype(f32)).astype(bf16)
+    out[:, at] = (far[...].astype(f32) + far_got[...].astype(f32)).astype(bf16)
 
 
 def low_kernel(where, act, act_got, members, down, near, far, out):
@@ -308,19 +308,23 @@
     give[:, rows:] = (low[...].astype(f32) + low_got[...].astype(f32)).astype(bf16)
 
 
-def held_kernel(where, keep, got, here, there, turn):
-    toks, rows = here.shape
-    held = (keep[...] + got[:, :rows].astype(f32)).astype(bf16)
+def held_kernel(where, keep, got, held):
+    held[...] = (keep[...] + got[:, : keep.shape[1]].astype(f32)).astype(bf16)
+
+
+def turn_kernel(where, held, got, lora_far, turn):
+    toks = turn.shape[0]
     in_pair = jnp.full((1, 1), where[IN_PAIR], jnp.int32) == 1
-    here[...] = held[:toks]
-    there[...] = held[toks:]
-    turn[...] = jnp.where(in_pair, held[toks:], held[:toks])
-
-
-def output_kernel(where, one, two, here, lora, lora_got, out):
+    base = held[toks:, :].astype(f32) + got[toks:, :].astype(f32)
+    turn[...] = (lora_far[...].astype(f32) + jnp.where(in_pair, base, 0.0)).astype(bf16)
+
+
+def output_kernel(where, held, got, lora, turned, out):
+    toks = out.shape[0]
     in_pair = jnp.full((1, 1), where[IN_PAIR], jnp.int32) == 1
-    base = one[...].astype(f32) + jnp.where(in_pair, here[...], two[...]).astype(f32)
-    out[...] = (base + lora[...].astype(f32) + lora_got[...].astype(f32)).astype(bf16)
+    base = held[:toks, :].astype(f32) + got[:toks, :].astype(f32)
+    total = turned[...].astype(f32) + jnp.where(in_pair, base, 0.0)
+    out[...] = (total + lora[...].astype(f32)).astype(bf16)
 
 
 def pair_plan(
@@ -353,18 +357,17 @@
     head = rows * 2 // 4
     piece0 = jnp.concatenate([d_mine, w_mine[:head]], axis=0)
     piece1 = w_mine[head:]
-    piece0, piece1 = after((piece0, piece1), cot_got, up_sib)
     near0 = swap(piece0, "fsdp", 1)
-    near1 = swap(piece1, "fsdp", 1)
+    act_got = swap(after(activations, cot_got, up_sib), "fsdp", 2)
+    near1 = swap(after(piece1, cot_got, up_sib), "fsdp", 1)
 
     mine, members = local_kernel(
         back_kernel,
         [((2 * toks, out_width + 2 * rank), bf16), ((2 * toks, 2 * rank), bf16)],
         where,
-        cotangent, cot_got, idx, up, up_sib, us=20,
+        cotangent, cot_got, idx, up, up_sib, us=0,
     )
     mine_x = swap(mine, "tp", 2)
-    act_got = swap(after(activations, mine), "fsdp", 2)
     near0 = after(near0, mine)
     far0 = swap(near0, "groups", 1)
     far1 = swap(near1, "groups", 1)
@@ -378,7 +381,7 @@
     act_got = after(act_got, near_sent)
     part = local_kernel(
         base_near_kernel, ((2 * toks, 2 * rows), f32), where,
-        activations, act_got, key_value_weight, near0, near1, us=15,
+        activations, act_got, key_value_weight, near0, near1, us=0,
     )
 
     far0 = after(far0, part)
@@ -397,19 +400,13 @@
         base_far_kernel,
         [((2 * toks, rows), f32), ((2 * toks, rows + 2 * rank), bf16)],
         where,
-        part, activations, act_got, far0, far1, low, low_x, us=10,
+        part, activations, act_got, far0, far1, low, low_x, us=0,
     )
     give_got = swap(give, "tp", 1)
-    here, there, turn = local_kernel(
-        held_kernel, [((toks, rows), bf16)] * 3, where, keep, give_got
-    )
-    one = both(
-        turn,
-        [((a, b, d), (a ^ 2, b, d) if b == a // 2 else (a, 1 - b, d)) for a, b, d in places],
-    )
-    two = both(there, [((a, b, d), (a ^ 2, 1 - b, d)) for a, b, d in places if b != a // 2])
-
-    give_got = after(give_got, here)
+    held = local_kernel(held_kernel, ((2 * toks, rows), bf16), where, keep, give_got)
+    held_got = both(held, [((a, b, d), (a, 1 - b, d)) for a, b, d in places if b != a // 2])
+
+    give_got = after(give_got, held)
     lora, lora_far, down_own, up_own, sib = local_kernel(
         adapter_kernel,
         [
@@ -420,9 +417,12 @@
             ((rank, width + out_width), bf16),
         ],
         where,
-        give, give_got, mine, got, activations, act_got, cotangent, cot_got, up, up_sib, us=5,
-    )
-    lora_got = swap(lora_far, "fsdp", 2)
+        give, give_got, mine, got, activations, act_got, cotangent, cot_got, up, up_sib, us=0,
+    )
+    turn = local_kernel(
+        turn_kernel, ((toks, out_width), bf16), where, held, held_got, lora_far
+    )
+    turned = swap(turn, "fsdp", 2)
     grad_down, up_gradient = local_kernel(
         adapter_end_kernel, [((1, rank, width), f32), ((1, rank, out_width), f32)], where,
         down_own, up_own, swap(sib, "fsdp", 1),
@@ -432,7 +432,7 @@
         gradient_end_kernel, ((toks, width), bf16), where, near, near_got, far, far_got
     )
     key_value_output = local_kernel(
-        output_kernel, ((toks, out_width), bf16), where, one, two, here, lora, lora_got
+        output_kernel, ((toks, out_width), bf16), where, held, held_got, lora, turned
     )
     return (key_value_output, input_gradient, grad_down, up_gradient)
 

time: 107 us -> 103 us (0.963)
  waiting for transfers between devices: 54.9 us -> 47 us
  starting transfers between devices: 20.6 us -> 25.3 us
  other arithmetic: 2.53 us -> 0.99 us
    ppermute x15, waiting for transfers between devices: 54.9 us -> 44.7 us  [swap(): lax.ppermute(x, axis, [(i, i ^ bit) for i in range(lax.axis_size(axis))])]
    ppermute x15, starting transfers between devices: 19.2 us -> 23.9 us  [swap(): lax.ppermute(x, axis, [(i, i ^ bit) for i in range(lax.axis_size(axis))])]
    ppermute x2 -> x1, waiting for transfers between devices: 0.01 us -> 2.28 us  [both(): return lax.ppermute(x, ('fsdp', 'tp'), flat)]
    pallas_call x10 -> x11, Pallas kernels: 14.8 us -> 15.3 us  [local_kernel(): pl.pallas_call(body, out_shape=shapes, in_specs=[pl.BlockSpec(memory_spac...]
    unnamed x40 -> x38, local copies, waits for them, and re-layouts: 3.38 us -> 3.37 us
  transfers between devices with their start and end apart: 17 -> 16, of which waited for: 8 -> 10; matrix products, arithmetic and copies ran while one was open for 5% -> 0% of each run, Pallas kernels for 15% -> 18%
where the time goes in v4:
time: 103 us; the launch traced here: 102 us
  waiting for transfers between devices  47 us (46%)
  starting transfers between devices  25.3 us (25%)
  Pallas kernels  21.6 us (21%)
  local copies, waits for them, and re-layouts  6.56 us (6%)
    ppermute x15, waiting for transfers between devices, swap(): lax.ppermute(x, axis, [(i, i ^ bit) for i in range(lax.axis_size(axis))])  44.7 us
    ppermute x15, starting transfers between devices, swap(): lax.ppermute(x, axis, [(i, i ^ bit) for i in range(lax.axis_size(axis))])  23.9 us
    pallas_call x11, Pallas kernels, local_kernel(): pl.pallas_call(body, out_shape=shapes, in_specs=[pl.BlockSpec(memory_spac...  15.3 us
    pallas_call x2, Pallas kernels, gradient_half(): pl.pallas_call(gradient_kernel, grid_spec=pltpu.PrefetchScalarGridSpec(nu...  6.34 us
    unnamed x38, local copies, waits for them, and re-layouts  3.37 us
    ppermute x1, waiting for transfers between devices, both(): return lax.ppermute(x, ('fsdp', 'tp'), flat)  2.28 us
    slice x1, local copies, waits for them, and re-layouts, pair_plan(): piece0 = jnp.concatenate([d_mine, w_mine[:head]], axis=0)  2.1 us
  transfers between devices with their start and end apart: 16, of which 10 were waited for; matrix products, arithmetic and copies ran while one was open for 0% of the time, Pallas kernels for 18%

profile of v4, /device:TPU:0, one launch (start us, length us, event | category | flops | bytes accessed | tf_op | source)
XLA Modules:
  0.0 102.3 jit_solution(4657942348112158815)
XLA Ops:
  0.6 0.9 dynamic-slice_bitcast_fusion
  1.6 0.0 copy-start.18
  1.6 0.0 copy-start.7
  1.6 2.1 %constant_dynamic-slice_fusion = (bf16[256,1024]{1,0:T(8,128)(2,1)S(1)}, bf16[256,1024]{1,0:T(8,128)(2,1)}) fusion(bf16[512,2048]{1,0:T(8,128)(2,1)} %weight.5, s32[]{:T(128)S(6)} %select_n.26, s32[]{:T(128)S(6)} %add.21), kind=kLoop, calls=%fused_computation.6 | loop fusion | bytes 2097160 | tf_op jit(solution)/shard_map/slice | solution.py:358
  3.7 0.9 pad_maximum_fusion
  4.6 3.0 %collective-permute-start.6 = (bf16[320,1024]{1,0:T(8,128)(2,1)}, bf16[320,1024]{1,0:T(8,128)(2,1)}, u32[]{:S(2)}, u32[]{:S(2)}) collective-permute-start(bf16[320,1024]{1,0:T(8,128)(2,1)} %pad_maximum_fusion), channel_id=1, source_target_pairs={{0,4},{4,0},{8,12},{12,8},{1,5},{5,1},{9,13},{13,9},{2,6},{6,2},{1... | collective-permute-start | bytes 1966088 | tf_op jit(solution)/shard_map/ppermute | solution.py:119
  7.6 0.0 copy-done.7
  7.6 2.7 %collective-permute-start = (bf16[144,512]{1,0:T(8,128)(2,1)S(1)}, bf16[144,512]{1,0:T(8,128)(2,1)S(1)}, u32[]{:S(2)}, u32[]{:S(2)}) collective-permute-start(bf16[144,512]{1,0:T(8,128)(2,1)S(1)} %fusion.1), channel_id=1, source_target_pairs={{0,8},{4,12},{8,0},{12,4},{1,9},{5,13},{9,1},{13,5},{2,10},{6,14},... | collective-permute-start | bytes 442376 | tf_op jit(solution)/shard_map/ppermute | solution.py:119
  10.3 0.0 copy-done.11
  10.3 0.4 collective-permute-start.1
  10.8 16.4 %collective-permute-done.1.up_sib = bf16[64,512]{1,0:T(8,128)(2,1)S(1)} collective-permute-done((bf16[64,512]{1,0:T(8,128)(2,1)S(1)}, bf16[64,512]{1,0:T(8,128)(2,1)S(1)}, u32[]{:S(2)}, u32[]{:S(2)}) %collective-permute-start.1) | collective-permute-done | bytes 65568 | tf_op jit(solution)/shard_map/ppermute | solution.py:119
  27.1 0.0 collective-permute-done.cot_got
  27.1 2.0 %collective-permute-start.4 = (bf16[256,1024]{1,0:T(8,128)(2,1)}, bf16[256,1024]{1,0:T(8,128)(2,1)}, u32[]{:S(2)}, u32[]{:S(2)}) collective-permute-start(bf16[256,1024]{1,0:T(8,128)(2,1)} %get-tuple-element.31), channel_id=1, source_target_pairs={{0,4},{4,0},{8,12},{12,8},{1,5},{5,1},{9,13},{13,9},{2,6},{6,2},{1... | collective-permute-start | bytes 1572872 | tf_op jit(solution)/shard_map/ppermute | solution.py:119
  29.2 0.1 pad_add_fusion.where
  29.2 0.8 shard_map.93
  30.1 0.0 copy-start.16
  30.1 0.6 copy-done.16
  30.7 1.5 %collective-permute-start.3 = (bf16[256,640]{1,0:T(8,128)(2,1)S(1)}, bf16[256,640]{1,0:T(8,128)(2,1)S(1)}, u32[]{:S(2)}, u32[]{:S(2)}) collective-permute-start(bf16[256,640]{1,0:T(8,128)(2,1)S(1)} %get-tuple-element.30.mine), channel_id=1, source_target_pairs={{0,2},{1,3},{2,0},{3,1},{4,6},{5,7},{6,4},{7,5},{8,10},{9,11},{10,... | collective-permute-start | bytes 983048 | tf_op jit(solution)/shard_map/ppermute | solution.py:119
  32.2 0.0 collective-permute-done.6.first.near
  32.2 1.6 %collective-permute-start.8 = (bf16[320,1024]{1,0:T(8,128)(2,1)}, bf16[320,1024]{1,0:T(8,128)(2,1)}, u32[]{:S(2)}, u32[]{:S(2)}) collective-permute-start(bf16[320,1024]{1,0:T(8,128)(2,1)} %collective-permute-done.6.first.near), channel_id=1, source_target_pairs={{0,16},{16,0},{1,17},{17,1},{2,18},{18,2},{3,19},{19,3},{4,20},{20... | collective-permute-start | bytes 1966088 | tf_op jit(solution)/shard_map/ppermute | solution.py:119
  33.8 2.3 %collective-permute-start.2 = (bf16[128,2048]{1,0:T(8,128)(2,1)S(1)}, bf16[128,2048]{1,0:T(8,128)(2,1)S(1)}, u32[]{:S(2)}, u32[]{:S(2)}) collective-permute-start(bf16[128,2048]{1,0:T(8,128)(2,1)S(1)} %copy-done.1), channel_id=1, source_target_pairs={{0,8},{4,12},{8,0},{12,4},{1,9},{5,13},{9,1},{13,5},{2,10},{6,14},... | collective-permute-start | bytes 1572872 | tf_op jit(solution)/shard_map/ppermute | solution.py:119
  36.1 2.6 %collective-permute-done.3.got = bf16[256,640]{1,0:T(8,128)(2,1)S(1)} collective-permute-done((bf16[256,640]{1,0:T(8,128)(2,1)S(1)}, bf16[256,640]{1,0:T(8,128)(2,1)S(1)}, u32[]{:S(2)}, u32[]{:S(2)}) %collective-permute-start.3) | collective-permute-done | bytes 327712 | tf_op jit(solution)/shard_map/ppermute | solution.py:119
  38.7 9.2 %collective-permute-done.4.second = bf16[256,1024]{1,0:T(8,128)(2,1)} collective-permute-done((bf16[256,1024]{1,0:T(8,128)(2,1)}, bf16[256,1024]{1,0:T(8,128)(2,1)}, u32[]{:S(2)}, u32[]{:S(2)}) %collective-permute-start.4) | collective-permute-done | bytes 524320 | tf_op jit(solution)/shard_map/ppermute | solution.py:119
  47.9 0.6 shard_map.94.mine
  48.5 0.1 collective-permute-start.5
  48.6 2.4 %collective-permute-start.9 = (bf16[256,1024]{1,0:T(8,128)(2,1)}, bf16[256,1024]{1,0:T(8,128)(2,1)}, u32[]{:S(2)}, u32[]{:S(2)}) collective-permute-start(bf16[256,1024]{1,0:T(8,128)(2,1)} %collective-permute-done.4.second), channel_id=1, source_target_pairs={{0,16},{16,0},{1,17},{17,1},{2,18},{18,2},{3,19},{19,3},{4,20},{20... | collective-permute-start | bytes 1572872 | tf_op jit(solution)/shard_map/ppermute | solution.py:119
  51.0 0.1 concatenate.15.where
  51.1 0.0 collective-permute-done.5.got
  51.1 0.9 copy-done.4
  52.1 3.5 %shard_map.95 = (bf16[128,1024]{1,0:T(8,128)(2,1)S(1)}, bf16[128,1024]{1,0:T(8,128)(2,1)}) custom-call(s32[5]{0:T(128)S(1)} %concatenate.15.where, bf16[256,640]{1,0:T(8,128)(2,1)S(1)} %shard_map.94.mine, bf16[256,640]{1,0:T(8,128)(2,1)} %collective-permute-done.5.got, bf16[512,2048]{1,0:T(8,128)(2,1)S(1)} %copy-done, bf16[64,2048]{1,0:T(8,128)(2,1)S(1)} %bitcast.11, ...), custom_call_target="tpu_custom_call" | custom-call | bytes 1000 | tf_op jit(solution)/shard_map/pallas_call | solution.py:217
  55.5 0.7 copy-done.14
  56.2 0.7 collective-permute-start.7
  56.9 0.9 collective-permute-done.2.act_got
  57.8 2.3 %shard_map.96.part = f32[256,1024]{1,0:T(8,128)S(1)} custom-call(s32[4]{0:T(128)S(1)} %pad_add_fusion.where, bf16[128,2048]{1,0:T(8,128)(2,1)S(1)} %copy-done.1, bf16[128,2048]{1,0:T(8,128)(2,1)S(1)} %collective-permute-done.2.act_got, bf16[512,2048]{1,0:T(8,128)(2,1)S(1)} %copy-done, bf16[320,1024]{1,0:T(8,128)(2,1)} %collective-permute-done.6.first.near, ...), custom_call_target="tpu_custom_call" | custom-call | bytes 1000 | tf_op jit(solution)/shard_map/pallas_call | solution.py:141
  60.1 0.0 collective-permute-done.8.far.first
  60.1 2.7 %shard_map.97.low = bf16[256,128]{1,0:T(8,128)(2,1)} custom-call(s32[4]{0:T(128)S(1)} %pad_add_fusion.where, bf16[128,2048]{1,0:T(8,128)(2,1)S(1)} %copy-done.1, bf16[128,2048]{1,0:T(8,128)(2,1)S(1)} %collective-permute-done.2.act_got, bf16[256,128]{1,0:T(8,128)(2,1)S(1)} %copy-done.17, bf16[64,2048]{1,0:T(8,128)(2,1)S(1)} %bitcast.12, ...), custom_call_target="tpu_custom_call" | custom-call | bytes 1000 | tf_op jit(solution)/shard_map/pallas_call | solution.py:141
  62.8 1.6 %collective-permute-start.10 = (bf16[256,128]{1,0:T(8,128)(2,1)}, bf16[256,128]{1,0:T(8,128)(2,1)}, u32[]{:S(2)}, u32[]{:S(2)}) collective-permute-start(bf16[256,128]{1,0:T(8,128)(2,1)} %shard_map.97.low), channel_id=1, source_target_pairs={{0,2},{1,3},{2,0},{3,1},{4,6},{5,7},{6,4},{7,5},{8,10},{9,11},{10,... | collective-permute-start | bytes 196616 | tf_op jit(solution)/shard_map/ppermute | solution.py:119
  64.4 0.1 concatenate.17.where
  64.5 0.0 collective-permute-done.9.second
  64.5 1.0 %copy-done.6 = bf16[1,64,2048]{2,1,0:T(8,128)(2,1)S(1)} copy-done((bf16[1,64,2048]{2,1,0:T(8,128)(2,1)S(1)}, bf16[1,64,2048]{2,1,0:T(8,128)(2,1)}, u32[]{:S(2)}) %copy-start.6) | copy-done | bytes 262168
  65.5 2.9 %shard_map.98 = (bf16[128,1024]{1,0:T(8,128)(2,1)S(1)}, bf16[128,1024]{1,0:T(8,128)(2,1)S(1)}) custom-call(s32[5]{0:T(128)S(1)} %concatenate.17.where, bf16[256,640]{1,0:T(8,128)(2,1)S(1)} %shard_map.94.mine, bf16[256,640]{1,0:T(8,128)(2,1)} %collective-permute-done.5.got, bf16[512,2048]{1,0:T(8,128)(2,1)S(1)} %copy-done, bf16[64,2048]{1,0:T(8,128)(2,1)S(1)} %bitcast.13, ...), custom_call_target="tpu_custom_call" | custom-call | bytes 1000 | tf_op jit(solution)/shard_map/pallas_call | solution.py:217
  68.4 3.0 %collective-permute-done.7.near_got = bf16[128,1024]{1,0:T(8,128)(2,1)} collective-permute-done((bf16[128,1024]{1,0:T(8,128)(2,1)}, bf16[128,1024]{1,0:T(8,128)(2,1)}, u32[]{:S(2)}, u32[]{:S(2)}) %collective-permute-start.7) | collective-permute-done | bytes 262176 | tf_op jit(solution)/shard_map/ppermute | solution.py:119
  71.4 0.0 collective-permute-done.10.low_got
  71.4 1.8 %shard_map.99 = (f32[256,512]{1,0:T(8,128)S(1)}, bf16[256,640]{1,0:T(8,128)(2,1)S(1)}) custom-call(s32[4]{0:T(128)S(1)} %pad_add_fusion.where, f32[256,1024]{1,0:T(8,128)S(1)} %copy-done.3, bf16[128,2048]{1,0:T(8,128)(2,1)S(1)} %copy-done.1, bf16[128,2048]{1,0:T(8,128)(2,1)S(1)} %collective-permute-done.2.act_got, ...), custom_call_target="tpu_custom_call" | custom-call | bytes 1000 | tf_op jit(solution)/shard_map/pallas_call | solution.py:141
  73.2 0.1 collective-permute-start.11
  73.3 1.6 %collective-permute-done.11.got.give_got = bf16[256,640]{1,0:T(8,128)(2,1)S(1)} collective-permute-done((bf16[256,640]{1,0:T(8,128)(2,1)S(1)}, bf16[256,640]{1,0:T(8,128)(2,1)S(1)}, u32[]{:S(2)}, u32[]{:S(2)}) %collective-permute-start.11) | collective-permute-done | bytes 327712 | tf_op jit(solution)/shard_map/ppermute | solution.py:119
  74.9 0.6 shard_map.100.held
  75.5 0.0 copy-start.15
  75.5 1.4 %collective-permute-start.12 = (bf16[256,512]{1,0:T(8,128)(2,1)S(1)}, bf16[256,512]{1,0:T(8,128)(2,1)S(1)}, u32[]{:S(2)}, u32[]{:S(2)}) collective-permute-start(bf16[256,512]{1,0:T(8,128)(2,1)S(1)} %shard_map.100.held), channel_id=1, source_target_pairs={{2,0},{3,1},{6,4},{7,5},{8,10},{9,11},{12,14},{13,15},{18,16},{19,... | collective-permute-start | bytes 786440 | tf_op jit(solution)/shard_map/ppermute | solution.py:124
  77.0 0.0 copy-done.8
  77.0 0.0 copy-done.10
  77.0 0.0 copy-done.13
  77.0 1.4 %shard_map.101 = (bf16[128,512]{1,0:T(8,128)(2,1)S(1)}, bf16[128,512]{1,0:T(8,128)(2,1)S(1)}, f32[64,2048]{1,0:T(8,128)S(1)}, f32[64,512]{1,0:T(8,128)S(1)}, bf16[64,2560]{1,0:T(8,128)(2,1)S(1)}) custom-call(s32[4]{0:T(128)S(1)} %pad_add_fusion.where, bf16[256,640]{1,0:T(8,128)(2,1)S(1)} %get-tuple-element.42.give, ...), custom_call_target="tpu_custom_call" | custom-call | bytes 1000 | tf_op jit(solution)/shard_map/pallas_call | solution.py:141
  78.4 0.1 collective-permute-start.15
  78.5 5.2 %collective-permute-start.14 = (bf16[128,1024]{1,0:T(8,128)(2,1)S(1)}, bf16[128,1024]{1,0:T(8,128)(2,1)S(1)}, u32[]{:S(2)}, u32[]{:S(2)}) collective-permute-start(bf16[128,1024]{1,0:T(8,128)(2,1)S(1)} %get-tuple-element.39), channel_id=1, source_target_pairs={{0,8},{4,12},{8,0},{12,4},{1,9},{5,13},{9,1},{13,5},{2,10},{6,14},... | collective-permute-start | bytes 786440 | tf_op jit(solution)/shard_map/ppermute | solution.py:119
  83.7 2.3 %collective-permute-done.12.got = bf16[256,512]{1,0:T(8,128)(2,1)S(1)} collective-permute-done((bf16[256,512]{1,0:T(8,128)(2,1)S(1)}, bf16[256,512]{1,0:T(8,128)(2,1)S(1)}, u32[]{:S(2)}, u32[]{:S(2)}) %collective-permute-start.12) | collective-permute-done | bytes 262176 | tf_op jit(solution)/shard_map/ppermute | solution.py:124
  86.0 0.6 shard_map.102
  86.6 0.1 collective-permute-start.13
  86.7 5.5 %collective-permute-done.14.far_got = bf16[128,1024]{1,0:T(8,128)(2,1)S(1)} collective-permute-done((bf16[128,1024]{1,0:T(8,128)(2,1)S(1)}, bf16[128,1024]{1,0:T(8,128)(2,1)S(1)}, u32[]{:S(2)}, u32[]{:S(2)}) %collective-permute-start.14) | collective-permute-done | bytes 262176 | tf_op jit(solution)/shard_map/ppermute | solution.py:119
  92.2 1.9 %shard_map.104 = bf16[128,2048]{1,0:T(8,128)(2,1)} custom-call(s32[4]{0:T(128)S(1)} %pad_add_fusion.where, bf16[128,1024]{1,0:T(8,128)(2,1)S(1)} %copy-done.15, bf16[128,1024]{1,0:T(8,128)(2,1)} %collective-permute-done.7.near_got, bf16[128,1024]{1,0:T(8,128)(2,1)S(1)} %get-tuple-element.48.far, bf16[128,1024]{1,0:T(8,128)(2,1)S(1)} %collective-permute-done.14.far_got), custom_call_target="tpu_custom_call" | custom-call | bytes 1000 | tf_op jit(solution)/shard_map/pallas_call | solution.py:141
  94.0 1.0 collective-permute-done.15.got
  95.0 1.4 %shard_map.105 = (f32[1,64,2048]{2,1,0:T(8,128)}, f32[1,64,512]{2,1,0:T(8,128)}) custom-call(s32[4]{0:T(128)S(1)} %pad_add_fusion.where, f32[64,2048]{1,0:T(8,128)S(1)} %get-tuple-element.49.down_own, f32[64,512]{1,0:T(8,128)S(1)} %get-tuple-element.50.up_own, bf16[64,2560]{1,0:T(8,128)(2,1)S(1)} %collective-permute-done.15.got), custom_call_target="tpu_custom_call" | custom-call | bytes 1000 | tf_op jit(solution)/shard_map/pallas_call | solution.py:141
  96.4 4.6 %collective-permute-done.13.turned = bf16[128,512]{1,0:T(8,128)(2,1)S(1)} collective-permute-done((bf16[128,512]{1,0:T(8,128)(2,1)S(1)}, bf16[128,512]{1,0:T(8,128)(2,1)S(1)}, u32[]{:S(2)}, u32[]{:S(2)}) %collective-permute-start.13) | collective-permute-done | bytes 131104 | tf_op jit(solution)/shard_map/ppermute | solution.py:119
  101.0 1.3 %shard_map.103 = bf16[128,512]{1,0:T(8,128)(2,1)} custom-call(s32[4]{0:T(128)S(1)} %pad_add_fusion.where, bf16[256,512]{1,0:T(8,128)(2,1)S(1)} %shard_map.100.held, bf16[256,512]{1,0:T(8,128)(2,1)S(1)} %collective-permute-done.12.got, bf16[128,512]{1,0:T(8,128)(2,1)S(1)} %get-tuple-element.44.lora, bf16[128,512]{1,0:T(8,128)(2,1)S(1)} %collective-permute-done.13.turned), custom_call_target="tpu_custom_call" | custom-call | bytes 1000 | tf_op jit(solution)/shard_map/pallas_call | solution.py:141
  (27 shorter events, 0.1 us)
Async XLA Ops:
  1.6 6.1 %copy-start.18 = (s32[128,1]{0,1:T(1,128)S(1)}, s32[128,1]{0,1:T(1,128)}, u32[]{:S(2)}) copy-start(s32[128,1]{0,1:T(1,128)} %param.8) | copy-start | bytes 1540
  1.6 6.1 %copy-start.7 = (bf16[128,512]{1,0:T(8,128)(2,1)S(1)}, bf16[128,512]{1,0:T(8,128)(2,1)}, u32[]{:S(2)}) copy-start(bf16[128,512]{1,0:T(8,128)(2,1)} %cot.3) | copy-start | bytes 393220
  3.7 6.6 %copy-start.11 = (bf16[1,64,512]{2,1,0:T(8,128)(2,1)S(1)}, bf16[1,64,512]{2,1,0:T(8,128)(2,1)}, u32[]{:S(2)}) copy-start(bf16[1,64,512]{2,1,0:T(8,128)(2,1)} %param.10) | copy-start | bytes 196612
  3.7 30.1 %copy-start.1 = (bf16[128,2048]{1,0:T(8,128)(2,1)S(1)}, bf16[128,2048]{1,0:T(8,128)(2,1)}, u32[]{:S(2)}) copy-start(bf16[128,2048]{1,0:T(8,128)(2,1)} %act.7) | copy-start | bytes 1572868
  3.7 47.4 %copy-start = (bf16[512,2048]{1,0:T(8,128)(2,1)S(1)}, bf16[512,2048]{1,0:T(8,128)(2,1)}, u32[]{:S(2)}) copy-start(bf16[512,2048]{1,0:T(8,128)(2,1)} %weight.5) | copy-start | bytes 6291460
  4.6 27.6 %collective-permute-start.6 = (bf16[320,1024]{1,0:T(8,128)(2,1)}, bf16[320,1024]{1,0:T(8,128)(2,1)}, u32[]{:S(2)}, u32[]{:S(2)}) collective-permute-start(bf16[320,1024]{1,0:T(8,128)(2,1)} %pad_maximum_fusion), channel_id=1, source_target_pairs={{0,4},{4,0},{8,12},{12,8},{1,5},{5,1},{9,13},{13,9},{2,6},{6,2},{1... | collective-permute-start | bytes 1966088 | tf_op jit(solution)/shard_map/ppermute | solution.py:119
  7.6 19.5 %collective-permute-start = (bf16[144,512]{1,0:T(8,128)(2,1)S(1)}, bf16[144,512]{1,0:T(8,128)(2,1)S(1)}, u32[]{:S(2)}, u32[]{:S(2)}) collective-permute-start(bf16[144,512]{1,0:T(8,128)(2,1)S(1)} %fusion.1), channel_id=1, source_target_pairs={{0,8},{4,12},{8,0},{12,4},{1,9},{5,13},{9,1},{13,5},{2,10},{6,14},... | collective-permute-start | bytes 442376 | tf_op jit(solution)/shard_map/ppermute | solution.py:119
  10.3 16.8 %collective-permute-start.1 = (bf16[64,512]{1,0:T(8,128)(2,1)S(1)}, bf16[64,512]{1,0:T(8,128)(2,1)S(1)}, u32[]{:S(2)}, u32[]{:S(2)}) collective-permute-start(bf16[64,512]{1,0:T(8,128)(2,1)S(1)} %bitcast.14), channel_id=1, source_target_pairs={{0,4},{4,0},{8,12},{12,8},{1,5},{5,1},{9,13},{13,9},{2,6},{6,2},{1... | collective-permute-start | bytes 196616 | tf_op jit(solution)/shard_map/ppermute | solution.py:119
  27.1 5.1 %copy-start.12 = (bf16[64,512]{1,0:T(8,128)(2,1)}, bf16[64,512]{1,0:T(8,128)(2,1)S(1)}, u32[]{:S(2)}) copy-start(bf16[64,512]{1,0:T(8,128)(2,1)S(1)} %collective-permute-done.1.up_sib) | copy-start | bytes 196612
  27.1 5.1 %copy-start.9 = (bf16[144,512]{1,0:T(8,128)(2,1)}, bf16[144,512]{1,0:T(8,128)(2,1)S(1)}, u32[]{:S(2)}) copy-start(bf16[144,512]{1,0:T(8,128)(2,1)S(1)} %collective-permute-done.cot_got) | copy-start | bytes 442372
  27.1 20.8 %collective-permute-start.4 = (bf16[256,1024]{1,0:T(8,128)(2,1)}, bf16[256,1024]{1,0:T(8,128)(2,1)}, u32[]{:S(2)}, u32[]{:S(2)}) collective-permute-start(bf16[256,1024]{1,0:T(8,128)(2,1)} %get-tuple-element.31), channel_id=1, source_target_pairs={{0,4},{4,0},{8,12},{12,8},{1,5},{5,1},{9,13},{13,9},{2,6},{6,2},{1... | collective-permute-start | bytes 1572872 | tf_op jit(solution)/shard_map/ppermute | solution.py:119
  30.1 0.6 copy-start.16
  30.7 8.1 %collective-permute-start.3 = (bf16[256,640]{1,0:T(8,128)(2,1)S(1)}, bf16[256,640]{1,0:T(8,128)(2,1)S(1)}, u32[]{:S(2)}, u32[]{:S(2)}) collective-permute-start(bf16[256,640]{1,0:T(8,128)(2,1)S(1)} %get-tuple-element.30.mine), channel_id=1, source_target_pairs={{0,2},{1,3},{2,0},{3,1},{4,6},{5,7},{6,4},{7,5},{8,10},{9,11},{10,... | collective-permute-start | bytes 983048 | tf_op jit(solution)/shard_map/ppermute | solution.py:119
  32.2 27.9 %collective-permute-start.8 = (bf16[320,1024]{1,0:T(8,128)(2,1)}, bf16[320,1024]{1,0:T(8,128)(2,1)}, u32[]{:S(2)}, u32[]{:S(2)}) collective-permute-start(bf16[320,1024]{1,0:T(8,128)(2,1)} %collective-permute-done.6.first.near), channel_id=1, source_target_pairs={{0,16},{16,0},{1,17},{17,1},{2,18},{18,2},{3,19},{19,3},{4,20},{20... | collective-permute-start | bytes 1966088 | tf_op jit(solution)/shard_map/ppermute | solution.py:119
  33.8 24.0 %collective-permute-start.2 = (bf16[128,2048]{1,0:T(8,128)(2,1)S(1)}, bf16[128,2048]{1,0:T(8,128)(2,1)S(1)}, u32[]{:S(2)}, u32[]{:S(2)}) collective-permute-start(bf16[128,2048]{1,0:T(8,128)(2,1)S(1)} %copy-done.1), channel_id=1, source_target_pairs={{0,8},{4,12},{8,0},{12,4},{1,9},{5,13},{9,1},{13,5},{2,10},{6,14},... | collective-permute-start | bytes 1572872 | tf_op jit(solution)/shard_map/ppermute | solution.py:119
  48.5 2.6 %collective-permute-start.5 = (bf16[256,640]{1,0:T(8,128)(2,1)S(1)}, bf16[256,640]{1,0:T(8,128)(2,1)}, u32[]{:S(2)}, u32[]{:S(2)}) collective-permute-start(bf16[256,640]{1,0:T(8,128)(2,1)S(1)} %shard_map.94.mine), channel_id=1, source_target_pairs={{0,1},{1,0},{2,3},{3,2},{4,5},{5,4},{6,7},{7,6},{8,9},{9,8},{10,11... | collective-permute-start | bytes 983048 | tf_op jit(solution)/shard_map/ppermute | solution.py:119
  48.6 15.9 %collective-permute-start.9 = (bf16[256,1024]{1,0:T(8,128)(2,1)}, bf16[256,1024]{1,0:T(8,128)(2,1)}, u32[]{:S(2)}, u32[]{:S(2)}) collective-permute-start(bf16[256,1024]{1,0:T(8,128)(2,1)} %collective-permute-done.4.second), channel_id=1, source_target_pairs={{0,16},{16,0},{1,17},{17,1},{2,18},{18,2},{3,19},{19,3},{4,20},{20... | collective-permute-start | bytes 1572872 | tf_op jit(solution)/shard_map/ppermute | solution.py:119
  51.1 1.0 copy-start.4
  55.5 0.7 copy-start.14
  56.2 3.8 %copy-start.5 = (bf16[1,64,2048]{2,1,0:T(8,128)(2,1)S(1)}, bf16[1,64,2048]{2,1,0:T(8,128)(2,1)}, u32[]{:S(2)}) copy-start(bf16[1,64,2048]{2,1,0:T(8,128)(2,1)} %param.9) | copy-start | bytes 786436
  56.2 3.8 %copy-start.17 = (bf16[256,128]{1,0:T(8,128)(2,1)S(1)}, bf16[256,128]{1,0:T(8,128)(2,1)}, u32[]{:S(2)}) copy-start(bf16[256,128]{1,0:T(8,128)(2,1)} %copy-done.16) | copy-start | bytes 196612
  56.2 15.2 %collective-permute-start.7 = (bf16[128,1024]{1,0:T(8,128)(2,1)}, bf16[128,1024]{1,0:T(8,128)(2,1)}, u32[]{:S(2)}, u32[]{:S(2)}) collective-permute-start(bf16[128,1024]{1,0:T(8,128)(2,1)} %get-tuple-element.34), channel_id=1, source_target_pairs={{0,8},{4,12},{8,0},{12,4},{1,9},{5,13},{9,1},{13,5},{2,10},{6,14},... | collective-permute-start | bytes 786440 | tf_op jit(solution)/shard_map/ppermute | solution.py:119
  60.1 2.8 %copy-start.2 = (f32[256,1024]{1,0:T(8,128)}, f32[256,1024]{1,0:T(8,128)S(1)}, u32[]{:S(2)}) copy-start(f32[256,1024]{1,0:T(8,128)S(1)} %shard_map.96.part) | copy-start | bytes 3145732
  62.8 8.6 %collective-permute-start.10 = (bf16[256,128]{1,0:T(8,128)(2,1)}, bf16[256,128]{1,0:T(8,128)(2,1)}, u32[]{:S(2)}, u32[]{:S(2)}) collective-permute-start(bf16[256,128]{1,0:T(8,128)(2,1)} %shard_map.97.low), channel_id=1, source_target_pairs={{0,2},{1,3},{2,0},{3,1},{4,6},{5,7},{6,4},{7,5},{8,10},{9,11},{10,... | collective-permute-start | bytes 196616 | tf_op jit(solution)/shard_map/ppermute | solution.py:119
  64.5 6.9 %copy-start.3 = (f32[256,1024]{1,0:T(8,128)S(1)}, f32[256,1024]{1,0:T(8,128)}, u32[]{:S(2)}) copy-start(f32[256,1024]{1,0:T(8,128)} %copy-done.2) | copy-start | bytes 3145732
  64.5 1.0 %copy-start.6 = (bf16[1,64,2048]{2,1,0:T(8,128)(2,1)S(1)}, bf16[1,64,2048]{2,1,0:T(8,128)(2,1)}, u32[]{:S(2)}) copy-start(bf16[1,64,2048]{2,1,0:T(8,128)(2,1)} %param.9) | copy-start | bytes 786436
  71.4 5.6 %copy-start.8 = (bf16[128,512]{1,0:T(8,128)(2,1)S(1)}, bf16[128,512]{1,0:T(8,128)(2,1)}, u32[]{:S(2)}) copy-start(bf16[128,512]{1,0:T(8,128)(2,1)} %cot.3) | copy-start | bytes 393220
  71.4 5.6 %copy-start.10 = (bf16[144,512]{1,0:T(8,128)(2,1)S(1)}, bf16[144,512]{1,0:T(8,128)(2,1)}, u32[]{:S(2)}) copy-start(bf16[144,512]{1,0:T(8,128)(2,1)} %copy-done.9) | copy-start | bytes 442372
  71.4 5.6 %copy-start.13 = (bf16[64,512]{1,0:T(8,128)(2,1)S(1)}, bf16[64,512]{1,0:T(8,128)(2,1)}, u32[]{:S(2)}) copy-start(bf16[64,512]{1,0:T(8,128)(2,1)} %copy-done.12) | copy-start | bytes 196612
  73.2 1.7 %collective-permute-start.11 = (bf16[256,640]{1,0:T(8,128)(2,1)S(1)}, bf16[256,640]{1,0:T(8,128)(2,1)S(1)}, u32[]{:S(2)}, u32[]{:S(2)}) collective-permute-start(bf16[256,640]{1,0:T(8,128)(2,1)S(1)} %get-tuple-element.42.give), channel_id=1, source_target_pairs={{0,1},{1,0},{2,3},{3,2},{4,5},{5,4},{6,7},{7,6},{8,9},{9,8},{10,11... | collective-permute-start | bytes 983048 | tf_op jit(solution)/shard_map/ppermute | solution.py:119
  75.5 16.6 %copy-start.15 = (bf16[128,1024]{1,0:T(8,128)(2,1)S(1)}, bf16[128,1024]{1,0:T(8,128)(2,1)}, u32[]{:S(2)}) copy-start(bf16[128,1024]{1,0:T(8,128)(2,1)} %copy-done.14) | copy-start | bytes 786436
  75.5 10.5 %collective-permute-start.12 = (bf16[256,512]{1,0:T(8,128)(2,1)S(1)}, bf16[256,512]{1,0:T(8,128)(2,1)S(1)}, u32[]{:S(2)}, u32[]{:S(2)}) collective-permute-start(bf16[256,512]{1,0:T(8,128)(2,1)S(1)} %shard_map.100.held), channel_id=1, source_target_pairs={{2,0},{3,1},{6,4},{7,5},{8,10},{9,11},{12,14},{13,15},{18,16},{19,... | collective-permute-start | bytes 786440 | tf_op jit(solution)/shard_map/ppermute | solution.py:124
  78.4 16.6 %collective-permute-start.15 = (bf16[64,2560]{1,0:T(8,128)(2,1)S(1)}, bf16[64,2560]{1,0:T(8,128)(2,1)S(1)}, u32[]{:S(2)}, u32[]{:S(2)}) collective-permute-start(bf16[64,2560]{1,0:T(8,128)(2,1)S(1)} %get-tuple-element.51), channel_id=1, source_target_pairs={{0,4},{4,0},{8,12},{12,8},{1,5},{5,1},{9,13},{13,9},{2,6},{6,2},{1... | collective-permute-start | bytes 983048 | tf_op jit(solution)/shard_map/ppermute | solution.py:119
  78.5 13.7 %collective-permute-start.14 = (bf16[128,1024]{1,0:T(8,128)(2,1)S(1)}, bf16[128,1024]{1,0:T(8,128)(2,1)S(1)}, u32[]{:S(2)}, u32[]{:S(2)}) collective-permute-start(bf16[128,1024]{1,0:T(8,128)(2,1)S(1)} %get-tuple-element.39), channel_id=1, source_target_pairs={{0,8},{4,12},{8,0},{12,4},{1,9},{5,13},{9,1},{13,5},{2,10},{6,14},... | collective-permute-start | bytes 786440 | tf_op jit(solution)/shard_map/ppermute | solution.py:119
  86.6 14.4 %collective-permute-start.13 = (bf16[128,512]{1,0:T(8,128)(2,1)S(1)}, bf16[128,512]{1,0:T(8,128)(2,1)S(1)}, u32[]{:S(2)}, u32[]{:S(2)}) collective-permute-start(bf16[128,512]{1,0:T(8,128)(2,1)S(1)} %shard_map.102), channel_id=1, source_target_pairs={{0,8},{4,12},{8,0},{12,4},{1,9},{5,13},{9,1},{13,5},{2,10},{6,14},... | collective-permute-start | bytes 393224 | tf_op jit(solution)/shard_map/ppermute | solution.py:119

commit v5 on v4

--- a/solution.py
+++ b/solution.py
@@ -150,6 +150,31 @@
     return got[0] if single else got
 
 
+def column_half(where, wide, arrays, counts, blocks):
+    def body(where, *refs):
+        place = 0
+        for ref in refs[:-1]:
+            refs[-1][place : place + ref.shape[0], :] = ref[...]
+            place += ref.shape[0]
+
+    def spec(count, block):
+        return pl.BlockSpec((count, wide), lambda j, s: (block, s[Y]))
+
+    total = sum(counts)
+    return pl.pallas_call(
+        body,
+        grid_spec=pltpu.PrefetchScalarGridSpec(
+            num_scalar_prefetch=1,
+            grid=(1,),
+            in_specs=[spec(n, b) for n, b in zip(counts, blocks)],
+            out_specs=pl.BlockSpec((total, wide), lambda j, s: (0, 0)),
+        ),
+        out_shape=jax.ShapeDtypeStruct((total, wide), bf16),
+        compiler_params=pltpu.CompilerParams(vmem_limit_bytes=12 * 1024 * 1024),
+        cost_estimate=cost(0),
+    )(where, *arrays)
+
+
 def member(where, idx, rank):
     lane = lax.broadcasted_iota(jnp.int32, (idx.shape[0], 2 * rank), 1)
     z = where[Z]
@@ -259,7 +284,7 @@
 
 def adapter_kernel(
     where, give, give_got, mine, got, act, act_got, cot, cot_got, up, up_sib,
-    lora, lora_far, down_own, up_own, sib,
+    lora, lora_far, down_own, up_own, sib, sib_end,
 ):
     rank, width, toks = up.shape[0], act.shape[1], act.shape[0]
     whole_low = whole_back(give, give_got)
@@ -268,16 +293,19 @@
     lora_far[...] = out[toks:]
     grad = tn(whole_back(mine, got), rows2(act[...], act_got[...]))
     down_own[...] = grad[:rank]
-    sib[:, :width] = grad[rank:].astype(bf16)
+    cut = sib.shape[1]
+    sib[...] = grad[rank:, :cut].astype(bf16)
+    sib_end[:, : width - cut] = grad[rank:, cut:].astype(bf16)
     grad = adapter_scale * tn(whole_low, rows2(cot[...], cot_got[: cot.shape[0], :]))
     up_own[...] = grad[:rank]
-    sib[:, width:] = grad[rank:].astype(bf16)
-
-
-def adapter_end_kernel(where, down_own, up_own, got, down_out, up_out):
-    width = down_own.shape[1]
-    down_out[0] = down_own[...] + got[:, :width].astype(f32)
-    up_out[0] = up_own[...] + got[:, width:].astype(f32)
+    sib_end[:, width - cut :] = grad[rank:].astype(bf16)
+
+
+def adapter_end_kernel(where, down_own, up_own, got, got_end, down_out, up_out):
+    cut, rest = got.shape[1], down_own.shape[1] - got.shape[1]
+    down_out[0, :, :cut] = down_own[:, :cut] + got[...].astype(f32)
+    down_out[0, :, cut:] = down_own[:, cut:] + got_end[:, :rest].astype(f32)
+    up_out[0] = up_own[...] + got_end[:, rest:].astype(f32)
 
 
 def base_near_kernel(where, act, act_got, weight, first, second, out):
@@ -352,11 +380,9 @@
     idx_row = jnp.pad(idx.astype(bf16), ((0, 15), (0, out_width - toks)))
     cot_got = swap(jnp.concatenate([cotangent, idx_row], axis=0), "fsdp", 2)
     up_sib = swap(up, "fsdp", 1)
-    w_mine = lax.dynamic_slice(key_value_weight, (0, y * wide), (rows, wide))
-    d_mine = lax.dynamic_slice(down, (0, y * wide), (rank, wide))
     head = rows * 2 // 4
-    piece0 = jnp.concatenate([d_mine, w_mine[:head]], axis=0)
-    piece1 = w_mine[head:]
+    piece0 = column_half(where, wide, (down, key_value_weight), (rank, head), (0, 0))
+    piece1 = column_half(where, wide, (key_value_weight,), (rows - head,), (1,))
     near0 = swap(piece0, "fsdp", 1)
     act_got = swap(after(activations, cot_got, up_sib), "fsdp", 2)
     near1 = swap(after(piece1, cot_got, up_sib), "fsdp", 1)
@@ -407,14 +433,15 @@
     held_got = both(held, [((a, b, d), (a, 1 - b, d)) for a, b, d in places if b != a // 2])
 
     give_got = after(give_got, held)
-    lora, lora_far, down_own, up_own, sib = local_kernel(
+    lora, lora_far, down_own, up_own, sib, sib_end = local_kernel(
         adapter_kernel,
         [
             ((toks, out_width), bf16),
             ((toks, out_width), bf16),
             ((rank, width), f32),
             ((rank, out_width), f32),
-            ((rank, width + out_width), bf16),
+            ((rank, (width + out_width) // 2), bf16),
+            ((rank, (width + out_width) // 2), bf16),
         ],
         where,
         give, give_got, mine, got, activations, act_got, cotangent, cot_got, up, up_sib, us=0,
@@ -425,7 +452,7 @@
     turned = swap(turn, "fsdp", 2)
     grad_down, up_gradient = local_kernel(
         adapter_end_kernel, [((1, rank, width), f32), ((1, rank, out_width), f32)], where,
-        down_own, up_own, swap(sib, "fsdp", 1),
+        down_own, up_own, swap(sib, "fsdp", 1), swap(sib_end, "fsdp", 1),
     )
 
     input_gradient = local_kernel(

time: 103 us -> 100 us (0.971)
  waiting for transfers between devices: 47 us -> 44.6 us
  Pallas kernels: 21.6 us -> 22.8 us
  local copies, waits for them, and re-layouts: 6.56 us -> 5.38 us
    ppermute x15 -> x16, waiting for transfers between devices: 44.7 us -> 42.4 us  [swap(): lax.ppermute(x, axis, [(i, i ^ bit) for i in range(lax.axis_size(axis))])]
    slice x1 -> x0, local copies, waits for them, and re-layouts: 2.1 us -> none  [pair_plan(): piece0 = jnp.concatenate([d_mine, w_mine[:head]], axis=0)]
    unnamed x38 -> x42, local copies, waits for them, and re-layouts: 3.37 us -> 5.21 us
    pallas_call x0 -> x2, Pallas kernels: none -> 1.16 us  [column_half(): pl.pallas_call(body, grid_spec=pltpu.PrefetchScalarGridSpec(num_scalar_pr...]
    ppermute x15 -> x16, starting transfers between devices: 23.9 us -> 24.7 us  [swap(): lax.ppermute(x, axis, [(i, i ^ bit) for i in range(lax.axis_size(axis))])]
  transfers between devices with their start and end apart: 16 -> 17, of which waited for: 10 -> 9; matrix products, arithmetic and copies ran while one was open for 0% -> 0% of each run, Pallas kernels for 18% -> 19%
where the time goes in v5:
time: 100 us; the launch traced here: 99.8 us
  waiting for transfers between devices  44.6 us (45%)
  starting transfers between devices  26 us (26%)
  Pallas kernels  22.8 us (23%)
  local copies, waits for them, and re-layouts  5.38 us (5%)
    ppermute x16, waiting for transfers between devices, swap(): lax.ppermute(x, axis, [(i, i ^ bit) for i in range(lax.axis_size(axis))])  42.4 us
    ppermute x16, starting transfers between devices, swap(): lax.ppermute(x, axis, [(i, i ^ bit) for i in range(lax.axis_size(axis))])  24.7 us
    pallas_call x11, Pallas kernels, local_kernel(): pl.pallas_call(body, out_shape=shapes, in_specs=[pl.BlockSpec(memory_spac...  15.3 us
    pallas_call x2, Pallas kernels, gradient_half(): pl.pallas_call(gradient_kernel, grid_spec=pltpu.PrefetchScalarGridSpec(nu...  6.34 us
    unnamed x42, local copies, waits for them, and re-layouts  5.21 us
    ppermute x1, waiting for transfers between devices, both(): return lax.ppermute(x, ('fsdp', 'tp'), flat)  2.26 us
  transfers between devices with their start and end apart: 17, of which 9 were waited for; matrix products, arithmetic and copies ran while one was open for 0% of the time, Pallas kernels for 19%

profile of v5, /device:TPU:0, one launch (start us, length us, event | category | flops | bytes accessed | tf_op | source)
XLA Modules:
  0.0 99.8 jit_solution(13400420093397831945)
XLA Ops:
  0.6 0.0 copy-start.20
  0.6 0.0 copy-start.13
  0.7 0.1 pad_add_fusion.where
  0.8 1.6 %copy-done = bf16[512,2048]{1,0:T(8,128)(2,1)S(1)} copy-done((bf16[512,2048]{1,0:T(8,128)(2,1)S(1)}, bf16[512,2048]{1,0:T(8,128)(2,1)}, u32[]{:S(2)}) %copy-start) | copy-done | bytes 2097176
  2.4 0.9 copy-done.3
  3.3 0.6 shard_map.96
  3.9 0.0 copy-start.2
  3.9 3.1 %collective-permute-start.6 = (bf16[320,1024]{1,0:T(8,128)(2,1)S(1)}, bf16[320,1024]{1,0:T(8,128)(2,1)}, u32[]{:S(2)}, u32[]{:S(2)}) collective-permute-start(bf16[320,1024]{1,0:T(8,128)(2,1)S(1)} %shard_map.96), channel_id=1, source_target_pairs={{0,4},{4,0},{8,12},{12,8},{1,5},{5,1},{9,13},{13,9},{2,6},{6,2},{1... | collective-permute-start | bytes 1966088 | tf_op jit(solution)/shard_map/ppermute | solution.py:119
  7.0 0.0 copy-done.20
  7.0 2.7 %collective-permute-start = (bf16[144,512]{1,0:T(8,128)(2,1)S(1)}, bf16[144,512]{1,0:T(8,128)(2,1)S(1)}, u32[]{:S(2)}, u32[]{:S(2)}) collective-permute-start(bf16[144,512]{1,0:T(8,128)(2,1)S(1)} %fusion.1), channel_id=1, source_target_pairs={{0,8},{4,12},{8,0},{12,4},{1,9},{5,13},{9,1},{13,5},{2,10},{6,14},... | collective-permute-start | bytes 442376 | tf_op jit(solution)/shard_map/ppermute | solution.py:119
  9.7 0.4 collective-permute-start.1
  10.2 0.6 shard_map.94
  10.7 15.6 %collective-permute-done.1.up_sib = bf16[64,512]{1,0:T(8,128)(2,1)S(1)} collective-permute-done((bf16[64,512]{1,0:T(8,128)(2,1)S(1)}, bf16[64,512]{1,0:T(8,128)(2,1)S(1)}, u32[]{:S(2)}, u32[]{:S(2)}) %collective-permute-start.1) | collective-permute-done | bytes 65568 | tf_op jit(solution)/shard_map/ppermute | solution.py:119
  26.3 0.0 collective-permute-done.cot_got
  26.3 2.0 %collective-permute-start.4 = (bf16[256,1024]{1,0:T(8,128)(2,1)S(1)}, bf16[256,1024]{1,0:T(8,128)(2,1)}, u32[]{:S(2)}, u32[]{:S(2)}) collective-permute-start(bf16[256,1024]{1,0:T(8,128)(2,1)S(1)} %shard_map.94), channel_id=1, source_target_pairs={{0,4},{4,0},{8,12},{12,8},{1,5},{5,1},{9,13},{13,9},{2,6},{6,2},{1... | collective-permute-start | bytes 1572872 | tf_op jit(solution)/shard_map/ppermute | solution.py:119
  28.4 0.8 shard_map.93
  29.2 0.0 copy-start.18
  29.2 1.6 %collective-permute-start.3 = (bf16[256,640]{1,0:T(8,128)(2,1)S(1)}, bf16[256,640]{1,0:T(8,128)(2,1)S(1)}, u32[]{:S(2)}, u32[]{:S(2)}) collective-permute-start(bf16[256,640]{1,0:T(8,128)(2,1)S(1)} %get-tuple-element.31.mine), channel_id=1, source_target_pairs={{0,2},{1,3},{2,0},{3,1},{4,6},{5,7},{6,4},{7,5},{8,10},{9,11},{10,... | collective-permute-start | bytes 983048 | tf_op jit(solution)/shard_map/ppermute | solution.py:119
  30.7 0.0 collective-permute-done.6.first.near
  30.8 1.5 %collective-permute-start.8 = (bf16[320,1024]{1,0:T(8,128)(2,1)}, bf16[320,1024]{1,0:T(8,128)(2,1)}, u32[]{:S(2)}, u32[]{:S(2)}) collective-permute-start(bf16[320,1024]{1,0:T(8,128)(2,1)} %collective-permute-done.6.first.near), channel_id=1, source_target_pairs={{0,16},{16,0},{1,17},{17,1},{2,18},{18,2},{3,19},{19,3},{4,20},{20... | collective-permute-start | bytes 1966088 | tf_op jit(solution)/shard_map/ppermute | solution.py:119
  32.3 2.3 %collective-permute-start.2 = (bf16[128,2048]{1,0:T(8,128)(2,1)S(1)}, bf16[128,2048]{1,0:T(8,128)(2,1)S(1)}, u32[]{:S(2)}, u32[]{:S(2)}) collective-permute-start(bf16[128,2048]{1,0:T(8,128)(2,1)S(1)} %copy-done.2), channel_id=1, source_target_pairs={{0,8},{4,12},{8,0},{12,4},{1,9},{5,13},{9,1},{13,5},{2,10},{6,14},... | collective-permute-start | bytes 1572872 | tf_op jit(solution)/shard_map/ppermute | solution.py:119
  34.6 2.7 %collective-permute-done.3.got = bf16[256,640]{1,0:T(8,128)(2,1)S(1)} collective-permute-done((bf16[256,640]{1,0:T(8,128)(2,1)S(1)}, bf16[256,640]{1,0:T(8,128)(2,1)S(1)}, u32[]{:S(2)}, u32[]{:S(2)}) %collective-permute-start.3) | collective-permute-done | bytes 327712 | tf_op jit(solution)/shard_map/ppermute | solution.py:119
  37.3 10.1 %collective-permute-done.4.second = bf16[256,1024]{1,0:T(8,128)(2,1)} collective-permute-done((bf16[256,1024]{1,0:T(8,128)(2,1)S(1)}, bf16[256,1024]{1,0:T(8,128)(2,1)}, u32[]{:S(2)}, u32[]{:S(2)}) %collective-permute-start.4) | collective-permute-done | bytes 524320 | tf_op jit(solution)/shard_map/ppermute | solution.py:119
  47.4 0.6 shard_map.95.mine
  48.0 0.0 copy-done.18
  48.0 0.1 collective-permute-start.5
  48.1 2.4 %collective-permute-start.9 = (bf16[256,1024]{1,0:T(8,128)(2,1)}, bf16[256,1024]{1,0:T(8,128)(2,1)}, u32[]{:S(2)}, u32[]{:S(2)}) collective-permute-start(bf16[256,1024]{1,0:T(8,128)(2,1)} %collective-permute-done.4.second), channel_id=1, source_target_pairs={{0,16},{16,0},{1,17},{17,1},{2,18},{18,2},{3,19},{19,3},{4,20},{20... | collective-permute-start | bytes 1572872 | tf_op jit(solution)/shard_map/ppermute | solution.py:119
  50.6 0.1 concatenate.12.where
  50.6 0.0 collective-permute-done.5.got
  50.6 0.9 copy-done.4
  51.6 3.5 %shard_map.97 = (bf16[128,1024]{1,0:T(8,128)(2,1)S(1)}, bf16[128,1024]{1,0:T(8,128)(2,1)}) custom-call(s32[5]{0:T(128)S(1)} %concatenate.12.where, bf16[256,640]{1,0:T(8,128)(2,1)S(1)} %shard_map.95.mine, bf16[256,640]{1,0:T(8,128)(2,1)} %collective-permute-done.5.got, bf16[512,2048]{1,0:T(8,128)(2,1)S(1)} %copy-done.1, bf16[64,2048]{1,0:T(8,128)(2,1)S(1)} %bitcast.10, ...), custom_call_target="tpu_custom_call" | custom-call | bytes 1000 | tf_op jit(solution)/shard_map/pallas_call | solution.py:242
  55.1 0.7 copy-done.16
  55.8 0.5 collective-permute-start.7
  56.3 0.0 collective-permute-done.2.act_got
  56.3 2.3 %shard_map.98.part = f32[256,1024]{1,0:T(8,128)S(1)} custom-call(s32[4]{0:T(128)S(1)} %pad_add_fusion.where, bf16[128,2048]{1,0:T(8,128)(2,1)S(1)} %copy-done.2, bf16[128,2048]{1,0:T(8,128)(2,1)S(1)} %collective-permute-done.2.act_got, bf16[512,2048]{1,0:T(8,128)(2,1)S(1)} %copy-done.1, bf16[320,1024]{1,0:T(8,128)(2,1)} %collective-permute-done.6.first.near, ...), custom_call_target="tpu_custom_call" | custom-call | bytes 1000 | tf_op jit(solution)/shard_map/pallas_call | solution.py:141
  58.5 0.0 collective-permute-done.8.far.first
  58.6 2.7 %shard_map.99.low = bf16[256,128]{1,0:T(8,128)(2,1)} custom-call(s32[4]{0:T(128)S(1)} %pad_add_fusion.where, bf16[128,2048]{1,0:T(8,128)(2,1)S(1)} %copy-done.2, bf16[128,2048]{1,0:T(8,128)(2,1)S(1)} %collective-permute-done.2.act_got, bf16[256,128]{1,0:T(8,128)(2,1)S(1)} %copy-done.19, bf16[64,2048]{1,0:T(8,128)(2,1)S(1)} %bitcast.11, ...), custom_call_target="tpu_custom_call" | custom-call | bytes 1000 | tf_op jit(solution)/shard_map/pallas_call | solution.py:141
  61.3 2.5 %collective-permute-start.10 = (bf16[256,128]{1,0:T(8,128)(2,1)}, bf16[256,128]{1,0:T(8,128)(2,1)}, u32[]{:S(2)}, u32[]{:S(2)}) collective-permute-start(bf16[256,128]{1,0:T(8,128)(2,1)} %shard_map.99.low), channel_id=1, source_target_pairs={{0,2},{1,3},{2,0},{3,1},{4,6},{5,7},{6,4},{7,5},{8,10},{9,11},{10,... | collective-permute-start | bytes 196616 | tf_op jit(solution)/shard_map/ppermute | solution.py:119
  63.8 0.1 concatenate.13.where
  63.8 0.0 collective-permute-done.9.second
  63.8 0.9 copy-done.6
  64.8 2.9 %shard_map.100 = (bf16[128,1024]{1,0:T(8,128)(2,1)S(1)}, bf16[128,1024]{1,0:T(8,128)(2,1)S(1)}) custom-call(s32[5]{0:T(128)S(1)} %concatenate.13.where, bf16[256,640]{1,0:T(8,128)(2,1)S(1)} %shard_map.95.mine, bf16[256,640]{1,0:T(8,128)(2,1)} %collective-permute-done.5.got, bf16[512,2048]{1,0:T(8,128)(2,1)S(1)} %copy-done.1, bf16[64,2048]{1,0:T(8,128)(2,1)S(1)} %bitcast.12, ...), custom_call_target="tpu_custom_call" | custom-call | bytes 1000 | tf_op jit(solution)/shard_map/pallas_call | solution.py:242
  67.7 3.2 %collective-permute-done.7.near_got = bf16[128,1024]{1,0:T(8,128)(2,1)} collective-permute-done((bf16[128,1024]{1,0:T(8,128)(2,1)}, bf16[128,1024]{1,0:T(8,128)(2,1)}, u32[]{:S(2)}, u32[]{:S(2)}) %collective-permute-start.7) | collective-permute-done | bytes 262176 | tf_op jit(solution)/shard_map/ppermute | solution.py:119
  70.9 0.0 collective-permute-done.10.low_got
  70.9 1.8 %shard_map.101 = (f32[256,512]{1,0:T(8,128)S(1)}, bf16[256,640]{1,0:T(8,128)(2,1)S(1)}) custom-call(s32[4]{0:T(128)S(1)} %pad_add_fusion.where, f32[256,1024]{1,0:T(8,128)S(1)} %copy-done.8, bf16[128,2048]{1,0:T(8,128)(2,1)S(1)} %copy-done.2, bf16[128,2048]{1,0:T(8,128)(2,1)S(1)} %collective-permute-done.2.act_got, ...), custom_call_target="tpu_custom_call" | custom-call | bytes 1000 | tf_op jit(solution)/shard_map/pallas_call | solution.py:141
  72.7 0.1 collective-permute-start.11
  72.8 1.6 %collective-permute-done.11.got.give_got = bf16[256,640]{1,0:T(8,128)(2,1)S(1)} collective-permute-done((bf16[256,640]{1,0:T(8,128)(2,1)S(1)}, bf16[256,640]{1,0:T(8,128)(2,1)S(1)}, u32[]{:S(2)}, u32[]{:S(2)}) %collective-permute-start.11) | collective-permute-done | bytes 327712 | tf_op jit(solution)/shard_map/ppermute | solution.py:119
  74.4 0.6 shard_map.102.held
  75.0 1.3 %collective-permute-start.12 = (bf16[256,512]{1,0:T(8,128)(2,1)S(1)}, bf16[256,512]{1,0:T(8,128)(2,1)S(1)}, u32[]{:S(2)}, u32[]{:S(2)}) collective-permute-start(bf16[256,512]{1,0:T(8,128)(2,1)S(1)} %shard_map.102.held), channel_id=1, source_target_pairs={{2,0},{3,1},{6,4},{7,5},{8,10},{9,11},{12,14},{13,15},{18,16},{19,... | collective-permute-start | bytes 786440 | tf_op jit(solution)/shard_map/ppermute | solution.py:124
  76.3 2.7 %collective-permute-start.14 = (bf16[128,1024]{1,0:T(8,128)(2,1)S(1)}, bf16[128,1024]{1,0:T(8,128)(2,1)S(1)}, u32[]{:S(2)}, u32[]{:S(2)}) collective-permute-start(bf16[128,1024]{1,0:T(8,128)(2,1)S(1)} %get-tuple-element.40), channel_id=1, source_target_pairs={{0,8},{4,12},{8,0},{12,4},{1,9},{5,13},{9,1},{13,5},{2,10},{6,14},... | collective-permute-start | bytes 786440 | tf_op jit(solution)/shard_map/ppermute | solution.py:119
  79.0 0.0 copy-done.10
  79.0 1.4 %shard_map.103 = (bf16[128,512]{1,0:T(8,128)(2,1)S(1)}, bf16[128,512]{1,0:T(8,128)(2,1)S(1)}, f32[64,2048]{1,0:T(8,128)S(1)}, f32[64,512]{1,0:T(8,128)S(1)}, bf1...) custom-call(s32[4]{0:T(128)S(1)} %pad_add_fusion.where, bf16[256,640]{1,0:T(8,128)(2,1)S(1)} %get-tuple-element.43.give, ...), custom_call_target="tpu_custom_call" | custom-call | bytes 1000 | tf_op jit(solution)/shard_map/pallas_call | solution.py:141
  80.4 2.6 %collective-permute-start.15 = (bf16[64,1280]{1,0:T(8,128)(2,1)S(1)}, bf16[64,1280]{1,0:T(8,128)(2,1)S(1)}, u32[]{:S(2)}, u32[]{:S(2)}) collective-permute-start(bf16[64,1280]{1,0:T(8,128)(2,1)S(1)} %get-tuple-element.52), channel_id=1, source_target_pairs={{0,4},{4,0},{8,12},{12,8},{1,5},{5,1},{9,13},{13,9},{2,6},{6,2},{1... | collective-permute-start | bytes 491528 | tf_op jit(solution)/shard_map/ppermute | solution.py:119
  83.0 0.1 collective-permute-start.16
  83.1 2.3 %collective-permute-done.12.got = bf16[256,512]{1,0:T(8,128)(2,1)S(1)} collective-permute-done((bf16[256,512]{1,0:T(8,128)(2,1)S(1)}, bf16[256,512]{1,0:T(8,128)(2,1)S(1)}, u32[]{:S(2)}, u32[]{:S(2)}) %collective-permute-start.12) | collective-permute-done | bytes 262176 | tf_op jit(solution)/shard_map/ppermute | solution.py:124
  85.3 0.6 shard_map.104
  85.9 0.1 collective-permute-start.13
  86.0 6.1 %collective-permute-done.14.far_got = bf16[128,1024]{1,0:T(8,128)(2,1)S(1)} collective-permute-done((bf16[128,1024]{1,0:T(8,128)(2,1)S(1)}, bf16[128,1024]{1,0:T(8,128)(2,1)S(1)}, u32[]{:S(2)}, u32[]{:S(2)}) %collective-permute-start.14) | collective-permute-done | bytes 262176 | tf_op jit(solution)/shard_map/ppermute | solution.py:119
  92.1 1.9 %shard_map.106 = bf16[128,2048]{1,0:T(8,128)(2,1)} custom-call(s32[4]{0:T(128)S(1)} %pad_add_fusion.where, bf16[128,1024]{1,0:T(8,128)(2,1)S(1)} %copy-done.17, bf16[128,1024]{1,0:T(8,128)(2,1)} %collective-permute-done.7.near_got, bf16[128,1024]{1,0:T(8,128)(2,1)S(1)} %get-tuple-element.49.far, bf16[128,1024]{1,0:T(8,128)(2,1)S(1)} %collective-permute-done.14.far_got), custom_call_target="tpu_custom_call" | custom-call | bytes 1000 | tf_op jit(solution)/shard_map/pallas_call | solution.py:141
  94.0 0.7 collective-permute-done.15.got
  94.7 2.4 %collective-permute-done.16.got_end = bf16[64,1280]{1,0:T(8,128)(2,1)S(1)} collective-permute-done((bf16[64,1280]{1,0:T(8,128)(2,1)S(1)}, bf16[64,1280]{1,0:T(8,128)(2,1)S(1)}, u32[]{:S(2)}, u32[]{:S(2)}) %collective-permute-start.16) | collective-permute-done | bytes 163872 | tf_op jit(solution)/shard_map/ppermute | solution.py:119
  97.1 1.4 %shard_map.107 = (f32[1,64,2048]{2,1,0:T(8,128)}, f32[1,64,512]{2,1,0:T(8,128)}) custom-call(s32[4]{0:T(128)S(1)} %pad_add_fusion.where, f32[64,2048]{1,0:T(8,128)S(1)} %get-tuple-element.50.down_own, f32[64,512]{1,0:T(8,128)S(1)} %get-tuple-element.51.up_own, bf16[64,1280]{1,0:T(8,128)(2,1)S(1)} %collective-permute-done.15.got, ...), custom_call_target="tpu_custom_call" | custom-call | bytes 1000 | tf_op jit(solution)/shard_map/pallas_call | solution.py:141
  98.5 0.0 collective-permute-done.13.turned
  98.5 1.3 %shard_map.105 = bf16[128,512]{1,0:T(8,128)(2,1)} custom-call(s32[4]{0:T(128)S(1)} %pad_add_fusion.where, bf16[256,512]{1,0:T(8,128)(2,1)S(1)} %shard_map.102.held, bf16[256,512]{1,0:T(8,128)(2,1)S(1)} %collective-permute-done.12.got, bf16[128,512]{1,0:T(8,128)(2,1)S(1)} %get-tuple-element.45.lora, bf16[128,512]{1,0:T(8,128)(2,1)S(1)} %collective-permute-done.13.turned), custom_call_target="tpu_custom_call" | custom-call | bytes 1000 | tf_op jit(solution)/shard_map/pallas_call | solution.py:141
  (32 shorter events, 0.1 us)
Async XLA Ops:
  0.6 6.4 %copy-start.20 = (s32[128,1]{0,1:T(1,128)S(1)}, s32[128,1]{0,1:T(1,128)}, u32[]{:S(2)}) copy-start(s32[128,1]{0,1:T(1,128)} %param.8) | copy-start | bytes 1540
  0.6 9.1 %copy-start.13 = (bf16[1,64,512]{2,1,0:T(8,128)(2,1)S(1)}, bf16[1,64,512]{2,1,0:T(8,128)(2,1)}, u32[]{:S(2)}) copy-start(bf16[1,64,512]{2,1,0:T(8,128)(2,1)} %param.10) | copy-start | bytes 196612
  0.8 1.6 %copy-start = (bf16[512,2048]{1,0:T(8,128)(2,1)S(1)}, bf16[512,2048]{1,0:T(8,128)(2,1)}, u32[]{:S(2)}) copy-start(bf16[512,2048]{1,0:T(8,128)(2,1)} %weight.5) | copy-start | bytes 6291460
  2.4 0.9 copy-start.3
  3.3 3.7 %copy-start.9 = (bf16[128,512]{1,0:T(8,128)(2,1)S(1)}, bf16[128,512]{1,0:T(8,128)(2,1)}, u32[]{:S(2)}) copy-start(bf16[128,512]{1,0:T(8,128)(2,1)} %cot.3) | copy-start | bytes 393220
  3.3 6.8 %copy-start.1 = (bf16[512,2048]{1,0:T(8,128)(2,1)S(1)}, bf16[512,2048]{1,0:T(8,128)(2,1)}, u32[]{:S(2)}) copy-start(bf16[512,2048]{1,0:T(8,128)(2,1)} %weight.5) | copy-start | bytes 6291460
  3.9 28.4 %copy-start.2 = (bf16[128,2048]{1,0:T(8,128)(2,1)S(1)}, bf16[128,2048]{1,0:T(8,128)(2,1)}, u32[]{:S(2)}) copy-start(bf16[128,2048]{1,0:T(8,128)(2,1)} %act.7) | copy-start | bytes 1572868
  3.9 26.8 %collective-permute-start.6 = (bf16[320,1024]{1,0:T(8,128)(2,1)S(1)}, bf16[320,1024]{1,0:T(8,128)(2,1)}, u32[]{:S(2)}, u32[]{:S(2)}) collective-permute-start(bf16[320,1024]{1,0:T(8,128)(2,1)S(1)} %shard_map.96), channel_id=1, source_target_pairs={{0,4},{4,0},{8,12},{12,8},{1,5},{5,1},{9,13},{13,9},{2,6},{6,2},{1... | collective-permute-start | bytes 1966088 | tf_op jit(solution)/shard_map/ppermute | solution.py:119
  7.0 19.3 %collective-permute-start = (bf16[144,512]{1,0:T(8,128)(2,1)S(1)}, bf16[144,512]{1,0:T(8,128)(2,1)S(1)}, u32[]{:S(2)}, u32[]{:S(2)}) collective-permute-start(bf16[144,512]{1,0:T(8,128)(2,1)S(1)} %fusion.1), channel_id=1, source_target_pairs={{0,8},{4,12},{8,0},{12,4},{1,9},{5,13},{9,1},{13,5},{2,10},{6,14},... | collective-permute-start | bytes 442376 | tf_op jit(solution)/shard_map/ppermute | solution.py:119
  9.7 16.6 %collective-permute-start.1 = (bf16[64,512]{1,0:T(8,128)(2,1)S(1)}, bf16[64,512]{1,0:T(8,128)(2,1)S(1)}, u32[]{:S(2)}, u32[]{:S(2)}) collective-permute-start(bf16[64,512]{1,0:T(8,128)(2,1)S(1)} %bitcast.13), channel_id=1, source_target_pairs={{0,4},{4,0},{8,12},{12,8},{1,5},{5,1},{9,13},{13,9},{2,6},{6,2},{1... | collective-permute-start | bytes 196616 | tf_op jit(solution)/shard_map/ppermute | solution.py:119
  26.3 2.9 %copy-start.14 = (bf16[64,512]{1,0:T(8,128)(2,1)}, bf16[64,512]{1,0:T(8,128)(2,1)S(1)}, u32[]{:S(2)}) copy-start(bf16[64,512]{1,0:T(8,128)(2,1)S(1)} %collective-permute-done.1.up_sib) | copy-start | bytes 196612
  26.3 21.1 %copy-start.11 = (bf16[144,512]{1,0:T(8,128)(2,1)}, bf16[144,512]{1,0:T(8,128)(2,1)S(1)}, u32[]{:S(2)}) copy-start(bf16[144,512]{1,0:T(8,128)(2,1)S(1)} %collective-permute-done.cot_got) | copy-start | bytes 442372
  26.3 21.1 %collective-permute-start.4 = (bf16[256,1024]{1,0:T(8,128)(2,1)S(1)}, bf16[256,1024]{1,0:T(8,128)(2,1)}, u32[]{:S(2)}, u32[]{:S(2)}) collective-permute-start(bf16[256,1024]{1,0:T(8,128)(2,1)S(1)} %shard_map.94), channel_id=1, source_target_pairs={{0,4},{4,0},{8,12},{12,8},{1,5},{5,1},{9,13},{13,9},{2,6},{6,2},{1... | collective-permute-start | bytes 1572872 | tf_op jit(solution)/shard_map/ppermute | solution.py:119
  29.2 18.8 %copy-start.18 = (bf16[256,128]{1,0:T(8,128)(2,1)}, bf16[256,128]{1,0:T(8,128)(2,1)S(1)}, u32[]{:S(2)}) copy-start(bf16[256,128]{1,0:T(8,128)(2,1)S(1)} %get-tuple-element.38.members) | copy-start | bytes 196612
  29.2 8.1 %collective-permute-start.3 = (bf16[256,640]{1,0:T(8,128)(2,1)S(1)}, bf16[256,640]{1,0:T(8,128)(2,1)S(1)}, u32[]{:S(2)}, u32[]{:S(2)}) collective-permute-start(bf16[256,640]{1,0:T(8,128)(2,1)S(1)} %get-tuple-element.31.mine), channel_id=1, source_target_pairs={{0,2},{1,3},{2,0},{3,1},{4,6},{5,7},{6,4},{7,5},{8,10},{9,11},{10,... | collective-permute-start | bytes 983048 | tf_op jit(solution)/shard_map/ppermute | solution.py:119
  30.8 27.8 %collective-permute-start.8 = (bf16[320,1024]{1,0:T(8,128)(2,1)}, bf16[320,1024]{1,0:T(8,128)(2,1)}, u32[]{:S(2)}, u32[]{:S(2)}) collective-permute-start(bf16[320,1024]{1,0:T(8,128)(2,1)} %collective-permute-done.6.first.near), channel_id=1, source_target_pairs={{0,16},{16,0},{1,17},{17,1},{2,18},{18,2},{3,19},{19,3},{4,20},{20... | collective-permute-start | bytes 1966088 | tf_op jit(solution)/shard_map/ppermute | solution.py:119
  32.3 24.0 %collective-permute-start.2 = (bf16[128,2048]{1,0:T(8,128)(2,1)S(1)}, bf16[128,2048]{1,0:T(8,128)(2,1)S(1)}, u32[]{:S(2)}, u32[]{:S(2)}) collective-permute-start(bf16[128,2048]{1,0:T(8,128)(2,1)S(1)} %copy-done.2), channel_id=1, source_target_pairs={{0,8},{4,12},{8,0},{12,4},{1,9},{5,13},{9,1},{13,5},{2,10},{6,14},... | collective-permute-start | bytes 1572872 | tf_op jit(solution)/shard_map/ppermute | solution.py:119
  48.0 2.6 %collective-permute-start.5 = (bf16[256,640]{1,0:T(8,128)(2,1)S(1)}, bf16[256,640]{1,0:T(8,128)(2,1)}, u32[]{:S(2)}, u32[]{:S(2)}) collective-permute-start(bf16[256,640]{1,0:T(8,128)(2,1)S(1)} %shard_map.95.mine), channel_id=1, source_target_pairs={{0,1},{1,0},{2,3},{3,2},{4,5},{5,4},{6,7},{7,6},{8,9},{9,8},{10,11... | collective-permute-start | bytes 983048 | tf_op jit(solution)/shard_map/ppermute | solution.py:119
  48.1 15.7 %collective-permute-start.9 = (bf16[256,1024]{1,0:T(8,128)(2,1)}, bf16[256,1024]{1,0:T(8,128)(2,1)}, u32[]{:S(2)}, u32[]{:S(2)}) collective-permute-start(bf16[256,1024]{1,0:T(8,128)(2,1)} %collective-permute-done.4.second), channel_id=1, source_target_pairs={{0,16},{16,0},{1,17},{17,1},{2,18},{18,2},{3,19},{19,3},{4,20},{20... | collective-permute-start | bytes 1572872 | tf_op jit(solution)/shard_map/ppermute | solution.py:119
  50.6 1.0 copy-start.4
  55.1 0.7 copy-start.16
  55.8 2.8 %copy-start.5 = (bf16[1,64,2048]{2,1,0:T(8,128)(2,1)S(1)}, bf16[1,64,2048]{2,1,0:T(8,128)(2,1)}, u32[]{:S(2)}) copy-start(bf16[1,64,2048]{2,1,0:T(8,128)(2,1)} %param.9) | copy-start | bytes 786436
  55.8 2.8 %copy-start.19 = (bf16[256,128]{1,0:T(8,128)(2,1)S(1)}, bf16[256,128]{1,0:T(8,128)(2,1)}, u32[]{:S(2)}) copy-start(bf16[256,128]{1,0:T(8,128)(2,1)} %copy-done.18) | copy-start | bytes 196612
  55.8 15.1 %collective-permute-start.7 = (bf16[128,1024]{1,0:T(8,128)(2,1)}, bf16[128,1024]{1,0:T(8,128)(2,1)}, u32[]{:S(2)}, u32[]{:S(2)}) collective-permute-start(bf16[128,1024]{1,0:T(8,128)(2,1)} %get-tuple-element.35), channel_id=1, source_target_pairs={{0,8},{4,12},{8,0},{12,4},{1,9},{5,13},{9,1},{13,5},{2,10},{6,14},... | collective-permute-start | bytes 786440 | tf_op jit(solution)/shard_map/ppermute | solution.py:119
  58.5 2.8 %copy-start.7 = (f32[256,1024]{1,0:T(8,128)}, f32[256,1024]{1,0:T(8,128)S(1)}, u32[]{:S(2)}) copy-start(f32[256,1024]{1,0:T(8,128)S(1)} %shard_map.98.part) | copy-start | bytes 3145732
  61.3 9.6 %collective-permute-start.10 = (bf16[256,128]{1,0:T(8,128)(2,1)}, bf16[256,128]{1,0:T(8,128)(2,1)}, u32[]{:S(2)}, u32[]{:S(2)}) collective-permute-start(bf16[256,128]{1,0:T(8,128)(2,1)} %shard_map.99.low), channel_id=1, source_target_pairs={{0,2},{1,3},{2,0},{3,1},{4,6},{5,7},{6,4},{7,5},{8,10},{9,11},{10,... | collective-permute-start | bytes 196616 | tf_op jit(solution)/shard_map/ppermute | solution.py:119
  63.8 1.0 copy-start.6
  64.8 6.1 %copy-start.8 = (f32[256,1024]{1,0:T(8,128)S(1)}, f32[256,1024]{1,0:T(8,128)}, u32[]{:S(2)}) copy-start(f32[256,1024]{1,0:T(8,128)} %copy-done.7) | copy-start | bytes 3145732
  70.9 8.1 %copy-start.10 = (bf16[128,512]{1,0:T(8,128)(2,1)S(1)}, bf16[128,512]{1,0:T(8,128)(2,1)}, u32[]{:S(2)}) copy-start(bf16[128,512]{1,0:T(8,128)(2,1)} %cot.3) | copy-start | bytes 393220
  70.9 8.1 %copy-start.12 = (bf16[144,512]{1,0:T(8,128)(2,1)S(1)}, bf16[144,512]{1,0:T(8,128)(2,1)}, u32[]{:S(2)}) copy-start(bf16[144,512]{1,0:T(8,128)(2,1)} %copy-done.11) | copy-start | bytes 442372
  70.9 8.1 %copy-start.15 = (bf16[64,512]{1,0:T(8,128)(2,1)S(1)}, bf16[64,512]{1,0:T(8,128)(2,1)}, u32[]{:S(2)}) copy-start(bf16[64,512]{1,0:T(8,128)(2,1)} %copy-done.14) | copy-start | bytes 196612
  72.7 1.7 %collective-permute-start.11 = (bf16[256,640]{1,0:T(8,128)(2,1)S(1)}, bf16[256,640]{1,0:T(8,128)(2,1)S(1)}, u32[]{:S(2)}, u32[]{:S(2)}) collective-permute-start(bf16[256,640]{1,0:T(8,128)(2,1)S(1)} %get-tuple-element.43.give), channel_id=1, source_target_pairs={{0,1},{1,0},{2,3},{3,2},{4,5},{5,4},{6,7},{7,6},{8,9},{9,8},{10,11... | collective-permute-start | bytes 983048 | tf_op jit(solution)/shard_map/ppermute | solution.py:119
  74.4 17.7 %copy-start.17 = (bf16[128,1024]{1,0:T(8,128)(2,1)S(1)}, bf16[128,1024]{1,0:T(8,128)(2,1)}, u32[]{:S(2)}) copy-start(bf16[128,1024]{1,0:T(8,128)(2,1)} %copy-done.16) | copy-start | bytes 786436
  75.0 10.3 %collective-permute-start.12 = (bf16[256,512]{1,0:T(8,128)(2,1)S(1)}, bf16[256,512]{1,0:T(8,128)(2,1)S(1)}, u32[]{:S(2)}, u32[]{:S(2)}) collective-permute-start(bf16[256,512]{1,0:T(8,128)(2,1)S(1)} %shard_map.102.held), channel_id=1, source_target_pairs={{2,0},{3,1},{6,4},{7,5},{8,10},{9,11},{12,14},{13,15},{18,16},{19,... | collective-permute-start | bytes 786440 | tf_op jit(solution)/shard_map/ppermute | solution.py:124
  76.3 15.8 %collective-permute-start.14 = (bf16[128,1024]{1,0:T(8,128)(2,1)S(1)}, bf16[128,1024]{1,0:T(8,128)(2,1)S(1)}, u32[]{:S(2)}, u32[]{:S(2)}) collective-permute-start(bf16[128,1024]{1,0:T(8,128)(2,1)S(1)} %get-tuple-element.40), channel_id=1, source_target_pairs={{0,8},{4,12},{8,0},{12,4},{1,9},{5,13},{9,1},{13,5},{2,10},{6,14},... | collective-permute-start | bytes 786440 | tf_op jit(solution)/shard_map/ppermute | solution.py:119
  80.4 14.3 %collective-permute-start.15 = (bf16[64,1280]{1,0:T(8,128)(2,1)S(1)}, bf16[64,1280]{1,0:T(8,128)(2,1)S(1)}, u32[]{:S(2)}, u32[]{:S(2)}) collective-permute-start(bf16[64,1280]{1,0:T(8,128)(2,1)S(1)} %get-tuple-element.52), channel_id=1, source_target_pairs={{0,4},{4,0},{8,12},{12,8},{1,5},{5,1},{9,13},{13,9},{2,6},{6,2},{1... | collective-permute-start | bytes 491528 | tf_op jit(solution)/shard_map/ppermute | solution.py:119
  83.0 14.1 %collective-permute-start.16 = (bf16[64,1280]{1,0:T(8,128)(2,1)S(1)}, bf16[64,1280]{1,0:T(8,128)(2,1)S(1)}, u32[]{:S(2)}, u32[]{:S(2)}) collective-permute-start(bf16[64,1280]{1,0:T(8,128)(2,1)S(1)} %get-tuple-element.53), channel_id=1, source_target_pairs={{0,4},{4,0},{8,12},{12,8},{1,5},{5,1},{9,13},{13,9},{2,6},{6,2},{1... | collective-permute-start | bytes 491528 | tf_op jit(solution)/shard_map/ppermute | solution.py:119
  85.9 12.6 %collective-permute-start.13 = (bf16[128,512]{1,0:T(8,128)(2,1)S(1)}, bf16[128,512]{1,0:T(8,128)(2,1)S(1)}, u32[]{:S(2)}, u32[]{:S(2)}) collective-permute-start(bf16[128,512]{1,0:T(8,128)(2,1)S(1)} %shard_map.104), channel_id=1, source_target_pairs={{0,8},{4,12},{8,0},{12,4},{1,9},{5,13},{9,1},{13,5},{2,10},{6,14},... | collective-permute-start | bytes 393224 | tf_op jit(solution)/shard_map/ppermute | solution.py:119

commit v6 on v5

--- a/solution.py
+++ b/solution.py
@@ -258,7 +258,7 @@
             jax.ShapeDtypeStruct((toks, steps * tile), bf16),
             jax.ShapeDtypeStruct((toks, steps * tile), bf16),
         ],
-        compiler_params=pltpu.CompilerParams(vmem_limit_bytes=12 * 1024 * 1024),
+        compiler_params=pltpu.CompilerParams(vmem_limit_bytes=56 * 1024 * 1024),
         cost_estimate=cost(0),
     )(jnp.concatenate([where, side[None]]), mine, got, weight, down, first, second)
 
@@ -282,12 +282,28 @@
     out[...] = jnp.where(members[...] != 0, part, 0.0).astype(bf16)
 
 
+def low_part(where, act, act_got, members, down, near, far):
+    whole = lambda a: pl.BlockSpec(a.shape, lambda j: (0, 0))
+    head = pl.BlockSpec((down.shape[0], near.shape[1]), lambda j: (0, 0))
+    return pl.pallas_call(
+        low_kernel,
+        grid=(1,),
+        in_specs=[pl.BlockSpec(memory_space=pltpu.SMEM)]
+        + [whole(a) for a in (act, act_got, members, down)]
+        + [head, head],
+        out_specs=whole(members),
+        out_shape=jax.ShapeDtypeStruct(members.shape, bf16),
+        compiler_params=pltpu.CompilerParams(vmem_limit_bytes=12 * 1024 * 1024),
+        cost_estimate=cost(0),
+    )(where, act, act_got, members, down, near, far)
+
+
 def adapter_kernel(
-    where, give, give_got, mine, got, act, act_got, cot, cot_got, up, up_sib,
+    where, give, give2, give_got, give_got2, mine, got, act, act_got, cot, cot_got, up, up_sib,
     lora, lora_far, down_own, up_own, sib, sib_end,
 ):
     rank, width, toks = up.shape[0], act.shape[1], act.shape[0]
-    whole_low = whole_back(give, give_got)
+    whole_low = rows2(whole_back(give, give_got), whole_back(give2, give_got2))
     out = (adapter_scale * nn(whole_low, rows2(up[...], up_sib[...]))).astype(bf16)
     lora[...] = out[:toks]
     lora_far[...] = out[toks:]
@@ -320,7 +336,7 @@
     out[:, rows + head :] = nt(near, second[...])
 
 
-def base_far_kernel(where, part, act, act_got, first, second, low, low_got, keep, give):
+def base_far_kernel(where, part, act, act_got, first, second, low, low_got, keep, give, give2):
     rows = keep.shape[1]
     head = rows - second.shape[0]
     cut = first.shape[0] - head
@@ -332,25 +348,30 @@
         mine = part[:, lo:hi]
         other = part[:, rows + lo : rows + hi] + nt(far, block)
         keep[:, lo:hi] = jnp.where(on_own, mine, other)
-        give[:, lo:hi] = jnp.where(on_own, other, mine).astype(bf16)
-    give[:, rows:] = (low[...].astype(f32) + low_got[...].astype(f32)).astype(bf16)
-
-
-def held_kernel(where, keep, got, held):
-    held[...] = (keep[...] + got[:, : keep.shape[1]].astype(f32)).astype(bf16)
+        out = jnp.where(on_own, other, mine).astype(bf16)
+        give[:, lo:hi] = out[: give.shape[0]]
+        give2[:, lo:hi] = out[give.shape[0] :]
+    total = (low[...].astype(f32) + low_got[...].astype(f32)).astype(bf16)
+    give[:, rows:] = total[: give.shape[0]]
+    give2[:, rows:] = total[give.shape[0] :]
+
+
+def held_kernel(where, keep, got, got2, here, there):
+    toks = here.shape[0]
+    held = (keep[...] + rows2(got[...], got2[...])[:, : keep.shape[1]].astype(f32)).astype(bf16)
+    here[...] = held[:toks]
+    there[...] = held[toks:]
 
 
 def turn_kernel(where, held, got, lora_far, turn):
-    toks = turn.shape[0]
     in_pair = jnp.full((1, 1), where[IN_PAIR], jnp.int32) == 1
-    base = held[toks:, :].astype(f32) + got[toks:, :].astype(f32)
+    base = held[...].astype(f32) + got[...].astype(f32)
     turn[...] = (lora_far[...].astype(f32) + jnp.where(in_pair, base, 0.0)).astype(bf16)
 
 
 def output_kernel(where, held, got, lora, turned, out):
-    toks = out.shape[0]
     in_pair = jnp.full((1, 1), where[IN_PAIR], jnp.int32) == 1
-    base = held[:toks, :].astype(f32) + got[:toks, :].astype(f32)
+    base = held[...].astype(f32) + got[...].astype(f32)
     total = turned[...].astype(f32) + jnp.where(in_pair, base, 0.0)
     out[...] = (total + lora[...].astype(f32)).astype(bf16)
 
@@ -411,26 +432,27 @@
     )
 
     far0 = after(far0, part)
-    low = local_kernel(
-        low_kernel, ((2 * toks, 2 * rank), bf16), where,
-        activations, act_got, members, down, near0, far0,
-    )
+    low = low_part(where, activations, act_got, members, down, near0, far0)
     low_x = swap(low, "tp", 2)
 
     far1 = after(far1, low)
     far, far_sent = gradient_half(where, 1 - y, mine, got, key_value_weight, down, far0, far1)
     far_got = swap(far_sent, "fsdp", 2)
 
-    part, near_got = after((part, near_got), far_sent)
-    keep, give = local_kernel(
+    part = after(part, far_sent)
+    keep, give, give2 = local_kernel(
         base_far_kernel,
-        [((2 * toks, rows), f32), ((2 * toks, rows + 2 * rank), bf16)],
+        [((2 * toks, rows), f32)] + [((toks, rows + 2 * rank), bf16)] * 2,
         where,
         part, activations, act_got, far0, far1, low, low_x, us=0,
     )
-    give_got = swap(give, "tp", 1)
-    held = local_kernel(held_kernel, ((2 * toks, rows), bf16), where, keep, give_got)
-    held_got = both(held, [((a, b, d), (a, 1 - b, d)) for a, b, d in places if b != a // 2])
+    keep, near_got = after((keep, near_got), give)
+    give_got, give_got2 = swap(give, "tp", 1), swap(give2, "tp", 1)
+    here, there = local_kernel(held_kernel, [((toks, rows), bf16)] * 2, where, keep, give_got, give_got2)
+    inward = [((a, b, d), (a, 1 - b, d)) for a, b, d in places if b != a // 2]
+    there_got = both(there, inward)
+    here_got = both(here, inward)
+    held = here
 
     give_got = after(give_got, held)
     lora, lora_far, down_own, up_own, sib, sib_end = local_kernel(
@@ -444,10 +466,10 @@
             ((rank, (width + out_width) // 2), bf16),
         ],
         where,
-        give, give_got, mine, got, activations, act_got, cotangent, cot_got, up, up_sib, us=0,
+        give, give2, give_got, give_got2, mine, got, activations, act_got, cotangent, cot_got, up, up_sib, us=0,
     )
     turn = local_kernel(
-        turn_kernel, ((toks, out_width), bf16), where, held, held_got, lora_far
+        turn_kernel, ((toks, out_width), bf16), where, there, there_got, lora_far
     )
     turned = swap(turn, "fsdp", 2)
     grad_down, up_gradient = local_kernel(
@@ -459,7 +481,7 @@
         gradient_end_kernel, ((toks, width), bf16), where, near, near_got, far, far_got
     )
     key_value_output = local_kernel(
-        output_kernel, ((toks, out_width), bf16), where, held, held_got, lora, turned
+        output_kernel, ((toks, out_width), bf16), where, here, here_got, lora, turned
     )
     return (key_value_output, input_gradient, grad_down, up_gradient)
 

time: 100 us -> 95.3 us (0.953)
  waiting for transfers between devices: 44.6 us -> 38.5 us
  starting transfers between devices: 26 us -> 27.7 us
  local copies, waits for them, and re-layouts: 5.38 us -> 3.99 us
    ppermute x16 -> x17, waiting for transfers between devices: 42.4 us -> 37.5 us  [swap(): lax.ppermute(x, axis, [(i, i ^ bit) for i in range(lax.axis_size(axis))])]
    pallas_call x11 -> x10, Pallas kernels: 15.3 us -> 12.6 us  [local_kernel(): pl.pallas_call(body, out_shape=shapes, in_specs=[pl.BlockSpec(memory_spac...]
    unnamed x42 -> x46, local copies, waits for them, and re-layouts: 5.21 us -> 2.64 us
    pallas_call x0 -> x1, Pallas kernels: none -> 1.75 us  [low_part(): pl.pallas_call(low_kernel, grid=(1,), in_specs=[pl.BlockSpec(memory_space...]
    pallas_call x2, Pallas kernels: 6.34 us -> 7.97 us  [gradient_half(): pl.pallas_call(gradient_kernel, grid_spec=pltpu.PrefetchScalarGridSpec(nu...]
    ppermute x1 -> x2, waiting for transfers between devices: 2.26 us -> 0.97 us  [both(): return lax.ppermute(x, ('fsdp', 'tp'), flat)]
    ppermute x1 -> x2, starting transfers between devices: 1.29 us -> 2.57 us  [both(): return lax.ppermute(x, ('fsdp', 'tp'), flat)]
    concatenate x2, local copies, waits for them, and re-layouts: 0.17 us -> 1.35 us  [gradient_half(): jnp.concatenate([where, side[None]])]
  transfers between devices with their start and end apart: 17 -> 19, of which waited for: 9 -> 7; matrix products, arithmetic and copies ran while one was open for 0% -> 1% of each run, Pallas kernels for 19% -> 23%
where the time goes in v6:
time: 95.3 us; the launch traced here: 94.8 us
  waiting for transfers between devices  38.5 us (40%)
  starting transfers between devices  27.7 us (29%)
  Pallas kernels  23.5 us (25%)
  local copies, waits for them, and re-layouts  3.99 us (4%)
  between operations  1.01 us (1%)
    ppermute x17, waiting for transfers between devices, swap(): lax.ppermute(x, axis, [(i, i ^ bit) for i in range(lax.axis_size(axis))])  37.5 us
    ppermute x17, starting transfers between devices, swap(): lax.ppermute(x, axis, [(i, i ^ bit) for i in range(lax.axis_size(axis))])  25.2 us
    pallas_call x10, Pallas kernels, local_kernel(): pl.pallas_call(body, out_shape=shapes, in_specs=[pl.BlockSpec(memory_spac...  12.6 us
    pallas_call x2, Pallas kernels, gradient_half(): pl.pallas_call(gradient_kernel, grid_spec=pltpu.PrefetchScalarGridSpec(nu...  7.97 us
    unnamed x46, local copies, waits for them, and re-layouts  2.64 us
    ppermute x2, starting transfers between devices, both(): return lax.ppermute(x, ('fsdp', 'tp'), flat)  2.57 us
  transfers between devices with their start and end apart: 19, of which 7 were waited for; matrix products, arithmetic and copies ran while one was open for 1% of the time, Pallas kernels for 23%

profile of v6, /device:TPU:0, one launch (start us, length us, event | category | flops | bytes accessed | tf_op | source)
XLA Modules:
  0.0 94.8 jit_solution(492468438357455641)
XLA Ops:
  0.7 0.1 pad_add_fusion.where
  0.8 1.6 %copy-done = bf16[512,2048]{1,0:T(8,128)(2,1)S(1)} copy-done((bf16[512,2048]{1,0:T(8,128)(2,1)S(1)}, bf16[512,2048]{1,0:T(8,128)(2,1)}, u32[]{:S(2)}) %copy-start) | copy-done | bytes 2097176
  2.4 0.9 copy-done.6
  3.3 0.6 shard_map.96
  3.9 0.0 copy-start.3
  3.9 3.1 %collective-permute-start.6 = (bf16[320,1024]{1,0:T(8,128)(2,1)S(1)}, bf16[320,1024]{1,0:T(8,128)(2,1)}, u32[]{:S(2)}, u32[]{:S(2)}) collective-permute-start(bf16[320,1024]{1,0:T(8,128)(2,1)S(1)} %shard_map.96), channel_id=1, source_target_pairs={{0,4},{4,0},{8,12},{12,8},{1,5},{5,1},{9,13},{13,9},{2,6},{6,2},{1... | collective-permute-start | bytes 1966088 | tf_op jit(solution)/shard_map/ppermute | solution.py:119
  7.0 2.7 %collective-permute-start = (bf16[144,512]{1,0:T(8,128)(2,1)S(1)}, bf16[144,512]{1,0:T(8,128)(2,1)S(1)}, u32[]{:S(2)}, u32[]{:S(2)}) collective-permute-start(bf16[144,512]{1,0:T(8,128)(2,1)S(1)} %fusion.1), channel_id=1, source_target_pairs={{0,8},{4,12},{8,0},{12,4},{1,9},{5,13},{9,1},{13,5},{2,10},{6,14},... | collective-permute-start | bytes 442376 | tf_op jit(solution)/shard_map/ppermute | solution.py:119
  9.7 0.4 collective-permute-start.1
  10.2 0.6 shard_map.94
  10.7 15.6 %collective-permute-done.1.up_sib = bf16[64,512]{1,0:T(8,128)(2,1)S(1)} collective-permute-done((bf16[64,512]{1,0:T(8,128)(2,1)S(1)}, bf16[64,512]{1,0:T(8,128)(2,1)S(1)}, u32[]{:S(2)}, u32[]{:S(2)}) %collective-permute-start.1) | collective-permute-done | bytes 65568 | tf_op jit(solution)/shard_map/ppermute | solution.py:119
  26.3 0.0 collective-permute-done.cot_got
  26.3 2.0 %collective-permute-start.4 = (bf16[256,1024]{1,0:T(8,128)(2,1)S(1)}, bf16[256,1024]{1,0:T(8,128)(2,1)}, u32[]{:S(2)}, u32[]{:S(2)}) collective-permute-start(bf16[256,1024]{1,0:T(8,128)(2,1)S(1)} %shard_map.94), channel_id=1, source_target_pairs={{0,4},{4,0},{8,12},{12,8},{1,5},{5,1},{9,13},{13,9},{2,6},{6,2},{1... | collective-permute-start | bytes 1572872 | tf_op jit(solution)/shard_map/ppermute | solution.py:119
  28.4 0.8 shard_map.93
  29.2 0.0 copy-start.19
  29.2 1.6 %collective-permute-start.3 = (bf16[256,640]{1,0:T(8,128)(2,1)S(1)}, bf16[256,640]{1,0:T(8,128)(2,1)S(1)}, u32[]{:S(2)}, u32[]{:S(2)}) collective-permute-start(bf16[256,640]{1,0:T(8,128)(2,1)S(1)} %get-tuple-element.35.mine), channel_id=1, source_target_pairs={{0,2},{1,3},{2,0},{3,1},{4,6},{5,7},{6,4},{7,5},{8,10},{9,11},{10,... | collective-permute-start | bytes 983048 | tf_op jit(solution)/shard_map/ppermute | solution.py:119
  30.7 0.0 collective-permute-done.6.first.near
  30.8 1.5 %collective-permute-start.7 = (bf16[320,1024]{1,0:T(8,128)(2,1)}, bf16[320,1024]{1,0:T(8,128)(2,1)}, u32[]{:S(2)}, u32[]{:S(2)}) collective-permute-start(bf16[320,1024]{1,0:T(8,128)(2,1)} %collective-permute-done.6.first.near), channel_id=1, source_target_pairs={{0,16},{16,0},{1,17},{17,1},{2,18},{18,2},{3,19},{19,3},{4,20},{20... | collective-permute-start | bytes 1966088 | tf_op jit(solution)/shard_map/ppermute | solution.py:119
  32.3 2.3 %collective-permute-start.2 = (bf16[128,2048]{1,0:T(8,128)(2,1)S(1)}, bf16[128,2048]{1,0:T(8,128)(2,1)S(1)}, u32[]{:S(2)}, u32[]{:S(2)}) collective-permute-start(bf16[128,2048]{1,0:T(8,128)(2,1)S(1)} %copy-done.3), channel_id=1, source_target_pairs={{0,8},{4,12},{8,0},{12,4},{1,9},{5,13},{9,1},{13,5},{2,10},{6,14},... | collective-permute-start | bytes 1572872 | tf_op jit(solution)/shard_map/ppermute | solution.py:119
  34.6 12.8 %collective-permute-done.4.second = bf16[256,1024]{1,0:T(8,128)(2,1)} collective-permute-done((bf16[256,1024]{1,0:T(8,128)(2,1)S(1)}, bf16[256,1024]{1,0:T(8,128)(2,1)}, u32[]{:S(2)}, u32[]{:S(2)}) %collective-permute-start.4) | collective-permute-done | bytes 524320 | tf_op jit(solution)/shard_map/ppermute | solution.py:119
  47.4 2.4 %collective-permute-start.8 = (bf16[256,1024]{1,0:T(8,128)(2,1)}, bf16[256,1024]{1,0:T(8,128)(2,1)}, u32[]{:S(2)}, u32[]{:S(2)}) collective-permute-start(bf16[256,1024]{1,0:T(8,128)(2,1)} %collective-permute-done.4.second), channel_id=1, source_target_pairs={{0,16},{16,0},{1,17},{17,1},{2,18},{18,2},{3,19},{19,3},{4,20},{20... | collective-permute-start | bytes 1572872 | tf_op jit(solution)/shard_map/ppermute | solution.py:119
  49.8 0.0 collective-permute-done.3.got
  49.8 0.6 shard_map.95.mine
  50.4 0.0 copy-start.4
  50.4 0.1 collective-permute-start.5
  50.5 0.7 concatenate.12.where
  51.2 1.1 %collective-permute-done.5.got = bf16[256,640]{1,0:T(8,128)(2,1)} collective-permute-done((bf16[256,640]{1,0:T(8,128)(2,1)S(1)}, bf16[256,640]{1,0:T(8,128)(2,1)}, u32[]{:S(2)}, u32[]{:S(2)}) %collective-permute-start.5) | collective-permute-done | bytes 327712 | tf_op jit(solution)/shard_map/ppermute | solution.py:119
  52.3 3.9 %shard_map.97 = (bf16[128,1024]{1,0:T(8,128)(2,1)}, bf16[128,1024]{1,0:T(8,128)(2,1)}) custom-call(s32[5]{0:T(128)} %concatenate.12.where, bf16[256,640]{1,0:T(8,128)(2,1)} %copy-done.4, bf16[256,640]{1,0:T(8,128)(2,1)} %collective-permute-done.5.got, bf16[512,2048]{1,0:T(8,128)(2,1)} %weight.5, bf16[64,2048]{1,0:T(8,128)(2,1)} %bitcast.9, ...), custom_call_target="tpu_custom_call" | custom-call | bytes 1000 | tf_op jit(solution)/shard_map/pallas_call | solution.py:242
  56.2 0.6 collective-permute-start.10
  56.7 0.0 collective-permute-done.2.act_got
  56.7 2.3 %shard_map.98.part = f32[256,1024]{1,0:T(8,128)S(1)} custom-call(s32[4]{0:T(128)S(1)} %pad_add_fusion.where, bf16[128,2048]{1,0:T(8,128)(2,1)S(1)} %copy-done.3, bf16[128,2048]{1,0:T(8,128)(2,1)S(1)} %collective-permute-done.2.act_got, bf16[512,2048]{1,0:T(8,128)(2,1)S(1)} %copy-done.2, bf16[320,1024]{1,0:T(8,128)(2,1)} %collective-permute-done.6.first.near, ...), custom_call_target="tpu_custom_call" | custom-call | bytes 1000 | tf_op jit(solution)/shard_map/pallas_call | solution.py:141
  59.0 0.0 collective-permute-done.7.far.first
  59.1 1.8 %shard_map.99.low = bf16[256,128]{1,0:T(8,128)(2,1)S(1)} custom-call(s32[4]{0:T(128)S(1)} %pad_add_fusion.where, bf16[128,2048]{1,0:T(8,128)(2,1)S(1)} %copy-done.3, bf16[128,2048]{1,0:T(8,128)(2,1)S(1)} %collective-permute-done.2.act_got, bf16[256,128]{1,0:T(8,128)(2,1)S(1)} %copy-done.20, bf16[64,2048]{1,0:T(8,128)(2,1)S(1)} %bitcast.12, ...), custom_call_target="tpu_custom_call" | custom-call | bytes 1000 | tf_op jit(solution)/shard_map/pallas_call | solution.py:288
  60.8 2.5 %collective-permute-start.9 = (bf16[256,128]{1,0:T(8,128)(2,1)S(1)}, bf16[256,128]{1,0:T(8,128)(2,1)S(1)}, u32[]{:S(2)}, u32[]{:S(2)}) collective-permute-start(bf16[256,128]{1,0:T(8,128)(2,1)S(1)} %shard_map.99.low), channel_id=1, source_target_pairs={{0,2},{1,3},{2,0},{3,1},{4,6},{5,7},{6,4},{7,5},{8,10},{9,11},{10,... | collective-permute-start | bytes 196616 | tf_op jit(solution)/shard_map/ppermute | solution.py:119
  63.3 0.7 concatenate.13.where
  64.0 0.0 collective-permute-done.8.second
  64.0 4.1 %shard_map.100 = (bf16[128,1024]{1,0:T(8,128)(2,1)}, bf16[128,1024]{1,0:T(8,128)(2,1)}) custom-call(s32[5]{0:T(128)} %concatenate.13.where, bf16[256,640]{1,0:T(8,128)(2,1)} %copy-done.4, bf16[256,640]{1,0:T(8,128)(2,1)} %collective-permute-done.5.got, bf16[512,2048]{1,0:T(8,128)(2,1)} %weight.5, bf16[64,2048]{1,0:T(8,128)(2,1)} %bitcast.10, ...), custom_call_target="tpu_custom_call" | custom-call | bytes 1000 | tf_op jit(solution)/shard_map/pallas_call | solution.py:242
  68.1 0.0 copy-start.11
  68.1 0.0 copy-start.16
  68.1 0.0 collective-permute-done.9.low_got
  68.1 1.8 %shard_map.101 = (f32[256,512]{1,0:T(8,128)S(1)}, bf16[128,640]{1,0:T(8,128)(2,1)S(1)}, bf16[128,640]{1,0:T(8,128)(2,1)S(1)}) custom-call(s32[4]{0:T(128)S(1)} %pad_add_fusion.where, f32[256,1024]{1,0:T(8,128)S(1)} %copy-done.9, bf16[128,2048]{1,0:T(8,128)(2,1)S(1)} %copy-done.3, bf16[128,2048]{1,0:T(8,128)(2,1)S(1)} %collective-permute-done.2.act_got, ...), custom_call_target="tpu_custom_call" | custom-call | bytes 1000 | tf_op jit(solution)/shard_map/pallas_call | solution.py:141
  70.0 0.0 copy-start.17
  70.0 0.1 collective-permute-start.12
  70.1 0.5 collective-permute-start.11
  70.6 2.4 %collective-permute-start.16 = (bf16[128,1024]{1,0:T(8,128)(2,1)S(1)}, bf16[128,1024]{1,0:T(8,128)(2,1)S(1)}, u32[]{:S(2)}, u32[]{:S(2)}) collective-permute-start(bf16[128,1024]{1,0:T(8,128)(2,1)S(1)} %copy-done.22), channel_id=1, source_target_pairs={{0,8},{4,12},{8,0},{12,4},{1,9},{5,13},{9,1},{13,5},{2,10},{6,14},... | collective-permute-start | bytes 786440 | tf_op jit(solution)/shard_map/ppermute | solution.py:119
  73.0 0.0 collective-permute-done.10.near_got
  73.0 0.0 collective-permute-done.12.got2.give_got2
  73.0 0.0 collective-permute-done.11.got.give_got
  73.0 0.6 shard_map.102
  73.6 1.3 %collective-permute-start.14 = (bf16[128,512]{1,0:T(8,128)(2,1)S(1)}, bf16[128,512]{1,0:T(8,128)(2,1)S(1)}, u32[]{:S(2)}, u32[]{:S(2)}) collective-permute-start(bf16[128,512]{1,0:T(8,128)(2,1)S(1)} %get-tuple-element.53.held), channel_id=1, source_target_pairs={{2,0},{3,1},{6,4},{7,5},{8,10},{9,11},{12,14},{13,15},{18,16},{19,... | collective-permute-start | bytes 393224 | tf_op jit(solution)/shard_map/ppermute | solution.py:124
  74.9 1.4 %shard_map.103 = (bf16[128,512]{1,0:T(8,128)(2,1)S(1)}, bf16[128,512]{1,0:T(8,128)(2,1)S(1)}, f32[64,2048]{1,0:T(8,128)S(1)}, f32[64,512]{1,0:T(8,128)S(1)}, bf1...) custom-call(s32[4]{0:T(128)S(1)} %pad_add_fusion.where, bf16[128,640]{1,0:T(8,128)(2,1)S(1)} %get-tuple-element.47.give, ...), custom_call_target="tpu_custom_call" | custom-call | bytes 1000 | tf_op jit(solution)/shard_map/pallas_call | solution.py:141
  76.3 1.3 %collective-permute-start.17 = (bf16[64,1280]{1,0:T(8,128)(2,1)S(1)}, bf16[64,1280]{1,0:T(8,128)(2,1)S(1)}, u32[]{:S(2)}, u32[]{:S(2)}) collective-permute-start(bf16[64,1280]{1,0:T(8,128)(2,1)S(1)} %get-tuple-element.60), channel_id=1, source_target_pairs={{0,4},{4,0},{8,12},{12,8},{1,5},{5,1},{9,13},{13,9},{2,6},{6,2},{1... | collective-permute-start | bytes 491528 | tf_op jit(solution)/shard_map/ppermute | solution.py:119
  77.7 0.8 collective-permute-start.18
  78.4 1.3 %collective-permute-start.13 = (bf16[128,512]{1,0:T(8,128)(2,1)S(1)}, bf16[128,512]{1,0:T(8,128)(2,1)S(1)}, u32[]{:S(2)}, u32[]{:S(2)}) collective-permute-start(bf16[128,512]{1,0:T(8,128)(2,1)S(1)} %get-tuple-element.50.held), channel_id=1, source_target_pairs={{2,0},{3,1},{6,4},{7,5},{8,10},{9,11},{12,14},{13,15},{18,16},{19,... | collective-permute-start | bytes 393224 | tf_op jit(solution)/shard_map/ppermute | solution.py:124
  79.7 1.0 %collective-permute-done.14.got = bf16[128,512]{1,0:T(8,128)(2,1)S(1)} collective-permute-done((bf16[128,512]{1,0:T(8,128)(2,1)S(1)}, bf16[128,512]{1,0:T(8,128)(2,1)S(1)}, u32[]{:S(2)}, u32[]{:S(2)}) %collective-permute-start.14) | collective-permute-done | bytes 131104 | tf_op jit(solution)/shard_map/ppermute | solution.py:124
  80.7 0.6 shard_map.104
  81.3 0.9 collective-permute-start.15
  82.2 4.1 %collective-permute-done.16.far_got = bf16[128,1024]{1,0:T(8,128)(2,1)S(1)} collective-permute-done((bf16[128,1024]{1,0:T(8,128)(2,1)S(1)}, bf16[128,1024]{1,0:T(8,128)(2,1)S(1)}, u32[]{:S(2)}, u32[]{:S(2)}) %collective-permute-start.16) | collective-permute-done | bytes 262176 | tf_op jit(solution)/shard_map/ppermute | solution.py:119
  86.3 1.9 %shard_map.106 = bf16[128,2048]{1,0:T(8,128)(2,1)} custom-call(s32[4]{0:T(128)S(1)} %pad_add_fusion.where, bf16[128,1024]{1,0:T(8,128)(2,1)S(1)} %copy-done.17, bf16[128,1024]{1,0:T(8,128)(2,1)} %collective-permute-done.10.near_got, bf16[128,1024]{1,0:T(8,128)(2,1)S(1)} %copy-done.18, bf16[128,1024]{1,0:T(8,128)(2,1)S(1)} %collective-permute-done.16.far_got), custom_call_target="tpu_custom_call" | custom-call | bytes 1000 | tf_op jit(solution)/shard_map/pallas_call | solution.py:141
  88.2 1.6 %collective-permute-done.17.got = bf16[64,1280]{1,0:T(8,128)(2,1)S(1)} collective-permute-done((bf16[64,1280]{1,0:T(8,128)(2,1)S(1)}, bf16[64,1280]{1,0:T(8,128)(2,1)S(1)}, u32[]{:S(2)}, u32[]{:S(2)}) %collective-permute-start.17) | collective-permute-done | bytes 163872 | tf_op jit(solution)/shard_map/ppermute | solution.py:119
  89.8 2.3 %collective-permute-done.18.got_end = bf16[64,1280]{1,0:T(8,128)(2,1)S(1)} collective-permute-done((bf16[64,1280]{1,0:T(8,128)(2,1)S(1)}, bf16[64,1280]{1,0:T(8,128)(2,1)S(1)}, u32[]{:S(2)}, u32[]{:S(2)}) %collective-permute-start.18) | collective-permute-done | bytes 163872 | tf_op jit(solution)/shard_map/ppermute | solution.py:119
  92.1 1.4 %shard_map.107 = (f32[1,64,2048]{2,1,0:T(8,128)}, f32[1,64,512]{2,1,0:T(8,128)}) custom-call(s32[4]{0:T(128)S(1)} %pad_add_fusion.where, f32[64,2048]{1,0:T(8,128)S(1)} %get-tuple-element.58.down_own, f32[64,512]{1,0:T(8,128)S(1)} %get-tuple-element.59.up_own, bf16[64,1280]{1,0:T(8,128)(2,1)S(1)} %collective-permute-done.17.got, ...), custom_call_target="tpu_custom_call" | custom-call | bytes 1000 | tf_op jit(solution)/shard_map/pallas_call | solution.py:141
  93.5 0.0 collective-permute-done.13.got
  93.5 0.0 collective-permute-done.15.turned
  93.5 1.3 %shard_map.105 = bf16[128,512]{1,0:T(8,128)(2,1)} custom-call(s32[4]{0:T(128)S(1)} %pad_add_fusion.where, bf16[128,512]{1,0:T(8,128)(2,1)S(1)} %get-tuple-element.50.held, bf16[128,512]{1,0:T(8,128)(2,1)S(1)} %collective-permute-done.13.got, bf16[128,512]{1,0:T(8,128)(2,1)S(1)} %get-tuple-element.52.lora, bf16[128,512]{1,0:T(8,128)(2,1)S(1)} %collective-permute-done.15.turned), custom_call_target="tpu_custom_call" | custom-call | bytes 1000 | tf_op jit(solution)/shard_map/pallas_call | solution.py:141
  (40 shorter events, 0.1 us)
Async XLA Ops:
  0.6 6.4 %copy-start.21 = (s32[128,1]{0,1:T(1,128)S(1)}, s32[128,1]{0,1:T(1,128)}, u32[]{:S(2)}) copy-start(s32[128,1]{0,1:T(1,128)} %param.8) | copy-start | bytes 1540
  0.6 9.1 %copy-start.14 = (bf16[1,64,512]{2,1,0:T(8,128)(2,1)S(1)}, bf16[1,64,512]{2,1,0:T(8,128)(2,1)}, u32[]{:S(2)}) copy-start(bf16[1,64,512]{2,1,0:T(8,128)(2,1)} %param.10) | copy-start | bytes 196612
  0.8 1.6 %copy-start = (bf16[512,2048]{1,0:T(8,128)(2,1)S(1)}, bf16[512,2048]{1,0:T(8,128)(2,1)}, u32[]{:S(2)}) copy-start(bf16[512,2048]{1,0:T(8,128)(2,1)} %weight.5) | copy-start | bytes 6291460
  2.4 0.9 %copy-start.6 = (bf16[1,64,2048]{2,1,0:T(8,128)(2,1)S(1)}, bf16[1,64,2048]{2,1,0:T(8,128)(2,1)}, u32[]{:S(2)}) copy-start(bf16[1,64,2048]{2,1,0:T(8,128)(2,1)} %param.9) | copy-start | bytes 786436
  3.3 3.7 %copy-start.10 = (bf16[128,512]{1,0:T(8,128)(2,1)S(1)}, bf16[128,512]{1,0:T(8,128)(2,1)}, u32[]{:S(2)}) copy-start(bf16[128,512]{1,0:T(8,128)(2,1)} %cot.3) | copy-start | bytes 393220
  3.3 6.8 %copy-start.1 = (bf16[512,2048]{1,0:T(8,128)(2,1)S(1)}, bf16[512,2048]{1,0:T(8,128)(2,1)}, u32[]{:S(2)}) copy-start(bf16[512,2048]{1,0:T(8,128)(2,1)} %weight.5) | copy-start | bytes 6291460
  3.9 28.4 %copy-start.3 = (bf16[128,2048]{1,0:T(8,128)(2,1)S(1)}, bf16[128,2048]{1,0:T(8,128)(2,1)}, u32[]{:S(2)}) copy-start(bf16[128,2048]{1,0:T(8,128)(2,1)} %act.7) | copy-start | bytes 1572868
  3.9 26.8 %collective-permute-start.6 = (bf16[320,1024]{1,0:T(8,128)(2,1)S(1)}, bf16[320,1024]{1,0:T(8,128)(2,1)}, u32[]{:S(2)}, u32[]{:S(2)}) collective-permute-start(bf16[320,1024]{1,0:T(8,128)(2,1)S(1)} %shard_map.96), channel_id=1, source_target_pairs={{0,4},{4,0},{8,12},{12,8},{1,5},{5,1},{9,13},{13,9},{2,6},{6,2},{1... | collective-permute-start | bytes 1966088 | tf_op jit(solution)/shard_map/ppermute | solution.py:119
  7.0 19.3 %collective-permute-start = (bf16[144,512]{1,0:T(8,128)(2,1)S(1)}, bf16[144,512]{1,0:T(8,128)(2,1)S(1)}, u32[]{:S(2)}, u32[]{:S(2)}) collective-permute-start(bf16[144,512]{1,0:T(8,128)(2,1)S(1)} %fusion.1), channel_id=1, source_target_pairs={{0,8},{4,12},{8,0},{12,4},{1,9},{5,13},{9,1},{13,5},{2,10},{6,14},... | collective-permute-start | bytes 442376 | tf_op jit(solution)/shard_map/ppermute | solution.py:119
  9.7 16.6 %collective-permute-start.1 = (bf16[64,512]{1,0:T(8,128)(2,1)S(1)}, bf16[64,512]{1,0:T(8,128)(2,1)S(1)}, u32[]{:S(2)}, u32[]{:S(2)}) collective-permute-start(bf16[64,512]{1,0:T(8,128)(2,1)S(1)} %bitcast.13), channel_id=1, source_target_pairs={{0,4},{4,0},{8,12},{12,8},{1,5},{5,1},{9,13},{13,9},{2,6},{6,2},{1... | collective-permute-start | bytes 196616 | tf_op jit(solution)/shard_map/ppermute | solution.py:119
  26.3 2.9 %copy-start.15 = (bf16[64,512]{1,0:T(8,128)(2,1)}, bf16[64,512]{1,0:T(8,128)(2,1)S(1)}, u32[]{:S(2)}) copy-start(bf16[64,512]{1,0:T(8,128)(2,1)S(1)} %collective-permute-done.1.up_sib) | copy-start | bytes 196612
  26.3 23.5 %copy-start.12 = (bf16[144,512]{1,0:T(8,128)(2,1)}, bf16[144,512]{1,0:T(8,128)(2,1)S(1)}, u32[]{:S(2)}) copy-start(bf16[144,512]{1,0:T(8,128)(2,1)S(1)} %collective-permute-done.cot_got) | copy-start | bytes 442372
  26.3 21.1 %collective-permute-start.4 = (bf16[256,1024]{1,0:T(8,128)(2,1)S(1)}, bf16[256,1024]{1,0:T(8,128)(2,1)}, u32[]{:S(2)}, u32[]{:S(2)}) collective-permute-start(bf16[256,1024]{1,0:T(8,128)(2,1)S(1)} %shard_map.94), channel_id=1, source_target_pairs={{0,4},{4,0},{8,12},{12,8},{1,5},{5,1},{9,13},{13,9},{2,6},{6,2},{1... | collective-permute-start | bytes 1572872 | tf_op jit(solution)/shard_map/ppermute | solution.py:119
  29.2 21.2 %copy-start.19 = (bf16[256,128]{1,0:T(8,128)(2,1)}, bf16[256,128]{1,0:T(8,128)(2,1)S(1)}, u32[]{:S(2)}) copy-start(bf16[256,128]{1,0:T(8,128)(2,1)S(1)} %get-tuple-element.42.members) | copy-start | bytes 196612
  29.2 20.6 %collective-permute-start.3 = (bf16[256,640]{1,0:T(8,128)(2,1)S(1)}, bf16[256,640]{1,0:T(8,128)(2,1)S(1)}, u32[]{:S(2)}, u32[]{:S(2)}) collective-permute-start(bf16[256,640]{1,0:T(8,128)(2,1)S(1)} %get-tuple-element.35.mine), channel_id=1, source_target_pairs={{0,2},{1,3},{2,0},{3,1},{4,6},{5,7},{6,4},{7,5},{8,10},{9,11},{10,... | collective-permute-start | bytes 983048 | tf_op jit(solution)/shard_map/ppermute | solution.py:119
  30.8 28.3 %collective-permute-start.7 = (bf16[320,1024]{1,0:T(8,128)(2,1)}, bf16[320,1024]{1,0:T(8,128)(2,1)}, u32[]{:S(2)}, u32[]{:S(2)}) collective-permute-start(bf16[320,1024]{1,0:T(8,128)(2,1)} %collective-permute-done.6.first.near), channel_id=1, source_target_pairs={{0,16},{16,0},{1,17},{17,1},{2,18},{18,2},{3,19},{19,3},{4,20},{20... | collective-permute-start | bytes 1966088 | tf_op jit(solution)/shard_map/ppermute | solution.py:119
  32.3 24.5 %collective-permute-start.2 = (bf16[128,2048]{1,0:T(8,128)(2,1)S(1)}, bf16[128,2048]{1,0:T(8,128)(2,1)S(1)}, u32[]{:S(2)}, u32[]{:S(2)}) collective-permute-start(bf16[128,2048]{1,0:T(8,128)(2,1)S(1)} %copy-done.3), channel_id=1, source_target_pairs={{0,8},{4,12},{8,0},{12,4},{1,9},{5,13},{9,1},{13,5},{2,10},{6,14},... | collective-permute-start | bytes 1572872 | tf_op jit(solution)/shard_map/ppermute | solution.py:119
  47.4 16.6 %collective-permute-start.8 = (bf16[256,1024]{1,0:T(8,128)(2,1)}, bf16[256,1024]{1,0:T(8,128)(2,1)}, u32[]{:S(2)}, u32[]{:S(2)}) collective-permute-start(bf16[256,1024]{1,0:T(8,128)(2,1)} %collective-permute-done.4.second), channel_id=1, source_target_pairs={{0,16},{16,0},{1,17},{17,1},{2,18},{18,2},{3,19},{19,3},{4,20},{20... | collective-permute-start | bytes 1572872 | tf_op jit(solution)/shard_map/ppermute | solution.py:119
  50.4 1.8 %copy-start.4 = (bf16[256,640]{1,0:T(8,128)(2,1)}, bf16[256,640]{1,0:T(8,128)(2,1)S(1)}, u32[]{:S(2)}) copy-start(bf16[256,640]{1,0:T(8,128)(2,1)S(1)} %shard_map.95.mine) | copy-start | bytes 983044
  50.4 1.8 %collective-permute-start.5 = (bf16[256,640]{1,0:T(8,128)(2,1)S(1)}, bf16[256,640]{1,0:T(8,128)(2,1)}, u32[]{:S(2)}, u32[]{:S(2)}) collective-permute-start(bf16[256,640]{1,0:T(8,128)(2,1)S(1)} %shard_map.95.mine), channel_id=1, source_target_pairs={{0,1},{1,0},{2,3},{3,2},{4,5},{5,4},{6,7},{7,6},{8,9},{9,8},{10,11... | collective-permute-start | bytes 983048 | tf_op jit(solution)/shard_map/ppermute | solution.py:119
  51.2 5.6 %copy-start.2 = (bf16[512,2048]{1,0:T(8,128)(2,1)S(1)}, bf16[512,2048]{1,0:T(8,128)(2,1)}, u32[]{:S(2)}) copy-start(bf16[512,2048]{1,0:T(8,128)(2,1)} %weight.5) | copy-start | bytes 6291460
  56.2 2.9 %copy-start.7 = (bf16[1,64,2048]{2,1,0:T(8,128)(2,1)S(1)}, bf16[1,64,2048]{2,1,0:T(8,128)(2,1)}, u32[]{:S(2)}) copy-start(bf16[1,64,2048]{2,1,0:T(8,128)(2,1)} %param.9) | copy-start | bytes 786436
  56.2 2.9 %copy-start.20 = (bf16[256,128]{1,0:T(8,128)(2,1)S(1)}, bf16[256,128]{1,0:T(8,128)(2,1)}, u32[]{:S(2)}) copy-start(bf16[256,128]{1,0:T(8,128)(2,1)} %copy-done.19) | copy-start | bytes 196612
  56.2 16.8 %collective-permute-start.10 = (bf16[128,1024]{1,0:T(8,128)(2,1)}, bf16[128,1024]{1,0:T(8,128)(2,1)}, u32[]{:S(2)}, u32[]{:S(2)}) collective-permute-start(bf16[128,1024]{1,0:T(8,128)(2,1)} %get-tuple-element.39), channel_id=1, source_target_pairs={{0,8},{4,12},{8,0},{12,4},{1,9},{5,13},{9,1},{13,5},{2,10},{6,14},... | collective-permute-start | bytes 786440 | tf_op jit(solution)/shard_map/ppermute | solution.py:119
  59.0 1.8 %copy-start.8 = (f32[256,1024]{1,0:T(8,128)}, f32[256,1024]{1,0:T(8,128)S(1)}, u32[]{:S(2)}) copy-start(f32[256,1024]{1,0:T(8,128)S(1)} %shard_map.98.part) | copy-start | bytes 3145732
  60.8 7.3 %collective-permute-start.9 = (bf16[256,128]{1,0:T(8,128)(2,1)S(1)}, bf16[256,128]{1,0:T(8,128)(2,1)S(1)}, u32[]{:S(2)}, u32[]{:S(2)}) collective-permute-start(bf16[256,128]{1,0:T(8,128)(2,1)S(1)} %shard_map.99.low), channel_id=1, source_target_pairs={{0,2},{1,3},{2,0},{3,1},{4,6},{5,7},{6,4},{7,5},{8,10},{9,11},{10,... | collective-permute-start | bytes 196616 | tf_op jit(solution)/shard_map/ppermute | solution.py:119
  64.0 4.1 %copy-start.9 = (f32[256,1024]{1,0:T(8,128)S(1)}, f32[256,1024]{1,0:T(8,128)}, u32[]{:S(2)}) copy-start(f32[256,1024]{1,0:T(8,128)} %copy-done.8) | copy-start | bytes 3145732
  68.1 2.5 %copy-start.22 = (bf16[128,1024]{1,0:T(8,128)(2,1)S(1)}, bf16[128,1024]{1,0:T(8,128)(2,1)}, u32[]{:S(2)}) copy-start(bf16[128,1024]{1,0:T(8,128)(2,1)} %get-tuple-element.44) | copy-start | bytes 786436
  68.1 6.8 %copy-start.5 = (bf16[256,640]{1,0:T(8,128)(2,1)S(1)}, bf16[256,640]{1,0:T(8,128)(2,1)}, u32[]{:S(2)}) copy-start(bf16[256,640]{1,0:T(8,128)(2,1)} %copy-done.4) | copy-start | bytes 983044
  68.1 6.8 %copy-start.11 = (bf16[128,512]{1,0:T(8,128)(2,1)S(1)}, bf16[128,512]{1,0:T(8,128)(2,1)}, u32[]{:S(2)}) copy-start(bf16[128,512]{1,0:T(8,128)(2,1)} %cot.3) | copy-start | bytes 393220
  68.1 6.8 %copy-start.13 = (bf16[144,512]{1,0:T(8,128)(2,1)S(1)}, bf16[144,512]{1,0:T(8,128)(2,1)}, u32[]{:S(2)}) copy-start(bf16[144,512]{1,0:T(8,128)(2,1)} %copy-done.12) | copy-start | bytes 442372
  68.1 6.8 %copy-start.16 = (bf16[64,512]{1,0:T(8,128)(2,1)S(1)}, bf16[64,512]{1,0:T(8,128)(2,1)}, u32[]{:S(2)}) copy-start(bf16[64,512]{1,0:T(8,128)(2,1)} %copy-done.15) | copy-start | bytes 196612
  70.0 16.4 %copy-start.17 = (bf16[128,1024]{1,0:T(8,128)(2,1)S(1)}, bf16[128,1024]{1,0:T(8,128)(2,1)}, u32[]{:S(2)}) copy-start(bf16[128,1024]{1,0:T(8,128)(2,1)} %get-tuple-element.55.near) | copy-start | bytes 786436
  70.0 16.4 %copy-start.18 = (bf16[128,1024]{1,0:T(8,128)(2,1)S(1)}, bf16[128,1024]{1,0:T(8,128)(2,1)}, u32[]{:S(2)}) copy-start(bf16[128,1024]{1,0:T(8,128)(2,1)} %get-tuple-element.57.far) | copy-start | bytes 786436
  70.0 3.0 %collective-permute-start.12 = (bf16[128,640]{1,0:T(8,128)(2,1)S(1)}, bf16[128,640]{1,0:T(8,128)(2,1)S(1)}, u32[]{:S(2)}, u32[]{:S(2)}) collective-permute-start(bf16[128,640]{1,0:T(8,128)(2,1)S(1)} %get-tuple-element.49.give2), channel_id=1, source_target_pairs={{0,1},{1,0},{2,3},{3,2},{4,5},{5,4},{6,7},{7,6},{8,9},{9,8},{10,11... | collective-permute-start | bytes 491528 | tf_op jit(solution)/shard_map/ppermute | solution.py:119
  70.1 2.9 %collective-permute-start.11 = (bf16[128,640]{1,0:T(8,128)(2,1)S(1)}, bf16[128,640]{1,0:T(8,128)(2,1)S(1)}, u32[]{:S(2)}, u32[]{:S(2)}) collective-permute-start(bf16[128,640]{1,0:T(8,128)(2,1)S(1)} %get-tuple-element.47.give), channel_id=1, source_target_pairs={{0,1},{1,0},{2,3},{3,2},{4,5},{5,4},{6,7},{7,6},{8,9},{9,8},{10,11... | collective-permute-start | bytes 491528 | tf_op jit(solution)/shard_map/ppermute | solution.py:119
  70.6 15.8 %collective-permute-start.16 = (bf16[128,1024]{1,0:T(8,128)(2,1)S(1)}, bf16[128,1024]{1,0:T(8,128)(2,1)S(1)}, u32[]{:S(2)}, u32[]{:S(2)}) collective-permute-start(bf16[128,1024]{1,0:T(8,128)(2,1)S(1)} %copy-done.22), channel_id=1, source_target_pairs={{0,8},{4,12},{8,0},{12,4},{1,9},{5,13},{9,1},{13,5},{2,10},{6,14},... | collective-permute-start | bytes 786440 | tf_op jit(solution)/shard_map/ppermute | solution.py:119
  73.6 7.1 %collective-permute-start.14 = (bf16[128,512]{1,0:T(8,128)(2,1)S(1)}, bf16[128,512]{1,0:T(8,128)(2,1)S(1)}, u32[]{:S(2)}, u32[]{:S(2)}) collective-permute-start(bf16[128,512]{1,0:T(8,128)(2,1)S(1)} %get-tuple-element.53.held), channel_id=1, source_target_pairs={{2,0},{3,1},{6,4},{7,5},{8,10},{9,11},{12,14},{13,15},{18,16},{19,... | collective-permute-start | bytes 393224 | tf_op jit(solution)/shard_map/ppermute | solution.py:124
  76.3 13.5 %collective-permute-start.17 = (bf16[64,1280]{1,0:T(8,128)(2,1)S(1)}, bf16[64,1280]{1,0:T(8,128)(2,1)S(1)}, u32[]{:S(2)}, u32[]{:S(2)}) collective-permute-start(bf16[64,1280]{1,0:T(8,128)(2,1)S(1)} %get-tuple-element.60), channel_id=1, source_target_pairs={{0,4},{4,0},{8,12},{12,8},{1,5},{5,1},{9,13},{13,9},{2,6},{6,2},{1... | collective-permute-start | bytes 491528 | tf_op jit(solution)/shard_map/ppermute | solution.py:119
  77.7 14.4 %collective-permute-start.18 = (bf16[64,1280]{1,0:T(8,128)(2,1)S(1)}, bf16[64,1280]{1,0:T(8,128)(2,1)S(1)}, u32[]{:S(2)}, u32[]{:S(2)}) collective-permute-start(bf16[64,1280]{1,0:T(8,128)(2,1)S(1)} %get-tuple-element.61), channel_id=1, source_target_pairs={{0,4},{4,0},{8,12},{12,8},{1,5},{5,1},{9,13},{13,9},{2,6},{6,2},{1... | collective-permute-start | bytes 491528 | tf_op jit(solution)/shard_map/ppermute | solution.py:119
  78.4 15.1 %collective-permute-start.13 = (bf16[128,512]{1,0:T(8,128)(2,1)S(1)}, bf16[128,512]{1,0:T(8,128)(2,1)S(1)}, u32[]{:S(2)}, u32[]{:S(2)}) collective-permute-start(bf16[128,512]{1,0:T(8,128)(2,1)S(1)} %get-tuple-element.50.held), channel_id=1, source_target_pairs={{2,0},{3,1},{6,4},{7,5},{8,10},{9,11},{12,14},{13,15},{18,16},{19,... | collective-permute-start | bytes 393224 | tf_op jit(solution)/shard_map/ppermute | solution.py:124
  81.3 12.3 %collective-permute-start.15 = (bf16[128,512]{1,0:T(8,128)(2,1)S(1)}, bf16[128,512]{1,0:T(8,128)(2,1)S(1)}, u32[]{:S(2)}, u32[]{:S(2)}) collective-permute-start(bf16[128,512]{1,0:T(8,128)(2,1)S(1)} %shard_map.104), channel_id=1, source_target_pairs={{0,8},{4,12},{8,0},{12,4},{1,9},{5,13},{9,1},{13,5},{2,10},{6,14},... | collective-permute-start | bytes 393224 | tf_op jit(solution)/shard_map/ppermute | solution.py:119

commit v7 on v6

--- a/solution.py
+++ b/solution.py
@@ -131,11 +131,10 @@
 Y, Z, IN_PAIR, ON_OWN = range(4)
 
 
-def cost(us):
-    return pl.CostEstimate(flops=us * 1_000_000_000, bytes_accessed=1000 + us * 3_000_000, transcendentals=0)
-
-
-def local_kernel(body, outs, where, *args, us=0):
+SMALL = pl.CostEstimate(flops=0, bytes_accessed=1000, transcendentals=0)
+
+
+def local_kernel(body, outs, where, *args):
     single = not isinstance(outs, list)
     shapes = [jax.ShapeDtypeStruct(s, d) for s, d in ([outs] if single else outs)]
     got = pl.pallas_call(
@@ -145,7 +144,7 @@
         + [pl.BlockSpec(memory_space=pltpu.VMEM)] * len(args),
         out_specs=[pl.BlockSpec(memory_space=pltpu.VMEM)] * len(shapes),
         compiler_params=pltpu.CompilerParams(vmem_limit_bytes=12 * 1024 * 1024),
-        cost_estimate=cost(us),
+        cost_estimate=SMALL,
     )(where, *args)
     return got[0] if single else got
 
@@ -171,7 +170,7 @@
         ),
         out_shape=jax.ShapeDtypeStruct((total, wide), bf16),
         compiler_params=pltpu.CompilerParams(vmem_limit_bytes=12 * 1024 * 1024),
-        cost_estimate=cost(0),
+        cost_estimate=SMALL,
     )(where, *arrays)
 
 
@@ -259,7 +258,7 @@
             jax.ShapeDtypeStruct((toks, steps * tile), bf16),
         ],
         compiler_params=pltpu.CompilerParams(vmem_limit_bytes=56 * 1024 * 1024),
-        cost_estimate=cost(0),
+        cost_estimate=SMALL,
     )(jnp.concatenate([where, side[None]]), mine, got, weight, down, first, second)
 
 
@@ -294,7 +293,7 @@
         out_specs=whole(members),
         out_shape=jax.ShapeDtypeStruct(members.shape, bf16),
         compiler_params=pltpu.CompilerParams(vmem_limit_bytes=12 * 1024 * 1024),
-        cost_estimate=cost(0),
+        cost_estimate=SMALL,
     )(where, act, act_got, members, down, near, far)
 
 
@@ -412,7 +411,7 @@
         back_kernel,
         [((2 * toks, out_width + 2 * rank), bf16), ((2 * toks, 2 * rank), bf16)],
         where,
-        cotangent, cot_got, idx, up, up_sib, us=0,
+        cotangent, cot_got, idx, up, up_sib,
     )
     mine_x = swap(mine, "tp", 2)
     near0 = after(near0, mine)
@@ -428,7 +427,7 @@
     act_got = after(act_got, near_sent)
     part = local_kernel(
         base_near_kernel, ((2 * toks, 2 * rows), f32), where,
-        activations, act_got, key_value_weight, near0, near1, us=0,
+        activations, act_got, key_value_weight, near0, near1,
     )
 
     far0 = after(far0, part)
@@ -444,7 +443,7 @@
         base_far_kernel,
         [((2 * toks, rows), f32)] + [((toks, rows + 2 * rank), bf16)] * 2,
         where,
-        part, activations, act_got, far0, far1, low, low_x, us=0,
+        part, activations, act_got, far0, far1, low, low_x,
     )
     keep, near_got = after((keep, near_got), give)
     give_got, give_got2 = swap(give, "tp", 1), swap(give2, "tp", 1)
@@ -466,23 +465,25 @@
             ((rank, (width + out_width) // 2), bf16),
         ],
         where,
-        give, give2, give_got, give_got2, mine, got, activations, act_got, cotangent, cot_got, up, up_sib, us=0,
+        give, give2, give_got, give_got2, mine, got, activations, act_got, cotangent, cot_got, up, up_sib,
     )
     turn = local_kernel(
         turn_kernel, ((toks, out_width), bf16), where, there, there_got, lora_far
     )
     turned = swap(turn, "fsdp", 2)
+    sib_got, sib_end_got = swap(sib, "fsdp", 1), swap(sib_end, "fsdp", 1)
+    input_gradient = local_kernel(
+        gradient_end_kernel, ((toks, width), bf16), where, near, near_got, far, far_got
+    )
+    key_value_output = local_kernel(
+        output_kernel, ((toks, out_width), bf16), where, here, here_got, lora, turned
+    )
+    sib_got, sib_end_got = after((sib_got, sib_end_got), key_value_output)
     grad_down, up_gradient = local_kernel(
         adapter_end_kernel, [((1, rank, width), f32), ((1, rank, out_width), f32)], where,
-        down_own, up_own, swap(sib, "fsdp", 1), swap(sib_end, "fsdp", 1),
-    )
-
-    input_gradient = local_kernel(
-        gradient_end_kernel, ((toks, width), bf16), where, near, near_got, far, far_got
-    )
-    key_value_output = local_kernel(
-        output_kernel, ((toks, out_width), bf16), where, here, here_got, lora, turned
-    )
+        down_own, up_own, sib_got, sib_end_got,
+    )
+
     return (key_value_output, input_gradient, grad_down, up_gradient)
 
 

time: 95.3 us -> 94 us (0.986)
  waiting for transfers between devices: 38.5 us -> 37.2 us
    ppermute x17, waiting for transfers between devices: 37.5 us -> 36.2 us  [swap(): lax.ppermute(x, axis, [(i, i ^ bit) for i in range(lax.axis_size(axis))])]
where the time goes in v7:
time: 94 us; the launch traced here: 93.5 us
  waiting for transfers between devices  37.2 us (40%)
  starting transfers between devices  27.7 us (29%)
  Pallas kernels  23.5 us (25%)
  local copies, waits for them, and re-layouts  3.99 us (4%)
  between operations  1.01 us (1%)
    ppermute x17, waiting for transfers between devices, swap(): lax.ppermute(x, axis, [(i, i ^ bit) for i in range(lax.axis_size(axis))])  36.2 us
    ppermute x17, starting transfers between devices, swap(): lax.ppermute(x, axis, [(i, i ^ bit) for i in range(lax.axis_size(axis))])  25.2 us
    pallas_call x10, Pallas kernels, local_kernel(): pl.pallas_call(body, out_shape=shapes, in_specs=[pl.BlockSpec(memory_spac...  12.6 us
    pallas_call x2, Pallas kernels, gradient_half(): pl.pallas_call(gradient_kernel, grid_spec=pltpu.PrefetchScalarGridSpec(nu...  7.97 us
    unnamed x46, local copies, waits for them, and re-layouts  2.64 us
    ppermute x2, starting transfers between devices, both(): return lax.ppermute(x, ('fsdp', 'tp'), flat)  2.57 us
  transfers between devices with their start and end apart: 19, of which 7 were waited for; matrix products, arithmetic and copies ran while one was open for 1% of the time, Pallas kernels for 23%

profile of v7, /device:TPU:0, one launch (start us, length us, event | category | flops | bytes accessed | tf_op | source)
XLA Modules:
  0.0 93.5 jit_solution(12290947557143467399)
XLA Ops:
  0.7 0.1 pad_add_fusion.where
  0.8 1.6 %copy-done = bf16[512,2048]{1,0:T(8,128)(2,1)S(1)} copy-done((bf16[512,2048]{1,0:T(8,128)(2,1)S(1)}, bf16[512,2048]{1,0:T(8,128)(2,1)}, u32[]{:S(2)}) %copy-start) | copy-done | bytes 2097176
  2.4 0.9 %copy-done.6 = bf16[1,64,2048]{2,1,0:T(8,128)(2,1)S(1)} copy-done((bf16[1,64,2048]{2,1,0:T(8,128)(2,1)S(1)}, bf16[1,64,2048]{2,1,0:T(8,128)(2,1)}, u32[]{:S(2)}) %copy-start.6) | copy-done | bytes 262168
  3.3 0.6 shard_map.96
  3.9 0.0 copy-start.3
  3.9 3.1 %collective-permute-start.6 = (bf16[320,1024]{1,0:T(8,128)(2,1)S(1)}, bf16[320,1024]{1,0:T(8,128)(2,1)}, u32[]{:S(2)}, u32[]{:S(2)}) collective-permute-start(bf16[320,1024]{1,0:T(8,128)(2,1)S(1)} %shard_map.96), channel_id=1, source_target_pairs={{0,4},{4,0},{8,12},{12,8},{1,5},{5,1},{9,13},{13,9},{2,6},{6,2},{1... | collective-permute-start | bytes 1966088 | tf_op jit(solution)/shard_map/ppermute | solution.py:119
  7.0 2.7 %collective-permute-start = (bf16[144,512]{1,0:T(8,128)(2,1)S(1)}, bf16[144,512]{1,0:T(8,128)(2,1)S(1)}, u32[]{:S(2)}, u32[]{:S(2)}) collective-permute-start(bf16[144,512]{1,0:T(8,128)(2,1)S(1)} %fusion.1), channel_id=1, source_target_pairs={{0,8},{4,12},{8,0},{12,4},{1,9},{5,13},{9,1},{13,5},{2,10},{6,14},... | collective-permute-start | bytes 442376 | tf_op jit(solution)/shard_map/ppermute | solution.py:119
  9.7 0.4 collective-permute-start.1
  10.2 0.6 shard_map.94
  10.7 15.6 %collective-permute-done.1.up_sib = bf16[64,512]{1,0:T(8,128)(2,1)S(1)} collective-permute-done((bf16[64,512]{1,0:T(8,128)(2,1)S(1)}, bf16[64,512]{1,0:T(8,128)(2,1)S(1)}, u32[]{:S(2)}, u32[]{:S(2)}) %collective-permute-start.1) | collective-permute-done | bytes 65568 | tf_op jit(solution)/shard_map/ppermute | solution.py:119
  26.3 0.0 collective-permute-done.cot_got
  26.3 2.0 %collective-permute-start.4 = (bf16[256,1024]{1,0:T(8,128)(2,1)S(1)}, bf16[256,1024]{1,0:T(8,128)(2,1)}, u32[]{:S(2)}, u32[]{:S(2)}) collective-permute-start(bf16[256,1024]{1,0:T(8,128)(2,1)S(1)} %shard_map.94), channel_id=1, source_target_pairs={{0,4},{4,0},{8,12},{12,8},{1,5},{5,1},{9,13},{13,9},{2,6},{6,2},{1... | collective-permute-start | bytes 1572872 | tf_op jit(solution)/shard_map/ppermute | solution.py:119
  28.4 0.8 shard_map.93
  29.2 0.0 copy-start.19
  29.2 1.6 %collective-permute-start.3 = (bf16[256,640]{1,0:T(8,128)(2,1)S(1)}, bf16[256,640]{1,0:T(8,128)(2,1)S(1)}, u32[]{:S(2)}, u32[]{:S(2)}) collective-permute-start(bf16[256,640]{1,0:T(8,128)(2,1)S(1)} %get-tuple-element.37.mine), channel_id=1, source_target_pairs={{0,2},{1,3},{2,0},{3,1},{4,6},{5,7},{6,4},{7,5},{8,10},{9,11},{10,... | collective-permute-start | bytes 983048 | tf_op jit(solution)/shard_map/ppermute | solution.py:119
  30.7 0.0 collective-permute-done.6.first.near
  30.8 1.5 %collective-permute-start.7 = (bf16[320,1024]{1,0:T(8,128)(2,1)}, bf16[320,1024]{1,0:T(8,128)(2,1)}, u32[]{:S(2)}, u32[]{:S(2)}) collective-permute-start(bf16[320,1024]{1,0:T(8,128)(2,1)} %collective-permute-done.6.first.near), channel_id=1, source_target_pairs={{0,16},{16,0},{1,17},{17,1},{2,18},{18,2},{3,19},{19,3},{4,20},{20... | collective-permute-start | bytes 1966088 | tf_op jit(solution)/shard_map/ppermute | solution.py:119
  32.3 2.3 %collective-permute-start.2 = (bf16[128,2048]{1,0:T(8,128)(2,1)S(1)}, bf16[128,2048]{1,0:T(8,128)(2,1)S(1)}, u32[]{:S(2)}, u32[]{:S(2)}) collective-permute-start(bf16[128,2048]{1,0:T(8,128)(2,1)S(1)} %copy-done.3), channel_id=1, source_target_pairs={{0,8},{4,12},{8,0},{12,4},{1,9},{5,13},{9,1},{13,5},{2,10},{6,14},... | collective-permute-start | bytes 1572872 | tf_op jit(solution)/shard_map/ppermute | solution.py:119
  34.6 12.8 %collective-permute-done.4.second = bf16[256,1024]{1,0:T(8,128)(2,1)} collective-permute-done((bf16[256,1024]{1,0:T(8,128)(2,1)S(1)}, bf16[256,1024]{1,0:T(8,128)(2,1)}, u32[]{:S(2)}, u32[]{:S(2)}) %collective-permute-start.4) | collective-permute-done | bytes 524320 | tf_op jit(solution)/shard_map/ppermute | solution.py:119
  47.4 2.4 %collective-permute-start.8 = (bf16[256,1024]{1,0:T(8,128)(2,1)}, bf16[256,1024]{1,0:T(8,128)(2,1)}, u32[]{:S(2)}, u32[]{:S(2)}) collective-permute-start(bf16[256,1024]{1,0:T(8,128)(2,1)} %collective-permute-done.4.second), channel_id=1, source_target_pairs={{0,16},{16,0},{1,17},{17,1},{2,18},{18,2},{3,19},{19,3},{4,20},{20... | collective-permute-start | bytes 1572872 | tf_op jit(solution)/shard_map/ppermute | solution.py:119
  49.8 0.0 collective-permute-done.3.got
  49.8 0.6 shard_map.95.mine
  50.4 0.0 copy-start.4
  50.4 0.1 collective-permute-start.5
  50.5 0.7 concatenate.12.where
  51.2 1.1 %collective-permute-done.5.got = bf16[256,640]{1,0:T(8,128)(2,1)} collective-permute-done((bf16[256,640]{1,0:T(8,128)(2,1)S(1)}, bf16[256,640]{1,0:T(8,128)(2,1)}, u32[]{:S(2)}, u32[]{:S(2)}) %collective-permute-start.5) | collective-permute-done | bytes 327712 | tf_op jit(solution)/shard_map/ppermute | solution.py:119
  52.3 3.9 %shard_map.97 = (bf16[128,1024]{1,0:T(8,128)(2,1)}, bf16[128,1024]{1,0:T(8,128)(2,1)}) custom-call(s32[5]{0:T(128)} %concatenate.12.where, bf16[256,640]{1,0:T(8,128)(2,1)} %copy-done.4, bf16[256,640]{1,0:T(8,128)(2,1)} %collective-permute-done.5.got, bf16[512,2048]{1,0:T(8,128)(2,1)} %weight.5, bf16[64,2048]{1,0:T(8,128)(2,1)} %bitcast.9, ...), custom_call_target="tpu_custom_call" | custom-call | bytes 1000 | tf_op jit(solution)/shard_map/pallas_call | solution.py:241
  56.2 0.6 collective-permute-start.10
  56.7 0.0 collective-permute-done.2.act_got
  56.7 2.3 %shard_map.98.part = f32[256,1024]{1,0:T(8,128)S(1)} custom-call(s32[4]{0:T(128)S(1)} %pad_add_fusion.where, bf16[128,2048]{1,0:T(8,128)(2,1)S(1)} %copy-done.3, bf16[128,2048]{1,0:T(8,128)(2,1)S(1)} %collective-permute-done.2.act_got, bf16[512,2048]{1,0:T(8,128)(2,1)S(1)} %copy-done.2, bf16[320,1024]{1,0:T(8,128)(2,1)} %collective-permute-done.6.first.near, ...), custom_call_target="tpu_custom_call" | custom-call | bytes 1000 | tf_op jit(solution)/shard_map/pallas_call | solution.py:140
  59.0 0.0 collective-permute-done.7.far.first
  59.1 1.8 %shard_map.99.low = bf16[256,128]{1,0:T(8,128)(2,1)S(1)} custom-call(s32[4]{0:T(128)S(1)} %pad_add_fusion.where, bf16[128,2048]{1,0:T(8,128)(2,1)S(1)} %copy-done.3, bf16[128,2048]{1,0:T(8,128)(2,1)S(1)} %collective-permute-done.2.act_got, bf16[256,128]{1,0:T(8,128)(2,1)S(1)} %copy-done.20, bf16[64,2048]{1,0:T(8,128)(2,1)S(1)} %bitcast.12, ...), custom_call_target="tpu_custom_call" | custom-call | bytes 1000 | tf_op jit(solution)/shard_map/pallas_call | solution.py:287
  60.8 2.5 %collective-permute-start.9 = (bf16[256,128]{1,0:T(8,128)(2,1)S(1)}, bf16[256,128]{1,0:T(8,128)(2,1)S(1)}, u32[]{:S(2)}, u32[]{:S(2)}) collective-permute-start(bf16[256,128]{1,0:T(8,128)(2,1)S(1)} %shard_map.99.low), channel_id=1, source_target_pairs={{0,2},{1,3},{2,0},{3,1},{4,6},{5,7},{6,4},{7,5},{8,10},{9,11},{10,... | collective-permute-start | bytes 196616 | tf_op jit(solution)/shard_map/ppermute | solution.py:119
  63.3 0.7 concatenate.13.where
  64.0 0.0 collective-permute-done.8.second
  64.0 4.1 %shard_map.100 = (bf16[128,1024]{1,0:T(8,128)(2,1)}, bf16[128,1024]{1,0:T(8,128)(2,1)}) custom-call(s32[5]{0:T(128)} %concatenate.13.where, bf16[256,640]{1,0:T(8,128)(2,1)} %copy-done.4, bf16[256,640]{1,0:T(8,128)(2,1)} %collective-permute-done.5.got, bf16[512,2048]{1,0:T(8,128)(2,1)} %weight.5, bf16[64,2048]{1,0:T(8,128)(2,1)} %bitcast.10, ...), custom_call_target="tpu_custom_call" | custom-call | bytes 1000 | tf_op jit(solution)/shard_map/pallas_call | solution.py:241
  68.1 0.0 copy-start.11
  68.1 0.0 copy-start.16
  68.1 0.0 collective-permute-done.9.low_got
  68.1 1.8 %shard_map.101 = (f32[256,512]{1,0:T(8,128)S(1)}, bf16[128,640]{1,0:T(8,128)(2,1)S(1)}, bf16[128,640]{1,0:T(8,128)(2,1)S(1)}) custom-call(s32[4]{0:T(128)S(1)} %pad_add_fusion.where, f32[256,1024]{1,0:T(8,128)S(1)} %copy-done.9, bf16[128,2048]{1,0:T(8,128)(2,1)S(1)} %copy-done.3, bf16[128,2048]{1,0:T(8,128)(2,1)S(1)} %collective-permute-done.2.act_got, ...), custom_call_target="tpu_custom_call" | custom-call | bytes 1000 | tf_op jit(solution)/shard_map/pallas_call | solution.py:140
  70.0 0.0 copy-start.17
  70.0 0.1 collective-permute-start.12
  70.1 0.5 collective-permute-start.11
  70.6 2.4 %collective-permute-start.16 = (bf16[128,1024]{1,0:T(8,128)(2,1)S(1)}, bf16[128,1024]{1,0:T(8,128)(2,1)S(1)}, u32[]{:S(2)}, u32[]{:S(2)}) collective-permute-start(bf16[128,1024]{1,0:T(8,128)(2,1)S(1)} %copy-done.22), channel_id=1, source_target_pairs={{0,8},{4,12},{8,0},{12,4},{1,9},{5,13},{9,1},{13,5},{2,10},{6,14},... | collective-permute-start | bytes 786440 | tf_op jit(solution)/shard_map/ppermute | solution.py:119
  73.0 0.0 collective-permute-done.10.near_got
  73.0 0.0 collective-permute-done.12.got2.give_got2
  73.0 0.0 collective-permute-done.11.got.give_got
  73.0 0.6 shard_map.102
  73.6 1.3 %collective-permute-start.14 = (bf16[128,512]{1,0:T(8,128)(2,1)S(1)}, bf16[128,512]{1,0:T(8,128)(2,1)S(1)}, u32[]{:S(2)}, u32[]{:S(2)}) collective-permute-start(bf16[128,512]{1,0:T(8,128)(2,1)S(1)} %get-tuple-element.55.held), channel_id=1, source_target_pairs={{2,0},{3,1},{6,4},{7,5},{8,10},{9,11},{12,14},{13,15},{18,16},{19,... | collective-permute-start | bytes 393224 | tf_op jit(solution)/shard_map/ppermute | solution.py:124
  74.9 1.4 %shard_map.103 = (bf16[128,512]{1,0:T(8,128)(2,1)S(1)}, bf16[128,512]{1,0:T(8,128)(2,1)S(1)}, f32[64,2048]{1,0:T(8,128)S(1)}, f32[64,512]{1,0:T(8,128)S(1)}, bf1...) custom-call(s32[4]{0:T(128)S(1)} %pad_add_fusion.where, bf16[128,640]{1,0:T(8,128)(2,1)S(1)} %get-tuple-element.49.give, ...), custom_call_target="tpu_custom_call" | custom-call | bytes 1000 | tf_op jit(solution)/shard_map/pallas_call | solution.py:140
  76.3 1.3 %collective-permute-start.17 = (bf16[64,1280]{1,0:T(8,128)(2,1)S(1)}, bf16[64,1280]{1,0:T(8,128)(2,1)S(1)}, u32[]{:S(2)}, u32[]{:S(2)}) collective-permute-start(bf16[64,1280]{1,0:T(8,128)(2,1)S(1)} %get-tuple-element.62), channel_id=1, source_target_pairs={{0,4},{4,0},{8,12},{12,8},{1,5},{5,1},{9,13},{13,9},{2,6},{6,2},{1... | collective-permute-start | bytes 491528 | tf_op jit(solution)/shard_map/ppermute | solution.py:119
  77.7 0.8 collective-permute-start.18
  78.4 1.3 %collective-permute-start.13 = (bf16[128,512]{1,0:T(8,128)(2,1)S(1)}, bf16[128,512]{1,0:T(8,128)(2,1)S(1)}, u32[]{:S(2)}, u32[]{:S(2)}) collective-permute-start(bf16[128,512]{1,0:T(8,128)(2,1)S(1)} %get-tuple-element.52.held), channel_id=1, source_target_pairs={{2,0},{3,1},{6,4},{7,5},{8,10},{9,11},{12,14},{13,15},{18,16},{19,... | collective-permute-start | bytes 393224 | tf_op jit(solution)/shard_map/ppermute | solution.py:124
  79.7 1.0 %collective-permute-done.14.got = bf16[128,512]{1,0:T(8,128)(2,1)S(1)} collective-permute-done((bf16[128,512]{1,0:T(8,128)(2,1)S(1)}, bf16[128,512]{1,0:T(8,128)(2,1)S(1)}, u32[]{:S(2)}, u32[]{:S(2)}) %collective-permute-start.14) | collective-permute-done | bytes 131104 | tf_op jit(solution)/shard_map/ppermute | solution.py:124
  80.7 0.6 shard_map.104
  81.3 0.9 collective-permute-start.15
  82.2 4.1 %collective-permute-done.16.far_got = bf16[128,1024]{1,0:T(8,128)(2,1)S(1)} collective-permute-done((bf16[128,1024]{1,0:T(8,128)(2,1)S(1)}, bf16[128,1024]{1,0:T(8,128)(2,1)S(1)}, u32[]{:S(2)}, u32[]{:S(2)}) %collective-permute-start.16) | collective-permute-done | bytes 262176 | tf_op jit(solution)/shard_map/ppermute | solution.py:119
  86.3 1.9 %shard_map.106 = bf16[128,2048]{1,0:T(8,128)(2,1)} custom-call(s32[4]{0:T(128)S(1)} %pad_add_fusion.where, bf16[128,1024]{1,0:T(8,128)(2,1)S(1)} %copy-done.17, bf16[128,1024]{1,0:T(8,128)(2,1)} %collective-permute-done.10.near_got, bf16[128,1024]{1,0:T(8,128)(2,1)S(1)} %copy-done.18, bf16[128,1024]{1,0:T(8,128)(2,1)S(1)} %collective-permute-done.16.far_got), custom_call_target="tpu_custom_call" | custom-call | bytes 1000 | tf_op jit(solution)/shard_map/pallas_call | solution.py:140
  88.2 0.0 collective-permute-done.13.got
  88.2 0.5 collective-permute-done.15.turned
  88.7 1.3 %shard_map.105 = bf16[128,512]{1,0:T(8,128)(2,1)} custom-call(s32[4]{0:T(128)S(1)} %pad_add_fusion.where, bf16[128,512]{1,0:T(8,128)(2,1)S(1)} %get-tuple-element.52.held, bf16[128,512]{1,0:T(8,128)(2,1)S(1)} %collective-permute-done.13.got, bf16[128,512]{1,0:T(8,128)(2,1)S(1)} %get-tuple-element.54.lora, bf16[128,512]{1,0:T(8,128)(2,1)S(1)} %collective-permute-done.15.turned), custom_call_target="tpu_custom_call" | custom-call | bytes 1000 | tf_op jit(solution)/shard_map/pallas_call | solution.py:140
  90.0 0.0 collective-permute-done.17.got
  90.0 2.1 %collective-permute-done.18.got_end = bf16[64,1280]{1,0:T(8,128)(2,1)S(1)} collective-permute-done((bf16[64,1280]{1,0:T(8,128)(2,1)S(1)}, bf16[64,1280]{1,0:T(8,128)(2,1)S(1)}, u32[]{:S(2)}, u32[]{:S(2)}) %collective-permute-start.18) | collective-permute-done | bytes 163872 | tf_op jit(solution)/shard_map/ppermute | solution.py:119
  92.1 1.4 %shard_map.107 = (f32[1,64,2048]{2,1,0:T(8,128)}, f32[1,64,512]{2,1,0:T(8,128)}) custom-call(s32[4]{0:T(128)S(1)} %pad_add_fusion.where, f32[64,2048]{1,0:T(8,128)S(1)} %get-tuple-element.60.down_own, f32[64,512]{1,0:T(8,128)S(1)} %get-tuple-element.61.up_own, bf16[64,1280]{1,0:T(8,128)(2,1)S(1)} %collective-permute-done.17.got, ...), custom_call_target="tpu_custom_call" | custom-call | bytes 1000 | tf_op jit(solution)/shard_map/pallas_call | solution.py:140
  (40 shorter events, 0.1 us)
Async XLA Ops:
  0.6 6.4 %copy-start.21 = (s32[128,1]{0,1:T(1,128)S(1)}, s32[128,1]{0,1:T(1,128)}, u32[]{:S(2)}) copy-start(s32[128,1]{0,1:T(1,128)} %param.8) | copy-start | bytes 1540
  0.6 9.1 %copy-start.14 = (bf16[1,64,512]{2,1,0:T(8,128)(2,1)S(1)}, bf16[1,64,512]{2,1,0:T(8,128)(2,1)}, u32[]{:S(2)}) copy-start(bf16[1,64,512]{2,1,0:T(8,128)(2,1)} %param.10) | copy-start | bytes 196612
  0.8 1.6 %copy-start = (bf16[512,2048]{1,0:T(8,128)(2,1)S(1)}, bf16[512,2048]{1,0:T(8,128)(2,1)}, u32[]{:S(2)}) copy-start(bf16[512,2048]{1,0:T(8,128)(2,1)} %weight.5) | copy-start | bytes 6291460
  2.4 0.9 %copy-start.6 = (bf16[1,64,2048]{2,1,0:T(8,128)(2,1)S(1)}, bf16[1,64,2048]{2,1,0:T(8,128)(2,1)}, u32[]{:S(2)}) copy-start(bf16[1,64,2048]{2,1,0:T(8,128)(2,1)} %param.9) | copy-start | bytes 786436
  3.3 3.7 %copy-start.10 = (bf16[128,512]{1,0:T(8,128)(2,1)S(1)}, bf16[128,512]{1,0:T(8,128)(2,1)}, u32[]{:S(2)}) copy-start(bf16[128,512]{1,0:T(8,128)(2,1)} %cot.3) | copy-start | bytes 393220
  3.3 6.8 %copy-start.1 = (bf16[512,2048]{1,0:T(8,128)(2,1)S(1)}, bf16[512,2048]{1,0:T(8,128)(2,1)}, u32[]{:S(2)}) copy-start(bf16[512,2048]{1,0:T(8,128)(2,1)} %weight.5) | copy-start | bytes 6291460
  3.9 28.4 %copy-start.3 = (bf16[128,2048]{1,0:T(8,128)(2,1)S(1)}, bf16[128,2048]{1,0:T(8,128)(2,1)}, u32[]{:S(2)}) copy-start(bf16[128,2048]{1,0:T(8,128)(2,1)} %act.7) | copy-start | bytes 1572868
  3.9 26.8 %collective-permute-start.6 = (bf16[320,1024]{1,0:T(8,128)(2,1)S(1)}, bf16[320,1024]{1,0:T(8,128)(2,1)}, u32[]{:S(2)}, u32[]{:S(2)}) collective-permute-start(bf16[320,1024]{1,0:T(8,128)(2,1)S(1)} %shard_map.96), channel_id=1, source_target_pairs={{0,4},{4,0},{8,12},{12,8},{1,5},{5,1},{9,13},{13,9},{2,6},{6,2},{1... | collective-permute-start | bytes 1966088 | tf_op jit(solution)/shard_map/ppermute | solution.py:119
  7.0 19.3 %collective-permute-start = (bf16[144,512]{1,0:T(8,128)(2,1)S(1)}, bf16[144,512]{1,0:T(8,128)(2,1)S(1)}, u32[]{:S(2)}, u32[]{:S(2)}) collective-permute-start(bf16[144,512]{1,0:T(8,128)(2,1)S(1)} %fusion.1), channel_id=1, source_target_pairs={{0,8},{4,12},{8,0},{12,4},{1,9},{5,13},{9,1},{13,5},{2,10},{6,14},... | collective-permute-start | bytes 442376 | tf_op jit(solution)/shard_map/ppermute | solution.py:119
  9.7 16.6 %collective-permute-start.1 = (bf16[64,512]{1,0:T(8,128)(2,1)S(1)}, bf16[64,512]{1,0:T(8,128)(2,1)S(1)}, u32[]{:S(2)}, u32[]{:S(2)}) collective-permute-start(bf16[64,512]{1,0:T(8,128)(2,1)S(1)} %bitcast.13), channel_id=1, source_target_pairs={{0,4},{4,0},{8,12},{12,8},{1,5},{5,1},{9,13},{13,9},{2,6},{6,2},{1... | collective-permute-start | bytes 196616 | tf_op jit(solution)/shard_map/ppermute | solution.py:119
  26.3 2.9 %copy-start.15 = (bf16[64,512]{1,0:T(8,128)(2,1)}, bf16[64,512]{1,0:T(8,128)(2,1)S(1)}, u32[]{:S(2)}) copy-start(bf16[64,512]{1,0:T(8,128)(2,1)S(1)} %collective-permute-done.1.up_sib) | copy-start | bytes 196612
  26.3 23.5 %copy-start.12 = (bf16[144,512]{1,0:T(8,128)(2,1)}, bf16[144,512]{1,0:T(8,128)(2,1)S(1)}, u32[]{:S(2)}) copy-start(bf16[144,512]{1,0:T(8,128)(2,1)S(1)} %collective-permute-done.cot_got) | copy-start | bytes 442372
  26.3 21.1 %collective-permute-start.4 = (bf16[256,1024]{1,0:T(8,128)(2,1)S(1)}, bf16[256,1024]{1,0:T(8,128)(2,1)}, u32[]{:S(2)}, u32[]{:S(2)}) collective-permute-start(bf16[256,1024]{1,0:T(8,128)(2,1)S(1)} %shard_map.94), channel_id=1, source_target_pairs={{0,4},{4,0},{8,12},{12,8},{1,5},{5,1},{9,13},{13,9},{2,6},{6,2},{1... | collective-permute-start | bytes 1572872 | tf_op jit(solution)/shard_map/ppermute | solution.py:119
  29.2 21.2 %copy-start.19 = (bf16[256,128]{1,0:T(8,128)(2,1)}, bf16[256,128]{1,0:T(8,128)(2,1)S(1)}, u32[]{:S(2)}) copy-start(bf16[256,128]{1,0:T(8,128)(2,1)S(1)} %get-tuple-element.44.members) | copy-start | bytes 196612
  29.2 20.6 %collective-permute-start.3 = (bf16[256,640]{1,0:T(8,128)(2,1)S(1)}, bf16[256,640]{1,0:T(8,128)(2,1)S(1)}, u32[]{:S(2)}, u32[]{:S(2)}) collective-permute-start(bf16[256,640]{1,0:T(8,128)(2,1)S(1)} %get-tuple-element.37.mine), channel_id=1, source_target_pairs={{0,2},{1,3},{2,0},{3,1},{4,6},{5,7},{6,4},{7,5},{8,10},{9,11},{10,... | collective-permute-start | bytes 983048 | tf_op jit(solution)/shard_map/ppermute | solution.py:119
  30.8 28.3 %collective-permute-start.7 = (bf16[320,1024]{1,0:T(8,128)(2,1)}, bf16[320,1024]{1,0:T(8,128)(2,1)}, u32[]{:S(2)}, u32[]{:S(2)}) collective-permute-start(bf16[320,1024]{1,0:T(8,128)(2,1)} %collective-permute-done.6.first.near), channel_id=1, source_target_pairs={{0,16},{16,0},{1,17},{17,1},{2,18},{18,2},{3,19},{19,3},{4,20},{20... | collective-permute-start | bytes 1966088 | tf_op jit(solution)/shard_map/ppermute | solution.py:119
  32.3 24.5 %collective-permute-start.2 = (bf16[128,2048]{1,0:T(8,128)(2,1)S(1)}, bf16[128,2048]{1,0:T(8,128)(2,1)S(1)}, u32[]{:S(2)}, u32[]{:S(2)}) collective-permute-start(bf16[128,2048]{1,0:T(8,128)(2,1)S(1)} %copy-done.3), channel_id=1, source_target_pairs={{0,8},{4,12},{8,0},{12,4},{1,9},{5,13},{9,1},{13,5},{2,10},{6,14},... | collective-permute-start | bytes 1572872 | tf_op jit(solution)/shard_map/ppermute | solution.py:119
  47.4 16.6 %collective-permute-start.8 = (bf16[256,1024]{1,0:T(8,128)(2,1)}, bf16[256,1024]{1,0:T(8,128)(2,1)}, u32[]{:S(2)}, u32[]{:S(2)}) collective-permute-start(bf16[256,1024]{1,0:T(8,128)(2,1)} %collective-permute-done.4.second), channel_id=1, source_target_pairs={{0,16},{16,0},{1,17},{17,1},{2,18},{18,2},{3,19},{19,3},{4,20},{20... | collective-permute-start | bytes 1572872 | tf_op jit(solution)/shard_map/ppermute | solution.py:119
  50.4 1.8 %copy-start.4 = (bf16[256,640]{1,0:T(8,128)(2,1)}, bf16[256,640]{1,0:T(8,128)(2,1)S(1)}, u32[]{:S(2)}) copy-start(bf16[256,640]{1,0:T(8,128)(2,1)S(1)} %shard_map.95.mine) | copy-start | bytes 983044
  50.4 1.8 %collective-permute-start.5 = (bf16[256,640]{1,0:T(8,128)(2,1)S(1)}, bf16[256,640]{1,0:T(8,128)(2,1)}, u32[]{:S(2)}, u32[]{:S(2)}) collective-permute-start(bf16[256,640]{1,0:T(8,128)(2,1)S(1)} %shard_map.95.mine), channel_id=1, source_target_pairs={{0,1},{1,0},{2,3},{3,2},{4,5},{5,4},{6,7},{7,6},{8,9},{9,8},{10,11... | collective-permute-start | bytes 983048 | tf_op jit(solution)/shard_map/ppermute | solution.py:119
  51.2 5.6 %copy-start.2 = (bf16[512,2048]{1,0:T(8,128)(2,1)S(1)}, bf16[512,2048]{1,0:T(8,128)(2,1)}, u32[]{:S(2)}) copy-start(bf16[512,2048]{1,0:T(8,128)(2,1)} %weight.5) | copy-start | bytes 6291460
  56.2 2.9 %copy-start.7 = (bf16[1,64,2048]{2,1,0:T(8,128)(2,1)S(1)}, bf16[1,64,2048]{2,1,0:T(8,128)(2,1)}, u32[]{:S(2)}) copy-start(bf16[1,64,2048]{2,1,0:T(8,128)(2,1)} %param.9) | copy-start | bytes 786436
  56.2 2.9 %copy-start.20 = (bf16[256,128]{1,0:T(8,128)(2,1)S(1)}, bf16[256,128]{1,0:T(8,128)(2,1)}, u32[]{:S(2)}) copy-start(bf16[256,128]{1,0:T(8,128)(2,1)} %copy-done.19) | copy-start | bytes 196612
  56.2 16.8 %collective-permute-start.10 = (bf16[128,1024]{1,0:T(8,128)(2,1)}, bf16[128,1024]{1,0:T(8,128)(2,1)}, u32[]{:S(2)}, u32[]{:S(2)}) collective-permute-start(bf16[128,1024]{1,0:T(8,128)(2,1)} %get-tuple-element.41), channel_id=1, source_target_pairs={{0,8},{4,12},{8,0},{12,4},{1,9},{5,13},{9,1},{13,5},{2,10},{6,14},... | collective-permute-start | bytes 786440 | tf_op jit(solution)/shard_map/ppermute | solution.py:119
  59.0 1.8 %copy-start.8 = (f32[256,1024]{1,0:T(8,128)}, f32[256,1024]{1,0:T(8,128)S(1)}, u32[]{:S(2)}) copy-start(f32[256,1024]{1,0:T(8,128)S(1)} %shard_map.98.part) | copy-start | bytes 3145732
  60.8 7.3 %collective-permute-start.9 = (bf16[256,128]{1,0:T(8,128)(2,1)S(1)}, bf16[256,128]{1,0:T(8,128)(2,1)S(1)}, u32[]{:S(2)}, u32[]{:S(2)}) collective-permute-start(bf16[256,128]{1,0:T(8,128)(2,1)S(1)} %shard_map.99.low), channel_id=1, source_target_pairs={{0,2},{1,3},{2,0},{3,1},{4,6},{5,7},{6,4},{7,5},{8,10},{9,11},{10,... | collective-permute-start | bytes 196616 | tf_op jit(solution)/shard_map/ppermute | solution.py:119
  64.0 4.1 %copy-start.9 = (f32[256,1024]{1,0:T(8,128)S(1)}, f32[256,1024]{1,0:T(8,128)}, u32[]{:S(2)}) copy-start(f32[256,1024]{1,0:T(8,128)} %copy-done.8) | copy-start | bytes 3145732
  68.1 2.5 %copy-start.22 = (bf16[128,1024]{1,0:T(8,128)(2,1)S(1)}, bf16[128,1024]{1,0:T(8,128)(2,1)}, u32[]{:S(2)}) copy-start(bf16[128,1024]{1,0:T(8,128)(2,1)} %get-tuple-element.46) | copy-start | bytes 786436
  68.1 6.8 %copy-start.5 = (bf16[256,640]{1,0:T(8,128)(2,1)S(1)}, bf16[256,640]{1,0:T(8,128)(2,1)}, u32[]{:S(2)}) copy-start(bf16[256,640]{1,0:T(8,128)(2,1)} %copy-done.4) | copy-start | bytes 983044
  68.1 6.8 %copy-start.11 = (bf16[128,512]{1,0:T(8,128)(2,1)S(1)}, bf16[128,512]{1,0:T(8,128)(2,1)}, u32[]{:S(2)}) copy-start(bf16[128,512]{1,0:T(8,128)(2,1)} %cot.3) | copy-start | bytes 393220
  68.1 6.8 %copy-start.13 = (bf16[144,512]{1,0:T(8,128)(2,1)S(1)}, bf16[144,512]{1,0:T(8,128)(2,1)}, u32[]{:S(2)}) copy-start(bf16[144,512]{1,0:T(8,128)(2,1)} %copy-done.12) | copy-start | bytes 442372
  68.1 6.8 %copy-start.16 = (bf16[64,512]{1,0:T(8,128)(2,1)S(1)}, bf16[64,512]{1,0:T(8,128)(2,1)}, u32[]{:S(2)}) copy-start(bf16[64,512]{1,0:T(8,128)(2,1)} %copy-done.15) | copy-start | bytes 196612
  70.0 16.4 %copy-start.17 = (bf16[128,1024]{1,0:T(8,128)(2,1)S(1)}, bf16[128,1024]{1,0:T(8,128)(2,1)}, u32[]{:S(2)}) copy-start(bf16[128,1024]{1,0:T(8,128)(2,1)} %get-tuple-element.57.near) | copy-start | bytes 786436
  70.0 16.4 %copy-start.18 = (bf16[128,1024]{1,0:T(8,128)(2,1)S(1)}, bf16[128,1024]{1,0:T(8,128)(2,1)}, u32[]{:S(2)}) copy-start(bf16[128,1024]{1,0:T(8,128)(2,1)} %get-tuple-element.59.far) | copy-start | bytes 786436
  70.0 3.0 %collective-permute-start.12 = (bf16[128,640]{1,0:T(8,128)(2,1)S(1)}, bf16[128,640]{1,0:T(8,128)(2,1)S(1)}, u32[]{:S(2)}, u32[]{:S(2)}) collective-permute-start(bf16[128,640]{1,0:T(8,128)(2,1)S(1)} %get-tuple-element.51.give2), channel_id=1, source_target_pairs={{0,1},{1,0},{2,3},{3,2},{4,5},{5,4},{6,7},{7,6},{8,9},{9,8},{10,11... | collective-permute-start | bytes 491528 | tf_op jit(solution)/shard_map/ppermute | solution.py:119
  70.1 2.9 %collective-permute-start.11 = (bf16[128,640]{1,0:T(8,128)(2,1)S(1)}, bf16[128,640]{1,0:T(8,128)(2,1)S(1)}, u32[]{:S(2)}, u32[]{:S(2)}) collective-permute-start(bf16[128,640]{1,0:T(8,128)(2,1)S(1)} %get-tuple-element.49.give), channel_id=1, source_target_pairs={{0,1},{1,0},{2,3},{3,2},{4,5},{5,4},{6,7},{7,6},{8,9},{9,8},{10,11... | collective-permute-start | bytes 491528 | tf_op jit(solution)/shard_map/ppermute | solution.py:119
  70.6 15.8 %collective-permute-start.16 = (bf16[128,1024]{1,0:T(8,128)(2,1)S(1)}, bf16[128,1024]{1,0:T(8,128)(2,1)S(1)}, u32[]{:S(2)}, u32[]{:S(2)}) collective-permute-start(bf16[128,1024]{1,0:T(8,128)(2,1)S(1)} %copy-done.22), channel_id=1, source_target_pairs={{0,8},{4,12},{8,0},{12,4},{1,9},{5,13},{9,1},{13,5},{2,10},{6,14},... | collective-permute-start | bytes 786440 | tf_op jit(solution)/shard_map/ppermute | solution.py:119
  73.6 7.1 %collective-permute-start.14 = (bf16[128,512]{1,0:T(8,128)(2,1)S(1)}, bf16[128,512]{1,0:T(8,128)(2,1)S(1)}, u32[]{:S(2)}, u32[]{:S(2)}) collective-permute-start(bf16[128,512]{1,0:T(8,128)(2,1)S(1)} %get-tuple-element.55.held), channel_id=1, source_target_pairs={{2,0},{3,1},{6,4},{7,5},{8,10},{9,11},{12,14},{13,15},{18,16},{19,... | collective-permute-start | bytes 393224 | tf_op jit(solution)/shard_map/ppermute | solution.py:124
  76.3 13.6 %collective-permute-start.17 = (bf16[64,1280]{1,0:T(8,128)(2,1)S(1)}, bf16[64,1280]{1,0:T(8,128)(2,1)S(1)}, u32[]{:S(2)}, u32[]{:S(2)}) collective-permute-start(bf16[64,1280]{1,0:T(8,128)(2,1)S(1)} %get-tuple-element.62), channel_id=1, source_target_pairs={{0,4},{4,0},{8,12},{12,8},{1,5},{5,1},{9,13},{13,9},{2,6},{6,2},{1... | collective-permute-start | bytes 491528 | tf_op jit(solution)/shard_map/ppermute | solution.py:119
  77.7 14.4 %collective-permute-start.18 = (bf16[64,1280]{1,0:T(8,128)(2,1)S(1)}, bf16[64,1280]{1,0:T(8,128)(2,1)S(1)}, u32[]{:S(2)}, u32[]{:S(2)}) collective-permute-start(bf16[64,1280]{1,0:T(8,128)(2,1)S(1)} %get-tuple-element.63), channel_id=1, source_target_pairs={{0,4},{4,0},{8,12},{12,8},{1,5},{5,1},{9,13},{13,9},{2,6},{6,2},{1... | collective-permute-start | bytes 491528 | tf_op jit(solution)/shard_map/ppermute | solution.py:119
  78.4 9.8 %collective-permute-start.13 = (bf16[128,512]{1,0:T(8,128)(2,1)S(1)}, bf16[128,512]{1,0:T(8,128)(2,1)S(1)}, u32[]{:S(2)}, u32[]{:S(2)}) collective-permute-start(bf16[128,512]{1,0:T(8,128)(2,1)S(1)} %get-tuple-element.52.held), channel_id=1, source_target_pairs={{2,0},{3,1},{6,4},{7,5},{8,10},{9,11},{12,14},{13,15},{18,16},{19,... | collective-permute-start | bytes 393224 | tf_op jit(solution)/shard_map/ppermute | solution.py:124
  81.3 7.4 %collective-permute-start.15 = (bf16[128,512]{1,0:T(8,128)(2,1)S(1)}, bf16[128,512]{1,0:T(8,128)(2,1)S(1)}, u32[]{:S(2)}, u32[]{:S(2)}) collective-permute-start(bf16[128,512]{1,0:T(8,128)(2,1)S(1)} %shard_map.104), channel_id=1, source_target_pairs={{0,8},{4,12},{8,0},{12,4},{1,9},{5,13},{9,1},{13,5},{2,10},{6,14},... | collective-permute-start | bytes 393224 | tf_op jit(solution)/shard_map/ppermute | solution.py:119

commit v8 on v7

--- a/solution.py
+++ b/solution.py
@@ -128,7 +128,7 @@
     return lax.optimization_barrier((values, earlier))[0]
 
 
-Y, Z, IN_PAIR, ON_OWN = range(4)
+Y, Z, IN_PAIR, ON_OWN, OTHER_Y = range(5)
 
 
 SMALL = pl.CostEstimate(flops=0, bytes_accessed=1000, transcendentals=0)
@@ -236,7 +236,7 @@
     toks, tile = mine.shape[0] // 2, 512
     steps = first.shape[1] // tile
     whole = lambda a: pl.BlockSpec(a.shape, lambda j, s: (0, 0))
-    by_side = lambda a: pl.BlockSpec((a.shape[0], tile), lambda j, s: (0, s[4] * steps + j))
+    by_side = lambda a: pl.BlockSpec((a.shape[0], tile), lambda j, s: (0, s[side] * steps + j))
     tiled = lambda n: pl.BlockSpec((n, tile), lambda j, s: (0, j))
     return pl.pallas_call(
         gradient_kernel,
@@ -257,9 +257,9 @@
             jax.ShapeDtypeStruct((toks, steps * tile), bf16),
             jax.ShapeDtypeStruct((toks, steps * tile), bf16),
         ],
-        compiler_params=pltpu.CompilerParams(vmem_limit_bytes=56 * 1024 * 1024),
+        compiler_params=pltpu.CompilerParams(vmem_limit_bytes=20 * 1024 * 1024),
         cost_estimate=SMALL,
-    )(jnp.concatenate([where, side[None]]), mine, got, weight, down, first, second)
+    )(where, mine, got, weight, down, first, second)
 
 
 def gradient_end_kernel(where, near, near_got, far, far_got, out):
@@ -387,7 +387,7 @@
     y = lax.axis_index("groups")
     t = lax.axis_index("tp")
     x, c = t // 2, t % 2
-    where = jnp.stack([y, z, x == z // 2, c == z % 2]).astype(jnp.int32)
+    where = jnp.stack([y, z, x == z // 2, c == z % 2, 1 - y]).astype(jnp.int32)
     rows, width = key_value_weight.shape
     toks, out_width = cotangent.shape
     half, wide = rows // 2, width // 2
@@ -421,7 +421,7 @@
     mine = local_kernel(block_kernel, (mine.shape, bf16), where, mine, mine_x)
     got = swap(mine, "tp", 1)
 
-    near, near_sent = gradient_half(where, y, mine, got, key_value_weight, down, near0, near1)
+    near, near_sent = gradient_half(where, Y, mine, got, key_value_weight, down, near0, near1)
     near_got = swap(near_sent, "fsdp", 2)
 
     act_got = after(act_got, near_sent)
@@ -435,7 +435,7 @@
     low_x = swap(low, "tp", 2)
 
     far1 = after(far1, low)
-    far, far_sent = gradient_half(where, 1 - y, mine, got, key_value_weight, down, far0, far1)
+    far, far_sent = gradient_half(where, OTHER_Y, mine, got, key_value_weight, down, far0, far1)
     far_got = swap(far_sent, "fsdp", 2)
 
     part = after(part, far_sent)

time: 94 us -> 92.6 us (0.985); the launches traced: 93.5 us -> 90.9 us
  waiting for transfers between devices: 37.2 us -> 45.2 us
  Pallas kernels: 23.5 us -> 16.1 us
  starting transfers between devices: 27.7 us -> 26.1 us
  local copies, waits for them, and re-layouts: 3.99 us -> 2.65 us
    ppermute x2, waiting for transfers between devices: 0.97 us -> 6.77 us  [both(): return lax.ppermute(x, ('fsdp', 'tp'), flat)]
    pallas_call x2, Pallas kernels: 7.97 us -> 3.7 us  [gradient_half(): pl.pallas_call(gradient_kernel, grid_spec=pltpu.PrefetchScalarGridSpec(nu...]
    pallas_call x10, Pallas kernels: 12.6 us -> 10.2 us  [local_kernel(): pl.pallas_call(body, out_shape=shapes, in_specs=[pl.BlockSpec(memory_spac...]
    ppermute x17, waiting for transfers between devices: 36.2 us -> 38.5 us  [swap(): lax.ppermute(x, axis, [(i, i ^ bit) for i in range(lax.axis_size(axis))])]
    ppermute x17, starting transfers between devices: 25.2 us -> 23.5 us  [swap(): lax.ppermute(x, axis, [(i, i ^ bit) for i in range(lax.axis_size(axis))])]
    concatenate x2 -> x0, local copies, waits for them, and re-layouts: 1.35 us -> none  [gradient_half(): jnp.concatenate([where, side[None]])]
    unnamed x46 -> x16, local copies, waits for them, and re-layouts: 2.64 us -> 2.57 us
  transfers between devices with their start and end apart: 19 -> 19, of which waited for: 7 -> 9; matrix products, arithmetic and copies ran while one was open for 1% -> 0% of each run, Pallas kernels for 23% -> 15%
where the time goes in v8:
time: 92.6 us; the launch traced here: 90.9 us
  waiting for transfers between devices  45.2 us (49%)
  starting transfers between devices  26.1 us (28%)
  Pallas kernels  16.1 us (17%)
  local copies, waits for them, and re-layouts  2.65 us (3%)
    ppermute x17, waiting for transfers between devices, swap(): lax.ppermute(x, axis, [(i, i ^ bit) for i in range(lax.axis_size(axis))])  38.5 us
    ppermute x17, starting transfers between devices, swap(): lax.ppermute(x, axis, [(i, i ^ bit) for i in range(lax.axis_size(axis))])  23.5 us
    pallas_call x10, Pallas kernels, local_kernel(): pl.pallas_call(body, out_shape=shapes, in_specs=[pl.BlockSpec(memory_spac...  10.2 us
    ppermute x2, waiting for transfers between devices, both(): return lax.ppermute(x, ('fsdp', 'tp'), flat)  6.77 us
    pallas_call x2, Pallas kernels, gradient_half(): pl.pallas_call(gradient_kernel, grid_spec=pltpu.PrefetchScalarGridSpec(nu...  3.7 us
    ppermute x2, starting transfers between devices, both(): return lax.ppermute(x, ('fsdp', 'tp'), flat)  2.57 us
    unnamed x16, local copies, waits for them, and re-layouts  2.57 us
  transfers between devices with their start and end apart: 19, of which 9 were waited for; matrix products, arithmetic and copies ran while one was open for 0% of the time, Pallas kernels for 15%

profile of v8, /device:TPU:0, one launch (start us, length us, event | category | flops | bytes accessed | tf_op | source)
XLA Modules:
  0.0 90.9 jit_solution(5982600670387253115)
XLA Ops:
  0.6 0.0 copy-start.7
  0.6 0.0 copy-start.6
  0.7 0.1 stack.31.where
  0.8 1.6 %copy-done = bf16[512,2048]{1,0:T(8,128)(2,1)S(1)} copy-done((bf16[512,2048]{1,0:T(8,128)(2,1)S(1)}, bf16[512,2048]{1,0:T(8,128)(2,1)}, u32[]{:S(2)}) %copy-start) | copy-done | bytes 2097176
  2.4 0.9 %copy-done.3 = bf16[1,64,2048]{2,1,0:T(8,128)(2,1)S(1)} copy-done((bf16[1,64,2048]{2,1,0:T(8,128)(2,1)S(1)}, bf16[1,64,2048]{2,1,0:T(8,128)(2,1)}, u32[]{:S(2)}) %copy-start.3) | copy-done | bytes 262168
  3.3 0.6 shard_map.96
  3.9 0.0 copy-start.2
  3.9 3.1 %collective-permute-start.6 = (bf16[320,1024]{1,0:T(8,128)(2,1)S(1)}, bf16[320,1024]{1,0:T(8,128)(2,1)S(1)}, u32[]{:S(2)}, u32[]{:S(2)}) collective-permute-start(bf16[320,1024]{1,0:T(8,128)(2,1)S(1)} %shard_map.96), channel_id=1, source_target_pairs={{0,4},{4,0},{8,12},{12,8},{1,5},{5,1},{9,13},{13,9},{2,6},{6,2},{1... | collective-permute-start | bytes 1966088 | tf_op jit(solution)/shard_map/ppermute | solution.py:119
  7.0 0.0 copy-done.7
  7.0 0.0 copy-done.5
  7.0 0.0 copy-start.4
  7.1 2.7 %collective-permute-start = (bf16[144,512]{1,0:T(8,128)(2,1)S(1)}, bf16[144,512]{1,0:T(8,128)(2,1)S(1)}, u32[]{:S(2)}, u32[]{:S(2)}) collective-permute-start(bf16[144,512]{1,0:T(8,128)(2,1)S(1)} %fusion.1), channel_id=1, source_target_pairs={{0,8},{4,12},{8,0},{12,4},{1,9},{5,13},{9,1},{13,5},{2,10},{6,14},... | collective-permute-start | bytes 442376 | tf_op jit(solution)/shard_map/ppermute | solution.py:119
  9.7 0.0 copy-done.6
  9.7 0.4 collective-permute-start.1
  10.2 0.0 copy-done.1
  10.2 0.6 shard_map.94
  10.8 15.6 %collective-permute-done.1.up_sib = bf16[64,512]{1,0:T(8,128)(2,1)S(1)} collective-permute-done((bf16[64,512]{1,0:T(8,128)(2,1)S(1)}, bf16[64,512]{1,0:T(8,128)(2,1)S(1)}, u32[]{:S(2)}, u32[]{:S(2)}) %collective-permute-start.1) | collective-permute-done | bytes 65568 | tf_op jit(solution)/shard_map/ppermute | solution.py:119
  26.3 0.0 collective-permute-done.cot_got
  26.3 2.0 %collective-permute-start.4 = (bf16[256,1024]{1,0:T(8,128)(2,1)S(1)}, bf16[256,1024]{1,0:T(8,128)(2,1)S(1)}, u32[]{:S(2)}, u32[]{:S(2)}) collective-permute-start(bf16[256,1024]{1,0:T(8,128)(2,1)S(1)} %shard_map.94), channel_id=1, source_target_pairs={{0,4},{4,0},{8,12},{12,8},{1,5},{5,1},{9,13},{13,9},{2,6},{6,2},{1... | collective-permute-start | bytes 1572872 | tf_op jit(solution)/shard_map/ppermute | solution.py:119
  28.4 0.8 shard_map.93
  29.2 1.6 %collective-permute-start.3 = (bf16[256,640]{1,0:T(8,128)(2,1)S(1)}, bf16[256,640]{1,0:T(8,128)(2,1)S(1)}, u32[]{:S(2)}, u32[]{:S(2)}) collective-permute-start(bf16[256,640]{1,0:T(8,128)(2,1)S(1)} %get-tuple-element.37.mine), channel_id=1, source_target_pairs={{0,2},{1,3},{2,0},{3,1},{4,6},{5,7},{6,4},{7,5},{8,10},{9,11},{10,... | collective-permute-start | bytes 983048 | tf_op jit(solution)/shard_map/ppermute | solution.py:119
  30.7 0.0 collective-permute-done.6.first.near
  30.7 1.5 %collective-permute-start.7 = (bf16[320,1024]{1,0:T(8,128)(2,1)S(1)}, bf16[320,1024]{1,0:T(8,128)(2,1)S(1)}, u32[]{:S(2)}, u32[]{:S(2)}) collective-permute-start(bf16[320,1024]{1,0:T(8,128)(2,1)S(1)} %collective-permute-done.6.first.near), channel_id=1, source_target_pairs={{0,16},{16,0},{1,17},{17,1},{2,18},{18,2},{3,19},{19,3},{4,20},{20... | collective-permute-start | bytes 1966088 | tf_op jit(solution)/shard_map/ppermute | solution.py:119
  32.3 2.3 %collective-permute-start.2 = (bf16[128,2048]{1,0:T(8,128)(2,1)S(1)}, bf16[128,2048]{1,0:T(8,128)(2,1)S(1)}, u32[]{:S(2)}, u32[]{:S(2)}) collective-permute-start(bf16[128,2048]{1,0:T(8,128)(2,1)S(1)} %copy-done.2), channel_id=1, source_target_pairs={{0,8},{4,12},{8,0},{12,4},{1,9},{5,13},{9,1},{13,5},{2,10},{6,14},... | collective-permute-start | bytes 1572872 | tf_op jit(solution)/shard_map/ppermute | solution.py:119
  34.5 12.7 %collective-permute-done.4.second = bf16[256,1024]{1,0:T(8,128)(2,1)S(1)} collective-permute-done((bf16[256,1024]{1,0:T(8,128)(2,1)S(1)}, bf16[256,1024]{1,0:T(8,128)(2,1)S(1)}, u32[]{:S(2)}, u32[]{:S(2)}) %collective-permute-start.4) | collective-permute-done | bytes 524320 | tf_op jit(solution)/shard_map/ppermute | solution.py:119
  47.2 2.4 %collective-permute-start.8 = (bf16[256,1024]{1,0:T(8,128)(2,1)S(1)}, bf16[256,1024]{1,0:T(8,128)(2,1)S(1)}, u32[]{:S(2)}, u32[]{:S(2)}) collective-permute-start(bf16[256,1024]{1,0:T(8,128)(2,1)S(1)} %collective-permute-done.4.second), channel_id=1, source_target_pairs={{0,16},{16,0},{1,17},{17,1},{2,18},{18,2},{3,19},{19,3},{4,20},{20... | collective-permute-start | bytes 1572872 | tf_op jit(solution)/shard_map/ppermute | solution.py:119
  49.6 0.0 collective-permute-done.3.got
  49.6 0.6 shard_map.95.mine
  50.2 0.1 collective-permute-start.5
  50.3 1.6 %collective-permute-done.5.got = bf16[256,640]{1,0:T(8,128)(2,1)S(1)} collective-permute-done((bf16[256,640]{1,0:T(8,128)(2,1)S(1)}, bf16[256,640]{1,0:T(8,128)(2,1)S(1)}, u32[]{:S(2)}, u32[]{:S(2)}) %collective-permute-start.5) | collective-permute-done | bytes 327712 | tf_op jit(solution)/shard_map/ppermute | solution.py:119
  51.9 1.8 %shard_map.97 = (bf16[128,1024]{1,0:T(8,128)(2,1)S(1)}, bf16[128,1024]{1,0:T(8,128)(2,1)S(1)}) custom-call(s32[5]{0:T(128)S(1)} %stack.31.where, bf16[256,640]{1,0:T(8,128)(2,1)S(1)} %shard_map.95.mine, bf16[256,640]{1,0:T(8,128)(2,1)S(1)} %collective-permute-done.5.got, bf16[512,2048]{1,0:T(8,128)(2,1)S(1)} %copy-done.1, bf16[64,2048]{1,0:T(8,128)(2,1)S(1)} %bitcast.10, ...), custom_call_target="tpu_custom_call" | custom-call | bytes 1000 | tf_op jit(solution)/shard_map/pallas_call | solution.py:241
  53.8 0.6 collective-permute-start.10
  54.4 1.7 %collective-permute-done.2.act_got = bf16[128,2048]{1,0:T(8,128)(2,1)S(1)} collective-permute-done((bf16[128,2048]{1,0:T(8,128)(2,1)S(1)}, bf16[128,2048]{1,0:T(8,128)(2,1)S(1)}, u32[]{:S(2)}, u32[]{:S(2)}) %collective-permute-start.2) | collective-permute-done | bytes 524320 | tf_op jit(solution)/shard_map/ppermute | solution.py:119
  56.1 1.5 %shard_map.98.part = f32[256,1024]{1,0:T(8,128)S(1)} custom-call(s32[5]{0:T(128)S(1)} %stack.31.where, bf16[128,2048]{1,0:T(8,128)(2,1)S(1)} %copy-done.2, bf16[128,2048]{1,0:T(8,128)(2,1)S(1)} %collective-permute-done.2.act_got, bf16[512,2048]{1,0:T(8,128)(2,1)S(1)} %copy-done.1, bf16[320,1024]{1,0:T(8,128)(2,1)S(1)} %collective-permute-done.6.first.near, ...), custom_call_target="tpu_custom_call" | custom-call | bytes 1000 | tf_op jit(solution)/shard_map/pallas_call | solution.py:140
  57.6 0.0 collective-permute-done.7.far.first
  57.6 1.0 %shard_map.99.low = bf16[256,128]{1,0:T(8,128)(2,1)S(1)} custom-call(s32[5]{0:T(128)S(1)} %stack.31.where, bf16[128,2048]{1,0:T(8,128)(2,1)S(1)} %copy-done.2, bf16[128,2048]{1,0:T(8,128)(2,1)S(1)} %collective-permute-done.2.act_got, bf16[256,128]{1,0:T(8,128)(2,1)S(1)} %get-tuple-element.44.members, bf16[64,2048]{1,0:T(8,128)(2,1)S(1)} %bitcast.11, ...), custom_call_target="tpu_custom_call" | custom-call | bytes 1000 | tf_op jit(solution)/shard_map/pallas_call | solution.py:287
  58.6 0.8 collective-permute-start.9
  59.5 0.3 collective-permute-done.8.second
  59.7 1.8 %shard_map.100 = (bf16[128,1024]{1,0:T(8,128)(2,1)S(1)}, bf16[128,1024]{1,0:T(8,128)(2,1)S(1)}) custom-call(s32[5]{0:T(128)S(1)} %stack.31.where, bf16[256,640]{1,0:T(8,128)(2,1)S(1)} %shard_map.95.mine, bf16[256,640]{1,0:T(8,128)(2,1)S(1)} %collective-permute-done.5.got, bf16[512,2048]{1,0:T(8,128)(2,1)S(1)} %copy-done.1, bf16[64,2048]{1,0:T(8,128)(2,1)S(1)} %bitcast.12, ...), custom_call_target="tpu_custom_call" | custom-call | bytes 1000 | tf_op jit(solution)/shard_map/pallas_call | solution.py:241
  61.6 1.4 %collective-permute-done.9.low_got = bf16[256,128]{1,0:T(8,128)(2,1)S(1)} collective-permute-done((bf16[256,128]{1,0:T(8,128)(2,1)S(1)}, bf16[256,128]{1,0:T(8,128)(2,1)S(1)}, u32[]{:S(2)}, u32[]{:S(2)}) %collective-permute-start.9) | collective-permute-done | bytes 65568 | tf_op jit(solution)/shard_map/ppermute | solution.py:119
  63.0 1.0 %shard_map.101 = (f32[256,512]{1,0:T(8,128)S(1)}, bf16[128,640]{1,0:T(8,128)(2,1)S(1)}, bf16[128,640]{1,0:T(8,128)(2,1)S(1)}) custom-call(s32[5]{0:T(128)S(1)} %stack.31.where, f32[256,1024]{1,0:T(8,128)S(1)} %shard_map.98.part, bf16[128,2048]{1,0:T(8,128)(2,1)S(1)} %copy-done.2, bf16[128,2048]{1,0:T(8,128)(2,1)S(1)} %collective-permute-done.2.act_got, ...), custom_call_target="tpu_custom_call" | custom-call | bytes 1000 | tf_op jit(solution)/shard_map/pallas_call | solution.py:140
  64.0 0.1 collective-permute-start.12
  64.1 0.5 collective-permute-start.11
  64.6 1.1 %collective-permute-start.16 = (bf16[128,1024]{1,0:T(8,128)(2,1)S(1)}, bf16[128,1024]{1,0:T(8,128)(2,1)S(1)}, u32[]{:S(2)}, u32[]{:S(2)}) collective-permute-start(bf16[128,1024]{1,0:T(8,128)(2,1)S(1)} %get-tuple-element.46), channel_id=1, source_target_pairs={{0,8},{4,12},{8,0},{12,4},{1,9},{5,13},{9,1},{13,5},{2,10},{6,14},... | collective-permute-start | bytes 786440 | tf_op jit(solution)/shard_map/ppermute | solution.py:119
  65.7 2.9 %collective-permute-done.10.near_got = bf16[128,1024]{1,0:T(8,128)(2,1)S(1)} collective-permute-done((bf16[128,1024]{1,0:T(8,128)(2,1)S(1)}, bf16[128,1024]{1,0:T(8,128)(2,1)S(1)}, u32[]{:S(2)}, u32[]{:S(2)}) %collective-permute-start.10) | collective-permute-done | bytes 262176 | tf_op jit(solution)/shard_map/ppermute | solution.py:119
  68.6 0.0 collective-permute-done.12.got2.give_got2
  68.6 0.0 collective-permute-done.11.got.give_got
  68.6 0.6 shard_map.102
  69.2 1.3 %collective-permute-start.14 = (bf16[128,512]{1,0:T(8,128)(2,1)S(1)}, bf16[128,512]{1,0:T(8,128)(2,1)S(1)}, u32[]{:S(2)}, u32[]{:S(2)}) collective-permute-start(bf16[128,512]{1,0:T(8,128)(2,1)S(1)} %get-tuple-element.55.held), channel_id=1, source_target_pairs={{2,0},{3,1},{6,4},{7,5},{8,10},{9,11},{12,14},{13,15},{18,16},{19,... | collective-permute-start | bytes 393224 | tf_op jit(solution)/shard_map/ppermute | solution.py:124
  70.5 0.9 %shard_map.103 = (bf16[128,512]{1,0:T(8,128)(2,1)S(1)}, bf16[128,512]{1,0:T(8,128)(2,1)S(1)}, f32[64,2048]{1,0:T(8,128)S(1)}, f32[64,512]{1,0:T(8,128)S(1)}, bf1...) custom-call(s32[5]{0:T(128)S(1)} %stack.31.where, bf16[128,640]{1,0:T(8,128)(2,1)S(1)} %get-tuple-element.49.give, ...), custom_call_target="tpu_custom_call" | custom-call | bytes 1000 | tf_op jit(solution)/shard_map/pallas_call | solution.py:140
  71.5 0.1 collective-permute-start.17
  71.5 2.0 %collective-permute-start.18 = (bf16[64,1280]{1,0:T(8,128)(2,1)S(1)}, bf16[64,1280]{1,0:T(8,128)(2,1)S(1)}, u32[]{:S(2)}, u32[]{:S(2)}) collective-permute-start(bf16[64,1280]{1,0:T(8,128)(2,1)S(1)} %get-tuple-element.63), channel_id=1, source_target_pairs={{0,4},{4,0},{8,12},{12,8},{1,5},{5,1},{9,13},{13,9},{2,6},{6,2},{1... | collective-permute-start | bytes 491528 | tf_op jit(solution)/shard_map/ppermute | solution.py:119
  73.5 1.3 %collective-permute-start.13 = (bf16[128,512]{1,0:T(8,128)(2,1)S(1)}, bf16[128,512]{1,0:T(8,128)(2,1)S(1)}, u32[]{:S(2)}, u32[]{:S(2)}) collective-permute-start(bf16[128,512]{1,0:T(8,128)(2,1)S(1)} %get-tuple-element.52.held), channel_id=1, source_target_pairs={{2,0},{3,1},{6,4},{7,5},{8,10},{9,11},{12,14},{13,15},{18,16},{19,... | collective-permute-start | bytes 393224 | tf_op jit(solution)/shard_map/ppermute | solution.py:124
  74.8 6.8 %collective-permute-done.14.got = bf16[128,512]{1,0:T(8,128)(2,1)S(1)} collective-permute-done((bf16[128,512]{1,0:T(8,128)(2,1)S(1)}, bf16[128,512]{1,0:T(8,128)(2,1)S(1)}, u32[]{:S(2)}, u32[]{:S(2)}) %collective-permute-start.14) | collective-permute-done | bytes 131104 | tf_op jit(solution)/shard_map/ppermute | solution.py:124
  81.6 0.6 shard_map.104
  82.2 2.2 %collective-permute-start.15 = (bf16[128,512]{1,0:T(8,128)(2,1)S(1)}, bf16[128,512]{1,0:T(8,128)(2,1)S(1)}, u32[]{:S(2)}, u32[]{:S(2)}) collective-permute-start(bf16[128,512]{1,0:T(8,128)(2,1)S(1)} %shard_map.104), channel_id=1, source_target_pairs={{0,8},{4,12},{8,0},{12,4},{1,9},{5,13},{9,1},{13,5},{2,10},{6,14},... | collective-permute-start | bytes 393224 | tf_op jit(solution)/shard_map/ppermute | solution.py:119
  84.4 0.0 collective-permute-done.16.far_got
  84.4 1.5 %shard_map.106 = bf16[128,2048]{1,0:T(8,128)(2,1)} custom-call(s32[5]{0:T(128)S(1)} %stack.31.where, bf16[128,1024]{1,0:T(8,128)(2,1)S(1)} %get-tuple-element.57.near, bf16[128,1024]{1,0:T(8,128)(2,1)S(1)} %collective-permute-done.10.near_got, bf16[128,1024]{1,0:T(8,128)(2,1)S(1)} %get-tuple-element.59.far, bf16[128,1024]{1,0:T(8,128)(2,1)S(1)} %collective-permute-done.16.far_got), custom_call_target="tpu_custom_call" | custom-call | bytes 1000 | tf_op jit(solution)/shard_map/pallas_call | solution.py:140
  85.9 0.0 collective-permute-done.13.got
  85.9 2.3 %collective-permute-done.15.turned = bf16[128,512]{1,0:T(8,128)(2,1)S(1)} collective-permute-done((bf16[128,512]{1,0:T(8,128)(2,1)S(1)}, bf16[128,512]{1,0:T(8,128)(2,1)S(1)}, u32[]{:S(2)}, u32[]{:S(2)}) %collective-permute-start.15) | collective-permute-done | bytes 131104 | tf_op jit(solution)/shard_map/ppermute | solution.py:119
  88.2 1.3 %shard_map.105 = bf16[128,512]{1,0:T(8,128)(2,1)} custom-call(s32[5]{0:T(128)S(1)} %stack.31.where, bf16[128,512]{1,0:T(8,128)(2,1)S(1)} %get-tuple-element.52.held, bf16[128,512]{1,0:T(8,128)(2,1)S(1)} %collective-permute-done.13.got, bf16[128,512]{1,0:T(8,128)(2,1)S(1)} %get-tuple-element.54.lora, bf16[128,512]{1,0:T(8,128)(2,1)S(1)} %collective-permute-done.15.turned), custom_call_target="tpu_custom_call" | custom-call | bytes 1000 | tf_op jit(solution)/shard_map/pallas_call | solution.py:140
  89.5 0.0 collective-permute-done.17.got
  89.5 0.0 collective-permute-done.18.got_end
  89.5 1.4 %shard_map.107 = (f32[1,64,2048]{2,1,0:T(8,128)}, f32[1,64,512]{2,1,0:T(8,128)}) custom-call(s32[5]{0:T(128)S(1)} %stack.31.where, f32[64,2048]{1,0:T(8,128)S(1)} %get-tuple-element.60.down_own, f32[64,512]{1,0:T(8,128)S(1)} %get-tuple-element.61.up_own, bf16[64,1280]{1,0:T(8,128)(2,1)S(1)} %collective-permute-done.17.got, ...), custom_call_target="tpu_custom_call" | custom-call | bytes 1000 | tf_op jit(solution)/shard_map/pallas_call | solution.py:140
  (8 shorter events, 0.0 us)
Async XLA Ops:
  0.6 6.4 %copy-start.7 = (s32[128,1]{0,1:T(1,128)S(1)}, s32[128,1]{0,1:T(1,128)}, u32[]{:S(2)}) copy-start(s32[128,1]{0,1:T(1,128)} %param.8) | copy-start | bytes 1540
  0.6 9.1 %copy-start.6 = (bf16[1,64,512]{2,1,0:T(8,128)(2,1)S(1)}, bf16[1,64,512]{2,1,0:T(8,128)(2,1)}, u32[]{:S(2)}) copy-start(bf16[1,64,512]{2,1,0:T(8,128)(2,1)} %param.10) | copy-start | bytes 196612
  0.8 1.6 %copy-start = (bf16[512,2048]{1,0:T(8,128)(2,1)S(1)}, bf16[512,2048]{1,0:T(8,128)(2,1)}, u32[]{:S(2)}) copy-start(bf16[512,2048]{1,0:T(8,128)(2,1)} %weight.5) | copy-start | bytes 6291460
  2.4 0.9 %copy-start.3 = (bf16[1,64,2048]{2,1,0:T(8,128)(2,1)S(1)}, bf16[1,64,2048]{2,1,0:T(8,128)(2,1)}, u32[]{:S(2)}) copy-start(bf16[1,64,2048]{2,1,0:T(8,128)(2,1)} %param.9) | copy-start | bytes 786436
  3.3 3.7 %copy-start.5 = (bf16[128,512]{1,0:T(8,128)(2,1)S(1)}, bf16[128,512]{1,0:T(8,128)(2,1)}, u32[]{:S(2)}) copy-start(bf16[128,512]{1,0:T(8,128)(2,1)} %cot.3) | copy-start | bytes 393220
  3.3 6.8 %copy-start.1 = (bf16[512,2048]{1,0:T(8,128)(2,1)S(1)}, bf16[512,2048]{1,0:T(8,128)(2,1)}, u32[]{:S(2)}) copy-start(bf16[512,2048]{1,0:T(8,128)(2,1)} %weight.5) | copy-start | bytes 6291460
  3.9 28.3 %copy-start.2 = (bf16[128,2048]{1,0:T(8,128)(2,1)S(1)}, bf16[128,2048]{1,0:T(8,128)(2,1)}, u32[]{:S(2)}) copy-start(bf16[128,2048]{1,0:T(8,128)(2,1)} %act.7) | copy-start | bytes 1572868
  3.9 26.8 %collective-permute-start.6 = (bf16[320,1024]{1,0:T(8,128)(2,1)S(1)}, bf16[320,1024]{1,0:T(8,128)(2,1)S(1)}, u32[]{:S(2)}, u32[]{:S(2)}) collective-permute-start(bf16[320,1024]{1,0:T(8,128)(2,1)S(1)} %shard_map.96), channel_id=1, source_target_pairs={{0,4},{4,0},{8,12},{12,8},{1,5},{5,1},{9,13},{13,9},{2,6},{6,2},{1... | collective-permute-start | bytes 1966088 | tf_op jit(solution)/shard_map/ppermute | solution.py:119
  7.0 44.9 %copy-start.4 = (bf16[1,64,2048]{2,1,0:T(8,128)(2,1)S(1)}, bf16[1,64,2048]{2,1,0:T(8,128)(2,1)}, u32[]{:S(2)}) copy-start(bf16[1,64,2048]{2,1,0:T(8,128)(2,1)} %param.9) | copy-start | bytes 786436
  7.1 19.3 %collective-permute-start = (bf16[144,512]{1,0:T(8,128)(2,1)S(1)}, bf16[144,512]{1,0:T(8,128)(2,1)S(1)}, u32[]{:S(2)}, u32[]{:S(2)}) collective-permute-start(bf16[144,512]{1,0:T(8,128)(2,1)S(1)} %fusion.1), channel_id=1, source_target_pairs={{0,8},{4,12},{8,0},{12,4},{1,9},{5,13},{9,1},{13,5},{2,10},{6,14},... | collective-permute-start | bytes 442376 | tf_op jit(solution)/shard_map/ppermute | solution.py:119
  9.7 16.6 %collective-permute-start.1 = (bf16[64,512]{1,0:T(8,128)(2,1)S(1)}, bf16[64,512]{1,0:T(8,128)(2,1)S(1)}, u32[]{:S(2)}, u32[]{:S(2)}) collective-permute-start(bf16[64,512]{1,0:T(8,128)(2,1)S(1)} %bitcast.13), channel_id=1, source_target_pairs={{0,4},{4,0},{8,12},{12,8},{1,5},{5,1},{9,13},{13,9},{2,6},{6,2},{1... | collective-permute-start | bytes 196616 | tf_op jit(solution)/shard_map/ppermute | solution.py:119
  26.3 20.9 %collective-permute-start.4 = (bf16[256,1024]{1,0:T(8,128)(2,1)S(1)}, bf16[256,1024]{1,0:T(8,128)(2,1)S(1)}, u32[]{:S(2)}, u32[]{:S(2)}) collective-permute-start(bf16[256,1024]{1,0:T(8,128)(2,1)S(1)} %shard_map.94), channel_id=1, source_target_pairs={{0,4},{4,0},{8,12},{12,8},{1,5},{5,1},{9,13},{13,9},{2,6},{6,2},{1... | collective-permute-start | bytes 1572872 | tf_op jit(solution)/shard_map/ppermute | solution.py:119
  29.2 20.4 %collective-permute-start.3 = (bf16[256,640]{1,0:T(8,128)(2,1)S(1)}, bf16[256,640]{1,0:T(8,128)(2,1)S(1)}, u32[]{:S(2)}, u32[]{:S(2)}) collective-permute-start(bf16[256,640]{1,0:T(8,128)(2,1)S(1)} %get-tuple-element.37.mine), channel_id=1, source_target_pairs={{0,2},{1,3},{2,0},{3,1},{4,6},{5,7},{6,4},{7,5},{8,10},{9,11},{10,... | collective-permute-start | bytes 983048 | tf_op jit(solution)/shard_map/ppermute | solution.py:119
  30.7 26.9 %collective-permute-start.7 = (bf16[320,1024]{1,0:T(8,128)(2,1)S(1)}, bf16[320,1024]{1,0:T(8,128)(2,1)S(1)}, u32[]{:S(2)}, u32[]{:S(2)}) collective-permute-start(bf16[320,1024]{1,0:T(8,128)(2,1)S(1)} %collective-permute-done.6.first.near), channel_id=1, source_target_pairs={{0,16},{16,0},{1,17},{17,1},{2,18},{18,2},{3,19},{19,3},{4,20},{20... | collective-permute-start | bytes 1966088 | tf_op jit(solution)/shard_map/ppermute | solution.py:119
  32.3 23.8 %collective-permute-start.2 = (bf16[128,2048]{1,0:T(8,128)(2,1)S(1)}, bf16[128,2048]{1,0:T(8,128)(2,1)S(1)}, u32[]{:S(2)}, u32[]{:S(2)}) collective-permute-start(bf16[128,2048]{1,0:T(8,128)(2,1)S(1)} %copy-done.2), channel_id=1, source_target_pairs={{0,8},{4,12},{8,0},{12,4},{1,9},{5,13},{9,1},{13,5},{2,10},{6,14},... | collective-permute-start | bytes 1572872 | tf_op jit(solution)/shard_map/ppermute | solution.py:119
  47.2 12.5 %collective-permute-start.8 = (bf16[256,1024]{1,0:T(8,128)(2,1)S(1)}, bf16[256,1024]{1,0:T(8,128)(2,1)S(1)}, u32[]{:S(2)}, u32[]{:S(2)}) collective-permute-start(bf16[256,1024]{1,0:T(8,128)(2,1)S(1)} %collective-permute-done.4.second), channel_id=1, source_target_pairs={{0,16},{16,0},{1,17},{17,1},{2,18},{18,2},{3,19},{19,3},{4,20},{20... | collective-permute-start | bytes 1572872 | tf_op jit(solution)/shard_map/ppermute | solution.py:119
  50.2 1.7 %collective-permute-start.5 = (bf16[256,640]{1,0:T(8,128)(2,1)S(1)}, bf16[256,640]{1,0:T(8,128)(2,1)S(1)}, u32[]{:S(2)}, u32[]{:S(2)}) collective-permute-start(bf16[256,640]{1,0:T(8,128)(2,1)S(1)} %shard_map.95.mine), channel_id=1, source_target_pairs={{0,1},{1,0},{2,3},{3,2},{4,5},{5,4},{6,7},{7,6},{8,9},{9,8},{10,11... | collective-permute-start | bytes 983048 | tf_op jit(solution)/shard_map/ppermute | solution.py:119
  53.8 14.8 %collective-permute-start.10 = (bf16[128,1024]{1,0:T(8,128)(2,1)S(1)}, bf16[128,1024]{1,0:T(8,128)(2,1)S(1)}, u32[]{:S(2)}, u32[]{:S(2)}) collective-permute-start(bf16[128,1024]{1,0:T(8,128)(2,1)S(1)} %get-tuple-element.41), channel_id=1, source_target_pairs={{0,8},{4,12},{8,0},{12,4},{1,9},{5,13},{9,1},{13,5},{2,10},{6,14},... | collective-permute-start | bytes 786440 | tf_op jit(solution)/shard_map/ppermute | solution.py:119
  58.6 4.3 %collective-permute-start.9 = (bf16[256,128]{1,0:T(8,128)(2,1)S(1)}, bf16[256,128]{1,0:T(8,128)(2,1)S(1)}, u32[]{:S(2)}, u32[]{:S(2)}) collective-permute-start(bf16[256,128]{1,0:T(8,128)(2,1)S(1)} %shard_map.99.low), channel_id=1, source_target_pairs={{0,2},{1,3},{2,0},{3,1},{4,6},{5,7},{6,4},{7,5},{8,10},{9,11},{10,... | collective-permute-start | bytes 196616 | tf_op jit(solution)/shard_map/ppermute | solution.py:119
  64.0 4.6 %collective-permute-start.12 = (bf16[128,640]{1,0:T(8,128)(2,1)S(1)}, bf16[128,640]{1,0:T(8,128)(2,1)S(1)}, u32[]{:S(2)}, u32[]{:S(2)}) collective-permute-start(bf16[128,640]{1,0:T(8,128)(2,1)S(1)} %get-tuple-element.51.give2), channel_id=1, source_target_pairs={{0,1},{1,0},{2,3},{3,2},{4,5},{5,4},{6,7},{7,6},{8,9},{9,8},{10,11... | collective-permute-start | bytes 491528 | tf_op jit(solution)/shard_map/ppermute | solution.py:119
  64.1 4.5 %collective-permute-start.11 = (bf16[128,640]{1,0:T(8,128)(2,1)S(1)}, bf16[128,640]{1,0:T(8,128)(2,1)S(1)}, u32[]{:S(2)}, u32[]{:S(2)}) collective-permute-start(bf16[128,640]{1,0:T(8,128)(2,1)S(1)} %get-tuple-element.49.give), channel_id=1, source_target_pairs={{0,1},{1,0},{2,3},{3,2},{4,5},{5,4},{6,7},{7,6},{8,9},{9,8},{10,11... | collective-permute-start | bytes 491528 | tf_op jit(solution)/shard_map/ppermute | solution.py:119
  64.6 19.9 %collective-permute-start.16 = (bf16[128,1024]{1,0:T(8,128)(2,1)S(1)}, bf16[128,1024]{1,0:T(8,128)(2,1)S(1)}, u32[]{:S(2)}, u32[]{:S(2)}) collective-permute-start(bf16[128,1024]{1,0:T(8,128)(2,1)S(1)} %get-tuple-element.46), channel_id=1, source_target_pairs={{0,8},{4,12},{8,0},{12,4},{1,9},{5,13},{9,1},{13,5},{2,10},{6,14},... | collective-permute-start | bytes 786440 | tf_op jit(solution)/shard_map/ppermute | solution.py:119
  69.2 12.4 %collective-permute-start.14 = (bf16[128,512]{1,0:T(8,128)(2,1)S(1)}, bf16[128,512]{1,0:T(8,128)(2,1)S(1)}, u32[]{:S(2)}, u32[]{:S(2)}) collective-permute-start(bf16[128,512]{1,0:T(8,128)(2,1)S(1)} %get-tuple-element.55.held), channel_id=1, source_target_pairs={{2,0},{3,1},{6,4},{7,5},{8,10},{9,11},{12,14},{13,15},{18,16},{19,... | collective-permute-start | bytes 393224 | tf_op jit(solution)/shard_map/ppermute | solution.py:124
  71.5 18.0 %collective-permute-start.17 = (bf16[64,1280]{1,0:T(8,128)(2,1)S(1)}, bf16[64,1280]{1,0:T(8,128)(2,1)S(1)}, u32[]{:S(2)}, u32[]{:S(2)}) collective-permute-start(bf16[64,1280]{1,0:T(8,128)(2,1)S(1)} %get-tuple-element.62), channel_id=1, source_target_pairs={{0,4},{4,0},{8,12},{12,8},{1,5},{5,1},{9,13},{13,9},{2,6},{6,2},{1... | collective-permute-start | bytes 491528 | tf_op jit(solution)/shard_map/ppermute | solution.py:119
  71.5 18.0 %collective-permute-start.18 = (bf16[64,1280]{1,0:T(8,128)(2,1)S(1)}, bf16[64,1280]{1,0:T(8,128)(2,1)S(1)}, u32[]{:S(2)}, u32[]{:S(2)}) collective-permute-start(bf16[64,1280]{1,0:T(8,128)(2,1)S(1)} %get-tuple-element.63), channel_id=1, source_target_pairs={{0,4},{4,0},{8,12},{12,8},{1,5},{5,1},{9,13},{13,9},{2,6},{6,2},{1... | collective-permute-start | bytes 491528 | tf_op jit(solution)/shard_map/ppermute | solution.py:119
  73.5 12.4 %collective-permute-start.13 = (bf16[128,512]{1,0:T(8,128)(2,1)S(1)}, bf16[128,512]{1,0:T(8,128)(2,1)S(1)}, u32[]{:S(2)}, u32[]{:S(2)}) collective-permute-start(bf16[128,512]{1,0:T(8,128)(2,1)S(1)} %get-tuple-element.52.held), channel_id=1, source_target_pairs={{2,0},{3,1},{6,4},{7,5},{8,10},{9,11},{12,14},{13,15},{18,16},{19,... | collective-permute-start | bytes 393224 | tf_op jit(solution)/shard_map/ppermute | solution.py:124
  82.2 6.0 %collective-permute-start.15 = (bf16[128,512]{1,0:T(8,128)(2,1)S(1)}, bf16[128,512]{1,0:T(8,128)(2,1)S(1)}, u32[]{:S(2)}, u32[]{:S(2)}) collective-permute-start(bf16[128,512]{1,0:T(8,128)(2,1)S(1)} %shard_map.104), channel_id=1, source_target_pairs={{0,8},{4,12},{8,0},{12,4},{1,9},{5,13},{9,1},{13,5},{2,10},{6,14},... | collective-permute-start | bytes 393224 | tf_op jit(solution)/shard_map/ppermute | solution.py:119

commit v9 on v8

--- a/solution.py
+++ b/solution.py
@@ -478,7 +478,7 @@
     key_value_output = local_kernel(
         output_kernel, ((toks, out_width), bf16), where, here, here_got, lora, turned
     )
-    sib_got, sib_end_got = after((sib_got, sib_end_got), key_value_output)
+    sib_got, sib_end_got = after((sib_got, sib_end_got), input_gradient)
     grad_down, up_gradient = local_kernel(
         adapter_end_kernel, [((1, rank, width), f32), ((1, rank, out_width), f32)], where,
         down_own, up_own, sib_got, sib_end_got,

time: 92.6 us -> 92 us (level); the launches traced: 90.9 us -> 91.8 us
  no operation moved by 1% of the time
where the time goes in v9:
time: 92 us; the launch traced here: 91.8 us
  waiting for transfers between devices  46.1 us (50%)
  starting transfers between devices  26.1 us (28%)
  Pallas kernels  16.1 us (18%)
  local copies, waits for them, and re-layouts  2.65 us (3%)
    ppermute x17, waiting for transfers between devices, swap(): lax.ppermute(x, axis, [(i, i ^ bit) for i in range(lax.axis_size(axis))])  39.4 us
    ppermute x17, starting transfers between devices, swap(): lax.ppermute(x, axis, [(i, i ^ bit) for i in range(lax.axis_size(axis))])  23.5 us
    pallas_call x10, Pallas kernels, local_kernel(): pl.pallas_call(body, out_shape=shapes, in_specs=[pl.BlockSpec(memory_spac...  10.2 us
    ppermute x2, waiting for transfers between devices, both(): return lax.ppermute(x, ('fsdp', 'tp'), flat)  6.75 us
    pallas_call x2, Pallas kernels, gradient_half(): pl.pallas_call(gradient_kernel, grid_spec=pltpu.PrefetchScalarGridSpec(nu...  3.7 us
    ppermute x2, starting transfers between devices, both(): return lax.ppermute(x, ('fsdp', 'tp'), flat)  2.57 us
    unnamed x16, local copies, waits for them, and re-layouts  2.57 us
  transfers between devices with their start and end apart: 19, of which 9 were waited for; matrix products, arithmetic and copies ran while one was open for 0% of the time, Pallas kernels for 15%

profile of v9, /device:TPU:0, one launch (start us, length us, event | category | flops | bytes accessed | tf_op | source)
XLA Modules:
  0.0 91.8 jit_solution(1690562237304999311)
XLA Ops:
  0.6 0.0 copy-start.7
  0.6 0.0 copy-start.6
  0.7 0.1 stack.31.where
  0.8 1.6 %copy-done = bf16[512,2048]{1,0:T(8,128)(2,1)S(1)} copy-done((bf16[512,2048]{1,0:T(8,128)(2,1)S(1)}, bf16[512,2048]{1,0:T(8,128)(2,1)}, u32[]{:S(2)}) %copy-start) | copy-done | bytes 2097176
  2.4 0.9 %copy-done.3 = bf16[1,64,2048]{2,1,0:T(8,128)(2,1)S(1)} copy-done((bf16[1,64,2048]{2,1,0:T(8,128)(2,1)S(1)}, bf16[1,64,2048]{2,1,0:T(8,128)(2,1)}, u32[]{:S(2)}) %copy-start.3) | copy-done | bytes 262168
  3.3 0.6 shard_map.96
  3.9 0.0 copy-start.2
  3.9 3.1 %collective-permute-start.6 = (bf16[320,1024]{1,0:T(8,128)(2,1)S(1)}, bf16[320,1024]{1,0:T(8,128)(2,1)S(1)}, u32[]{:S(2)}, u32[]{:S(2)}) collective-permute-start(bf16[320,1024]{1,0:T(8,128)(2,1)S(1)} %shard_map.96), channel_id=1, source_target_pairs={{0,4},{4,0},{8,12},{12,8},{1,5},{5,1},{9,13},{13,9},{2,6},{6,2},{1... | collective-permute-start | bytes 1966088 | tf_op jit(solution)/shard_map/ppermute | solution.py:119
  7.0 0.0 copy-done.7
  7.0 0.0 copy-done.5
  7.0 0.0 copy-start.4
  7.1 2.7 %collective-permute-start = (bf16[144,512]{1,0:T(8,128)(2,1)S(1)}, bf16[144,512]{1,0:T(8,128)(2,1)S(1)}, u32[]{:S(2)}, u32[]{:S(2)}) collective-permute-start(bf16[144,512]{1,0:T(8,128)(2,1)S(1)} %fusion.1), channel_id=1, source_target_pairs={{0,8},{4,12},{8,0},{12,4},{1,9},{5,13},{9,1},{13,5},{2,10},{6,14},... | collective-permute-start | bytes 442376 | tf_op jit(solution)/shard_map/ppermute | solution.py:119
  9.7 0.0 copy-done.6
  9.7 0.4 collective-permute-start.1
  10.2 0.0 copy-done.1
  10.2 0.6 shard_map.94
  10.8 15.6 %collective-permute-done.1.up_sib = bf16[64,512]{1,0:T(8,128)(2,1)S(1)} collective-permute-done((bf16[64,512]{1,0:T(8,128)(2,1)S(1)}, bf16[64,512]{1,0:T(8,128)(2,1)S(1)}, u32[]{:S(2)}, u32[]{:S(2)}) %collective-permute-start.1) | collective-permute-done | bytes 65568 | tf_op jit(solution)/shard_map/ppermute | solution.py:119
  26.3 0.0 collective-permute-done.cot_got
  26.3 2.0 %collective-permute-start.4 = (bf16[256,1024]{1,0:T(8,128)(2,1)S(1)}, bf16[256,1024]{1,0:T(8,128)(2,1)S(1)}, u32[]{:S(2)}, u32[]{:S(2)}) collective-permute-start(bf16[256,1024]{1,0:T(8,128)(2,1)S(1)} %shard_map.94), channel_id=1, source_target_pairs={{0,4},{4,0},{8,12},{12,8},{1,5},{5,1},{9,13},{13,9},{2,6},{6,2},{1... | collective-permute-start | bytes 1572872 | tf_op jit(solution)/shard_map/ppermute | solution.py:119
  28.4 0.8 shard_map.93
  29.2 1.6 %collective-permute-start.3 = (bf16[256,640]{1,0:T(8,128)(2,1)S(1)}, bf16[256,640]{1,0:T(8,128)(2,1)S(1)}, u32[]{:S(2)}, u32[]{:S(2)}) collective-permute-start(bf16[256,640]{1,0:T(8,128)(2,1)S(1)} %get-tuple-element.37.mine), channel_id=1, source_target_pairs={{0,2},{1,3},{2,0},{3,1},{4,6},{5,7},{6,4},{7,5},{8,10},{9,11},{10,... | collective-permute-start | bytes 983048 | tf_op jit(solution)/shard_map/ppermute | solution.py:119
  30.7 0.0 collective-permute-done.6.first.near
  30.7 1.5 %collective-permute-start.7 = (bf16[320,1024]{1,0:T(8,128)(2,1)S(1)}, bf16[320,1024]{1,0:T(8,128)(2,1)S(1)}, u32[]{:S(2)}, u32[]{:S(2)}) collective-permute-start(bf16[320,1024]{1,0:T(8,128)(2,1)S(1)} %collective-permute-done.6.first.near), channel_id=1, source_target_pairs={{0,16},{16,0},{1,17},{17,1},{2,18},{18,2},{3,19},{19,3},{4,20},{20... | collective-permute-start | bytes 1966088 | tf_op jit(solution)/shard_map/ppermute | solution.py:119
  32.3 2.3 %collective-permute-start.2 = (bf16[128,2048]{1,0:T(8,128)(2,1)S(1)}, bf16[128,2048]{1,0:T(8,128)(2,1)S(1)}, u32[]{:S(2)}, u32[]{:S(2)}) collective-permute-start(bf16[128,2048]{1,0:T(8,128)(2,1)S(1)} %copy-done.2), channel_id=1, source_target_pairs={{0,8},{4,12},{8,0},{12,4},{1,9},{5,13},{9,1},{13,5},{2,10},{6,14},... | collective-permute-start | bytes 1572872 | tf_op jit(solution)/shard_map/ppermute | solution.py:119
  34.5 12.7 %collective-permute-done.4.second = bf16[256,1024]{1,0:T(8,128)(2,1)S(1)} collective-permute-done((bf16[256,1024]{1,0:T(8,128)(2,1)S(1)}, bf16[256,1024]{1,0:T(8,128)(2,1)S(1)}, u32[]{:S(2)}, u32[]{:S(2)}) %collective-permute-start.4) | collective-permute-done | bytes 524320 | tf_op jit(solution)/shard_map/ppermute | solution.py:119
  47.2 2.4 %collective-permute-start.8 = (bf16[256,1024]{1,0:T(8,128)(2,1)S(1)}, bf16[256,1024]{1,0:T(8,128)(2,1)S(1)}, u32[]{:S(2)}, u32[]{:S(2)}) collective-permute-start(bf16[256,1024]{1,0:T(8,128)(2,1)S(1)} %collective-permute-done.4.second), channel_id=1, source_target_pairs={{0,16},{16,0},{1,17},{17,1},{2,18},{18,2},{3,19},{19,3},{4,20},{20... | collective-permute-start | bytes 1572872 | tf_op jit(solution)/shard_map/ppermute | solution.py:119
  49.6 0.0 collective-permute-done.3.got
  49.6 0.6 shard_map.95.mine
  50.2 0.1 collective-permute-start.5
  50.3 1.6 %collective-permute-done.5.got = bf16[256,640]{1,0:T(8,128)(2,1)S(1)} collective-permute-done((bf16[256,640]{1,0:T(8,128)(2,1)S(1)}, bf16[256,640]{1,0:T(8,128)(2,1)S(1)}, u32[]{:S(2)}, u32[]{:S(2)}) %collective-permute-start.5) | collective-permute-done | bytes 327712 | tf_op jit(solution)/shard_map/ppermute | solution.py:119
  51.9 1.8 %shard_map.97 = (bf16[128,1024]{1,0:T(8,128)(2,1)S(1)}, bf16[128,1024]{1,0:T(8,128)(2,1)S(1)}) custom-call(s32[5]{0:T(128)S(1)} %stack.31.where, bf16[256,640]{1,0:T(8,128)(2,1)S(1)} %shard_map.95.mine, bf16[256,640]{1,0:T(8,128)(2,1)S(1)} %collective-permute-done.5.got, bf16[512,2048]{1,0:T(8,128)(2,1)S(1)} %copy-done.1, bf16[64,2048]{1,0:T(8,128)(2,1)S(1)} %bitcast.10, ...), custom_call_target="tpu_custom_call" | custom-call | bytes 1000 | tf_op jit(solution)/shard_map/pallas_call | solution.py:241
  53.8 0.6 collective-permute-start.10
  54.4 1.7 %collective-permute-done.2.act_got = bf16[128,2048]{1,0:T(8,128)(2,1)S(1)} collective-permute-done((bf16[128,2048]{1,0:T(8,128)(2,1)S(1)}, bf16[128,2048]{1,0:T(8,128)(2,1)S(1)}, u32[]{:S(2)}, u32[]{:S(2)}) %collective-permute-start.2) | collective-permute-done | bytes 524320 | tf_op jit(solution)/shard_map/ppermute | solution.py:119
  56.1 1.5 %shard_map.98.part = f32[256,1024]{1,0:T(8,128)S(1)} custom-call(s32[5]{0:T(128)S(1)} %stack.31.where, bf16[128,2048]{1,0:T(8,128)(2,1)S(1)} %copy-done.2, bf16[128,2048]{1,0:T(8,128)(2,1)S(1)} %collective-permute-done.2.act_got, bf16[512,2048]{1,0:T(8,128)(2,1)S(1)} %copy-done.1, bf16[320,1024]{1,0:T(8,128)(2,1)S(1)} %collective-permute-done.6.first.near, ...), custom_call_target="tpu_custom_call" | custom-call | bytes 1000 | tf_op jit(solution)/shard_map/pallas_call | solution.py:140
  57.6 0.0 collective-permute-done.7.far.first
  57.6 1.0 %shard_map.99.low = bf16[256,128]{1,0:T(8,128)(2,1)S(1)} custom-call(s32[5]{0:T(128)S(1)} %stack.31.where, bf16[128,2048]{1,0:T(8,128)(2,1)S(1)} %copy-done.2, bf16[128,2048]{1,0:T(8,128)(2,1)S(1)} %collective-permute-done.2.act_got, bf16[256,128]{1,0:T(8,128)(2,1)S(1)} %get-tuple-element.44.members, bf16[64,2048]{1,0:T(8,128)(2,1)S(1)} %bitcast.11, ...), custom_call_target="tpu_custom_call" | custom-call | bytes 1000 | tf_op jit(solution)/shard_map/pallas_call | solution.py:287
  58.6 0.8 collective-permute-start.9
  59.5 0.3 collective-permute-done.8.second
  59.7 1.8 %shard_map.100 = (bf16[128,1024]{1,0:T(8,128)(2,1)S(1)}, bf16[128,1024]{1,0:T(8,128)(2,1)S(1)}) custom-call(s32[5]{0:T(128)S(1)} %stack.31.where, bf16[256,640]{1,0:T(8,128)(2,1)S(1)} %shard_map.95.mine, bf16[256,640]{1,0:T(8,128)(2,1)S(1)} %collective-permute-done.5.got, bf16[512,2048]{1,0:T(8,128)(2,1)S(1)} %copy-done.1, bf16[64,2048]{1,0:T(8,128)(2,1)S(1)} %bitcast.12, ...), custom_call_target="tpu_custom_call" | custom-call | bytes 1000 | tf_op jit(solution)/shard_map/pallas_call | solution.py:241
  61.6 1.4 %collective-permute-done.9.low_got = bf16[256,128]{1,0:T(8,128)(2,1)S(1)} collective-permute-done((bf16[256,128]{1,0:T(8,128)(2,1)S(1)}, bf16[256,128]{1,0:T(8,128)(2,1)S(1)}, u32[]{:S(2)}, u32[]{:S(2)}) %collective-permute-start.9) | collective-permute-done | bytes 65568 | tf_op jit(solution)/shard_map/ppermute | solution.py:119
  63.0 1.0 %shard_map.101 = (f32[256,512]{1,0:T(8,128)S(1)}, bf16[128,640]{1,0:T(8,128)(2,1)S(1)}, bf16[128,640]{1,0:T(8,128)(2,1)S(1)}) custom-call(s32[5]{0:T(128)S(1)} %stack.31.where, f32[256,1024]{1,0:T(8,128)S(1)} %shard_map.98.part, bf16[128,2048]{1,0:T(8,128)(2,1)S(1)} %copy-done.2, bf16[128,2048]{1,0:T(8,128)(2,1)S(1)} %collective-permute-done.2.act_got, ...), custom_call_target="tpu_custom_call" | custom-call | bytes 1000 | tf_op jit(solution)/shard_map/pallas_call | solution.py:140
  64.0 0.1 collective-permute-start.12
  64.1 0.5 collective-permute-start.11
  64.6 1.1 %collective-permute-start.16 = (bf16[128,1024]{1,0:T(8,128)(2,1)S(1)}, bf16[128,1024]{1,0:T(8,128)(2,1)S(1)}, u32[]{:S(2)}, u32[]{:S(2)}) collective-permute-start(bf16[128,1024]{1,0:T(8,128)(2,1)S(1)} %get-tuple-element.46), channel_id=1, source_target_pairs={{0,8},{4,12},{8,0},{12,4},{1,9},{5,13},{9,1},{13,5},{2,10},{6,14},... | collective-permute-start | bytes 786440 | tf_op jit(solution)/shard_map/ppermute | solution.py:119
  65.7 2.9 %collective-permute-done.10.near_got = bf16[128,1024]{1,0:T(8,128)(2,1)S(1)} collective-permute-done((bf16[128,1024]{1,0:T(8,128)(2,1)S(1)}, bf16[128,1024]{1,0:T(8,128)(2,1)S(1)}, u32[]{:S(2)}, u32[]{:S(2)}) %collective-permute-start.10) | collective-permute-done | bytes 262176 | tf_op jit(solution)/shard_map/ppermute | solution.py:119
  68.6 0.0 collective-permute-done.12.got2.give_got2
  68.6 0.0 collective-permute-done.11.got.give_got
  68.6 0.6 shard_map.102
  69.2 1.3 %collective-permute-start.14 = (bf16[128,512]{1,0:T(8,128)(2,1)S(1)}, bf16[128,512]{1,0:T(8,128)(2,1)S(1)}, u32[]{:S(2)}, u32[]{:S(2)}) collective-permute-start(bf16[128,512]{1,0:T(8,128)(2,1)S(1)} %get-tuple-element.55.held), channel_id=1, source_target_pairs={{2,0},{3,1},{6,4},{7,5},{8,10},{9,11},{12,14},{13,15},{18,16},{19,... | collective-permute-start | bytes 393224 | tf_op jit(solution)/shard_map/ppermute | solution.py:124
  70.5 0.9 %shard_map.103 = (bf16[128,512]{1,0:T(8,128)(2,1)S(1)}, bf16[128,512]{1,0:T(8,128)(2,1)S(1)}, f32[64,2048]{1,0:T(8,128)S(1)}, f32[64,512]{1,0:T(8,128)S(1)}, bf1...) custom-call(s32[5]{0:T(128)S(1)} %stack.31.where, bf16[128,640]{1,0:T(8,128)(2,1)S(1)} %get-tuple-element.49.give, ...), custom_call_target="tpu_custom_call" | custom-call | bytes 1000 | tf_op jit(solution)/shard_map/pallas_call | solution.py:140
  71.5 0.1 collective-permute-start.17
  71.5 2.0 %collective-permute-start.18 = (bf16[64,1280]{1,0:T(8,128)(2,1)S(1)}, bf16[64,1280]{1,0:T(8,128)(2,1)S(1)}, u32[]{:S(2)}, u32[]{:S(2)}) collective-permute-start(bf16[64,1280]{1,0:T(8,128)(2,1)S(1)} %get-tuple-element.63), channel_id=1, source_target_pairs={{0,4},{4,0},{8,12},{12,8},{1,5},{5,1},{9,13},{13,9},{2,6},{6,2},{1... | collective-permute-start | bytes 491528 | tf_op jit(solution)/shard_map/ppermute | solution.py:119
  73.5 1.3 %collective-permute-start.13 = (bf16[128,512]{1,0:T(8,128)(2,1)S(1)}, bf16[128,512]{1,0:T(8,128)(2,1)S(1)}, u32[]{:S(2)}, u32[]{:S(2)}) collective-permute-start(bf16[128,512]{1,0:T(8,128)(2,1)S(1)} %get-tuple-element.52.held), channel_id=1, source_target_pairs={{2,0},{3,1},{6,4},{7,5},{8,10},{9,11},{12,14},{13,15},{18,16},{19,... | collective-permute-start | bytes 393224 | tf_op jit(solution)/shard_map/ppermute | solution.py:124
  74.8 6.8 %collective-permute-done.14.got = bf16[128,512]{1,0:T(8,128)(2,1)S(1)} collective-permute-done((bf16[128,512]{1,0:T(8,128)(2,1)S(1)}, bf16[128,512]{1,0:T(8,128)(2,1)S(1)}, u32[]{:S(2)}, u32[]{:S(2)}) %collective-permute-start.14) | collective-permute-done | bytes 131104 | tf_op jit(solution)/shard_map/ppermute | solution.py:124
  81.6 0.6 shard_map.104
  82.2 2.2 %collective-permute-start.15 = (bf16[128,512]{1,0:T(8,128)(2,1)S(1)}, bf16[128,512]{1,0:T(8,128)(2,1)S(1)}, u32[]{:S(2)}, u32[]{:S(2)}) collective-permute-start(bf16[128,512]{1,0:T(8,128)(2,1)S(1)} %shard_map.104), channel_id=1, source_target_pairs={{0,8},{4,12},{8,0},{12,4},{1,9},{5,13},{9,1},{13,5},{2,10},{6,14},... | collective-permute-start | bytes 393224 | tf_op jit(solution)/shard_map/ppermute | solution.py:119
  84.4 0.0 collective-permute-done.16.far_got
  84.4 1.5 %shard_map.106 = bf16[128,2048]{1,0:T(8,128)(2,1)} custom-call(s32[5]{0:T(128)S(1)} %stack.31.where, bf16[128,1024]{1,0:T(8,128)(2,1)S(1)} %get-tuple-element.57.near, bf16[128,1024]{1,0:T(8,128)(2,1)S(1)} %collective-permute-done.10.near_got, bf16[128,1024]{1,0:T(8,128)(2,1)S(1)} %get-tuple-element.59.far, bf16[128,1024]{1,0:T(8,128)(2,1)S(1)} %collective-permute-done.16.far_got), custom_call_target="tpu_custom_call" | custom-call | bytes 1000 | tf_op jit(solution)/shard_map/pallas_call | solution.py:140
  85.9 0.0 collective-permute-done.17.got
  85.9 3.2 %collective-permute-done.18.got_end = bf16[64,1280]{1,0:T(8,128)(2,1)S(1)} collective-permute-done((bf16[64,1280]{1,0:T(8,128)(2,1)S(1)}, bf16[64,1280]{1,0:T(8,128)(2,1)S(1)}, u32[]{:S(2)}, u32[]{:S(2)}) %collective-permute-start.18) | collective-permute-done | bytes 163872 | tf_op jit(solution)/shard_map/ppermute | solution.py:119
  89.1 1.4 %shard_map.107 = (f32[1,64,2048]{2,1,0:T(8,128)}, f32[1,64,512]{2,1,0:T(8,128)}) custom-call(s32[5]{0:T(128)S(1)} %stack.31.where, f32[64,2048]{1,0:T(8,128)S(1)} %get-tuple-element.60.down_own, f32[64,512]{1,0:T(8,128)S(1)} %get-tuple-element.61.up_own, bf16[64,1280]{1,0:T(8,128)(2,1)S(1)} %collective-permute-done.17.got, ...), custom_call_target="tpu_custom_call" | custom-call | bytes 1000 | tf_op jit(solution)/shard_map/pallas_call | solution.py:140
  90.5 0.0 collective-permute-done.13.got
  90.5 0.0 collective-permute-done.15.turned
  90.6 1.3 %shard_map.105 = bf16[128,512]{1,0:T(8,128)(2,1)} custom-call(s32[5]{0:T(128)S(1)} %stack.31.where, bf16[128,512]{1,0:T(8,128)(2,1)S(1)} %get-tuple-element.52.held, bf16[128,512]{1,0:T(8,128)(2,1)S(1)} %collective-permute-done.13.got, bf16[128,512]{1,0:T(8,128)(2,1)S(1)} %get-tuple-element.54.lora, bf16[128,512]{1,0:T(8,128)(2,1)S(1)} %collective-permute-done.15.turned), custom_call_target="tpu_custom_call" | custom-call | bytes 1000 | tf_op jit(solution)/shard_map/pallas_call | solution.py:140
  (8 shorter events, 0.0 us)
Async XLA Ops:
  0.6 6.4 %copy-start.7 = (s32[128,1]{0,1:T(1,128)S(1)}, s32[128,1]{0,1:T(1,128)}, u32[]{:S(2)}) copy-start(s32[128,1]{0,1:T(1,128)} %param.8) | copy-start | bytes 1540
  0.6 9.1 %copy-start.6 = (bf16[1,64,512]{2,1,0:T(8,128)(2,1)S(1)}, bf16[1,64,512]{2,1,0:T(8,128)(2,1)}, u32[]{:S(2)}) copy-start(bf16[1,64,512]{2,1,0:T(8,128)(2,1)} %param.10) | copy-start | bytes 196612
  0.8 1.6 %copy-start = (bf16[512,2048]{1,0:T(8,128)(2,1)S(1)}, bf16[512,2048]{1,0:T(8,128)(2,1)}, u32[]{:S(2)}) copy-start(bf16[512,2048]{1,0:T(8,128)(2,1)} %weight.5) | copy-start | bytes 6291460
  2.4 0.9 %copy-start.3 = (bf16[1,64,2048]{2,1,0:T(8,128)(2,1)S(1)}, bf16[1,64,2048]{2,1,0:T(8,128)(2,1)}, u32[]{:S(2)}) copy-start(bf16[1,64,2048]{2,1,0:T(8,128)(2,1)} %param.9) | copy-start | bytes 786436
  3.3 3.7 %copy-start.5 = (bf16[128,512]{1,0:T(8,128)(2,1)S(1)}, bf16[128,512]{1,0:T(8,128)(2,1)}, u32[]{:S(2)}) copy-start(bf16[128,512]{1,0:T(8,128)(2,1)} %cot.3) | copy-start | bytes 393220
  3.3 6.8 %copy-start.1 = (bf16[512,2048]{1,0:T(8,128)(2,1)S(1)}, bf16[512,2048]{1,0:T(8,128)(2,1)}, u32[]{:S(2)}) copy-start(bf16[512,2048]{1,0:T(8,128)(2,1)} %weight.5) | copy-start | bytes 6291460
  3.9 28.3 %copy-start.2 = (bf16[128,2048]{1,0:T(8,128)(2,1)S(1)}, bf16[128,2048]{1,0:T(8,128)(2,1)}, u32[]{:S(2)}) copy-start(bf16[128,2048]{1,0:T(8,128)(2,1)} %act.7) | copy-start | bytes 1572868
  3.9 26.8 %collective-permute-start.6 = (bf16[320,1024]{1,0:T(8,128)(2,1)S(1)}, bf16[320,1024]{1,0:T(8,128)(2,1)S(1)}, u32[]{:S(2)}, u32[]{:S(2)}) collective-permute-start(bf16[320,1024]{1,0:T(8,128)(2,1)S(1)} %shard_map.96), channel_id=1, source_target_pairs={{0,4},{4,0},{8,12},{12,8},{1,5},{5,1},{9,13},{13,9},{2,6},{6,2},{1... | collective-permute-start | bytes 1966088 | tf_op jit(solution)/shard_map/ppermute | solution.py:119
  7.0 44.9 %copy-start.4 = (bf16[1,64,2048]{2,1,0:T(8,128)(2,1)S(1)}, bf16[1,64,2048]{2,1,0:T(8,128)(2,1)}, u32[]{:S(2)}) copy-start(bf16[1,64,2048]{2,1,0:T(8,128)(2,1)} %param.9) | copy-start | bytes 786436
  7.1 19.3 %collective-permute-start = (bf16[144,512]{1,0:T(8,128)(2,1)S(1)}, bf16[144,512]{1,0:T(8,128)(2,1)S(1)}, u32[]{:S(2)}, u32[]{:S(2)}) collective-permute-start(bf16[144,512]{1,0:T(8,128)(2,1)S(1)} %fusion.1), channel_id=1, source_target_pairs={{0,8},{4,12},{8,0},{12,4},{1,9},{5,13},{9,1},{13,5},{2,10},{6,14},... | collective-permute-start | bytes 442376 | tf_op jit(solution)/shard_map/ppermute | solution.py:119
  9.7 16.6 %collective-permute-start.1 = (bf16[64,512]{1,0:T(8,128)(2,1)S(1)}, bf16[64,512]{1,0:T(8,128)(2,1)S(1)}, u32[]{:S(2)}, u32[]{:S(2)}) collective-permute-start(bf16[64,512]{1,0:T(8,128)(2,1)S(1)} %bitcast.13), channel_id=1, source_target_pairs={{0,4},{4,0},{8,12},{12,8},{1,5},{5,1},{9,13},{13,9},{2,6},{6,2},{1... | collective-permute-start | bytes 196616 | tf_op jit(solution)/shard_map/ppermute | solution.py:119
  26.3 20.9 %collective-permute-start.4 = (bf16[256,1024]{1,0:T(8,128)(2,1)S(1)}, bf16[256,1024]{1,0:T(8,128)(2,1)S(1)}, u32[]{:S(2)}, u32[]{:S(2)}) collective-permute-start(bf16[256,1024]{1,0:T(8,128)(2,1)S(1)} %shard_map.94), channel_id=1, source_target_pairs={{0,4},{4,0},{8,12},{12,8},{1,5},{5,1},{9,13},{13,9},{2,6},{6,2},{1... | collective-permute-start | bytes 1572872 | tf_op jit(solution)/shard_map/ppermute | solution.py:119
  29.2 20.4 %collective-permute-start.3 = (bf16[256,640]{1,0:T(8,128)(2,1)S(1)}, bf16[256,640]{1,0:T(8,128)(2,1)S(1)}, u32[]{:S(2)}, u32[]{:S(2)}) collective-permute-start(bf16[256,640]{1,0:T(8,128)(2,1)S(1)} %get-tuple-element.37.mine), channel_id=1, source_target_pairs={{0,2},{1,3},{2,0},{3,1},{4,6},{5,7},{6,4},{7,5},{8,10},{9,11},{10,... | collective-permute-start | bytes 983048 | tf_op jit(solution)/shard_map/ppermute | solution.py:119
  30.7 26.9 %collective-permute-start.7 = (bf16[320,1024]{1,0:T(8,128)(2,1)S(1)}, bf16[320,1024]{1,0:T(8,128)(2,1)S(1)}, u32[]{:S(2)}, u32[]{:S(2)}) collective-permute-start(bf16[320,1024]{1,0:T(8,128)(2,1)S(1)} %collective-permute-done.6.first.near), channel_id=1, source_target_pairs={{0,16},{16,0},{1,17},{17,1},{2,18},{18,2},{3,19},{19,3},{4,20},{20... | collective-permute-start | bytes 1966088 | tf_op jit(solution)/shard_map/ppermute | solution.py:119
  32.3 23.8 %collective-permute-start.2 = (bf16[128,2048]{1,0:T(8,128)(2,1)S(1)}, bf16[128,2048]{1,0:T(8,128)(2,1)S(1)}, u32[]{:S(2)}, u32[]{:S(2)}) collective-permute-start(bf16[128,2048]{1,0:T(8,128)(2,1)S(1)} %copy-done.2), channel_id=1, source_target_pairs={{0,8},{4,12},{8,0},{12,4},{1,9},{5,13},{9,1},{13,5},{2,10},{6,14},... | collective-permute-start | bytes 1572872 | tf_op jit(solution)/shard_map/ppermute | solution.py:119
  47.2 12.5 %collective-permute-start.8 = (bf16[256,1024]{1,0:T(8,128)(2,1)S(1)}, bf16[256,1024]{1,0:T(8,128)(2,1)S(1)}, u32[]{:S(2)}, u32[]{:S(2)}) collective-permute-start(bf16[256,1024]{1,0:T(8,128)(2,1)S(1)} %collective-permute-done.4.second), channel_id=1, source_target_pairs={{0,16},{16,0},{1,17},{17,1},{2,18},{18,2},{3,19},{19,3},{4,20},{20... | collective-permute-start | bytes 1572872 | tf_op jit(solution)/shard_map/ppermute | solution.py:119
  50.2 1.7 %collective-permute-start.5 = (bf16[256,640]{1,0:T(8,128)(2,1)S(1)}, bf16[256,640]{1,0:T(8,128)(2,1)S(1)}, u32[]{:S(2)}, u32[]{:S(2)}) collective-permute-start(bf16[256,640]{1,0:T(8,128)(2,1)S(1)} %shard_map.95.mine), channel_id=1, source_target_pairs={{0,1},{1,0},{2,3},{3,2},{4,5},{5,4},{6,7},{7,6},{8,9},{9,8},{10,11... | collective-permute-start | bytes 983048 | tf_op jit(solution)/shard_map/ppermute | solution.py:119
  53.8 14.8 %collective-permute-start.10 = (bf16[128,1024]{1,0:T(8,128)(2,1)S(1)}, bf16[128,1024]{1,0:T(8,128)(2,1)S(1)}, u32[]{:S(2)}, u32[]{:S(2)}) collective-permute-start(bf16[128,1024]{1,0:T(8,128)(2,1)S(1)} %get-tuple-element.41), channel_id=1, source_target_pairs={{0,8},{4,12},{8,0},{12,4},{1,9},{5,13},{9,1},{13,5},{2,10},{6,14},... | collective-permute-start | bytes 786440 | tf_op jit(solution)/shard_map/ppermute | solution.py:119
  58.6 4.3 %collective-permute-start.9 = (bf16[256,128]{1,0:T(8,128)(2,1)S(1)}, bf16[256,128]{1,0:T(8,128)(2,1)S(1)}, u32[]{:S(2)}, u32[]{:S(2)}) collective-permute-start(bf16[256,128]{1,0:T(8,128)(2,1)S(1)} %shard_map.99.low), channel_id=1, source_target_pairs={{0,2},{1,3},{2,0},{3,1},{4,6},{5,7},{6,4},{7,5},{8,10},{9,11},{10,... | collective-permute-start | bytes 196616 | tf_op jit(solution)/shard_map/ppermute | solution.py:119
  64.0 4.6 %collective-permute-start.12 = (bf16[128,640]{1,0:T(8,128)(2,1)S(1)}, bf16[128,640]{1,0:T(8,128)(2,1)S(1)}, u32[]{:S(2)}, u32[]{:S(2)}) collective-permute-start(bf16[128,640]{1,0:T(8,128)(2,1)S(1)} %get-tuple-element.51.give2), channel_id=1, source_target_pairs={{0,1},{1,0},{2,3},{3,2},{4,5},{5,4},{6,7},{7,6},{8,9},{9,8},{10,11... | collective-permute-start | bytes 491528 | tf_op jit(solution)/shard_map/ppermute | solution.py:119
  64.1 4.5 %collective-permute-start.11 = (bf16[128,640]{1,0:T(8,128)(2,1)S(1)}, bf16[128,640]{1,0:T(8,128)(2,1)S(1)}, u32[]{:S(2)}, u32[]{:S(2)}) collective-permute-start(bf16[128,640]{1,0:T(8,128)(2,1)S(1)} %get-tuple-element.49.give), channel_id=1, source_target_pairs={{0,1},{1,0},{2,3},{3,2},{4,5},{5,4},{6,7},{7,6},{8,9},{9,8},{10,11... | collective-permute-start | bytes 491528 | tf_op jit(solution)/shard_map/ppermute | solution.py:119
  64.6 19.9 %collective-permute-start.16 = (bf16[128,1024]{1,0:T(8,128)(2,1)S(1)}, bf16[128,1024]{1,0:T(8,128)(2,1)S(1)}, u32[]{:S(2)}, u32[]{:S(2)}) collective-permute-start(bf16[128,1024]{1,0:T(8,128)(2,1)S(1)} %get-tuple-element.46), channel_id=1, source_target_pairs={{0,8},{4,12},{8,0},{12,4},{1,9},{5,13},{9,1},{13,5},{2,10},{6,14},... | collective-permute-start | bytes 786440 | tf_op jit(solution)/shard_map/ppermute | solution.py:119
  69.2 12.4 %collective-permute-start.14 = (bf16[128,512]{1,0:T(8,128)(2,1)S(1)}, bf16[128,512]{1,0:T(8,128)(2,1)S(1)}, u32[]{:S(2)}, u32[]{:S(2)}) collective-permute-start(bf16[128,512]{1,0:T(8,128)(2,1)S(1)} %get-tuple-element.55.held), channel_id=1, source_target_pairs={{2,0},{3,1},{6,4},{7,5},{8,10},{9,11},{12,14},{13,15},{18,16},{19,... | collective-permute-start | bytes 393224 | tf_op jit(solution)/shard_map/ppermute | solution.py:124
  71.5 14.4 %collective-permute-start.17 = (bf16[64,1280]{1,0:T(8,128)(2,1)S(1)}, bf16[64,1280]{1,0:T(8,128)(2,1)S(1)}, u32[]{:S(2)}, u32[]{:S(2)}) collective-permute-start(bf16[64,1280]{1,0:T(8,128)(2,1)S(1)} %get-tuple-element.62), channel_id=1, source_target_pairs={{0,4},{4,0},{8,12},{12,8},{1,5},{5,1},{9,13},{13,9},{2,6},{6,2},{1... | collective-permute-start | bytes 491528 | tf_op jit(solution)/shard_map/ppermute | solution.py:119
  71.5 17.6 %collective-permute-start.18 = (bf16[64,1280]{1,0:T(8,128)(2,1)S(1)}, bf16[64,1280]{1,0:T(8,128)(2,1)S(1)}, u32[]{:S(2)}, u32[]{:S(2)}) collective-permute-start(bf16[64,1280]{1,0:T(8,128)(2,1)S(1)} %get-tuple-element.63), channel_id=1, source_target_pairs={{0,4},{4,0},{8,12},{12,8},{1,5},{5,1},{9,13},{13,9},{2,6},{6,2},{1... | collective-permute-start | bytes 491528 | tf_op jit(solution)/shard_map/ppermute | solution.py:119
  73.5 17.0 %collective-permute-start.13 = (bf16[128,512]{1,0:T(8,128)(2,1)S(1)}, bf16[128,512]{1,0:T(8,128)(2,1)S(1)}, u32[]{:S(2)}, u32[]{:S(2)}) collective-permute-start(bf16[128,512]{1,0:T(8,128)(2,1)S(1)} %get-tuple-element.52.held), channel_id=1, source_target_pairs={{2,0},{3,1},{6,4},{7,5},{8,10},{9,11},{12,14},{13,15},{18,16},{19,... | collective-permute-start | bytes 393224 | tf_op jit(solution)/shard_map/ppermute | solution.py:124
  82.2 8.4 %collective-permute-start.15 = (bf16[128,512]{1,0:T(8,128)(2,1)S(1)}, bf16[128,512]{1,0:T(8,128)(2,1)S(1)}, u32[]{:S(2)}, u32[]{:S(2)}) collective-permute-start(bf16[128,512]{1,0:T(8,128)(2,1)S(1)} %shard_map.104), channel_id=1, source_target_pairs={{0,8},{4,12},{8,0},{12,4},{1,9},{5,13},{9,1},{13,5},{2,10},{6,14},... | collective-permute-start | bytes 393224 | tf_op jit(solution)/shard_map/ppermute | solution.py:119
